TPU v7x, 32 devices: a whole 2x2x4 slice. The times are simulated.
32 devices in a mesh: sub: 8 (over z, y), rep: 4 (over x, core).
Axes of the slice: x: 2, y: 2, z: 4, core: 2. Of those that a mesh axis runs over, the one named last changes fastest.
Arguments:
- regions: bfloat16 [512, 128, 256], P('rep', 'sub'), may hold values from -6 to 6
- leaf_map: int32 [128], P('sub'), may hold values from 0 to 15, as said below
- leaf_bond_weight: bfloat16 [32, 4, 256, 1024], P(('sub', 'rep')), may hold values from -0.375 to 0.375
- mid_weight: bfloat16 [8, 4, 1024, 1024], P('sub', 'rep'), may hold values from -0.1875 to 0.1875
- upper_weight: bfloat16 [8, 1024, 2, 1024], P('sub'), may hold values from -0.1875 to 0.1875
- head_cotangent: float32 [512, 1024], P('rep', 'sub'), may hold values from -0.75 to 0.75
Outputs:
- leaf_grad: bfloat16 [32, 4, 256, 1024], P(('sub', 'rep'))
- middle_weight_gradient: bfloat16 [8, 4, 1024, 1024], P('sub', 'rep')
- upper_grad: bfloat16 [8, 1024, 2, 1024], P('sub', 'rep')
Inputs may be any that keep to these rules, and one draw needn't show every extreme that they name: `leaf_map`: each aligned block of 16 entries is a permutation of 0 .. 15.
All inputs are finite; a program needn't handle non-finite values.
Results may differ from a plain program's by a relative error of at most 0.04.
Values may be sent and summed in bfloat16 or wider, within the bound.
No kernel may reach another device: no remote copies, remote signals or barrier semaphores. Data moves between devices by JAX's collectives and lax.ppermute only.
A program may use at most 128 MiB of HBM per device.

v0:
```python
import jax
import jax.numpy as jnp
from jax import lax
from jax.sharding import PartitionSpec as P

EPSILON = 1e-06


def partner(value, axis, bit):
    return lax.ppermute(value, axis, [(i, i ^ 1 << bit) for i in range(lax.axis_size(axis))])


def rms_factor(values):
    return lax.rsqrt(jnp.mean(values * values, axis=-1, keepdims=True) + EPSILON)


def norm_back(gradient, normed, factor):
    return factor * (gradient - normed * jnp.mean(gradient * normed, axis=-1, keepdims=True))


def product_of(factors):
    running = factors[..., 0, :]
    for position in range(1, factors.shape[-2]):
        running = running * factors[..., position, :]
    return running


def leave_one(factors):
    how_many = factors.shape[-2]
    results = []
    for position in range(how_many):
        remaining = [
            factors[..., partner_idx, :]
            for partner_idx in range(how_many)
            if partner_idx != position
        ]
        running = remaining[0]
        for factor in remaining[1:]:
            running = running * factor
        results.append(running)
    return jnp.stack(results, axis=-2)


def matmul(left_arr, right_arr):
    return jnp.dot(left_arr, right_arr, preferred_element_type=jnp.float32)


def matmul_t(left_arr, right_arr):
    return lax.dot_general(
        left_arr, right_arr, (((1,), (1,)), ((), ())), preferred_element_type=jnp.float32
    )


def inner_t(left_arr, right_arr):
    return lax.dot_general(
        left_arr, right_arr, (((0,), (0,)), ((), ())), preferred_element_type=jnp.float32
    )


def block_terms(inputs_rows, grads_all, widths):
    segments = []
    column = 0
    for level_pos in range(len(widths)):
        span = widths[level_pos]
        segments.append(
            jnp.einsum(
                "bsr,bsc->rsc",
                inputs_rows[:, level_pos],
                grads_all[:, :, column : column + span],
                preferred_element_type=jnp.float32,
            )
        )
        column = column + span
    return jnp.concatenate(segments, axis=-1)


def on_device(regions, leaf_map, leaf_bond_weight, mid_weight, upper_weight, head_cotangent):
    rows_dev = regions.shape[0]
    features = regions.shape[2]
    bond_width = upper_weight.shape[1]
    sub_count = lax.axis_size("sub")
    tree_depth = sub_count.bit_length() - 1
    sub_index = lax.axis_index("sub")
    placed = jnp.take(regions, leaf_map, axis=1).reshape(rows_dev, 4, 4, features)
    leaf_region_input = lax.all_to_all(placed, "rep", split_axis=1, concat_axis=0, tiled=True)[:, 0]
    leaf_terms = jnp.einsum(
        "zyu,yul->zyl", leaf_region_input, leaf_bond_weight[0], preferred_element_type=jnp.float32
    )
    leaf_prod = product_of(1.0 + leaf_terms)
    leaf_scale = rms_factor(leaf_prod)
    leaf_norm = leaf_prod * leaf_scale
    leaf_message_rows = leaf_norm.astype(jnp.bfloat16)
    mid_local = matmul(leaf_message_rows, mid_weight[0, 0]).astype(jnp.bfloat16)
    middle_node_terms = lax.all_to_all(
        mid_local[:, None, :], "rep", split_axis=0, concat_axis=1, tiled=True
    )
    mid_factors = 1.0 + middle_node_terms.astype(jnp.float32)
    mid_prod = product_of(mid_factors)
    mid_scale = rms_factor(mid_prod)
    mid_norm = mid_prod * mid_scale
    message = mid_norm.astype(jnp.bfloat16)
    maps = upper_weight[0]
    widths = []
    saved = []
    for tier_level in range(tree_depth):
        group_size = 2 ** (tier_level + 1)
        block_width = bond_width // group_size
        first_col = bond_width - 2 * block_width
        widths.append(block_width)
        sibling = partner(message, "sub", tier_level)
        is_right = (sub_index >> tier_level) % 2 == 1
        left_msg = jnp.where(is_right, sibling, message)
        right_msg = jnp.where(is_right, message, sibling)
        pieces = jnp.stack(
            [
                matmul(left_msg, maps[:, 0, first_col : first_col + block_width]),
                matmul(right_msg, maps[:, 1, first_col : first_col + block_width]),
            ],
            axis=0,
        )
        for bit_pos in range(tier_level + 1):
            other = partner(pieces.astype(jnp.bfloat16), "sub", bit_pos).astype(pieces.dtype)
            upper_side = (sub_index >> bit_pos) % 2 == 1
            pieces = jnp.where(
                upper_side,
                jnp.concatenate([other, pieces], axis=-1),
                jnp.concatenate([pieces, other], axis=-1),
            )
        up_left = pieces[0]
        up_right = pieces[1]
        joined = (1.0 + up_left) * (1.0 + up_right)
        scaling = rms_factor(joined)
        message = (joined * scaling).astype(jnp.bfloat16)
        saved.append((left_msg, right_msg, up_left, up_right, scaling))
    head_width = bond_width // sub_count
    head_col = bond_width - head_width
    head_left = maps[:, 0, head_col:]
    head_right = maps[:, 1, head_col:]
    head_value = matmul(message, head_left)
    gating = jax.nn.sigmoid(matmul(message, head_right))
    grad_value = (head_cotangent * gating).astype(jnp.bfloat16)
    grad_gate = (head_cotangent * head_value * gating * (1.0 - gating)).astype(jnp.bfloat16)
    root_term = matmul_t(grad_value, head_left) + matmul_t(grad_gate, head_right)
    grad_msg = lax.psum(root_term.astype(jnp.bfloat16), "sub").astype(jnp.float32)
    grad_blocks = [None] * tree_depth
    for tier_level in reversed(range(tree_depth)):
        group_size = 2 ** (tier_level + 1)
        block_width = bond_width // group_size
        first_col = bond_width - 2 * block_width
        left_msg, right_msg, up_left, up_right, scaling = saved[tier_level]
        normed = (1.0 + up_left) * (1.0 + up_right) * scaling
        joined_grad = norm_back(grad_msg, normed, scaling)
        grad_left = (joined_grad * (1.0 + up_right)).astype(jnp.bfloat16)
        grad_right = (joined_grad * (1.0 + up_left)).astype(jnp.bfloat16)
        own_start = sub_index % group_size * block_width
        left_block = lax.dynamic_slice_in_dim(grad_left, own_start, block_width, 1)
        right_block = lax.dynamic_slice_in_dim(grad_right, own_start, block_width, 1)
        grad_blocks[tier_level] = jnp.stack([left_block, right_block], axis=1)
        sums = jnp.stack(
            [
                matmul_t(left_block, maps[:, 0, first_col : first_col + block_width]),
                matmul_t(right_block, maps[:, 1, first_col : first_col + block_width]),
            ],
            axis=0,
        )
        for bit_pos in range(tier_level + 1):
            sums = sums + partner(sums.astype(jnp.bfloat16), "sub", bit_pos).astype(sums.dtype)
        is_right = (sub_index >> tier_level) % 2 == 1
        grad_msg = jnp.where(is_right, sums[1], sums[0])
    sub_back = norm_back(grad_msg, mid_norm, mid_scale)
    middle_gradient_list = (sub_back[:, None, :] * leave_one(mid_factors)).astype(jnp.bfloat16)
    child_grad = lax.all_to_all(
        middle_gradient_list, "rep", split_axis=1, concat_axis=0, tiled=True
    )[:, 0]
    middle_weight_gradient = inner_t(leaf_message_rows, child_grad).astype(jnp.bfloat16)[None, None]
    leaf_backward_pass = matmul_t(child_grad, mid_weight[0, 0])
    node_back = norm_back(leaf_backward_pass, leaf_norm, leaf_scale)
    leaf_weight_gradients = (node_back[:, None, :] * leave_one(1.0 + leaf_terms)).astype(
        jnp.bfloat16
    )
    leaf_grad = jnp.einsum(
        "yor,yon->orn", leaf_region_input, leaf_weight_gradients, preferred_element_type=jnp.float32
    ).astype(jnp.bfloat16)[None]
    widths.append(head_width)
    inputs_all = jnp.stack(
        [jnp.stack([entry[0], entry[1]], axis=1) for entry in saved]
        + [jnp.stack([message, message], axis=1)],
        axis=1,
    )
    grads_all = jnp.concatenate(grad_blocks + [jnp.stack([grad_value, grad_gate], axis=1)], axis=-1)
    upper_sum = lax.psum_scatter(
        block_terms(inputs_all, grads_all, widths).astype(jnp.bfloat16),
        "rep",
        scatter_dimension=0,
        tiled=True,
    )
    return (leaf_grad, middle_weight_gradient, upper_sum[None])


def solution(mesh):
    placed = (
        P("rep", "sub", None),
        P("sub"),
        P(("sub", "rep"), None, None, None),
        P("sub", "rep", None, None),
        P("sub", None, None, None),
        P("rep", "sub"),
    )
    return jax.shard_map(
        on_device,
        mesh=mesh,
        in_specs=placed,
        out_specs=(
            P(("sub", "rep"), None, None, None),
            P("sub", "rep", None, None),
            P("sub", "rep", None, None),
        ),
        check_vma=False,
    )
```

profile of v0, /device:TPU:0, one launch (start us, length us, event | category | flops | bytes accessed | tf_op | source)
XLA Modules:
  0.0 383.2 jit_solution(7617573988643199937)
XLA Ops:
  8.7 3.7 gather_fusion
  15.2 18.5 %all_to_all.39 = bf16[128,4,4,256]{3,0,2,1:T(8,128)(2,1)S(1)} all-to-all(bf16[128,4,4,256]{3,0,2,1:T(8,128)(2,1)S(1)} %broadcast_select_fusion), channel_id=1, replica_groups=mesh['sub'=8,'rep'=4] {'rep'}, dimensions={1} | all-to-all | bytes 2097152 | tf_op jit(solution)/shard_map/all_to_all | solution.py:85
  37.8 2.4 copy-done.2
  44.3 16.9 %all_to_all.40 = bf16[4,2,65536]{2,1,0:T(2,128)(2,1)S(1)} all-to-all(bf16[4,2,65536]{2,1,0:T(2,128)(2,1)S(1)} %reshape.236), channel_id=1, replica_groups=mesh['sub'=8,'rep'=4] {'rep'}, dimensions={0} | all-to-all | bytes 2097152 | tf_op jit(solution)/shard_map/all_to_all | solution.py:94
  62.2 2.2 convert_add_fusion
  68.3 5.6 %copy.52 = bf16[1,1024,2,1024]{3,1,2,0:T(8,128)(2,1)} copy(bf16[1,1024,2,1024]{3,2,1,0:T(2,128)(2,1)} %param.10) | data formatting | bytes 8388608 | tf_op args[4]
  79.2 5.3 %collective-permute-done.1 = bf16[2,128,512]{2,1,0:T(8,128)(2,1)S(1)} collective-permute-done((bf16[2,128,512]{2,1,0:T(8,128)(2,1)S(1)}, bf16[2,128,512]{2,1,0:T(8,128)(2,1)S(1)}, u32[]{:S(2)}, u32[]{:S(2)}) %collective-permute-start.1) | collective-permute-done | bytes 262176 | tf_op jit(solution)/shard_map/ppermute | solution.py:10
  86.6 4.8 %collective-permute-done.2 = bf16[128,1024]{1,0:T(8,128)(2,1)S(1)} collective-permute-done((bf16[128,1024]{1,0:T(8,128)(2,1)S(1)}, bf16[128,1024]{1,0:T(8,128)(2,1)S(1)}, u32[]{:S(2)}, u32[]{:S(2)}) %collective-permute-start.2) | collective-permute-done | bytes 262176 | tf_op jit(solution)/shard_map/ppermute | solution.py:10
  95.6 3.5 collective-permute-done.3
  100.9 7.4 %collective-permute-done.4 = bf16[2,128,512]{2,1,0:T(8,128)(2,1)S(1)} collective-permute-done((bf16[2,128,512]{2,1,0:T(8,128)(2,1)S(1)}, bf16[2,128,512]{2,1,0:T(8,128)(2,1)S(1)}, u32[]{:S(2)}, u32[]{:S(2)}) %collective-permute-start.4) | collective-permute-done | bytes 262176 | tf_op jit(solution)/shard_map/ppermute | solution.py:10
  108.8 2.7 collective-permute-start.5
  111.6 7.4 %collective-permute-done.5 = bf16[128,1024]{1,0:T(8,128)(2,1)S(1)} collective-permute-done((bf16[128,1024]{1,0:T(8,128)(2,1)S(1)}, bf16[128,1024]{1,0:T(8,128)(2,1)S(1)}, u32[]{:S(2)}, u32[]{:S(2)}) %collective-permute-start.5) | collective-permute-done | bytes 262176 | tf_op jit(solution)/shard_map/ppermute | solution.py:10
  123.1 2.7 collective-permute-done.6
  125.9 5.0 %collective-permute-done.7 = bf16[2,128,256]{2,1,0:T(8,128)(2,1)S(1)} collective-permute-done((bf16[2,128,256]{2,1,0:T(8,128)(2,1)S(1)}, bf16[2,128,256]{2,1,0:T(8,128)(2,1)S(1)}, u32[]{:S(2)}, u32[]{:S(2)}) %collective-permute-start.7) | collective-permute-done | bytes 131104 | tf_op jit(solution)/shard_map/ppermute | solution.py:10
  132.1 8.6 %collective-permute-done.8 = bf16[2,128,512]{2,1,0:T(8,128)(2,1)S(1)} collective-permute-done((bf16[2,128,512]{2,1,0:T(8,128)(2,1)S(1)}, bf16[2,128,512]{2,1,0:T(8,128)(2,1)S(1)}, u32[]{:S(2)}, u32[]{:S(2)}) %collective-permute-start.8) | collective-permute-done | bytes 262176 | tf_op jit(solution)/shard_map/ppermute | solution.py:10
  148.3 69.7 %all-reduce.2.cloned.1.call-done = bf16[128,1024]{1,0:T(8,128)(2,1)} async-done(((bf16[128,1024]{1,0:T(8,128)(2,1)}), bf16[128,1024]{1,0:T(8,128)(2,1)}) %all-reduce.2.cloned.1.call-update) | async-done | bytes 262160 | tf_op jit(solution)/shard_map/psum | solution.py:144
  223.6 11.1 %collective-permute-done.9 = bf16[2,128,1024]{2,1,0:T(8,128)(2,1)S(1)} collective-permute-done((bf16[2,128,1024]{2,1,0:T(8,128)(2,1)S(1)}, bf16[2,128,1024]{2,1,0:T(8,128)(2,1)S(1)}, u32[]{:S(2)}, u32[]{:S(2)}) %collective-permute-start.9) | collective-permute-done | bytes 524320 | tf_op jit(solution)/shard_map/ppermute | solution.py:10
  235.7 10.2 %collective-permute-done.10 = bf16[2,128,1024]{2,1,0:T(8,128)(2,1)S(1)} collective-permute-done((bf16[2,128,1024]{2,1,0:T(8,128)(2,1)S(1)}, bf16[2,128,1024]{2,1,0:T(8,128)(2,1)S(1)}, u32[]{:S(2)}, u32[]{:S(2)}) %collective-permute-start.10) | collective-permute-done | bytes 524320 | tf_op jit(solution)/shard_map/ppermute | solution.py:10
  249.0 2.1 fusion.75
  252.4 17.4 %collective-permute-done.11 = bf16[2,128,1024]{2,1,0:T(8,128)(2,1)} collective-permute-done((bf16[2,128,1024]{2,1,0:T(8,128)(2,1)}, bf16[2,128,1024]{2,1,0:T(8,128)(2,1)}, u32[]{:S(2)}, u32[]{:S(2)}) %collective-permute-start.11) | collective-permute-done | bytes 524320 | tf_op jit(solution)/shard_map/ppermute | solution.py:10
  278.7 9.7 %collective-permute-done.12 = bf16[2,128,1024]{2,1,0:T(8,128)(2,1)S(1)} collective-permute-done((bf16[2,128,1024]{2,1,0:T(8,128)(2,1)S(1)}, bf16[2,128,1024]{2,1,0:T(8,128)(2,1)S(1)}, u32[]{:S(2)}, u32[]{:S(2)}) %collective-permute-start.12) | collective-permute-done | bytes 524320 | tf_op jit(solution)/shard_map/ppermute | solution.py:10
  293.8 2.3 fusion.15
  296.2 6.5 %collective-permute-done.13 = bf16[2,128,1024]{2,1,0:T(8,128)(2,1)} collective-permute-done((bf16[2,128,1024]{2,1,0:T(8,128)(2,1)}, bf16[2,128,1024]{2,1,0:T(8,128)(2,1)}, u32[]{:S(2)}, u32[]{:S(2)}) %collective-permute-start.13) | collective-permute-done | bytes 524320 | tf_op jit(solution)/shard_map/ppermute | solution.py:10
  307.9 6.1 %pad_maximum_fusion = bf16[1024,2,1024]{0,2,1:T(8,128)(2,1)} fusion(bf16[1024,2,128]{0,2,1:T(8,128)(2,1)} %fusion.20, bf16[1024,2,128]{0,2,1:T(8,128)(2,1)} %fusion.19, bf16[1024,2,256]{0,2,1:T(8,128)(2,1)S(1)} %copy-done.16, bf16[1024,2,512]{0,2,1:T(8,128)(2,1)S(1)} %convert_bitcast_fusion), kind=kLoop, calls=%fused_computation.4 | loop fusion | flops 16777216 | bytes 8388608 | tf_op jit(solution)/shard_map/concatenate | solution.py:74
  318.0 11.8 %collective-permute-done.14 = bf16[2,128,1024]{2,1,0:T(8,128)(2,1)S(1)} collective-permute-done((bf16[2,128,1024]{2,1,0:T(8,128)(2,1)S(1)}, bf16[2,128,1024]{2,1,0:T(8,128)(2,1)S(1)}, u32[]{:S(2)}, u32[]{:S(2)}) %collective-permute-start.14) | collective-permute-done | bytes 524320 | tf_op jit(solution)/shard_map/ppermute | solution.py:10
  332.3 3.8 all-to-all-start.2
  336.1 7.9 %multiply_multiply_fusion.1 = (f32[512,1,1024]{2,0,1:T(8,128)}, f32[512,1,1024]{2,0,1:T(8,128)}, f32[512,1,1024]{2,0,1:T(8,128)}) fusion(f32[512,4,1024]{2,0,1:T(8,128)} %copy-done.2), kind=kLoop, calls=%fused_computation.21 | loop fusion | flops 3145728 | bytes 14680064 | tf_op jit(solution)/shard_map/mul | solution.py:39
  343.9 17.8 %all-to-all-done.2 = bf16[128,4,1024]{2,0,1:T(8,128)(2,1)S(1)} async-done(((bf16[128,4,1024]{2,0,1:T(8,128)(2,1)}), bf16[128,4,1024]{2,0,1:T(8,128)(2,1)S(1)}, u32[]{:S(2)}, u32[]{:S(2)}) %all-to-all-start.2) | async-done | bytes 1048608 | tf_op jit(solution)/shard_map/all_to_all | solution.py:172
  361.8 3.0 multiply_reduce_fusion
  364.8 2.7 convert_bitcast_fusion.1
  370.1 2.5 convert_bitcast_fusion.2
  372.6 3.7 copy.44
  (208 shorter events, 83.3 us)
Async XLA Ops:
  7.2 27.6 %copy-start = (bf16[1,4,256,1024]{3,2,1,0:T(8,128)(2,1)S(1)}, bf16[1,4,256,1024]{3,2,1,0:T(8,128)(2,1)}, u32[]{:S(2)}) copy-start(bf16[1,4,256,1024]{3,2,1,0:T(8,128)(2,1)} %param.8) | copy-start | bytes 6291460
  7.2 210.8 %all-reduce.2.cloned.1.call-start = ((), (), s32[]{:S(2)}) async-start(), calls=%async_computation.4 | async-start | bytes 524288 | tf_op jit(solution)/shard_map/psum | solution.py:144
  66.7 7.7 %collective-permute-start = (bf16[128,1024]{1,0:T(8,128)(2,1)S(1)}, bf16[128,1024]{1,0:T(8,128)(2,1)S(1)}, u32[]{:S(2)}, u32[]{:S(2)}) collective-permute-start(bf16[128,1024]{1,0:T(8,128)(2,1)S(1)} %fusion.59), channel_id=1, source_target_pairs={{0,4},{4,0},{8,12},{12,8},{16,20},{20,16},{24,28},{28,24},{1,5},{5... | collective-permute-start | bytes 786440 | tf_op jit(solution)/shard_map/ppermute | solution.py:10
  77.6 6.9 %collective-permute-start.1 = (bf16[2,128,512]{2,1,0:T(8,128)(2,1)S(1)}, bf16[2,128,512]{2,1,0:T(8,128)(2,1)S(1)}, u32[]{:S(2)}, u32[]{:S(2)}) collective-permute-start(bf16[2,128,512]{2,1,0:T(8,128)(2,1)S(1)} %maximum_convert_fusion), channel_id=1, source_target_pairs={{0,4},{4,0},{8,12},{12,8},{16,20},{20,16},{24,28},{28,24},{1,5},{5... | collective-permute-start | bytes 786440 | tf_op jit(solution)/shard_map/ppermute | solution.py:10
  84.9 6.4 %collective-permute-start.2 = (bf16[128,1024]{1,0:T(8,128)(2,1)S(1)}, bf16[128,1024]{1,0:T(8,128)(2,1)S(1)}, u32[]{:S(2)}, u32[]{:S(2)}) collective-permute-start(bf16[128,1024]{1,0:T(8,128)(2,1)S(1)} %multiply_convert_fusion.3), channel_id=1, source_target_pairs={{0,8},{4,12},{8,0},{12,4},{16,24},{20,28},{24,16},{28,20},{1,9},{5... | collective-permute-start | bytes 786440 | tf_op jit(solution)/shard_map/ppermute | solution.py:10
  94.1 5.0 %collective-permute-start.3 = (bf16[2,128,256]{2,1,0:T(8,128)(2,1)S(1)}, bf16[2,128,256]{2,1,0:T(8,128)(2,1)S(1)}, u32[]{:S(2)}, u32[]{:S(2)}) collective-permute-start(bf16[2,128,256]{2,1,0:T(8,128)(2,1)S(1)} %maximum_convert_fusion.1), channel_id=1, source_target_pairs={{0,4},{4,0},{8,12},{12,8},{16,20},{20,16},{24,28},{28,24},{1,5},{5... | collective-permute-start | bytes 393224 | tf_op jit(solution)/shard_map/ppermute | solution.py:10
  99.2 9.0 %collective-permute-start.4 = (bf16[2,128,512]{2,1,0:T(8,128)(2,1)S(1)}, bf16[2,128,512]{2,1,0:T(8,128)(2,1)S(1)}, u32[]{:S(2)}, u32[]{:S(2)}) collective-permute-start(bf16[2,128,512]{2,1,0:T(8,128)(2,1)S(1)} %get-tuple-element.18), channel_id=1, source_target_pairs={{0,8},{4,12},{8,0},{12,4},{16,24},{20,28},{24,16},{28,20},{1,9},{5... | collective-permute-start | bytes 786440 | tf_op jit(solution)/shard_map/ppermute | solution.py:10
  108.5 12.9 %copy-start.11 = (f32[2,128,1024]{2,1,0:T(8,128)}, f32[2,128,1024]{2,1,0:T(8,128)S(1)}, u32[]{:S(2)}) copy-start(f32[2,128,1024]{2,1,0:T(8,128)S(1)} %maximum_select_fusion.1) | copy-start | bytes 3145732
  108.8 10.2 %collective-permute-start.5 = (bf16[128,1024]{1,0:T(8,128)(2,1)S(1)}, bf16[128,1024]{1,0:T(8,128)(2,1)S(1)}, u32[]{:S(2)}, u32[]{:S(2)}) collective-permute-start(bf16[128,1024]{1,0:T(8,128)(2,1)S(1)} %multiply_convert_fusion.2), channel_id=1, source_target_pairs={{0,16},{4,20},{8,24},{12,28},{16,0},{20,4},{24,8},{28,12},{1,17},{... | collective-permute-start | bytes 786440 | tf_op jit(solution)/shard_map/ppermute | solution.py:10
  119.0 12.0 %copy-start.35 = (bf16[128,1024]{1,0:T(8,128)(2,1)}, bf16[128,1024]{1,0:T(8,128)(2,1)S(1)}, u32[]{:S(2)}) copy-start(bf16[128,1024]{1,0:T(8,128)(2,1)S(1)} %collective-permute-done.5) | copy-start | bytes 786436
  121.5 4.3 %collective-permute-start.6 = (bf16[2,128,128]{2,1,0:T(8,128)(2,1)S(1)}, bf16[2,128,128]{2,1,0:T(8,128)(2,1)S(1)}, u32[]{:S(2)}, u32[]{:S(2)}) collective-permute-start(bf16[2,128,128]{2,1,0:T(8,128)(2,1)S(1)} %maximum_convert_fusion.2), channel_id=1, source_target_pairs={{0,4},{4,0},{8,12},{12,8},{16,20},{20,16},{24,28},{28,24},{1,5},{5... | collective-permute-start | bytes 196616 | tf_op jit(solution)/shard_map/ppermute | solution.py:10
  125.8 5.0 %collective-permute-start.7 = (bf16[2,128,256]{2,1,0:T(8,128)(2,1)S(1)}, bf16[2,128,256]{2,1,0:T(8,128)(2,1)S(1)}, u32[]{:S(2)}, u32[]{:S(2)}) collective-permute-start(bf16[2,128,256]{2,1,0:T(8,128)(2,1)S(1)} %get-tuple-element.14), channel_id=1, source_target_pairs={{0,8},{4,12},{8,0},{12,4},{16,24},{20,28},{24,16},{28,20},{1,9},{5... | collective-permute-start | bytes 393224 | tf_op jit(solution)/shard_map/ppermute | solution.py:10
  131.0 9.8 %collective-permute-start.8 = (bf16[2,128,512]{2,1,0:T(8,128)(2,1)S(1)}, bf16[2,128,512]{2,1,0:T(8,128)(2,1)S(1)}, u32[]{:S(2)}, u32[]{:S(2)}) collective-permute-start(bf16[2,128,512]{2,1,0:T(8,128)(2,1)S(1)} %get-tuple-element.12), channel_id=1, source_target_pairs={{0,16},{4,20},{8,24},{12,28},{16,0},{20,4},{24,8},{28,12},{1,17},{... | collective-permute-start | bytes 786440 | tf_op jit(solution)/shard_map/ppermute | solution.py:10
  141.2 77.9 %copy-start.42 = (f32[128]{0:T(128)}, f32[128]{0:T(128)S(1)}, u32[]{:S(2)}) copy-start(f32[128]{0:T(128)S(1)} %add_rsqrt_fusion.1) | copy-start | bytes 1540
  148.0 224.7 %reduce-scatter.2.cloned.1.call-start = ((), (), s32[]{:S(2)}) async-start(), calls=%async_computation.5 | async-start | bytes 5242880 | tf_op jit(solution)/shard_map/reduce_scatter | solution.py:191
  222.8 11.9 %collective-permute-start.9 = (bf16[2,128,1024]{2,1,0:T(8,128)(2,1)S(1)}, bf16[2,128,1024]{2,1,0:T(8,128)(2,1)S(1)}, u32[]{:S(2)}, u32[]{:S(2)}) collective-permute-start(bf16[2,128,1024]{2,1,0:T(8,128)(2,1)S(1)} %fusion.31), channel_id=1, source_target_pairs={{0,4},{4,0},{8,12},{12,8},{16,20},{20,16},{24,28},{28,24},{1,5},{5... | collective-permute-start | bytes 1572872 | tf_op jit(solution)/shard_map/ppermute | solution.py:10
  234.8 13.0 %copy-start.14 = (bf16[2,128,1024]{2,1,0:T(8,128)(2,1)}, bf16[2,128,1024]{2,1,0:T(8,128)(2,1)S(1)}, u32[]{:S(2)}) copy-start(bf16[2,128,1024]{2,1,0:T(8,128)(2,1)S(1)} %collective-permute-done.9) | copy-start | bytes 1572868
  234.9 11.0 %collective-permute-start.10 = (bf16[2,128,1024]{2,1,0:T(8,128)(2,1)S(1)}, bf16[2,128,1024]{2,1,0:T(8,128)(2,1)S(1)}, u32[]{:S(2)}, u32[]{:S(2)}) collective-permute-start(bf16[2,128,1024]{2,1,0:T(8,128)(2,1)S(1)} %fusion.89), channel_id=1, source_target_pairs={{0,8},{4,12},{8,0},{12,4},{16,24},{20,28},{24,16},{28,20},{1,9},{5... | collective-permute-start | bytes 1572872 | tf_op jit(solution)/shard_map/ppermute | solution.py:10
  247.8 22.0 %collective-permute-start.11 = (bf16[2,128,1024]{2,1,0:T(8,128)(2,1)}, bf16[2,128,1024]{2,1,0:T(8,128)(2,1)}, u32[]{:S(2)}, u32[]{:S(2)}) collective-permute-start(bf16[2,128,1024]{2,1,0:T(8,128)(2,1)} %fusion.32), channel_id=1, source_target_pairs={{0,16},{4,20},{8,24},{12,28},{16,0},{20,4},{24,8},{28,12},{1,17},{... | collective-permute-start | bytes 1572872 | tf_op jit(solution)/shard_map/ppermute | solution.py:10
  249.0 20.8 %copy-start.15 = (bf16[2,128,1024]{2,1,0:T(8,128)(2,1)S(1)}, bf16[2,128,1024]{2,1,0:T(8,128)(2,1)}, u32[]{:S(2)}) copy-start(bf16[2,128,1024]{2,1,0:T(8,128)(2,1)} %copy-done.14) | copy-start | bytes 1572868
  249.0 20.8 %copy-start.22 = (bf16[2,128,1024]{2,1,0:T(8,128)(2,1)S(1)}, bf16[2,128,1024]{2,1,0:T(8,128)(2,1)}, u32[]{:S(2)}) copy-start(bf16[2,128,1024]{2,1,0:T(8,128)(2,1)} %copy-done.21) | copy-start | bytes 1572868
  274.5 13.9 %collective-permute-start.12 = (bf16[2,128,1024]{2,1,0:T(8,128)(2,1)S(1)}, bf16[2,128,1024]{2,1,0:T(8,128)(2,1)S(1)}, u32[]{:S(2)}, u32[]{:S(2)}) collective-permute-start(bf16[2,128,1024]{2,1,0:T(8,128)(2,1)S(1)} %fusion.30), channel_id=1, source_target_pairs={{0,4},{4,0},{8,12},{12,8},{16,20},{20,16},{24,28},{28,24},{1,5},{5... | collective-permute-start | bytes 1572872 | tf_op jit(solution)/shard_map/ppermute | solution.py:10
  276.9 12.5 %copy-start.43 = (f32[128]{0:T(128)S(1)}, f32[128]{0:T(128)}, u32[]{:S(2)}) copy-start(f32[128]{0:T(128)} %copy-done.42) | copy-start | bytes 1540
  277.9 11.6 %copy-start.38 = (bf16[128,128]{1,0:T(8,128)(2,1)S(1)}, bf16[128,128]{1,0:T(8,128)(2,1)}, u32[]{:S(2)}) copy-start(bf16[128,128]{1,0:T(8,128)(2,1)} %copy-done.37) | copy-start | bytes 98308
  277.9 11.6 %copy-start.41 = (bf16[128,128]{1,0:T(8,128)(2,1)S(1)}, bf16[128,128]{1,0:T(8,128)(2,1)}, u32[]{:S(2)}) copy-start(bf16[128,128]{1,0:T(8,128)(2,1)} %copy-done.40) | copy-start | bytes 98308
  278.7 13.8 %copy-start.29 = (bf16[128,1,1024]{2,0,1:T(8,128)(2,1)S(1)}, bf16[128,1,1024]{2,0,1:T(8,128)(2,1)}, u32[]{:S(2)}) copy-start(bf16[128,1,1024]{2,0,1:T(8,128)(2,1)} %get-tuple-element.46) | copy-start | bytes 786436
  289.4 13.3 %collective-permute-start.13 = (bf16[2,128,1024]{2,1,0:T(8,128)(2,1)}, bf16[2,128,1024]{2,1,0:T(8,128)(2,1)}, u32[]{:S(2)}, u32[]{:S(2)}) collective-permute-start(bf16[2,128,1024]{2,1,0:T(8,128)(2,1)} %fusion.33), channel_id=1, source_target_pairs={{0,8},{4,12},{8,0},{12,4},{16,24},{20,28},{24,16},{28,20},{1,9},{5... | collective-permute-start | bytes 1572872 | tf_op jit(solution)/shard_map/ppermute | solution.py:10
  290.7 12.0 %copy-start.26 = (bf16[2,128,1024]{2,1,0:T(8,128)(2,1)S(1)}, bf16[2,128,1024]{2,1,0:T(8,128)(2,1)}, u32[]{:S(2)}) copy-start(bf16[2,128,1024]{2,1,0:T(8,128)(2,1)} %copy-done.25) | copy-start | bytes 1572868
  317.7 12.1 %collective-permute-start.14 = (bf16[2,128,1024]{2,1,0:T(8,128)(2,1)S(1)}, bf16[2,128,1024]{2,1,0:T(8,128)(2,1)S(1)}, u32[]{:S(2)}, u32[]{:S(2)}) collective-permute-start(bf16[2,128,1024]{2,1,0:T(8,128)(2,1)S(1)} %fusion.29), channel_id=1, source_target_pairs={{0,4},{4,0},{8,12},{12,8},{16,20},{20,16},{24,28},{28,24},{1,5},{5... | collective-permute-start | bytes 1572872 | tf_op jit(solution)/shard_map/ppermute | solution.py:10
  317.9 12.0 %copy-start.8 = (f32[128,1,1024]{2,0,1:T(8,128)S(1)}, f32[128,1,1024]{2,0,1:T(8,128)}, u32[]{:S(2)}) copy-start(f32[128,1,1024]{2,0,1:T(8,128)} %copy-done.7) | copy-start | bytes 1572868
  332.3 29.5 %all-to-all-start.2 = ((bf16[128,4,1024]{2,0,1:T(8,128)(2,1)}), bf16[128,4,1024]{2,0,1:T(8,128)(2,1)S(1)}, u32[]{:S(2)}, u32[]{:S(2)}) async-start(bf16[128,4,1024]{2,0,1:T(8,128)(2,1)} %fusion.3), calls=%async_computation.2 | async-start | bytes 2097152 | tf_op jit(solution)/shard_map/all_to_all | solution.py:172
  336.1 25.7 %copy-start.6 = (f32[512,1,1024]{2,0,1:T(8,128)S(1)}, f32[512,1,1024]{2,0,1:T(8,128)}, u32[]{:S(2)}) copy-start(f32[512,1,1024]{2,0,1:T(8,128)} %copy-done.5) | copy-start | bytes 6291460
  (30 other events, 88.6 us)
Sparse Core Ops, SparseCore 0:
  148.1 69.8 all-reduce.1
  314.1 54.8 reduce-scatter.1
where the time goes:
time: 385 us; the launch traced here: 383 us
  waiting for transfers between devices  200 us (52%)
  other arithmetic  42 us (11%)
  matrix products  39.4 us (10%)
  blocking collectives  35.4 us (9%)
  local copies, waits for them, and re-layouts  30 us (8%)
  starting transfers between devices  21.8 us (6%)
  between operations  14.9 us (4%)
    ppermute x15, waiting for transfers between devices, partner(): lax.ppermute(value, axis, [(i, i ^ 1 << bit) for i in range(lax.axis_size...  112 us
    psum x1, waiting for transfers between devices, on_device(): lax.psum(root_term.astype(jnp.bfloat16), 'sub').astype(jnp.float32)  69.7 us
    unnamed x93, local copies, waits for them, and re-layouts  21.4 us
    all_to_all x1, blocking collectives, on_device(): lax.all_to_all(placed, 'rep', split_axis=1, concat_axis=0, tiled=True)[:, 0]  18.5 us
    all_to_all x1, waiting for transfers between devices, on_device(): lax.all_to_all(middle_gradient_list, 'rep', split_axis=1, concat_axis=0,...  17.8 us
    ppermute x15, starting transfers between devices, partner(): lax.ppermute(value, axis, [(i, i ^ 1 << bit) for i in range(lax.axis_size...  17.8 us
    all_to_all x1, blocking collectives, on_device(): lax.all_to_all(mid_local[:, None, :], 'rep', split_axis=0, concat_axis=1,...  16.9 us
    dot_general x9, matrix products, matmul_t(): lax.dot_general(left_arr, right_arr, (((1,), (1,)), ((), ())), preferred_...  14.7 us
  transfers between devices with their start and end apart: 18, of which 17 were waited for; matrix products, arithmetic and copies ran while one was open for 11% of the time, Pallas kernels for 0%

commit v1 on v0

v1 whole, which is shorter than its diff:
```python
import functools

import jax
import jax.numpy as jnp
from jax import lax
from jax.experimental import pallas as pl
from jax.experimental.pallas import tpu as pltpu
from jax.sharding import PartitionSpec as P

EPSILON = 1e-06
CHILDREN = 4
MIB = 1024 * 1024


def partner(value, axis, offset):
    return lax.ppermute(value, axis, [(i, i ^ offset) for i in range(lax.axis_size(axis))])


def rms_factor(values):
    return lax.rsqrt(jnp.mean(values * values, axis=-1, keepdims=True) + EPSILON)


def norm_back(gradient, normed, factor):
    return factor * (gradient - normed * jnp.mean(gradient * normed, axis=-1, keepdims=True))


def matmul(left_arr, right_arr):
    return jnp.dot(left_arr, right_arr, preferred_element_type=jnp.float32)


def matmul_t(left_arr, right_arr):
    return lax.dot_general(
        left_arr, right_arr, (((1,), (1,)), ((), ())), preferred_element_type=jnp.float32
    )


def inner_t(left_arr, right_arr):
    return lax.dot_general(
        left_arr, right_arr, (((0,), (0,)), ((), ())), preferred_element_type=jnp.float32
    )


def bf16(value):
    return value.astype(jnp.bfloat16)


def f32(value):
    return value.astype(jnp.float32)


def join_rows(first, second, axis):
    if axis == 0 and first.ndim > 2 or first.shape[axis] % 16 == 0:
        return jnp.concatenate([first, second], axis=axis)
    first, second = lax.optimization_barrier((f32(first), f32(second)))
    return bf16(lax.optimization_barrier(jnp.concatenate([first, second], axis=axis)))


def whole_block():
    return pl.BlockSpec(memory_space=pltpu.VMEM)


def place_kernel(slots, ids_ref, map_ref, regions_ref, *rest):
    outs, wide = rest[:CHILDREN], rest[CHILDREN]
    rows = regions_ref.shape[0] // slots
    parts = wide.shape[0]
    for part in range(parts):
        wide[part] = regions_ref[:, part * 128 : (part + 1) * 128].astype(jnp.float32)
    row = lax.broadcasted_iota(jnp.int32, (rows, rows), 0)
    col = lax.broadcasted_iota(jnp.int32, (rows, rows), 1)
    select = (jnp.bitwise_xor(row, ids_ref[1]) == col).astype(jnp.bfloat16)
    for offset in range(CHILDREN):
        node = jnp.bitwise_xor(ids_ref[0], offset)
        for child in range(CHILDREN):
            region = map_ref[node * CHILDREN + child]
            for part in range(parts):
                values = wide[part, pl.ds(region, rows, stride=slots), :].astype(jnp.bfloat16)
                outs[offset][child, :, part * 128 : (part + 1) * 128] = matmul(
                    select, values
                ).astype(jnp.bfloat16)


def place(regions, leaf_map, ids):
    rows, slots, feats = regions.shape
    flat = regions.reshape(rows * slots, feats)
    smem = pl.BlockSpec(memory_space=pltpu.SMEM)
    return pl.pallas_call(
        functools.partial(place_kernel, slots),
        out_shape=[jax.ShapeDtypeStruct((CHILDREN, rows, feats), jnp.bfloat16)] * CHILDREN,
        in_specs=[smem, smem, whole_block()],
        out_specs=[whole_block()] * CHILDREN,
        scratch_shapes=[pltpu.VMEM((feats // 128, rows * slots, 128), jnp.float32)],
        compiler_params=pltpu.CompilerParams(vmem_limit_bytes=16 * MIB),
        name="place",
    )(ids, leaf_map, flat)


def leaf_forward_kernel(count, *refs):
    placed, leaf_w, mid_w = refs[:count], refs[count], refs[count + 1]
    msgs, terms = refs[count + 2 : 2 * count + 2], refs[2 * count + 2 :]
    rows = placed[0].shape[1]
    product = None
    for child in range(CHILDREN):
        values = jnp.concatenate([ref[child] for ref in placed], axis=0)
        factor = 1.0 + matmul(values, leaf_w[child])
        product = factor if product is None else product * factor
    message = bf16(product * rms_factor(product))
    out = bf16(matmul(message, mid_w[...]))
    for i in range(count):
        msgs[i][...] = message[i * rows : (i + 1) * rows]
        terms[i][...] = out[i * rows : (i + 1) * rows]


def leaf_forward(placed, leaf_w, mid_w):
    count = len(placed)
    rows = placed[0].shape[1]
    width = mid_w.shape[0]
    return pl.pallas_call(
        functools.partial(leaf_forward_kernel, count),
        out_shape=[jax.ShapeDtypeStruct((rows, width), jnp.bfloat16)] * (2 * count),
        in_specs=[whole_block()] * (count + 2),
        out_specs=[whole_block()] * (2 * count),
        compiler_params=pltpu.CompilerParams(vmem_limit_bytes=24 * MIB),
        name="leaf_forward",
    )(*placed, leaf_w, mid_w)


def leaf_backward_kernel(*refs):
    placed, msgs, grads = refs[0:4], refs[4:8], refs[8:12]
    leaf_w, mid_w, leaf_out, mid_out, cot = refs[12:17]
    rows = placed[0].shape[1]
    for pair in range(2):
        chunk = [2 * pair, 2 * pair + 1]
        factors = [
            1.0 + matmul(jnp.concatenate([placed[c][child] for c in chunk], axis=0), leaf_w[child])
            for child in range(CHILDREN)
        ]
        low = factors[0] * factors[1]
        high = factors[2] * factors[3]
        product = low * high
        scale = rms_factor(product)
        back = matmul_t(jnp.concatenate([grads[c][...] for c in chunk], axis=0), mid_w[...])
        node = norm_back(back, product * scale, scale)
        node_high = node * high
        node_low = node * low
        where = slice(pair * 2 * rows, (pair + 1) * 2 * rows)
        cot[0, where] = bf16(node_high * factors[1])
        cot[1, where] = bf16(node_high * factors[0])
        cot[2, where] = bf16(node_low * factors[3])
        cot[3, where] = bf16(node_low * factors[2])
    all_grads = jnp.concatenate([ref[...] for ref in grads], axis=0)
    all_msgs = jnp.concatenate([ref[...] for ref in msgs], axis=0)
    mid_out[...] = bf16(inner_t(all_msgs, all_grads))
    for child in range(CHILDREN):
        values = jnp.concatenate([ref[child] for ref in placed], axis=0)
        leaf_out[child] = bf16(inner_t(values, cot[child]))


def leaf_backward(placed, msgs, grads, leaf_w, mid_w):
    rows = placed[0].shape[1]
    return pl.pallas_call(
        leaf_backward_kernel,
        out_shape=[
            jax.ShapeDtypeStruct(leaf_w.shape, jnp.bfloat16),
            jax.ShapeDtypeStruct(mid_w.shape, jnp.bfloat16),
        ],
        in_specs=[whole_block()] * 14,
        out_specs=[whole_block()] * 2,
        scratch_shapes=[pltpu.VMEM((CHILDREN, 4 * rows, mid_w.shape[0]), jnp.bfloat16)],
        compiler_params=pltpu.CompilerParams(vmem_limit_bytes=48 * MIB),
        name="leaf_backward",
    )(*placed, *msgs, *grads, leaf_w, mid_w)


def swap_blocks(array, size, axis):
    count = array.shape[axis] // size
    parts = [lax.slice_in_dim(array, i * size, (i + 1) * size, axis=axis) for i in range(count)]
    return jnp.concatenate([parts[i ^ 1] for i in range(count)], axis=axis)


def reverse_bits(value, count):
    out = 0
    for i in range(count):
        out = out * 2 + (value >> i) % 2
    return out


def assemble_kernel(group_bits, ids_ref, mine_ref, other_ref, out_ref):
    half, width = mine_ref.shape
    size = width >> group_bits
    for ref, core in ((mine_ref, ids_ref[0]), (other_ref, 1 - ids_ref[0])):
        rows = pl.ds(pl.multiple_of(core * half, half), half)
        for position in range(1 << group_bits):
            block = jnp.bitwise_xor(ids_ref[1], reverse_bits(position, group_bits))
            cols = pl.ds(pl.multiple_of(block * size, size), size)
            out_ref[rows, cols] = ref[:, position * size : (position + 1) * size]


def assemble(mine, other, core, block, group_bits):
    half, width = mine.shape
    size = width >> group_bits
    if size % 128 == 0:
        ids = jnp.stack([core, block]).astype(jnp.int32)
        return pl.pallas_call(
            functools.partial(assemble_kernel, group_bits),
            out_shape=jax.ShapeDtypeStruct((2 * half, width), mine.dtype),
            in_specs=[pl.BlockSpec(memory_space=pltpu.SMEM), whole_block(), whole_block()],
            out_specs=whole_block(),
            compiler_params=pltpu.CompilerParams(vmem_limit_bytes=16 * MIB),
            name="assemble",
        )(ids, mine, other)
    full = jnp.where(
        core == 1, jnp.concatenate([other, mine], axis=0), jnp.concatenate([mine, other], axis=0)
    )
    for i in range(group_bits):
        span = width >> (i + 1)
        full = jnp.where((block >> i) % 2 == 1, swap_blocks(full, span, 1), full)
    order = [reverse_bits(i, group_bits) for i in range(1 << group_bits)]
    return jnp.concatenate([full[:, i * size : (i + 1) * size] for i in order], axis=1)


def gather_maps(maps, sub_index, core, depth):
    width = maps.shape[1]
    half = width // 2
    own_rows = lax.dynamic_slice_in_dim(maps, core * half, half, 1)
    state = [None] * depth
    for stage in reversed(range(depth)):
        span = width >> (stage + 1)
        first = width - 2 * span
        side = (sub_index >> stage) % 2
        block = own_rows[:, :, first : first + span]
        mine = jnp.where(side == 1, block[1], block[0])
        send = jnp.where(side == 1, block[0], block[1])
        if stage > 0:
            for level in range(stage + 1, depth):
                send = jnp.concatenate([send, state[level]], axis=1)
            got = partner(send, "sub", 1 << stage)
            state[stage] = jnp.concatenate([mine, got[:, :span]], axis=1)
            at = span
            for level in range(stage + 1, depth):
                size = state[level].shape[1]
                state[level] = jnp.concatenate([state[level], got[:, at : at + size]], axis=1)
                at += size
        else:
            state[0] = jnp.concatenate([mine, partner(send, "sub", 1)], axis=1)
    if depth > 1:
        merged = jnp.concatenate(state[1:], axis=1)
        got = partner(merged, "sub", 1)
        at = 0
        for level in range(1, depth):
            size = state[level].shape[1]
            state[level] = jnp.concatenate([state[level], got[:, at : at + size]], axis=1)
            at += size
    others = [partner(state[0], "rep", 1)]
    if depth > 1:
        got = partner(jnp.stack(state[1:]), "rep", 1)
        others += [got[i] for i in range(depth - 1)]
    return [
        assemble(state[level], others[level], core, sub_index % (2 << level), level + 1)
        for level in range(depth)
    ]


def on_device(regions, leaf_map, leaf_bond_weight, mid_weight, upper_weight, head_cotangent):
    rows = regions.shape[0]
    width = upper_weight.shape[1]
    sub_count = lax.axis_size("sub")
    depth = sub_count.bit_length() - 1
    sub_index = lax.axis_index("sub")
    rep_index = lax.axis_index("rep")
    core = rep_index % 2
    far = rep_index // 2
    bits = [(sub_index >> level) % 2 == 1 for level in range(depth)]
    flip = sum(((sub_index >> level) % 2) * (rows >> (level + 1)) for level in range(depth))
    leaf_w = leaf_bond_weight[0]
    mid_w = mid_weight[0, 0]

    ids = jnp.stack([rep_index, flip]).astype(jnp.int32)
    sent = place(regions, leaf_map, ids)
    far_both = partner(sent[3], "rep", 3)
    far_one = partner(sent[2], "rep", 2)
    near = partner(sent[1], "rep", 1)
    placed = [sent[0], near, far_one, far_both]

    maps = jnp.transpose(upper_weight[0], (1, 0, 2))
    cotangent = head_cotangent
    for level in range(depth):
        cotangent = jnp.where(
            bits[level], swap_blocks(cotangent, rows >> (level + 1), 0), cotangent
        )
    weights = gather_maps(maps, sub_index, core, depth)

    msg0, msg1, term0, term1 = leaf_forward(placed[:2], leaf_w, mid_w)
    near0 = f32(partner(term1, "rep", 1))
    msg2, msg3, term2, term3 = leaf_forward(placed[2:], leaf_w, mid_w)
    near2 = f32(partner(term3, "rep", 1))
    own0, own2 = 1.0 + f32(term0), 1.0 + f32(term2)
    near0, near2 = 1.0 + near0, 1.0 + near2
    pair0 = own0 * near0
    far_pair0 = f32(partner(bf16(own2 * near2), "rep", 2))
    mid_prod = pair0 * far_pair0
    mid_scale = rms_factor(mid_prod)
    mid_norm = mid_prod * mid_scale
    message = bf16(mid_norm)

    saved = []
    for level in range(depth):
        keep = rows >> (level + 1)
        own_up = matmul(message, weights[level])
        other_up = 1.0 + f32(partner(bf16(own_up[keep:]), "sub", 1 << level))
        own_up = 1.0 + own_up[:keep]
        joined = own_up * other_up
        scaling = rms_factor(joined)
        saved.append((message, own_up, other_up, joined * scaling, scaling))
        message = bf16(joined * scaling)

    root = message
    for level in reversed(range(depth)):
        root = join_rows(root, partner(root, "sub", 1 << level), 0)
    head_width = width // sub_count
    head_col = width - head_width
    head_left = maps[0, :, head_col:]
    head_right = maps[1, :, head_col:]
    head_value = matmul(root, head_left)
    gating = jax.nn.sigmoid(matmul(root, head_right))
    grad_value = bf16(cotangent * gating)
    grad_gate = bf16(cotangent * head_value * gating * (1.0 - gating))
    grad_msg = matmul_t(grad_value, head_left) + matmul_t(grad_gate, head_right)
    for level in range(depth):
        keep = rows >> (level + 1)
        grad_msg = grad_msg[:keep] + f32(partner(bf16(grad_msg[keep:]), "sub", 1 << level))

    grads = [None] * depth
    for level in reversed(range(depth)):
        _, own_up, other_up, normed, scaling = saved[level]
        joined_grad = norm_back(grad_msg, normed, scaling)
        other_grad = partner(bf16(joined_grad * own_up), "sub", 1 << level)
        grads[level] = join_rows(bf16(joined_grad * other_up), other_grad, 0)
        grad_msg = matmul_t(grads[level], weights[level])

    sub_back = norm_back(grad_msg, mid_norm, mid_scale)
    pair_back2 = f32(partner(bf16(sub_back * pair0), "rep", 2))
    pair_back0 = sub_back * far_pair0
    back0, back2 = bf16(pair_back0 * near0), bf16(pair_back2 * near2)
    back1 = partner(bf16(pair_back0 * own0), "rep", 1)
    back3 = partner(bf16(pair_back2 * own2), "rep", 1)
    leaf_grad, mid_grad = leaf_backward(
        placed, [msg0, msg1, msg2, msg3], [back0, back1, back2, back3], leaf_w, mid_w
    )

    inputs = [entry[0][None] for entry in saved]
    for stage in reversed(range(depth)):
        levels = list(range(stage, depth))
        sizes = [inputs[i].shape[0] * inputs[i].shape[1] for i in levels]
        send = jnp.concatenate([inputs[i].reshape(-1, width) for i in levels], axis=0)
        got = partner(send, "sub", 1 << stage)
        at = 0
        for i, size in zip(levels, sizes):
            part = got[at : at + size].reshape(inputs[i].shape)
            inputs[i] = join_rows(inputs[i], part, 0 if i == stage else 1)
            at += size

    outgoing = [grad[None] for grad in grads]

    def exchange(stage, levels):
        keeps, sends = [], []
        for i in levels:
            half = outgoing[i].shape[2] // 2
            low, high = outgoing[i][:, :, :half], outgoing[i][:, :, half:]
            keeps.append(jnp.where(bits[stage], high, low))
            sends.append(jnp.where(bits[stage], low, high))
        got = partner(
            jnp.concatenate([part.reshape(-1, 128) for part in sends], axis=0), "sub", 1 << stage
        )
        at = 0
        for i, keep in zip(levels, keeps):
            size = keep.size // 128
            part = got[at : at + size].reshape(keep.shape)
            outgoing[i] = join_rows(keep, part, 0 if i == stage else 1)
            at += size

    for stage in reversed(range(1, depth)):
        exchange(stage, list(range(stage, depth)))
    if depth > 1:
        exchange(0, list(range(1, depth)))
    exchange(0, [0])

    def by_rep(values):
        return values.reshape(values.shape[0], 2, 2, width // 4)

    def sides(level, pair):
        if level == depth:
            return pair
        return [jnp.where(bits[level], pair[1 - i], pair[i]) for i in range(2)]

    def rep_sum(levels):
        near_parts, far_parts = [], []
        for level in levels:
            if level == depth:
                x_pair, g_pair = [root, root], [grad_value, grad_gate]
            else:
                x_pair = [inputs[level][i] for i in range(2)]
                g_pair = [outgoing[level][i] for i in range(2)]
            x_pair, g_pair = sides(level, x_pair), sides(level, g_pair)
            kept, given = [], []
            for x_side, g_side in zip(x_pair, g_pair):
                x_side = by_rep(x_side)
                low, high = x_side[:, :, 0], x_side[:, :, 1]
                keep = jnp.where(core == 1, high, low).reshape(rows, -1)
                give = jnp.where(core == 1, low, high).reshape(rows, -1)
                kept.append(inner_t(keep, g_side))
                given.append(bf16(inner_t(give, g_side)))
            near_parts.append(jnp.stack(kept))
            far_parts.append(jnp.stack(given))
        kept = jnp.concatenate(near_parts, axis=2)
        total = kept + f32(partner(jnp.concatenate(far_parts, axis=2), "rep", 1))
        quarter = width // 4
        low, high = total[:, :quarter], total[:, quarter:]
        keep = jnp.where(far == 1, high, low)
        give = jnp.where(far == 1, low, high)
        return bf16(keep + f32(partner(bf16(give), "rep", 2)))

    upper = rep_sum(list(range(1, depth + 1)))
    upper = jnp.concatenate([rep_sum([0]), upper], axis=2)
    upper = jnp.transpose(upper, (1, 0, 2))
    return leaf_grad[None], mid_grad[None, None], upper[None]


def solution(mesh):
    placed = (
        P("rep", "sub", None),
        P("sub"),
        P(("sub", "rep"), None, None, None),
        P("sub", "rep", None, None),
        P("sub", None, None, None),
        P("rep", "sub"),
    )
    return jax.shard_map(
        on_device,
        mesh=mesh,
        in_specs=placed,
        out_specs=(
            P(("sub", "rep"), None, None, None),
            P("sub", "rep", None, None),
            P("sub", "rep", None, None),
        ),
        check_vma=False,
    )
```

time: 385 us -> 282 us (0.73)
  waiting for transfers between devices: 200 us -> 55.3 us
  local copies, waits for them, and re-layouts: 30 us -> 79.6 us
  blocking collectives: 35.4 us -> 0 us
  starting transfers between devices: 21.8 us -> 48.9 us
  Pallas kernels: 0 us -> 17.6 us
  matrix products: 39.4 us -> 24.5 us
  between operations: 14.9 us -> 1.99 us
  other arithmetic: 42 us -> 51.6 us
    psum x1 -> x0, waiting for transfers between devices: 69.7 us -> none  [on_device(): lax.psum(root_term.astype(jnp.bfloat16), 'sub').astype(jnp.float32)]
    ppermute x15 -> x38, waiting for transfers between devices: 112 us -> 55.3 us  [partner(): lax.ppermute(value, axis, [(i, i ^ offset) for i in range(lax.axis_size(a...]
    all_to_all x2 -> x0, blocking collectives: 35.4 us -> none  [the longest x1 18.5 us: on_device(): lax.all_to_all(placed, 'rep', split_axis=1, concat_axis=0, tiled=True)[:, 0]]
    ppermute x15 -> x38, starting transfers between devices: 17.8 us -> 48.9 us  [partner(): lax.ppermute(value, axis, [(i, i ^ offset) for i in range(lax.axis_size(a...]
    unnamed x93 -> x203, local copies, waits for them, and re-layouts: 21.4 us -> 40 us
    all_to_all x1 -> x0, waiting for transfers between devices: 17.8 us -> none  [on_device(): lax.all_to_all(middle_gradient_list, 'rep', split_axis=1, concat_axis=0,...]
    pallas_call x0 -> x7, Pallas kernels: none -> 17.6 us  [the longest x1 8.71 us: leaf_backward(): pl.pallas_call(leaf_backward_kernel, out_shape=[jax.ShapeDtypeStruct(leaf...]
    reshape x0 -> x15, local copies, waits for them, and re-layouts: none -> 14.1 us  [the longest x5 5.22 us: exchange(): part.reshape(-1, 128)]
  transfers between devices with their start and end apart: 18 -> 38, of which waited for: 17 -> 15; matrix products, arithmetic and copies ran while one was open for 11% -> 49% of each run, Pallas kernels for 0% -> 5%
where the time goes in v1:
time: 282 us; the launch traced here: 280 us
  local copies, waits for them, and re-layouts  79.6 us (28%)
  waiting for transfers between devices  55.3 us (20%)
  other arithmetic  51.6 us (18%)
  starting transfers between devices  48.9 us (17%)
  matrix products  24.5 us (9%)
  Pallas kernels  17.6 us (6%)
    ppermute x38, waiting for transfers between devices, partner(): lax.ppermute(value, axis, [(i, i ^ offset) for i in range(lax.axis_size(a...  55.3 us
    ppermute x38, starting transfers between devices, partner(): lax.ppermute(value, axis, [(i, i ^ offset) for i in range(lax.axis_size(a...  48.9 us
    unnamed x203, local copies, waits for them, and re-layouts  40 us
    dot_general x5, matrix products, matmul_t(): lax.dot_general(left_arr, right_arr, (((1,), (1,)), ((), ())), preferred_...  11.4 us
    convert_element_type x14, other arithmetic, bf16(): return value.astype(jnp.bfloat16)  9.34 us
    pallas_call x1, Pallas kernels, leaf_backward(): pl.pallas_call(leaf_backward_kernel, out_shape=[jax.ShapeDtypeStruct(leaf...  8.71 us
    dot_general x16, matrix products, inner_t(): lax.dot_general(left_arr, right_arr, (((0,), (0,)), ((), ())), preferred_...  8.63 us
    concatenate x10, other arithmetic, join_rows(): return jnp.concatenate([first, second], axis=axis)  5.7 us
  transfers between devices with their start and end apart: 38, of which 15 were waited for; matrix products, arithmetic and copies ran while one was open for 49% of the time, Pallas kernels for 5%

profile of v1, /device:TPU:0, one launch (start us, length us, event | category | flops | bytes accessed | tf_op | source)
XLA Modules:
  0.0 279.6 jit_solution(17902496295562483186)
XLA Ops:
  2.6 2.8 place.1
  5.4 2.9 %collective-permute-start.1 = (bf16[4,128,256]{2,1,0:T(8,128)(2,1)}, bf16[4,128,256]{2,1,0:T(8,128)(2,1)S(1)}, u32[]{:S(2)}, u32[]{:S(2)}) collective-permute-start(bf16[4,128,256]{2,1,0:T(8,128)(2,1)} %get-tuple-element.19), channel_id=1, source_target_pairs={{0,2},{1,3},{2,0},{3,1},{4,6},{5,7},{6,4},{7,5},{8,10},{9,11},{10,... | collective-permute-start | bytes 786440 | tf_op jit(solution)/shard_map/ppermute | solution.py:16
  8.5 3.0 %constant_dynamic-slice_fusion = bf16[1,512,2,1024]{3,2,1,0:T(2,128)(2,1)S(1)} fusion(bf16[1,1024,2,1024]{3,2,1,0:T(2,128)(2,1)} %param.10, s32[]{:T(128)S(6)} %select_n.450), kind=kLoop, calls=%fused_computation.238 | loop fusion | bytes 4194308 | tf_op jit(solution)/shard_map/dynamic-slice.1
  13.3 2.0 collective-permute-start.6
  16.1 2.6 collective-permute-start.9
  20.3 4.9 %collective-permute-done.9 = bf16[512,128]{1,0:T(8,128)(2,1)} collective-permute-done((bf16[512,128]{1,0:T(8,128)(2,1)}, bf16[512,128]{1,0:T(8,128)(2,1)}, u32[]{:S(2)}, u32[]{:S(2)}) %collective-permute-start.9) | collective-permute-done | bytes 131104 | tf_op jit(solution)/shard_map/ppermute | solution.py:16
  29.0 10.2 %collective-permute-done.10 = bf16[512,512]{1,0:T(8,128)(2,1)S(1)} collective-permute-done((bf16[512,512]{1,0:T(8,128)(2,1)S(1)}, bf16[512,512]{1,0:T(8,128)(2,1)S(1)}, u32[]{:S(2)}, u32[]{:S(2)}) %collective-permute-start.10) | collective-permute-done | bytes 524320 | tf_op jit(solution)/shard_map/ppermute | solution.py:16
  44.3 2.1 leaf_forward.3
  57.1 9.8 %collective-permute-done.11 = bf16[512,1024]{1,0:T(8,128)(2,1)} collective-permute-done((bf16[512,1024]{1,0:T(8,128)(2,1)}, bf16[512,1024]{1,0:T(8,128)(2,1)}, u32[]{:S(2)}, u32[]{:S(2)}) %collective-permute-start.11) | collective-permute-done | bytes 1048608 | tf_op jit(solution)/shard_map/ppermute | solution.py:16
  68.2 2.4 pad_maximum_fusion.3
  79.8 4.2 %collective-permute-done.8 = bf16[64,1024]{1,0:T(8,128)(2,1)S(1)} collective-permute-done((bf16[64,1024]{1,0:T(8,128)(2,1)}, bf16[64,1024]{1,0:T(8,128)(2,1)S(1)}, u32[]{:S(2)}, u32[]{:S(2)}) %collective-permute-start.8) | collective-permute-done | bytes 131104 | tf_op jit(solution)/shard_map/ppermute | solution.py:16
  90.8 2.5 collective-permute-start.13
  96.4 4.0 %collective-permute-start.14 = (bf16[16,1024]{1,0:T(8,128)(2,1)S(1)}, bf16[16,1024]{1,0:T(8,128)(2,1)S(1)}, u32[]{:S(2)}, u32[]{:S(2)}) collective-permute-start(bf16[16,1024]{1,0:T(8,128)(2,1)S(1)} %slice.660), channel_id=1, source_target_pairs={{0,16},{4,20},{8,24},{12,28},{16,0},{20,4},{24,8},{28,12},{1,17},{... | collective-permute-start | bytes 98312 | tf_op jit(solution)/shard_map/ppermute | solution.py:16
  102.5 3.1 %collective-permute-start.15 = (bf16[16,1024]{1,0:T(8,128)(2,1)S(1)}, bf16[16,1024]{1,0:T(8,128)(2,1)S(1)}, u32[]{:S(2)}, u32[]{:S(2)}) collective-permute-start(bf16[16,1024]{1,0:T(8,128)(2,1)S(1)} %multiply_convert_fusion.14), channel_id=1, source_target_pairs={{0,16},{4,20},{8,24},{12,28},{16,0},{20,4},{24,8},{28,12},{1,17},{... | collective-permute-start | bytes 98312 | tf_op jit(solution)/shard_map/ppermute | solution.py:16
  109.8 3.5 %copy.68 = bf16[1,1024,2,1024]{3,1,2,0:T(8,128)(2,1)} copy(bf16[1,1024,2,1024]{3,2,1,0:T(2,128)(2,1)S(1)} %copy-done.29) | data formatting | bytes 8388608 | tf_op args[4]
  113.3 3.1 %collective-permute-start.27 = (bf16[32,1024]{1,0:T(8,128)(2,1)S(1)}, bf16[32,1024]{1,0:T(8,128)(2,1)S(1)}, u32[]{:S(2)}, u32[]{:S(2)}) collective-permute-start(bf16[32,1024]{1,0:T(8,128)(2,1)S(1)} %multiply_convert_fusion.10), channel_id=1, source_target_pairs={{0,16},{4,20},{8,24},{12,28},{16,0},{20,4},{24,8},{28,12},{1,17},{... | collective-permute-start | bytes 196616 | tf_op jit(solution)/shard_map/ppermute | solution.py:16
  117.0 2.2 collective-permute-done.27
  141.5 2.7 collective-permute-done.19
  144.2 3.0 %collective-permute-start.20 = (bf16[16,1024]{1,0:T(8,128)(2,1)S(1)}, bf16[16,1024]{1,0:T(8,128)(2,1)S(1)}, u32[]{:S(2)}, u32[]{:S(2)}) collective-permute-start(bf16[16,1024]{1,0:T(8,128)(2,1)S(1)} %slice.659), channel_id=1, source_target_pairs={{0,16},{4,20},{8,24},{12,28},{16,0},{20,4},{24,8},{28,12},{1,17},{... | collective-permute-start | bytes 98312 | tf_op jit(solution)/shard_map/ppermute | solution.py:16
  150.0 2.9 %collective-permute-start.21 = (bf16[16,1024]{1,0:T(8,128)(2,1)}, bf16[16,1024]{1,0:T(8,128)(2,1)}, u32[]{:S(2)}, u32[]{:S(2)}) collective-permute-start(bf16[16,1024]{1,0:T(8,128)(2,1)} %get-tuple-element.73), channel_id=1, source_target_pairs={{0,16},{4,20},{8,24},{12,28},{16,0},{20,4},{24,8},{28,12},{1,17},{... | collective-permute-start | bytes 98312 | tf_op jit(solution)/shard_map/ppermute | solution.py:16
  153.9 2.0 copy.41
  156.3 3.1 %multiply_reduce_fusion.4 = (f32[32]{0:T(128)S(1)}, f32[32,1024]{1,0:T(8,128)}) fusion(f32[32]{0:T(128)S(1)} %add_rsqrt_fusion.1, bf16[32,1024]{1,0:T(8,128)(2,1)} %copy-done.59, f32[64,1024]{1,0:T(8,128)S(1)} %copy-done.41, bf16[1024,1024]{1,0:T(8,128)(2,1)} %copy-done.5, bf16[16,1024]{1,0:T(8,128)(2,1)} %collective-permute-done.21, ...), kind=kOutput, calls=%fused_computation.126 | convolution fusion | flops 67469280 | bytes 2490624 | tf_op jit(solution)/shard_map/dot_general | solution.py:32
  162.2 2.0 collective-permute-start.33
  165.9 2.0 collective-permute-start.22
  170.8 3.2 %multiply_reduce_fusion.2 = (f32[64]{0:T(128)S(1)}, f32[64,1024]{1,0:T(8,128)}) fusion(f32[64]{0:T(128)S(1)} %add_rsqrt_fusion.2, bf16[64,1024]{1,0:T(8,128)(2,1)} %copy-done.45, f32[128,1024]{1,0:T(8,128)S(1)} %copy-done.31, bf16[1024,1024]{1,0:T(8,128)(2,1)} %copy-done.4, bf16[32,1024]{1,0:T(8,128)(2,1)S(1)} %collective-permute-done.22, ...), kind=kOutput, calls=%fused_computation.89 | convolution fusion | flops 134938560 | bytes 2884096 | tf_op jit(solution)/shard_map/dot_general | solution.py:32
  195.4 2.7 multiply_reduce_fusion
  211.0 2.1 broadcast_select_fusion.5
  242.0 2.0 copy.42
  254.8 8.7 %leaf_backward.1 = (bf16[4,256,1024]{2,1,0:T(8,128)(2,1)}, bf16[1024,1024]{1,0:T(8,128)(2,1)}) custom-call(bf16[4,128,256]{2,1,0:T(8,128)(2,1)S(1)} %copy-done.8, bf16[4,128,256]{2,1,0:T(8,128)(2,1)S(1)} %copy-done.14, bf16[4,128,256]{2,1,0:T(8,128)(2,1)S(1)} %copy-done.10, bf16[4,128,256]{2,1,0:T(8,128)(2,1)S(1)} %copy-done.12, ...), custom_call_target="tpu_custom_call" | custom-call | tf_op jit(solution)/shard_map/leaf_backward/pallas_call | solution.py:160
  263.5 3.4 %collective-permute-done.32 = bf16[2,256,512]{1,2,0:T(8,128)(2,1)S(1)} collective-permute-done((bf16[2,256,512]{1,2,0:T(8,128)(2,1)S(1)}, bf16[2,256,512]{1,2,0:T(8,128)(2,1)S(1)}, u32[]{:S(2)}, u32[]{:S(2)}) %collective-permute-start.32) | collective-permute-done | bytes 524320 | tf_op jit(solution)/shard_map/ppermute | solution.py:16
  267.1 10.1 %collective-permute-done.37 = bf16[2,256,512]{1,2,0:T(8,128)(2,1)S(1)} collective-permute-done((bf16[2,256,512]{1,2,0:T(8,128)(2,1)S(1)}, bf16[2,256,512]{1,2,0:T(8,128)(2,1)S(1)}, u32[]{:S(2)}, u32[]{:S(2)}) %collective-permute-start.37) | collective-permute-done | bytes 524320 | tf_op jit(solution)/shard_map/ppermute | solution.py:16
  277.5 2.1 copy.49
  (407 shorter events, 160.3 us)
Async XLA Ops:
  5.4 38.9 %collective-permute-start.1 = (bf16[4,128,256]{2,1,0:T(8,128)(2,1)}, bf16[4,128,256]{2,1,0:T(8,128)(2,1)S(1)}, u32[]{:S(2)}, u32[]{:S(2)}) collective-permute-start(bf16[4,128,256]{2,1,0:T(8,128)(2,1)} %get-tuple-element.19), channel_id=1, source_target_pairs={{0,2},{1,3},{2,0},{3,1},{4,6},{5,7},{6,4},{7,5},{8,10},{9,11},{10,... | collective-permute-start | bytes 786440 | tf_op jit(solution)/shard_map/ppermute | solution.py:16
  8.3 36.0 %collective-permute-start.2 = (bf16[4,128,256]{2,1,0:T(8,128)(2,1)}, bf16[4,128,256]{2,1,0:T(8,128)(2,1)S(1)}, u32[]{:S(2)}, u32[]{:S(2)}) collective-permute-start(bf16[4,128,256]{2,1,0:T(8,128)(2,1)} %get-tuple-element.20), channel_id=1, source_target_pairs={{0,3},{1,2},{2,1},{3,0},{4,7},{5,6},{6,5},{7,4},{8,11},{9,10},{10,... | collective-permute-start | bytes 786440 | tf_op jit(solution)/shard_map/ppermute | solution.py:16
  8.3 42.1 %collective-permute-start = (bf16[4,128,256]{2,1,0:T(8,128)(2,1)S(1)}, bf16[4,128,256]{2,1,0:T(8,128)(2,1)S(1)}, u32[]{:S(2)}, u32[]{:S(2)}) collective-permute-start(bf16[4,128,256]{2,1,0:T(8,128)(2,1)S(1)} %get-tuple-element.18), channel_id=1, source_target_pairs={{0,1},{1,0},{2,3},{3,2},{4,5},{5,4},{6,7},{7,6},{8,9},{9,8},{10,11... | collective-permute-start | bytes 786440 | tf_op jit(solution)/shard_map/ppermute | solution.py:16
  13.3 42.5 %collective-permute-start.6 = (bf16[512,512]{1,0:T(8,128)(2,1)}, bf16[512,512]{1,0:T(8,128)(2,1)}, u32[]{:S(2)}, u32[]{:S(2)}) collective-permute-start(bf16[512,512]{1,0:T(8,128)(2,1)} %get-tuple-element.47), channel_id=1, source_target_pairs={{0,4},{4,0},{8,12},{12,8},{16,20},{20,16},{24,28},{28,24},{1,5},{5... | collective-permute-start | bytes 1572872 | tf_op jit(solution)/shard_map/ppermute | solution.py:16
  16.1 9.1 %collective-permute-start.9 = (bf16[512,128]{1,0:T(8,128)(2,1)}, bf16[512,128]{1,0:T(8,128)(2,1)}, u32[]{:S(2)}, u32[]{:S(2)}) collective-permute-start(bf16[512,128]{1,0:T(8,128)(2,1)} %get-tuple-element.45), channel_id=1, source_target_pairs={{0,16},{4,20},{8,24},{12,28},{16,0},{20,4},{24,8},{28,12},{1,17},{... | collective-permute-start | bytes 393224 | tf_op jit(solution)/shard_map/ppermute | solution.py:16
  26.3 12.9 %collective-permute-start.10 = (bf16[512,512]{1,0:T(8,128)(2,1)S(1)}, bf16[512,512]{1,0:T(8,128)(2,1)S(1)}, u32[]{:S(2)}, u32[]{:S(2)}) collective-permute-start(bf16[512,512]{1,0:T(8,128)(2,1)S(1)} %pad_maximum_fusion.6), channel_id=1, source_target_pairs={{0,8},{4,12},{8,0},{12,4},{16,24},{20,28},{24,16},{28,20},{1,9},{5... | collective-permute-start | bytes 1572872 | tf_op jit(solution)/shard_map/ppermute | solution.py:16
  43.1 23.8 %collective-permute-start.11 = (bf16[512,1024]{1,0:T(8,128)(2,1)}, bf16[512,1024]{1,0:T(8,128)(2,1)}, u32[]{:S(2)}, u32[]{:S(2)}) collective-permute-start(bf16[512,1024]{1,0:T(8,128)(2,1)} %constant_dynamic-update-slice_fusion), channel_id=1, source_target_pairs={{0,4},{4,0},{8,12},{12,8},{16,20},{20,16},{24,28},{28,24},{1,5},{5... | collective-permute-start | bytes 3145736 | tf_op jit(solution)/shard_map/ppermute | solution.py:16
  48.6 5.6 %collective-permute-start.4 = (bf16[128,1024]{1,0:T(8,128)(2,1)}, bf16[128,1024]{1,0:T(8,128)(2,1)S(1)}, u32[]{:S(2)}, u32[]{:S(2)}) collective-permute-start(bf16[128,1024]{1,0:T(8,128)(2,1)} %get-tuple-element.28), channel_id=1, source_target_pairs={{0,1},{1,0},{2,3},{3,2},{4,5},{5,4},{6,7},{7,6},{8,9},{9,8},{10,11... | collective-permute-start | bytes 786440 | tf_op jit(solution)/shard_map/ppermute | solution.py:16
  53.6 19.9 %collective-permute-start.3 = (bf16[128,1024]{1,0:T(8,128)(2,1)S(1)}, bf16[128,1024]{1,0:T(8,128)(2,1)S(1)}, u32[]{:S(2)}, u32[]{:S(2)}) collective-permute-start(bf16[128,1024]{1,0:T(8,128)(2,1)S(1)} %get-tuple-element.26), channel_id=1, source_target_pairs={{0,1},{1,0},{2,3},{3,2},{4,5},{5,4},{6,7},{7,6},{8,9},{9,8},{10,11... | collective-permute-start | bytes 786440 | tf_op jit(solution)/shard_map/ppermute | solution.py:16
  54.3 19.2 %collective-permute-start.5 = (bf16[128,1024]{1,0:T(8,128)(2,1)S(1)}, bf16[128,1024]{1,0:T(8,128)(2,1)S(1)}, u32[]{:S(2)}, u32[]{:S(2)}) collective-permute-start(bf16[128,1024]{1,0:T(8,128)(2,1)S(1)} %multiply_convert_fusion.3), channel_id=1, source_target_pairs={{0,2},{1,3},{2,0},{3,1},{4,6},{5,7},{6,4},{7,5},{8,10},{9,11},{10,... | collective-permute-start | bytes 786440 | tf_op jit(solution)/shard_map/ppermute | solution.py:16
  57.0 16.9 %collective-permute-start.7 = (bf16[512,1024]{1,0:T(8,128)(2,1)S(1)}, bf16[512,1024]{1,0:T(8,128)(2,1)S(1)}, u32[]{:S(2)}, u32[]{:S(2)}) collective-permute-start(bf16[512,1024]{1,0:T(8,128)(2,1)S(1)} %pad_maximum_fusion.1.mine_ref), channel_id=1, source_target_pairs={{0,1},{1,0},{2,3},{3,2},{4,5},{5,4},{6,7},{7,6},{8,9},{9,8},{10,11... | collective-permute-start | bytes 3145736 | tf_op jit(solution)/shard_map/ppermute | solution.py:16
  72.1 14.2 %collective-permute-start.12 = (bf16[2,512,1024]{2,1,0:T(8,128)(2,1)}, bf16[2,512,1024]{2,1,0:T(8,128)(2,1)}, u32[]{:S(2)}, u32[]{:S(2)}) collective-permute-start(bf16[2,512,1024]{2,1,0:T(8,128)(2,1)} %pad_maximum_fusion), channel_id=1, source_target_pairs={{0,1},{1,0},{2,3},{3,2},{4,5},{5,4},{6,7},{7,6},{8,9},{9,8},{10,11... | collective-permute-start | bytes 6291464 | tf_op jit(solution)/shard_map/ppermute | solution.py:16
  77.9 6.1 %collective-permute-start.8 = (bf16[64,1024]{1,0:T(8,128)(2,1)}, bf16[64,1024]{1,0:T(8,128)(2,1)S(1)}, u32[]{:S(2)}, u32[]{:S(2)}) collective-permute-start(bf16[64,1024]{1,0:T(8,128)(2,1)} %slice.656), channel_id=1, source_target_pairs={{0,4},{4,0},{8,12},{12,8},{16,20},{20,16},{24,28},{28,24},{1,5},{5... | collective-permute-start | bytes 393224 | tf_op jit(solution)/shard_map/ppermute | solution.py:16
  96.4 5.9 %collective-permute-start.14 = (bf16[16,1024]{1,0:T(8,128)(2,1)S(1)}, bf16[16,1024]{1,0:T(8,128)(2,1)S(1)}, u32[]{:S(2)}, u32[]{:S(2)}) collective-permute-start(bf16[16,1024]{1,0:T(8,128)(2,1)S(1)} %slice.660), channel_id=1, source_target_pairs={{0,16},{4,20},{8,24},{12,28},{16,0},{20,4},{24,8},{28,12},{1,17},{... | collective-permute-start | bytes 98312 | tf_op jit(solution)/shard_map/ppermute | solution.py:16
  102.5 5.1 %collective-permute-start.15 = (bf16[16,1024]{1,0:T(8,128)(2,1)S(1)}, bf16[16,1024]{1,0:T(8,128)(2,1)S(1)}, u32[]{:S(2)}, u32[]{:S(2)}) collective-permute-start(bf16[16,1024]{1,0:T(8,128)(2,1)S(1)} %multiply_convert_fusion.14), channel_id=1, source_target_pairs={{0,16},{4,20},{8,24},{12,28},{16,0},{20,4},{24,8},{28,12},{1,17},{... | collective-permute-start | bytes 98312 | tf_op jit(solution)/shard_map/ppermute | solution.py:16
  107.6 8.8 %collective-permute-start.16 = (bf16[32,1024]{1,0:T(8,128)(2,1)S(1)}, bf16[32,1024]{1,0:T(8,128)(2,1)S(1)}, u32[]{:S(2)}, u32[]{:S(2)}) collective-permute-start(bf16[32,1024]{1,0:T(8,128)(2,1)S(1)} %pad_maximum_fusion.23), channel_id=1, source_target_pairs={{0,8},{4,12},{8,0},{12,4},{16,24},{20,28},{24,16},{28,20},{1,9},{5... | collective-permute-start | bytes 196616 | tf_op jit(solution)/shard_map/ppermute | solution.py:16
  113.3 5.8 %collective-permute-start.27 = (bf16[32,1024]{1,0:T(8,128)(2,1)S(1)}, bf16[32,1024]{1,0:T(8,128)(2,1)S(1)}, u32[]{:S(2)}, u32[]{:S(2)}) collective-permute-start(bf16[32,1024]{1,0:T(8,128)(2,1)S(1)} %multiply_convert_fusion.10), channel_id=1, source_target_pairs={{0,16},{4,20},{8,24},{12,28},{16,0},{20,4},{24,8},{28,12},{1,17},{... | collective-permute-start | bytes 196616 | tf_op jit(solution)/shard_map/ppermute | solution.py:16
  116.5 5.0 %collective-permute-start.17 = (bf16[64,1024]{1,0:T(8,128)(2,1)S(1)}, bf16[64,1024]{1,0:T(8,128)(2,1)S(1)}, u32[]{:S(2)}, u32[]{:S(2)}) collective-permute-start(bf16[64,1024]{1,0:T(8,128)(2,1)S(1)} %pad_maximum_fusion.15), channel_id=1, source_target_pairs={{0,4},{4,0},{8,12},{12,8},{16,20},{20,16},{24,28},{28,24},{1,5},{5... | collective-permute-start | bytes 393224 | tf_op jit(solution)/shard_map/ppermute | solution.py:16
  121.0 16.1 %collective-permute-start.28 = (bf16[128,1024]{1,0:T(8,128)(2,1)}, bf16[128,1024]{1,0:T(8,128)(2,1)}, u32[]{:S(2)}, u32[]{:S(2)}) collective-permute-start(bf16[128,1024]{1,0:T(8,128)(2,1)} %pad_maximum_fusion.11), channel_id=1, source_target_pairs={{0,8},{4,12},{8,0},{12,4},{16,24},{20,28},{24,16},{28,20},{1,9},{5... | collective-permute-start | bytes 786440 | tf_op jit(solution)/shard_map/ppermute | solution.py:16
  134.7 5.0 %collective-permute-start.18 = (bf16[64,1024]{1,0:T(8,128)(2,1)S(1)}, bf16[64,1024]{1,0:T(8,128)(2,1)S(1)}, u32[]{:S(2)}, u32[]{:S(2)}) collective-permute-start(bf16[64,1024]{1,0:T(8,128)(2,1)S(1)} %slice.655), channel_id=1, source_target_pairs={{0,4},{4,0},{8,12},{12,8},{16,20},{20,16},{24,28},{28,24},{1,5},{5... | collective-permute-start | bytes 393224 | tf_op jit(solution)/shard_map/ppermute | solution.py:16
  150.0 6.2 %collective-permute-start.21 = (bf16[16,1024]{1,0:T(8,128)(2,1)}, bf16[16,1024]{1,0:T(8,128)(2,1)}, u32[]{:S(2)}, u32[]{:S(2)}) collective-permute-start(bf16[16,1024]{1,0:T(8,128)(2,1)} %get-tuple-element.73), channel_id=1, source_target_pairs={{0,16},{4,20},{8,24},{12,28},{16,0},{20,4},{24,8},{28,12},{1,17},{... | collective-permute-start | bytes 98312 | tf_op jit(solution)/shard_map/ppermute | solution.py:16
  155.8 55.1 %collective-permute-start.29 = (bf16[384,1024]{1,0:T(8,128)(2,1)}, bf16[384,1024]{1,0:T(8,128)(2,1)}, u32[]{:S(2)}, u32[]{:S(2)}) collective-permute-start(bf16[384,1024]{1,0:T(8,128)(2,1)} %pad_maximum_fusion.5), channel_id=1, source_target_pairs={{0,4},{4,0},{8,12},{12,8},{16,20},{20,16},{24,28},{28,24},{1,5},{5... | collective-permute-start | bytes 2359304 | tf_op jit(solution)/shard_map/ppermute | solution.py:16
  162.2 5.7 %collective-permute-start.33 = (bf16[128,128]{1,0:T(8,128)(2,1)}, bf16[128,128]{1,0:T(8,128)(2,1)}, u32[]{:S(2)}, u32[]{:S(2)}) collective-permute-start(bf16[128,128]{1,0:T(8,128)(2,1)} %reshape.248), channel_id=1, source_target_pairs={{0,16},{4,20},{8,24},{12,28},{16,0},{20,4},{24,8},{28,12},{1,17},{... | collective-permute-start | bytes 98312 | tf_op jit(solution)/shard_map/ppermute | solution.py:16
  181.4 8.6 %collective-permute-start.23 = (bf16[64,1024]{1,0:T(8,128)(2,1)}, bf16[64,1024]{1,0:T(8,128)(2,1)S(1)}, u32[]{:S(2)}, u32[]{:S(2)}) collective-permute-start(bf16[64,1024]{1,0:T(8,128)(2,1)} %get-tuple-element.60), channel_id=1, source_target_pairs={{0,4},{4,0},{8,12},{12,8},{16,20},{20,16},{24,28},{28,24},{1,5},{5... | collective-permute-start | bytes 393224 | tf_op jit(solution)/shard_map/ppermute | solution.py:16
  189.3 12.5 %collective-permute-start.35 = (bf16[384,128]{1,0:T(8,128)(2,1)}, bf16[384,128]{1,0:T(8,128)(2,1)}, u32[]{:S(2)}, u32[]{:S(2)}) collective-permute-start(bf16[384,128]{1,0:T(8,128)(2,1)} %pad_maximum_fusion.19), channel_id=1, source_target_pairs={{0,4},{4,0},{8,12},{12,8},{16,20},{20,16},{24,28},{28,24},{1,5},{5... | collective-permute-start | bytes 294920 | tf_op jit(solution)/shard_map/ppermute | solution.py:16
  194.1 12.1 %collective-permute-start.30 = (bf16[512,128]{1,0:T(8,128)(2,1)}, bf16[512,128]{1,0:T(8,128)(2,1)}, u32[]{:S(2)}, u32[]{:S(2)}) collective-permute-start(bf16[512,128]{1,0:T(8,128)(2,1)} %reshape.244), channel_id=1, source_target_pairs={{0,4},{4,0},{8,12},{12,8},{16,20},{20,16},{24,28},{28,24},{1,5},{5... | collective-permute-start | bytes 393224 | tf_op jit(solution)/shard_map/ppermute | solution.py:16
  200.2 8.4 %collective-permute-start.25 = (bf16[128,1024]{1,0:T(8,128)(2,1)}, bf16[128,1024]{1,0:T(8,128)(2,1)}, u32[]{:S(2)}, u32[]{:S(2)}) collective-permute-start(bf16[128,1024]{1,0:T(8,128)(2,1)} %get-tuple-element.48), channel_id=1, source_target_pairs={{0,2},{1,3},{2,0},{3,1},{4,6},{5,7},{6,4},{7,5},{8,10},{9,11},{10,... | collective-permute-start | bytes 786440 | tf_op jit(solution)/shard_map/ppermute | solution.py:16
  201.7 53.0 %collective-permute-start.24 = (bf16[128,1024]{1,0:T(8,128)(2,1)}, bf16[128,1024]{1,0:T(8,128)(2,1)S(1)}, u32[]{:S(2)}, u32[]{:S(2)}) collective-permute-start(bf16[128,1024]{1,0:T(8,128)(2,1)} %get-tuple-element.49), channel_id=1, source_target_pairs={{0,1},{1,0},{2,3},{3,2},{4,5},{5,4},{6,7},{7,6},{8,9},{9,8},{10,11... | collective-permute-start | bytes 786440 | tf_op jit(solution)/shard_map/ppermute | solution.py:16
  210.5 44.3 %collective-permute-start.26 = (bf16[128,1024]{1,0:T(8,128)(2,1)}, bf16[128,1024]{1,0:T(8,128)(2,1)S(1)}, u32[]{:S(2)}, u32[]{:S(2)}) collective-permute-start(bf16[128,1024]{1,0:T(8,128)(2,1)} %get-tuple-element.102), channel_id=1, source_target_pairs={{0,1},{1,0},{2,3},{3,2},{4,5},{5,4},{6,7},{7,6},{8,9},{9,8},{10,11... | collective-permute-start | bytes 786440 | tf_op jit(solution)/shard_map/ppermute | solution.py:16
  230.6 19.6 %collective-permute-start.31 = (bf16[2,512,512]{1,2,0:T(8,128)(2,1)}, bf16[2,512,512]{1,2,0:T(8,128)(2,1)}, u32[]{:S(2)}, u32[]{:S(2)}) collective-permute-start(bf16[2,512,512]{1,2,0:T(8,128)(2,1)} %pad_maximum_fusion.4), channel_id=1, source_target_pairs={{0,1},{1,0},{2,3},{3,2},{4,5},{5,4},{6,7},{7,6},{8,9},{9,8},{10,11... | collective-permute-start | bytes 3145736 | tf_op jit(solution)/shard_map/ppermute | solution.py:16
  252.1 14.9 %collective-permute-start.32 = (bf16[2,256,512]{1,2,0:T(8,128)(2,1)S(1)}, bf16[2,256,512]{1,2,0:T(8,128)(2,1)S(1)}, u32[]{:S(2)}, u32[]{:S(2)}) collective-permute-start(bf16[2,256,512]{1,2,0:T(8,128)(2,1)S(1)} %select_convert_fusion.1), channel_id=1, source_target_pairs={{0,2},{1,3},{2,0},{3,1},{4,6},{5,7},{6,4},{7,5},{8,10},{9,11},{10,... | collective-permute-start | bytes 1572872 | tf_op jit(solution)/shard_map/ppermute | solution.py:16
  253.2 24.0 %collective-permute-start.37 = (bf16[2,256,512]{1,2,0:T(8,128)(2,1)S(1)}, bf16[2,256,512]{1,2,0:T(8,128)(2,1)S(1)}, u32[]{:S(2)}, u32[]{:S(2)}) collective-permute-start(bf16[2,256,512]{1,2,0:T(8,128)(2,1)S(1)} %select_convert_fusion), channel_id=1, source_target_pairs={{0,2},{1,3},{2,0},{3,1},{4,6},{5,7},{6,4},{7,5},{8,10},{9,11},{10,... | collective-permute-start | bytes 1572872 | tf_op jit(solution)/shard_map/ppermute | solution.py:16
  (97 other events, 661.0 us)

commit v2 on v1

v2 whole, which is shorter than its diff:
```python
import functools

import jax
import jax.numpy as jnp
from jax import lax
from jax.experimental import pallas as pl
from jax.experimental.pallas import tpu as pltpu
from jax.sharding import PartitionSpec as P

EPSILON = 1e-06
CHILDREN = 4
MIB = 1024 * 1024


def partner(value, axis, offset):
    return lax.ppermute(value, axis, [(i, i ^ offset) for i in range(lax.axis_size(axis))])


def rms_factor(values):
    return lax.rsqrt(jnp.mean(values * values, axis=-1, keepdims=True) + EPSILON)


def norm_back(gradient, normed, factor):
    return factor * (gradient - normed * jnp.mean(gradient * normed, axis=-1, keepdims=True))


def matmul(left_arr, right_arr):
    return jnp.dot(left_arr, right_arr, preferred_element_type=jnp.float32)


def matmul_t(left_arr, right_arr):
    return lax.dot_general(
        left_arr, right_arr, (((1,), (1,)), ((), ())), preferred_element_type=jnp.float32
    )


def inner_t(left_arr, right_arr):
    return lax.dot_general(
        left_arr, right_arr, (((0,), (0,)), ((), ())), preferred_element_type=jnp.float32
    )


def bf16(value):
    return value.astype(jnp.bfloat16)


def f32(value):
    return value.astype(jnp.float32)


def whole_block():
    return pl.BlockSpec(memory_space=pltpu.VMEM)


def place_kernel(slots, ids_ref, map_ref, regions_ref, *rest):
    outs, wide = rest[:CHILDREN], rest[CHILDREN]
    rows = regions_ref.shape[0] // slots
    parts = wide.shape[0]
    for part in range(parts):
        wide[part] = regions_ref[:, part * 128 : (part + 1) * 128].astype(jnp.float32)
    row = lax.broadcasted_iota(jnp.int32, (rows, rows), 0)
    col = lax.broadcasted_iota(jnp.int32, (rows, rows), 1)
    select = (jnp.bitwise_xor(row, ids_ref[1]) == col).astype(jnp.bfloat16)
    for offset in range(CHILDREN):
        node = jnp.bitwise_xor(ids_ref[0], offset)
        for child in range(CHILDREN):
            region = map_ref[node * CHILDREN + child]
            for part in range(parts):
                values = wide[part, pl.ds(region, rows, stride=slots), :].astype(jnp.bfloat16)
                outs[offset][child, :, part * 128 : (part + 1) * 128] = matmul(
                    select, values
                ).astype(jnp.bfloat16)


def place(regions, leaf_map, ids):
    rows, slots, feats = regions.shape
    flat = regions.reshape(rows * slots, feats)
    smem = pl.BlockSpec(memory_space=pltpu.SMEM)
    return pl.pallas_call(
        functools.partial(place_kernel, slots),
        out_shape=[jax.ShapeDtypeStruct((CHILDREN, rows, feats), jnp.bfloat16)] * CHILDREN,
        in_specs=[smem, smem, whole_block()],
        out_specs=[whole_block()] * CHILDREN,
        scratch_shapes=[pltpu.VMEM((feats // 128, rows * slots, 128), jnp.float32)],
        compiler_params=pltpu.CompilerParams(vmem_limit_bytes=16 * MIB),
        name="place",
    )(ids, leaf_map, flat)


def leaf_forward_kernel(count, *refs):
    placed, leaf_w, mid_w = refs[:count], refs[count], refs[count + 1]
    msgs, terms = refs[count + 2 : 2 * count + 2], refs[2 * count + 2 :]
    rows = placed[0].shape[1]
    product = None
    for child in range(CHILDREN):
        values = jnp.concatenate([ref[child] for ref in placed], axis=0)
        factor = 1.0 + matmul(values, leaf_w[child])
        product = factor if product is None else product * factor
    message = bf16(product * rms_factor(product))
    out = bf16(matmul(message, mid_w[...]))
    for i in range(count):
        msgs[i][...] = message[i * rows : (i + 1) * rows]
        terms[i][...] = out[i * rows : (i + 1) * rows]


def leaf_forward(placed, leaf_w, mid_w):
    count = len(placed)
    rows = placed[0].shape[1]
    width = mid_w.shape[0]
    return pl.pallas_call(
        functools.partial(leaf_forward_kernel, count),
        out_shape=[jax.ShapeDtypeStruct((rows, width), jnp.bfloat16)] * (2 * count),
        in_specs=[whole_block()] * (count + 2),
        out_specs=[whole_block()] * (2 * count),
        compiler_params=pltpu.CompilerParams(vmem_limit_bytes=24 * MIB),
        name="leaf_forward",
    )(*placed, leaf_w, mid_w)


def leaf_backward_kernel(*refs):
    placed, msgs, grads = refs[0:4], refs[4:8], refs[8:12]
    leaf_w, mid_w, leaf_out, mid_out, cot = refs[12:17]
    rows = placed[0].shape[1]
    for pair in range(2):
        chunk = [2 * pair, 2 * pair + 1]
        factors = [
            1.0 + matmul(jnp.concatenate([placed[c][child] for c in chunk], axis=0), leaf_w[child])
            for child in range(CHILDREN)
        ]
        low = factors[0] * factors[1]
        high = factors[2] * factors[3]
        product = low * high
        scale = rms_factor(product)
        back = matmul_t(jnp.concatenate([grads[c][...] for c in chunk], axis=0), mid_w[...])
        node = norm_back(back, product * scale, scale)
        node_high = node * high
        node_low = node * low
        where = slice(pair * 2 * rows, (pair + 1) * 2 * rows)
        cot[0, where] = bf16(node_high * factors[1])
        cot[1, where] = bf16(node_high * factors[0])
        cot[2, where] = bf16(node_low * factors[3])
        cot[3, where] = bf16(node_low * factors[2])
    all_grads = jnp.concatenate([ref[...] for ref in grads], axis=0)
    all_msgs = jnp.concatenate([ref[...] for ref in msgs], axis=0)
    mid_out[...] = bf16(inner_t(all_msgs, all_grads))
    for child in range(CHILDREN):
        values = jnp.concatenate([ref[child] for ref in placed], axis=0)
        leaf_out[child] = bf16(inner_t(values, cot[child]))


def leaf_backward(placed, msgs, grads, leaf_w, mid_w):
    rows = placed[0].shape[1]
    return pl.pallas_call(
        leaf_backward_kernel,
        out_shape=[
            jax.ShapeDtypeStruct(leaf_w.shape, jnp.bfloat16),
            jax.ShapeDtypeStruct(mid_w.shape, jnp.bfloat16),
        ],
        in_specs=[whole_block()] * 14,
        out_specs=[whole_block()] * 2,
        scratch_shapes=[pltpu.VMEM((CHILDREN, 4 * rows, mid_w.shape[0]), jnp.bfloat16)],
        compiler_params=pltpu.CompilerParams(vmem_limit_bytes=48 * MIB),
        name="leaf_backward",
    )(*placed, *msgs, *grads, leaf_w, mid_w)


def fused(body, name, *args):
    if any(arg.shape[-2] % 16 for arg in args):
        return body(*args)
    shapes = jax.eval_shape(body, *args)

    def kernel(*refs):
        results = body(*[ref[...] for ref in refs[: len(args)]])
        for ref, result in zip(refs[len(args) :], results):
            ref[...] = result

    return pl.pallas_call(
        kernel,
        out_shape=shapes,
        in_specs=[whole_block()] * len(args),
        out_specs=[whole_block()] * len(shapes),
        compiler_params=pltpu.CompilerParams(vmem_limit_bytes=24 * MIB),
        name=name,
    )(*args)


def ids_of(*values):
    return jnp.stack(values).astype(jnp.int32)


def smem_block():
    return pl.BlockSpec(memory_space=pltpu.SMEM)


def reverse_bits(value, count):
    out = 0
    for i in range(count):
        out = out * 2 + (value >> i) % 2
    return out


def join(pieces):
    if pieces[0].shape[0] % 16 == 0:
        return jnp.concatenate(pieces, axis=0)
    wide = lax.optimization_barrier(tuple(f32(piece) for piece in pieces))
    return bf16(lax.optimization_barrier(jnp.concatenate(wide, axis=0)))


def cut_kernel(depth, ids_ref, maps_ref, *outs):
    width = maps_ref.shape[1]
    half = width // 2
    rows = pl.ds(pl.multiple_of(ids_ref[0] * half, half), half)
    for level in range(depth):
        span = width >> (level + 1)
        cols = pl.ds(width - 2 * span, span)
        side = ids_ref[1 + level]
        outs[3 * level][...] = maps_ref[side, :, cols]
        outs[3 * level + 1][...] = maps_ref[side, rows, cols]
        outs[3 * level + 2][...] = maps_ref[1 - side, rows, cols]
    span = width >> depth
    for side in range(2):
        outs[3 * depth + side][...] = maps_ref[side, :, pl.ds(width - span, span)]


def cut_maps(maps, core, sides):
    depth = len(sides)
    width = maps.shape[1]
    half = width // 2
    spans = [width >> (level + 1) for level in range(depth)]
    if spans[-1] % 128 == 0:
        shapes = []
        for span in spans:
            shapes += [(width, span), (half, span), (half, span)]
        shapes += [(width, spans[-1])] * 2
        outs = pl.pallas_call(
            functools.partial(cut_kernel, depth),
            out_shape=[jax.ShapeDtypeStruct(shape, maps.dtype) for shape in shapes],
            in_specs=[smem_block(), whole_block()],
            out_specs=[whole_block()] * len(shapes),
            compiler_params=pltpu.CompilerParams(vmem_limit_bytes=24 * MIB),
            name="cut_maps",
        )(ids_of(core, *sides), maps)
    else:
        outs = []
        for span, side in zip(spans, sides):
            first = width - 2 * span
            outs.append(lax.dynamic_slice(maps, (side, 0, first), (1, width, span))[0])
            for which in (side, 1 - side):
                outs.append(lax.dynamic_slice(maps, (which, core * half, first), (1, half, span))[0])
        outs += [maps[0, :, width - spans[-1] :], maps[1, :, width - spans[-1] :]]
    return [outs[3 * i : 3 * i + 3] for i in range(depth)], outs[3 * depth :]


def assemble_kernel(count, ids_ref, own_ref, *refs):
    mine, other, out_ref = refs[:count], refs[count : 2 * count], refs[2 * count]
    half, span = mine[0].shape
    for offset in range(count + 1):
        block = jnp.bitwise_xor(ids_ref[1], offset)
        cols = pl.ds(pl.multiple_of(block * span, span), span)
        if offset == 0:
            out_ref[:, cols] = own_ref[...]
            continue
        for ref, core in ((mine[offset - 1], ids_ref[0]), (other[offset - 1], 1 - ids_ref[0])):
            out_ref[pl.ds(pl.multiple_of(core * half, half), half), cols] = ref[...]


def assemble(own, mine, other, core, block):
    width, span = own.shape
    count = len(mine)
    if span % 128 == 0:
        return pl.pallas_call(
            functools.partial(assemble_kernel, count),
            out_shape=jax.ShapeDtypeStruct((width, span * (count + 1)), own.dtype),
            in_specs=[smem_block()] + [whole_block()] * (2 * count + 1),
            out_specs=whole_block(),
            compiler_params=pltpu.CompilerParams(vmem_limit_bytes=16 * MIB),
            name="assemble",
        )(ids_of(core, block), own, *mine, *other)
    out = jnp.zeros((width, span * (count + 1)), own.dtype)
    out = lax.dynamic_update_slice(out, own, (0, block * span))
    for i in range(count):
        col = (block ^ (i + 1)) * span
        out = lax.dynamic_update_slice(out, mine[i], (core * (width // 2), col))
        out = lax.dynamic_update_slice(out, other[i], ((1 - core) * (width // 2), col))
    return out


def cut_grads_kernel(count, ids_ref, low_ref, high_ref, *outs):
    rows, width = low_ref.shape
    span = width // count
    for offset in range(count):
        block = jnp.bitwise_xor(ids_ref[0], offset)
        cols = pl.ds(pl.multiple_of(block * span, span), span)
        outs[offset][:rows] = low_ref[:, cols]
        outs[offset][rows:] = high_ref[:, cols]


def cut_grads(low, high, block, count):
    rows, width = low.shape
    span = width // count
    if span % 128 == 0 and rows % 16 == 0:
        return pl.pallas_call(
            functools.partial(cut_grads_kernel, count),
            out_shape=[jax.ShapeDtypeStruct((2 * rows, span), low.dtype)] * count,
            in_specs=[smem_block(), whole_block(), whole_block()],
            out_specs=[whole_block()] * count,
            name="cut_grads",
        )(ids_of(block), low, high)
    full = join([low, high])
    return [
        lax.dynamic_slice_in_dim(full, (block ^ offset) * span, span, 1) for offset in range(count)
    ]


def upper_grads_kernel(counts, ids_ref, *refs):
    keep_ref, give_ref = refs[-2:]
    quarter = keep_ref.shape[1] // 2
    at, col = 0, 0
    for index, count in enumerate(counts):
        inputs, grads = refs[at : at + count], refs[at + count : at + 2 * count]
        at += 2 * count
        span = grads[0].shape[1]
        half = count // 2
        for turn in range(2):
            pick = range(turn * half, (turn + 1) * half)
            grad = jnp.concatenate([grads[i][...] for i in pick], axis=0)
            side = jnp.bitwise_xor(ids_ref[1 + index], turn)
            for far in range(2):
                for which, out in ((ids_ref[0], keep_ref), (1 - ids_ref[0], give_ref)):
                    lanes = pl.ds(pl.multiple_of((2 * far + which) * quarter, quarter), quarter)
                    rows = jnp.concatenate([inputs[i][:, lanes] for i in pick], axis=0)
                    out[side, far * quarter : (far + 1) * quarter, col : col + span] = inner_t(
                        rows, grad
                    ).astype(out.dtype)
        col += span


def upper_grads(entries, core):
    width = entries[0][1][0].shape[1]
    spans = [entry[2][0].shape[1] for entry in entries]
    shape = (2, width // 2, sum(spans))
    pieces = []
    for _, inputs, grads in entries:
        pieces += list(inputs) + list(grads)
    if all(piece.shape[0] % 16 == 0 and piece.shape[1] % 128 == 0 for piece in pieces):
        return pl.pallas_call(
            functools.partial(upper_grads_kernel, [len(entry[1]) for entry in entries]),
            out_shape=[
                jax.ShapeDtypeStruct(shape, jnp.float32),
                jax.ShapeDtypeStruct(shape, jnp.bfloat16),
            ],
            in_specs=[smem_block()] + [whole_block()] * len(pieces),
            out_specs=[whole_block()] * 2,
            compiler_params=pltpu.CompilerParams(vmem_limit_bytes=24 * MIB),
            name="upper_grads",
        )(ids_of(core, *[entry[0] for entry in entries]), *pieces)
    kept, given = [], []
    for first, inputs, grads in entries:
        half = len(inputs) // 2
        both = []
        for turn in range(2):
            pick = slice(turn * half, (turn + 1) * half)
            both.append(inner_t(join(inputs[pick]), join(grads[pick])))
        pair = jnp.stack([jnp.where(first == 1, both[1 - i], both[i]) for i in range(2)])
        pair = pair.reshape(2, 2, 2, width // 4, -1)
        keep = jnp.where(core == 1, pair[:, :, 1], pair[:, :, 0])
        give = jnp.where(core == 1, pair[:, :, 0], pair[:, :, 1])
        kept.append(keep.reshape(2, width // 2, -1))
        given.append(bf16(give.reshape(2, width // 2, -1)))
    return jnp.concatenate(kept, axis=2), jnp.concatenate(given, axis=2)


def mid_forward(term, near, far, weight):
    product = (1.0 + f32(term)) * (1.0 + f32(near)) * f32(far)
    return up_product(bf16(product * rms_factor(product)), weight)


def up_product(message, weight):
    up = matmul(message, weight)
    keep = up.shape[0] // 2
    return message, up[:keep], bf16(up[keep:])


def up_forward(own_up, other_up, weight):
    joined = (1.0 + own_up) * (1.0 + f32(other_up))
    return up_product(bf16(joined * rms_factor(joined)), weight)


def top_forward(own_up, other_up):
    joined = (1.0 + own_up) * (1.0 + f32(other_up))
    return (bf16(joined * rms_factor(joined)),)


def head_body(count, cotangent, left, right, *pieces):
    root = jnp.concatenate(pieces, axis=0) if len(pieces) > 1 else pieces[0]
    value = matmul(root, left)
    gating = jax.nn.sigmoid(matmul(root, right))
    grad_value = bf16(cotangent * gating)
    grad_gate = bf16(cotangent * value * gating * (1.0 - gating))
    back = matmul_t(grad_value, left) + matmul_t(grad_gate, right)
    rows = root.shape[0] // count
    outs = [back[:rows]] + [bf16(back[i * rows : (i + 1) * rows]) for i in range(1, count)]
    return [root, grad_value, grad_gate] + outs


def level_back(grad_msg, own_up, other_up):
    own_up, other_up = 1.0 + own_up, 1.0 + f32(other_up)
    joined = own_up * other_up
    scaling = rms_factor(joined)
    grad = norm_back(grad_msg, joined * scaling, scaling)
    return bf16(grad * other_up), bf16(grad * own_up)


def top_back(own_up, other_up, own_part, *parts):
    total = own_part
    for part in parts:
        total = total + f32(part)
    return level_back(total, own_up, other_up)


def down_back(own_up, other_up, weight, low, high):
    return level_back(matmul_t(join([low, high]), weight), own_up, other_up)


def mid_back(term, near, far, weight, low, high):
    own, near, far = 1.0 + f32(term), 1.0 + f32(near), f32(far)
    pair = own * near
    product = pair * far
    scale = rms_factor(product)
    grad_msg = matmul_t(join([low, high]), weight)
    grad = norm_back(grad_msg, product * scale, scale)
    grad_pair = grad * far
    return bf16(grad_pair * near), bf16(grad_pair * own), bf16(grad * pair)


def far_back(grad_pair, term, near):
    grad_pair = f32(grad_pair)
    return bf16(grad_pair * (1.0 + f32(near))), bf16(grad_pair * (1.0 + f32(term)))


def pair_product(term, near):
    return (bf16((1.0 + f32(term)) * (1.0 + f32(near))),)


def swap_blocks(array, size, axis):
    count = array.shape[axis] // size
    parts = [lax.slice_in_dim(array, i * size, (i + 1) * size, axis=axis) for i in range(count)]
    return jnp.concatenate([parts[i ^ 1] for i in range(count)], axis=axis)


def on_device(regions, leaf_map, leaf_bond_weight, mid_weight, upper_weight, head_cotangent):
    rows = regions.shape[0]
    width = upper_weight.shape[1]
    sub_count = lax.axis_size("sub")
    depth = sub_count.bit_length() - 1
    sub_index = lax.axis_index("sub")
    rep_index = lax.axis_index("rep")
    core = rep_index % 2
    far = rep_index // 2
    bits = [(sub_index >> level) % 2 for level in range(depth)]
    flip = sum(bits[level] * (rows >> (level + 1)) for level in range(depth))
    leaf_w = leaf_bond_weight[0]
    mid_w = mid_weight[0, 0]

    sent = place(regions, leaf_map, ids_of(rep_index, flip))
    far_both = partner(sent[3], "rep", 3)
    far_one = partner(sent[2], "rep", 2)
    near = partner(sent[1], "rep", 1)
    placed = [sent[0], near, far_one, far_both]

    maps = lax.optimization_barrier(jnp.transpose(upper_weight[0], (1, 0, 2)))
    blocks, (head_left, head_right) = cut_maps(maps, core, bits)
    mine = [
        [
            partner(blocks[level][1 if offset < 1 << level else 2], "sub", offset)
            for offset in range(1, 2 << level)
        ]
        for level in range(depth)
    ]
    other = [[partner(piece, "rep", 1) for piece in pieces] for pieces in mine]
    weights = [
        assemble(blocks[level][0], mine[level], other[level], core, sub_index % (2 << level))
        for level in range(depth)
    ]
    cotangent = head_cotangent
    for level in range(depth):
        swapped = swap_blocks(cotangent, rows >> (level + 1), 0)
        cotangent = jnp.where(bits[level] == 1, swapped, cotangent)

    msg0, msg1, term0, term1 = leaf_forward(placed[:2], leaf_w, mid_w)
    near0 = partner(term1, "rep", 1)
    msg2, msg3, term2, term3 = leaf_forward(placed[2:], leaf_w, mid_w)
    near2 = partner(term3, "rep", 1)
    far_pair = partner(fused(pair_product, "pair_product", term2, near2)[0], "rep", 2)

    messages, own_ups, other_ups = [], [], []
    for level in range(depth):
        if level == 0:
            step = fused(mid_forward, "mid_forward", term0, near0, far_pair, weights[0])
        else:
            step = fused(up_forward, "up_forward", own_ups[-1], other_ups[-1], weights[level])
        messages.append(step[0])
        own_ups.append(step[1])
        other_ups.append(partner(step[2], "sub", 1 << level))
    (root,) = fused(top_forward, "top_forward", own_ups[-1], other_ups[-1])

    order = [reverse_bits(i, depth) for i in range(sub_count)]
    roots = [root] + [partner(root, "sub", offset) for offset in range(1, sub_count)]
    pieces = [roots[offset] for offset in order]
    if root.shape[0] % 16:
        pieces = [join(pieces)]
    root, grad_value, grad_gate, *parts = fused(
        functools.partial(head_body, sub_count),
        "head",
        cotangent,
        head_left,
        head_right,
        *pieces,
    )
    parts = [parts[0]] + [
        partner(parts[block], "sub", order[block]) for block in range(1, sub_count)
    ]

    lows, highs = [None] * depth, [None] * depth
    for level in reversed(range(depth)):
        if level == depth - 1:
            low, high = fused(top_back, "top_back", own_ups[level], other_ups[level], *parts)
        else:
            low, high = fused(
                down_back,
                "down_back",
                own_ups[level],
                other_ups[level],
                weights[level + 1],
                lows[level + 1],
                highs[level + 1],
            )
        lows[level] = low
        highs[level] = partner(high, "sub", 1 << level)

    back0, back1, pair_back = fused(
        mid_back, "mid_back", term0, near0, far_pair, weights[0], lows[0], highs[0]
    )
    pair_back = partner(pair_back, "rep", 2)
    back1 = partner(back1, "rep", 1)
    back2, back3 = fused(far_back, "far_back", pair_back, term2, near2)
    back3 = partner(back3, "rep", 1)
    leaf_grad, mid_grad = leaf_backward(
        placed, [msg0, msg1, msg2, msg3], [back0, back1, back2, back3], leaf_w, mid_w
    )

    entries = []
    for level in range(depth):
        count = 2 << level
        inputs = [messages[level]] + [
            partner(messages[level], "sub", offset) for offset in range(1, count)
        ]
        cut = cut_grads(lows[level], highs[level], sub_index % count, count)
        grads = [cut[0]] + [partner(cut[offset], "sub", offset) for offset in range(1, count)]
        entries.append((bits[level], inputs, grads))
    entries.append((0, [root, root], [grad_value, grad_gate]))

    def rep_sum(entries):
        keep, give = upper_grads(entries, core)
        got = partner(give, "rep", 1)
        quarter = width // 4

        def part(index):
            return lax.dynamic_slice_in_dim(keep, index * quarter, quarter, 1) + f32(
                lax.dynamic_slice_in_dim(got, index * quarter, quarter, 1)
            )

        return bf16(part(far) + f32(partner(bf16(part(1 - far)), "rep", 2)))

    upper = rep_sum(entries[1:])
    upper = jnp.concatenate([rep_sum(entries[:1]), upper], axis=2)
    upper = jnp.transpose(upper, (1, 0, 2))
    return leaf_grad[None], mid_grad[None, None], upper[None]


def solution(mesh):
    placed = (
        P("rep", "sub", None),
        P("sub"),
        P(("sub", "rep"), None, None, None),
        P("sub", "rep", None, None),
        P("sub", None, None, None),
        P("rep", "sub"),
    )
    return jax.shard_map(
        on_device,
        mesh=mesh,
        in_specs=placed,
        out_specs=(
            P(("sub", "rep"), None, None, None),
            P("sub", "rep", None, None),
            P("sub", "rep", None, None),
        ),
        check_vma=False,
    )
```

time: 282 us -> 261 us (0.926)
  other arithmetic: 51.6 us -> 9.47 us
  starting transfers between devices: 48.9 us -> 81.1 us
  Pallas kernels: 17.6 us -> 45.8 us
  matrix products: 24.5 us -> 0 us
  local copies, waits for them, and re-layouts: 79.6 us -> 65.1 us
    ppermute x38 -> x77, starting transfers between devices: 48.9 us -> 81.1 us  [partner(): lax.ppermute(value, axis, [(i, i ^ offset) for i in range(lax.axis_size(a...]
    pallas_call x3 -> x20, Pallas kernels: 2.56 us -> 29.2 us  [the longest x11 12.1 us: fused(): pl.pallas_call(kernel, out_shape=shapes, in_specs=[whole_block()] * len(a...]
    dot_general x26 -> x0, matrix products: 24.5 us -> none  [the longest x5 11.4 us: matmul_t(): lax.dot_general(left_arr, right_arr, (((1,), (1,)), ((), ())), preferred_...]
    unnamed x203 -> x223, local copies, waits for them, and re-layouts: 40 us -> 63.1 us
    select_n x22 -> x3, other arithmetic: 16.4 us -> 1.71 us  [on_device(): cotangent = jnp.where(bits[level] == 1, swapped, cotangent)]
    concatenate x18 -> x0, other arithmetic: 14.5 us -> none  [the longest x10 5.7 us: join_rows(): return jnp.concatenate([first, second], axis=axis)]
    reshape x15 -> x0, local copies, waits for them, and re-layouts: 14.1 us -> none  [the longest x5 5.22 us: exchange(): part.reshape(-1, 128)]
    slice x17 -> x0, local copies, waits for them, and re-layouts: 11 us -> none  [the longest x5 5.67 us: rep_sum(): low, high = (x_side[:, :, 0], x_side[:, :, 1])]
  transfers between devices with their start and end apart: 38 -> 77, of which waited for: 15 -> 23; matrix products, arithmetic and copies ran while one was open for 49% -> 6% of each run, Pallas kernels for 5% -> 17%
where the time goes in v2:
time: 261 us; the launch traced here: 259 us
  starting transfers between devices  81.1 us (31%)
  local copies, waits for them, and re-layouts  65.1 us (25%)
  waiting for transfers between devices  56.6 us (22%)
  Pallas kernels  45.8 us (18%)
  other arithmetic  9.47 us (4%)
    ppermute x77, starting transfers between devices, partner(): lax.ppermute(value, axis, [(i, i ^ offset) for i in range(lax.axis_size(a...  81.1 us
    unnamed x223, local copies, waits for them, and re-layouts  63.1 us
    ppermute x77, waiting for transfers between devices, partner(): lax.ppermute(value, axis, [(i, i ^ offset) for i in range(lax.axis_size(a...  56.6 us
    pallas_call x11, Pallas kernels, fused(): pl.pallas_call(kernel, out_shape=shapes, in_specs=[whole_block()] * len(a...  12.1 us
    pallas_call x1, Pallas kernels, leaf_backward(): pl.pallas_call(leaf_backward_kernel, out_shape=[jax.ShapeDtypeStruct(leaf...  9.09 us
    convert_element_type x4, other arithmetic, bf16(): return value.astype(jnp.bfloat16)  7.11 us
    pallas_call x2, Pallas kernels, upper_grads(): pl.pallas_call(functools.partial(upper_grads_kernel, [len(entry[1]) for e...  5.43 us
  transfers between devices with their start and end apart: 77, of which 23 were waited for; matrix products, arithmetic and copies ran while one was open for 6% of the time, Pallas kernels for 17%

profile of v2, /device:TPU:0, one launch (start us, length us, event | category | flops | bytes accessed | tf_op | source)
XLA Modules:
  0.0 259.3 jit_solution(9650261855053881072)
XLA Ops:
  0.7 5.5 %copy.12 = bf16[1,1024,2,1024]{3,1,2,0:T(8,128)(2,1)} copy(bf16[1,1024,2,1024]{3,2,1,0:T(2,128)(2,1)} %param.10) | data formatting | bytes 8388608 | tf_op args[4]
  6.2 2.2 copy-done.9
  15.4 3.0 %collective-permute-start.16 = (bf16[512,128]{1,0:T(8,128)(2,1)}, bf16[512,128]{1,0:T(8,128)(2,1)}, u32[]{:S(2)}, u32[]{:S(2)}) collective-permute-start(bf16[512,128]{1,0:T(8,128)(2,1)} %get-tuple-element.98), channel_id=1, source_target_pairs={{0,4},{4,0},{8,12},{12,8},{16,20},{20,16},{24,28},{28,24},{1,5},{5... | collective-permute-start | bytes 393224 | tf_op jit(solution)/shard_map/ppermute | solution.py:16
  21.3 2.8 %place.1 = (bf16[4,128,256]{2,1,0:T(8,128)(2,1)S(1)}, bf16[4,128,256]{2,1,0:T(8,128)(2,1)S(1)}, bf16[4,128,256]{2,1,0:T(8,128)(2,1)}, bf16[4,128,256]{2,1,0:T(8,128)(2,1)}) custom-call(s32[2]{0:T(128)S(1)} %pad_add_fusion.ids_ref, s32[16]{0:T(128)S(1)} %copy-done.95, bf16[2048,256]{1,0:T(8,128)(2,1)S(1)} %bitcast.30), custom_call_target="tpu_custom_call" | custom-call | tf_op jit(solution)/shard_map/place/pallas_call | solution.py:79
  29.5 4.8 %collective-permute-done.1.refs_0_.refs_2_ = bf16[4,128,256]{2,1,0:T(8,128)(2,1)} collective-permute-done((bf16[4,128,256]{2,1,0:T(8,128)(2,1)}, bf16[4,128,256]{2,1,0:T(8,128)(2,1)}, u32[]{:S(2)}, u32[]{:S(2)}) %collective-permute-start.1) | collective-permute-done | bytes 262176 | tf_op jit(solution)/shard_map/ppermute | solution.py:16
  37.3 2.6 collective-permute-start.19
  41.5 2.6 %leaf_forward.3 = (bf16[128,1024]{1,0:T(8,128)(2,1)S(1)}, bf16[128,1024]{1,0:T(8,128)(2,1)S(1)}, bf16[128,1024]{1,0:T(8,128)(2,1)S(1)}, bf16[128,1024]{1,0:T(8,128)(2,1)S(1)}) custom-call(bf16[4,128,256]{2,1,0:T(8,128)(2,1)} %collective-permute-done.1.refs_0_.refs_2_, bf16[4,128,256]{2,1,0:T(8,128)(2,1)} %collective-permute-done.2.refs_1_.refs_3_, ...), custom_call_target="tpu_custom_call" | custom-call | tf_op jit(solution)/shard_map/leaf_forward/pallas_call | solution.py:110
  48.0 3.6 %collective-permute-start.21 = (bf16[512,128]{1,0:T(8,128)(2,1)S(1)}, bf16[512,128]{1,0:T(8,128)(2,1)S(1)}, u32[]{:S(2)}, u32[]{:S(2)}) collective-permute-start(bf16[512,128]{1,0:T(8,128)(2,1)S(1)} %get-tuple-element.99), channel_id=1, source_target_pairs={{0,24},{4,28},{8,16},{12,20},{16,8},{20,12},{24,0},{28,4},{1,25},{... | collective-permute-start | bytes 393224 | tf_op jit(solution)/shard_map/ppermute | solution.py:16
  51.6 7.7 %collective-permute-done.20.refs_4_ = bf16[512,128]{1,0:T(8,128)(2,1)S(1)} collective-permute-done((bf16[512,128]{1,0:T(8,128)(2,1)S(1)}, bf16[512,128]{1,0:T(8,128)(2,1)S(1)}, u32[]{:S(2)}, u32[]{:S(2)}) %collective-permute-start.20) | collective-permute-done | bytes 131104 | tf_op jit(solution)/shard_map/ppermute | solution.py:16
  62.7 2.6 %collective-permute-start.11 = (bf16[512,256]{1,0:T(8,128)(2,1)S(1)}, bf16[512,256]{1,0:T(8,128)(2,1)}, u32[]{:S(2)}, u32[]{:S(2)}) collective-permute-start(bf16[512,256]{1,0:T(8,128)(2,1)S(1)} %copy-done.98), channel_id=1, source_target_pairs={{0,12},{4,8},{8,4},{12,0},{16,28},{20,24},{24,20},{28,16},{1,13},{... | collective-permute-start | bytes 786440 | tf_op jit(solution)/shard_map/ppermute | solution.py:16
  66.0 2.1 leaf_forward.2
  73.6 5.9 %collective-permute-done.11.refs_2_ = bf16[512,256]{1,0:T(8,128)(2,1)} collective-permute-done((bf16[512,256]{1,0:T(8,128)(2,1)S(1)}, bf16[512,256]{1,0:T(8,128)(2,1)}, u32[]{:S(2)}, u32[]{:S(2)}) %collective-permute-start.11) | collective-permute-done | bytes 262176 | tf_op jit(solution)/shard_map/ppermute | solution.py:16
  82.6 2.4 mid_forward.1
  88.9 3.6 %collective-permute-done.8.refs_1_ = bf16[64,1024]{1,0:T(8,128)(2,1)S(1)} collective-permute-done((bf16[64,1024]{1,0:T(8,128)(2,1)}, bf16[64,1024]{1,0:T(8,128)(2,1)S(1)}, u32[]{:S(2)}, u32[]{:S(2)}) %collective-permute-start.8) | collective-permute-done | bytes 131104 | tf_op jit(solution)/shard_map/ppermute | solution.py:16
  104.0 3.2 %collective-permute-done.30.refs_1_ = bf16[16,1024]{1,0:T(8,128)(2,1)S(1)} collective-permute-done((bf16[16,1024]{1,0:T(8,128)(2,1)S(1)}, bf16[16,1024]{1,0:T(8,128)(2,1)S(1)}, u32[]{:S(2)}, u32[]{:S(2)}) %collective-permute-start.30) | collective-permute-done | bytes 32800 | tf_op jit(solution)/shard_map/ppermute | solution.py:16
  114.5 3.7 %collective-permute-start.36 = (bf16[16,1024]{1,0:T(8,128)(2,1)S(1)}, bf16[16,1024]{1,0:T(8,128)(2,1)S(1)}, u32[]{:S(2)}, u32[]{:S(2)}) collective-permute-start(bf16[16,1024]{1,0:T(8,128)(2,1)S(1)} %top_forward.1.refs_3_), channel_id=1, source_target_pairs={{0,12},{4,8},{8,4},{12,0},{16,28},{20,24},{24,20},{28,16},{1,13},{... | collective-permute-start | bytes 98312 | tf_op jit(solution)/shard_map/ppermute | solution.py:16
  120.9 3.9 %collective-permute-done.37.refs_10_ = bf16[16,1024]{1,0:T(8,128)(2,1)S(1)} collective-permute-done((bf16[16,1024]{1,0:T(8,128)(2,1)S(1)}, bf16[16,1024]{1,0:T(8,128)(2,1)S(1)}, u32[]{:S(2)}, u32[]{:S(2)}) %collective-permute-start.37) | collective-permute-done | bytes 32800 | tf_op jit(solution)/shard_map/ppermute | solution.py:16
  132.7 2.3 collective-permute-start.40
  140.0 2.5 collective-permute-start.44
  144.4 2.4 collective-permute-done.44.refs_9_
  148.7 3.0 %collective-permute-start.45 = (bf16[16,1024]{1,0:T(8,128)(2,1)S(1)}, bf16[16,1024]{1,0:T(8,128)(2,1)S(1)}, u32[]{:S(2)}, u32[]{:S(2)}) collective-permute-start(bf16[16,1024]{1,0:T(8,128)(2,1)S(1)} %get-tuple-element.113), channel_id=1, source_target_pairs={{0,16},{4,20},{8,24},{12,28},{16,0},{20,4},{24,8},{28,12},{1,17},{... | collective-permute-start | bytes 98312 | tf_op jit(solution)/shard_map/ppermute | solution.py:16
  153.0 3.6 %collective-permute-start.65 = (bf16[32,1024]{1,0:T(8,128)(2,1)}, bf16[32,1024]{1,0:T(8,128)(2,1)}, u32[]{:S(2)}, u32[]{:S(2)}) collective-permute-start(bf16[32,1024]{1,0:T(8,128)(2,1)} %copy-done.73), channel_id=1, source_target_pairs={{0,20},{4,16},{8,28},{12,24},{16,4},{20,0},{24,12},{28,8},{1,21},{... | collective-permute-start | bytes 196616 | tf_op jit(solution)/shard_map/ppermute | solution.py:16
  158.5 2.7 %collective-permute-start.67 = (bf16[32,1024]{1,0:T(8,128)(2,1)}, bf16[32,1024]{1,0:T(8,128)(2,1)}, u32[]{:S(2)}, u32[]{:S(2)}) collective-permute-start(bf16[32,1024]{1,0:T(8,128)(2,1)} %copy-done.73), channel_id=1, source_target_pairs={{0,28},{4,24},{8,20},{12,16},{16,12},{20,8},{24,4},{28,0},{1,29},{... | collective-permute-start | bytes 196616 | tf_op jit(solution)/shard_map/ppermute | solution.py:16
  170.1 2.1 collective-permute-start.71
  176.0 2.3 collective-permute-start.74
  188.8 2.5 collective-permute-done.58.refs_5_
  200.7 2.8 %upper_grads.3 = (f32[2,512,512]{2,1,0:T(8,128)S(1)}, bf16[2,512,512]{2,1,0:T(8,128)(2,1)}) custom-call(s32[4]{0:T(128)S(1)} %pad_add_fusion.6.ids_ref, bf16[64,1024]{1,0:T(8,128)(2,1)} %get-tuple-element.130.refs_0_, bf16[64,1024]{1,0:T(8,128)(2,1)S(1)} %copy-done.66, bf16[64,1024]{1,0:T(8,128)(2,1)S(1)} %copy-done.68, bf16[64,1024]{1,0:T(8,128)(2,1)S(1)} %copy-done.70, ...), custom_call_target="tpu_custom_call" | custom-call | tf_op jit(solution)/shard_map/upper_grads/pallas_call | solution.py:346
  208.5 4.8 %collective-permute-done.52.refs_3_ = bf16[128,512]{1,0:T(8,128)(2,1)S(1)} collective-permute-done((bf16[128,512]{1,0:T(8,128)(2,1)}, bf16[128,512]{1,0:T(8,128)(2,1)S(1)}, u32[]{:S(2)}, u32[]{:S(2)}) %collective-permute-start.52) | collective-permute-done | bytes 131104 | tf_op jit(solution)/shard_map/ppermute | solution.py:16
  214.2 2.7 %upper_grads.2 = (f32[2,512,512]{2,1,0:T(8,128)S(1)}, bf16[2,512,512]{2,1,0:T(8,128)(2,1)}) custom-call(s32[2]{0:T(128)S(1)} %pad_add_fusion.5.ids_ref, bf16[128,1024]{1,0:T(8,128)(2,1)S(1)} %get-tuple-element.125.refs_0_, bf16[128,1024]{1,0:T(8,128)(2,1)} %collective-permute-done.51.refs_1_, bf16[128,512]{1,0:T(8,128)(2,1)S(1)} %copy-done.64, ...), custom_call_target="tpu_custom_call" | custom-call | tf_op jit(solution)/shard_map/upper_grads/pallas_call | solution.py:346
  220.7 3.0 %mid_back.1 = (bf16[128,1024]{1,0:T(8,128)(2,1)S(1)}, bf16[128,1024]{1,0:T(8,128)(2,1)}, bf16[128,1024]{1,0:T(8,128)(2,1)S(1)}) custom-call(bf16[128,1024]{1,0:T(8,128)(2,1)S(1)} %copy-done.25, bf16[128,1024]{1,0:T(8,128)(2,1)} %collective-permute-done.3.refs_1_, bf16[128,1024]{1,0:T(8,128)(2,1)} %collective-permute-done.5.refs_2_, ...), custom_call_target="tpu_custom_call" | custom-call | tf_op jit(solution)/shard_map/mid_back/pallas_call | solution.py:177
  239.8 9.1 %leaf_backward.1 = (bf16[4,256,1024]{2,1,0:T(8,128)(2,1)}, bf16[1024,1024]{1,0:T(8,128)(2,1)}) custom-call(bf16[4,128,256]{2,1,0:T(8,128)(2,1)S(1)} %get-tuple-element.76.refs_0_, bf16[4,128,256]{2,1,0:T(8,128)(2,1)S(1)} %copy-done.17, bf16[4,128,256]{2,1,0:T(8,128)(2,1)} %collective-permute-done.1.refs_0_.refs_2_, ...), custom_call_target="tpu_custom_call" | custom-call | tf_op jit(solution)/shard_map/leaf_backward/pallas_call | solution.py:153
  250.4 5.2 %collective-permute-done.54 = bf16[2,256,512]{2,1,0:T(8,128)(2,1)} collective-permute-done((bf16[2,256,512]{2,1,0:T(8,128)(2,1)}, bf16[2,256,512]{2,1,0:T(8,128)(2,1)}, u32[]{:S(2)}, u32[]{:S(2)}) %collective-permute-start.54) | collective-permute-done | bytes 524320 | tf_op jit(solution)/shard_map/ppermute | solution.py:16
  (387 shorter events, 144.9 us)
Async XLA Ops:
  15.4 30.1 %collective-permute-start.16 = (bf16[512,128]{1,0:T(8,128)(2,1)}, bf16[512,128]{1,0:T(8,128)(2,1)}, u32[]{:S(2)}, u32[]{:S(2)}) collective-permute-start(bf16[512,128]{1,0:T(8,128)(2,1)} %get-tuple-element.98), channel_id=1, source_target_pairs={{0,4},{4,0},{8,12},{12,8},{16,20},{20,16},{24,28},{28,24},{1,5},{5... | collective-permute-start | bytes 393224 | tf_op jit(solution)/shard_map/ppermute | solution.py:16
  18.4 28.4 %collective-permute-start.17 = (bf16[512,128]{1,0:T(8,128)(2,1)}, bf16[512,128]{1,0:T(8,128)(2,1)}, u32[]{:S(2)}, u32[]{:S(2)}) collective-permute-start(bf16[512,128]{1,0:T(8,128)(2,1)} %get-tuple-element.98), channel_id=1, source_target_pairs={{0,8},{4,12},{8,0},{12,4},{16,24},{20,28},{24,16},{28,20},{1,9},{5... | collective-permute-start | bytes 393224 | tf_op jit(solution)/shard_map/ppermute | solution.py:16
  20.0 27.1 %collective-permute-start.18 = (bf16[512,128]{1,0:T(8,128)(2,1)}, bf16[512,128]{1,0:T(8,128)(2,1)}, u32[]{:S(2)}, u32[]{:S(2)}) collective-permute-start(bf16[512,128]{1,0:T(8,128)(2,1)} %get-tuple-element.98), channel_id=1, source_target_pairs={{0,12},{4,8},{8,4},{12,0},{16,28},{20,24},{24,20},{28,16},{1,13},{... | collective-permute-start | bytes 393224 | tf_op jit(solution)/shard_map/ppermute | solution.py:16
  34.3 28.3 %collective-permute-start.6 = (bf16[512,512]{1,0:T(8,128)(2,1)}, bf16[512,512]{1,0:T(8,128)(2,1)}, u32[]{:S(2)}, u32[]{:S(2)}) collective-permute-start(bf16[512,512]{1,0:T(8,128)(2,1)} %copy-done.96), channel_id=1, source_target_pairs={{0,4},{4,0},{8,12},{12,8},{16,20},{20,16},{24,28},{28,24},{1,5},{5... | collective-permute-start | bytes 1572872 | tf_op jit(solution)/shard_map/ppermute | solution.py:16
  45.5 13.7 %collective-permute-start.20 = (bf16[512,128]{1,0:T(8,128)(2,1)S(1)}, bf16[512,128]{1,0:T(8,128)(2,1)S(1)}, u32[]{:S(2)}, u32[]{:S(2)}) collective-permute-start(bf16[512,128]{1,0:T(8,128)(2,1)S(1)} %get-tuple-element.99), channel_id=1, source_target_pairs={{0,20},{4,16},{8,28},{12,24},{16,4},{20,0},{24,12},{28,8},{1,21},{... | collective-permute-start | bytes 393224 | tf_op jit(solution)/shard_map/ppermute | solution.py:16
  46.8 15.4 %collective-permute-start = (bf16[4,128,256]{2,1,0:T(8,128)(2,1)S(1)}, bf16[4,128,256]{2,1,0:T(8,128)(2,1)S(1)}, u32[]{:S(2)}, u32[]{:S(2)}) collective-permute-start(bf16[4,128,256]{2,1,0:T(8,128)(2,1)S(1)} %copy-done.102), channel_id=1, source_target_pairs={{0,1},{1,0},{2,3},{3,2},{4,5},{5,4},{6,7},{7,6},{8,9},{9,8},{10,11... | collective-permute-start | bytes 786440 | tf_op jit(solution)/shard_map/ppermute | solution.py:16
  47.1 18.2 %collective-permute-start.4 = (bf16[128,1024]{1,0:T(8,128)(2,1)S(1)}, bf16[128,1024]{1,0:T(8,128)(2,1)S(1)}, u32[]{:S(2)}, u32[]{:S(2)}) collective-permute-start(bf16[128,1024]{1,0:T(8,128)(2,1)S(1)} %get-tuple-element.87), channel_id=1, source_target_pairs={{0,1},{1,0},{2,3},{3,2},{4,5},{5,4},{6,7},{7,6},{8,9},{9,8},{10,11... | collective-permute-start | bytes 786440 | tf_op jit(solution)/shard_map/ppermute | solution.py:16
  48.0 13.4 %collective-permute-start.21 = (bf16[512,128]{1,0:T(8,128)(2,1)S(1)}, bf16[512,128]{1,0:T(8,128)(2,1)S(1)}, u32[]{:S(2)}, u32[]{:S(2)}) collective-permute-start(bf16[512,128]{1,0:T(8,128)(2,1)S(1)} %get-tuple-element.99), channel_id=1, source_target_pairs={{0,24},{4,28},{8,16},{12,20},{16,8},{20,12},{24,0},{28,4},{1,25},{... | collective-permute-start | bytes 393224 | tf_op jit(solution)/shard_map/ppermute | solution.py:16
  59.3 11.9 %collective-permute-start.9 = (bf16[512,256]{1,0:T(8,128)(2,1)S(1)}, bf16[512,256]{1,0:T(8,128)(2,1)}, u32[]{:S(2)}, u32[]{:S(2)}) collective-permute-start(bf16[512,256]{1,0:T(8,128)(2,1)S(1)} %copy-done.100), channel_id=1, source_target_pairs={{0,4},{4,0},{8,12},{12,8},{16,20},{20,16},{24,28},{28,24},{1,5},{5... | collective-permute-start | bytes 786440 | tf_op jit(solution)/shard_map/ppermute | solution.py:16
  62.2 11.3 %collective-permute-start.10 = (bf16[512,256]{1,0:T(8,128)(2,1)S(1)}, bf16[512,256]{1,0:T(8,128)(2,1)}, u32[]{:S(2)}, u32[]{:S(2)}) collective-permute-start(bf16[512,256]{1,0:T(8,128)(2,1)S(1)} %copy-done.98), channel_id=1, source_target_pairs={{0,8},{4,12},{8,0},{12,4},{16,24},{20,28},{24,16},{28,20},{1,9},{5... | collective-permute-start | bytes 786440 | tf_op jit(solution)/shard_map/ppermute | solution.py:16
  62.7 16.8 %collective-permute-start.11 = (bf16[512,256]{1,0:T(8,128)(2,1)S(1)}, bf16[512,256]{1,0:T(8,128)(2,1)}, u32[]{:S(2)}, u32[]{:S(2)}) collective-permute-start(bf16[512,256]{1,0:T(8,128)(2,1)S(1)} %copy-done.98), channel_id=1, source_target_pairs={{0,12},{4,8},{8,4},{12,0},{16,28},{20,24},{24,20},{28,16},{1,13},{... | collective-permute-start | bytes 786440 | tf_op jit(solution)/shard_map/ppermute | solution.py:16
  65.3 15.4 %collective-permute-start.7 = (bf16[512,512]{1,0:T(8,128)(2,1)}, bf16[512,512]{1,0:T(8,128)(2,1)}, u32[]{:S(2)}, u32[]{:S(2)}) collective-permute-start(bf16[512,512]{1,0:T(8,128)(2,1)} %collective-permute-done.6.refs_0_), channel_id=1, source_target_pairs={{0,1},{1,0},{2,3},{3,2},{4,5},{5,4},{6,7},{7,6},{8,9},{9,8},{10,11... | collective-permute-start | bytes 1572872 | tf_op jit(solution)/shard_map/ppermute | solution.py:16
  73.6 12.8 %collective-permute-start.23 = (bf16[512,128]{1,0:T(8,128)(2,1)}, bf16[512,128]{1,0:T(8,128)(2,1)}, u32[]{:S(2)}, u32[]{:S(2)}) collective-permute-start(bf16[512,128]{1,0:T(8,128)(2,1)} %collective-permute-done.16.refs_0_), channel_id=1, source_target_pairs={{0,1},{1,0},{2,3},{3,2},{4,5},{5,4},{6,7},{7,6},{8,9},{9,8},{10,11... | collective-permute-start | bytes 393224 | tf_op jit(solution)/shard_map/ppermute | solution.py:16
  112.4 20.3 %collective-permute-start.55 = (bf16[64,1024]{1,0:T(8,128)(2,1)}, bf16[64,1024]{1,0:T(8,128)(2,1)S(1)}, u32[]{:S(2)}, u32[]{:S(2)}) collective-permute-start(bf16[64,1024]{1,0:T(8,128)(2,1)} %get-tuple-element.130.refs_0_), channel_id=1, source_target_pairs={{0,4},{4,0},{8,12},{12,8},{16,20},{20,16},{24,28},{28,24},{1,5},{5... | collective-permute-start | bytes 393224 | tf_op jit(solution)/shard_map/ppermute | solution.py:16
  119.7 28.3 %collective-permute-start.56 = (bf16[64,1024]{1,0:T(8,128)(2,1)}, bf16[64,1024]{1,0:T(8,128)(2,1)S(1)}, u32[]{:S(2)}, u32[]{:S(2)}) collective-permute-start(bf16[64,1024]{1,0:T(8,128)(2,1)} %get-tuple-element.130.refs_0_), channel_id=1, source_target_pairs={{0,8},{4,12},{8,0},{12,4},{16,24},{20,28},{24,16},{28,20},{1,9},{5... | collective-permute-start | bytes 393224 | tf_op jit(solution)/shard_map/ppermute | solution.py:16
  132.7 19.0 %collective-permute-start.57 = (bf16[64,1024]{1,0:T(8,128)(2,1)}, bf16[64,1024]{1,0:T(8,128)(2,1)S(1)}, u32[]{:S(2)}, u32[]{:S(2)}) collective-permute-start(bf16[64,1024]{1,0:T(8,128)(2,1)} %get-tuple-element.130.refs_0_), channel_id=1, source_target_pairs={{0,12},{4,8},{8,4},{12,0},{16,28},{20,24},{24,20},{28,16},{1,13},{... | collective-permute-start | bytes 393224 | tf_op jit(solution)/shard_map/ppermute | solution.py:16
  144.1 12.5 %collective-permute-start.62 = (bf16[32,1024]{1,0:T(8,128)(2,1)}, bf16[32,1024]{1,0:T(8,128)(2,1)S(1)}, u32[]{:S(2)}, u32[]{:S(2)}) collective-permute-start(bf16[32,1024]{1,0:T(8,128)(2,1)} %copy-done.73), channel_id=1, source_target_pairs={{0,8},{4,12},{8,0},{12,4},{16,24},{20,28},{24,16},{28,20},{1,9},{5... | collective-permute-start | bytes 196616 | tf_op jit(solution)/shard_map/ppermute | solution.py:16
  146.7 17.6 %collective-permute-start.63 = (bf16[32,1024]{1,0:T(8,128)(2,1)}, bf16[32,1024]{1,0:T(8,128)(2,1)S(1)}, u32[]{:S(2)}, u32[]{:S(2)}) collective-permute-start(bf16[32,1024]{1,0:T(8,128)(2,1)} %copy-done.73), channel_id=1, source_target_pairs={{0,12},{4,8},{8,4},{12,0},{16,28},{20,24},{24,20},{28,16},{1,13},{... | collective-permute-start | bytes 196616 | tf_op jit(solution)/shard_map/ppermute | solution.py:16
  152.3 14.1 %collective-permute-start.64 = (bf16[32,1024]{1,0:T(8,128)(2,1)}, bf16[32,1024]{1,0:T(8,128)(2,1)}, u32[]{:S(2)}, u32[]{:S(2)}) collective-permute-start(bf16[32,1024]{1,0:T(8,128)(2,1)} %copy-done.73), channel_id=1, source_target_pairs={{0,16},{4,20},{8,24},{12,28},{16,0},{20,4},{24,8},{28,12},{1,17},{... | collective-permute-start | bytes 196616 | tf_op jit(solution)/shard_map/ppermute | solution.py:16
  153.0 14.7 %collective-permute-start.65 = (bf16[32,1024]{1,0:T(8,128)(2,1)}, bf16[32,1024]{1,0:T(8,128)(2,1)}, u32[]{:S(2)}, u32[]{:S(2)}) collective-permute-start(bf16[32,1024]{1,0:T(8,128)(2,1)} %copy-done.73), channel_id=1, source_target_pairs={{0,20},{4,16},{8,28},{12,24},{16,4},{20,0},{24,12},{28,8},{1,21},{... | collective-permute-start | bytes 196616 | tf_op jit(solution)/shard_map/ppermute | solution.py:16
  157.2 12.5 %collective-permute-start.66 = (bf16[32,1024]{1,0:T(8,128)(2,1)}, bf16[32,1024]{1,0:T(8,128)(2,1)}, u32[]{:S(2)}, u32[]{:S(2)}) collective-permute-start(bf16[32,1024]{1,0:T(8,128)(2,1)} %copy-done.73), channel_id=1, source_target_pairs={{0,24},{4,28},{8,16},{12,20},{16,8},{20,12},{24,0},{28,4},{1,25},{... | collective-permute-start | bytes 196616 | tf_op jit(solution)/shard_map/ppermute | solution.py:16
  158.5 11.5 %collective-permute-start.67 = (bf16[32,1024]{1,0:T(8,128)(2,1)}, bf16[32,1024]{1,0:T(8,128)(2,1)}, u32[]{:S(2)}, u32[]{:S(2)}) collective-permute-start(bf16[32,1024]{1,0:T(8,128)(2,1)} %copy-done.73), channel_id=1, source_target_pairs={{0,28},{4,24},{8,20},{12,16},{16,12},{20,8},{24,4},{28,0},{1,29},{... | collective-permute-start | bytes 196616 | tf_op jit(solution)/shard_map/ppermute | solution.py:16
  165.0 11.0 %collective-permute-start.46 = (bf16[32,1024]{1,0:T(8,128)(2,1)}, bf16[32,1024]{1,0:T(8,128)(2,1)S(1)}, u32[]{:S(2)}, u32[]{:S(2)}) collective-permute-start(bf16[32,1024]{1,0:T(8,128)(2,1)} %get-tuple-element.115), channel_id=1, source_target_pairs={{0,8},{4,12},{8,0},{12,4},{16,24},{20,28},{24,16},{28,20},{1,9},{5... | collective-permute-start | bytes 196616 | tf_op jit(solution)/shard_map/ppermute | solution.py:16
  169.8 13.3 %collective-permute-start.70 = (bf16[32,128]{1,0:T(8,128)(2,1)}, bf16[32,128]{1,0:T(8,128)(2,1)}, u32[]{:S(2)}, u32[]{:S(2)}) collective-permute-start(bf16[32,128]{1,0:T(8,128)(2,1)} %get-tuple-element.139), channel_id=1, source_target_pairs={{0,12},{4,8},{8,4},{12,0},{16,28},{20,24},{24,20},{28,16},{1,13},{... | collective-permute-start | bytes 24584 | tf_op jit(solution)/shard_map/ppermute | solution.py:16
  170.1 14.3 %collective-permute-start.71 = (bf16[32,128]{1,0:T(8,128)(2,1)}, bf16[32,128]{1,0:T(8,128)(2,1)}, u32[]{:S(2)}, u32[]{:S(2)}) collective-permute-start(bf16[32,128]{1,0:T(8,128)(2,1)} %get-tuple-element.140), channel_id=1, source_target_pairs={{0,16},{4,20},{8,24},{12,28},{16,0},{20,4},{24,8},{28,12},{1,17},{... | collective-permute-start | bytes 24584 | tf_op jit(solution)/shard_map/ppermute | solution.py:16
  172.2 13.0 %collective-permute-start.72 = (bf16[32,128]{1,0:T(8,128)(2,1)}, bf16[32,128]{1,0:T(8,128)(2,1)}, u32[]{:S(2)}, u32[]{:S(2)}) collective-permute-start(bf16[32,128]{1,0:T(8,128)(2,1)} %get-tuple-element.141), channel_id=1, source_target_pairs={{0,20},{4,16},{8,28},{12,24},{16,4},{20,0},{24,12},{28,8},{1,21},{... | collective-permute-start | bytes 24584 | tf_op jit(solution)/shard_map/ppermute | solution.py:16
  174.3 12.2 %collective-permute-start.73 = (bf16[32,128]{1,0:T(8,128)(2,1)}, bf16[32,128]{1,0:T(8,128)(2,1)}, u32[]{:S(2)}, u32[]{:S(2)}) collective-permute-start(bf16[32,128]{1,0:T(8,128)(2,1)} %get-tuple-element.142), channel_id=1, source_target_pairs={{0,24},{4,28},{8,16},{12,20},{16,8},{20,12},{24,0},{28,4},{1,25},{... | collective-permute-start | bytes 24584 | tf_op jit(solution)/shard_map/ppermute | solution.py:16
  183.1 25.4 %collective-permute-start.51 = (bf16[128,1024]{1,0:T(8,128)(2,1)S(1)}, bf16[128,1024]{1,0:T(8,128)(2,1)}, u32[]{:S(2)}, u32[]{:S(2)}) collective-permute-start(bf16[128,1024]{1,0:T(8,128)(2,1)S(1)} %get-tuple-element.125.refs_0_), channel_id=1, source_target_pairs={{0,4},{4,0},{8,12},{12,8},{16,20},{20,16},{24,28},{28,24},{1,5},{5... | collective-permute-start | bytes 786440 | tf_op jit(solution)/shard_map/ppermute | solution.py:16
  184.4 20.4 %collective-permute-start.47 = (bf16[64,1024]{1,0:T(8,128)(2,1)}, bf16[64,1024]{1,0:T(8,128)(2,1)S(1)}, u32[]{:S(2)}, u32[]{:S(2)}) collective-permute-start(bf16[64,1024]{1,0:T(8,128)(2,1)} %copy-done.103), channel_id=1, source_target_pairs={{0,4},{4,0},{8,12},{12,8},{16,20},{20,16},{24,28},{28,24},{1,5},{5... | collective-permute-start | bytes 393224 | tf_op jit(solution)/shard_map/ppermute | solution.py:16
  204.8 20.9 %collective-permute-start.75 = (bf16[2,512,512]{2,1,0:T(8,128)(2,1)}, bf16[2,512,512]{2,1,0:T(8,128)(2,1)}, u32[]{:S(2)}, u32[]{:S(2)}) collective-permute-start(bf16[2,512,512]{2,1,0:T(8,128)(2,1)} %get-tuple-element.148), channel_id=1, source_target_pairs={{0,1},{1,0},{2,3},{3,2},{4,5},{5,4},{6,7},{7,6},{8,9},{9,8},{10,11... | collective-permute-start | bytes 3145736 | tf_op jit(solution)/shard_map/ppermute | solution.py:16
  227.9 21.0 %collective-permute-start.76 = (bf16[2,256,512]{2,1,0:T(8,128)(2,1)}, bf16[2,256,512]{2,1,0:T(8,128)(2,1)}, u32[]{:S(2)}, u32[]{:S(2)}) collective-permute-start(bf16[2,256,512]{2,1,0:T(8,128)(2,1)} %add_convert_fusion.1), channel_id=1, source_target_pairs={{0,2},{1,3},{2,0},{3,1},{4,6},{5,7},{6,4},{7,5},{8,10},{9,11},{10,... | collective-permute-start | bytes 1572872 | tf_op jit(solution)/shard_map/ppermute | solution.py:16
  230.6 25.1 %collective-permute-start.54 = (bf16[2,256,512]{2,1,0:T(8,128)(2,1)}, bf16[2,256,512]{2,1,0:T(8,128)(2,1)}, u32[]{:S(2)}, u32[]{:S(2)}) collective-permute-start(bf16[2,256,512]{2,1,0:T(8,128)(2,1)} %add_convert_fusion.3), channel_id=1, source_target_pairs={{0,2},{1,3},{2,0},{3,1},{4,6},{5,7},{6,4},{7,5},{8,10},{9,11},{10,... | collective-permute-start | bytes 1572872 | tf_op jit(solution)/shard_map/ppermute | solution.py:16
  (152 other events, 1000.8 us)

commit v3 on v2

v3 whole, which is shorter than its diff:
```python
import functools

import jax
import jax.numpy as jnp
from jax import lax
from jax.experimental import pallas as pl
from jax.experimental.pallas import tpu as pltpu
from jax.sharding import PartitionSpec as P

EPSILON = 1e-06
CHILDREN = 4
MIB = 1024 * 1024


def partner(value, axis, offset):
    return lax.ppermute(value, axis, [(i, i ^ offset) for i in range(lax.axis_size(axis))])


def rms_factor(values):
    return lax.rsqrt(jnp.mean(values * values, axis=-1, keepdims=True) + EPSILON)


def norm_back(gradient, normed, factor):
    return factor * (gradient - normed * jnp.mean(gradient * normed, axis=-1, keepdims=True))


def matmul(left_arr, right_arr):
    return jnp.dot(left_arr, right_arr, preferred_element_type=jnp.float32)


def matmul_t(left_arr, right_arr):
    return lax.dot_general(
        left_arr, right_arr, (((1,), (1,)), ((), ())), preferred_element_type=jnp.float32
    )


def inner_t(left_arr, right_arr):
    return lax.dot_general(
        left_arr, right_arr, (((0,), (0,)), ((), ())), preferred_element_type=jnp.float32
    )


def bf16(value):
    return value.astype(jnp.bfloat16)


def f32(value):
    return value.astype(jnp.float32)


def whole_block():
    return pl.BlockSpec(memory_space=pltpu.VMEM)


def place_kernel(slots, ids_ref, map_ref, regions_ref, *rest):
    outs, wide = rest[:CHILDREN], rest[CHILDREN]
    rows = regions_ref.shape[0] // slots
    parts = wide.shape[0]
    for part in range(parts):
        wide[part] = regions_ref[:, part * 128 : (part + 1) * 128].astype(jnp.float32)
    row = lax.broadcasted_iota(jnp.int32, (rows, rows), 0)
    col = lax.broadcasted_iota(jnp.int32, (rows, rows), 1)
    select = (jnp.bitwise_xor(row, ids_ref[1]) == col).astype(jnp.bfloat16)
    for offset in range(CHILDREN):
        node = jnp.bitwise_xor(ids_ref[0], offset)
        for child in range(CHILDREN):
            region = map_ref[node * CHILDREN + child]
            for part in range(parts):
                values = wide[part, pl.ds(region, rows, stride=slots), :].astype(jnp.bfloat16)
                outs[offset][child, :, part * 128 : (part + 1) * 128] = matmul(
                    select, values
                ).astype(jnp.bfloat16)


def place(regions, leaf_map, ids):
    rows, slots, feats = regions.shape
    flat = regions.reshape(rows * slots, feats)
    smem = pl.BlockSpec(memory_space=pltpu.SMEM)
    return pl.pallas_call(
        functools.partial(place_kernel, slots),
        out_shape=[jax.ShapeDtypeStruct((CHILDREN, rows, feats), jnp.bfloat16)] * CHILDREN,
        in_specs=[smem, smem, whole_block()],
        out_specs=[whole_block()] * CHILDREN,
        scratch_shapes=[pltpu.VMEM((feats // 128, rows * slots, 128), jnp.float32)],
        compiler_params=pltpu.CompilerParams(vmem_limit_bytes=6 * MIB),
        name="place",
    )(ids, leaf_map, flat)


def leaf_forward_kernel(count, *refs):
    placed, leaf_w, mid_w = refs[:count], refs[count], refs[count + 1]
    msgs, terms = refs[count + 2 : 2 * count + 2], refs[2 * count + 2 :]
    rows = placed[0].shape[1]
    product = None
    for child in range(CHILDREN):
        values = jnp.concatenate([ref[child] for ref in placed], axis=0)
        factor = 1.0 + matmul(values, leaf_w[child])
        product = factor if product is None else product * factor
    message = bf16(product * rms_factor(product))
    out = bf16(matmul(message, mid_w[...]))
    for i in range(count):
        msgs[i][...] = message[i * rows : (i + 1) * rows]
        terms[i][...] = out[i * rows : (i + 1) * rows]


def leaf_forward(placed, leaf_w, mid_w):
    count = len(placed)
    rows = placed[0].shape[1]
    width = mid_w.shape[0]
    return pl.pallas_call(
        functools.partial(leaf_forward_kernel, count),
        out_shape=[jax.ShapeDtypeStruct((rows, width), jnp.bfloat16)] * (2 * count),
        in_specs=[whole_block()] * (count + 2),
        out_specs=[whole_block()] * (2 * count),
        compiler_params=pltpu.CompilerParams(vmem_limit_bytes=14 * MIB),
        name="leaf_forward",
    )(*placed, leaf_w, mid_w)


def leaf_cotangents(placed, grads, leaf_w, mid_w):
    factors = [
        1.0 + matmul(jnp.concatenate([ref[child] for ref in placed], axis=0), leaf_w[child])
        for child in range(CHILDREN)
    ]
    low = factors[0] * factors[1]
    high = factors[2] * factors[3]
    product = low * high
    scale = rms_factor(product)
    back = matmul_t(jnp.concatenate([ref[...] for ref in grads], axis=0), mid_w[...])
    node = norm_back(back, product * scale, scale)
    high, low = node * high, node * low
    return [
        bf16(high * factors[1]),
        bf16(high * factors[0]),
        bf16(low * factors[3]),
        bf16(low * factors[2]),
    ]


def leaf_first_kernel(*refs):
    placed, grads, leaf_w, mid_w, out = refs[0:2], refs[2:4], refs[4], refs[5], refs[6]
    for child, value in enumerate(leaf_cotangents(placed, grads, leaf_w, mid_w)):
        out[child] = value


def leaf_first(placed, grads, leaf_w, mid_w):
    rows = placed[0].shape[1]
    return pl.pallas_call(
        leaf_first_kernel,
        out_shape=jax.ShapeDtypeStruct((CHILDREN, 2 * rows, mid_w.shape[0]), jnp.bfloat16),
        in_specs=[whole_block()] * 6,
        out_specs=whole_block(),
        compiler_params=pltpu.CompilerParams(vmem_limit_bytes=18 * MIB),
        name="leaf_first",
    )(*placed, *grads, leaf_w, mid_w)


def leaf_backward_kernel(*refs):
    placed, msgs, grads = refs[0:4], refs[4:8], refs[8:12]
    leaf_w, mid_w, first, leaf_out, mid_out = refs[12:17]
    all_grads = jnp.concatenate([ref[...] for ref in grads], axis=0)
    all_msgs = jnp.concatenate([ref[...] for ref in msgs], axis=0)
    mid_out[...] = bf16(inner_t(all_msgs, all_grads))
    second = leaf_cotangents(placed[2:], grads[2:], leaf_w, mid_w)
    for child in range(CHILDREN):
        values = jnp.concatenate([ref[child] for ref in placed], axis=0)
        cot = jnp.concatenate([first[child], second[child]], axis=0)
        leaf_out[child] = bf16(inner_t(values, cot))


def leaf_backward(placed, msgs, grads, leaf_w, mid_w, first):
    return pl.pallas_call(
        leaf_backward_kernel,
        out_shape=[
            jax.ShapeDtypeStruct(leaf_w.shape, jnp.bfloat16),
            jax.ShapeDtypeStruct(mid_w.shape, jnp.bfloat16),
        ],
        in_specs=[whole_block()] * 15,
        out_specs=[whole_block()] * 2,
        compiler_params=pltpu.CompilerParams(vmem_limit_bytes=30 * MIB),
        name="leaf_backward",
    )(*placed, *msgs, *grads, leaf_w, mid_w, first)


def fused(body, name, *args, limit=8):
    if any(arg.shape[-2] % 16 or arg.shape[-1] % 128 for arg in args):
        return body(*args)
    shapes = jax.eval_shape(body, *args)

    def kernel(*refs):
        results = body(*[ref[...] for ref in refs[: len(args)]])
        for ref, result in zip(refs[len(args) :], results):
            ref[...] = result

    return pl.pallas_call(
        kernel,
        out_shape=shapes,
        in_specs=[whole_block()] * len(args),
        out_specs=[whole_block()] * len(shapes),
        compiler_params=pltpu.CompilerParams(vmem_limit_bytes=limit * MIB),
        name=name,
    )(*args)


def ids_of(*values):
    return jnp.stack(values).astype(jnp.int32)


def smem_block():
    return pl.BlockSpec(memory_space=pltpu.SMEM)


def reverse_bits(value, count):
    out = 0
    for i in range(count):
        out = out * 2 + (value >> i) % 2
    return out


def join(pieces):
    if pieces[0].shape[0] % 16 == 0:
        return jnp.concatenate(pieces, axis=0)
    wide = lax.optimization_barrier(tuple(f32(piece) for piece in pieces))
    return bf16(lax.optimization_barrier(jnp.concatenate(wide, axis=0)))


def pack(pieces):
    arrays = []
    for array, _, _ in pieces:
        if not any(array is known for known in arrays):
            arrays.append(array)
    spots = [next(i for i, known in enumerate(arrays) if known is piece[0]) for piece in pieces]

    def body(*values):
        parts = [values[i][:, at : at + span] for i, (_, at, span) in zip(spots, pieces)]
        return (jnp.concatenate(parts, axis=1),)

    if any(piece[2] % 128 for piece in pieces):
        return body(*arrays)[0]
    return fused(body, "pack", *arrays, limit=6)[0]


def cut_kernel(depth, ids_ref, maps_ref, *refs):
    outs, split = refs[:-1], refs[-1]
    split[...] = jnp.swapaxes(maps_ref[...], 0, 1)
    width = maps_ref.shape[0]
    half = width // 2
    rows = pl.ds(pl.multiple_of(ids_ref[0] * half, half), half)
    for level in range(depth):
        span = width >> (level + 1)
        cols = pl.ds(width - 2 * span, span)
        side = ids_ref[1 + level]
        outs[3 * level][...] = split[side, :, cols]
        outs[3 * level + 1][...] = split[side, rows, cols]
        outs[3 * level + 2][...] = split[1 - side, rows, cols]
    span = width >> depth
    for side in range(2):
        outs[3 * depth + side][...] = split[side, :, width - span :]


def cut_maps(maps, core, sides):
    depth = len(sides)
    width = maps.shape[0]
    half = width // 2
    spans = [width >> (level + 1) for level in range(depth)]
    if spans[-1] % 128 == 0:
        shapes = []
        for span in spans:
            shapes += [(width, span), (half, span), (half, span)]
        shapes += [(width, spans[-1])] * 2
        outs = pl.pallas_call(
            functools.partial(cut_kernel, depth),
            out_shape=[jax.ShapeDtypeStruct(shape, maps.dtype) for shape in shapes],
            in_specs=[smem_block(), whole_block()],
            out_specs=[whole_block()] * len(shapes),
            scratch_shapes=[pltpu.VMEM((2, width, width), maps.dtype)],
            compiler_params=pltpu.CompilerParams(vmem_limit_bytes=18 * MIB),
            name="cut_maps",
        )(ids_of(core, *sides), maps)
    else:
        maps = jnp.transpose(maps, (1, 0, 2))
        outs = []
        for span, side in zip(spans, sides):
            first = width - 2 * span
            outs.append(lax.dynamic_slice(maps, (side, 0, first), (1, width, span))[0])
            for which in (side, 1 - side):
                outs.append(lax.dynamic_slice(maps, (which, core * half, first), (1, half, span))[0])
        outs += [maps[0, :, width - spans[-1] :], maps[1, :, width - spans[-1] :]]
    return [outs[3 * i : 3 * i + 3] for i in range(depth)], outs[3 * depth :]


def assemble_kernel(spots, count, ids_ref, own_ref, *refs):
    out_ref = refs[-1]
    width, span = own_ref.shape
    half = width // 2
    block = ids_ref[1]
    out_ref[:, pl.ds(pl.multiple_of(block * span, span), span)] = own_ref[...]
    for offset, index, at in spots:
        col = jnp.bitwise_xor(block, offset) * span
        for ref, core in ((refs[index], ids_ref[0]), (refs[count + index], 1 - ids_ref[0])):
            out_ref[
                pl.ds(pl.multiple_of(core * half, half), half),
                pl.ds(pl.multiple_of(col, span), span),
            ] = ref[:, at : at + span]


def assemble(own, pieces, core, block):
    width, span = own.shape
    count = len(pieces) + 1
    if span % 128 == 0:
        mine, other, spots = [], [], []
        for offset, (near_half, far_half, at) in pieces.items():
            known = [i for i, array in enumerate(mine) if array is near_half]
            if not known:
                mine.append(near_half)
                other.append(far_half)
                known = [len(mine) - 1]
            spots.append((offset, known[0], at))
        return pl.pallas_call(
            functools.partial(assemble_kernel, spots, len(mine)),
            out_shape=jax.ShapeDtypeStruct((width, span * count), own.dtype),
            in_specs=[smem_block()] + [whole_block()] * (2 * len(mine) + 1),
            out_specs=whole_block(),
            compiler_params=pltpu.CompilerParams(vmem_limit_bytes=8 * MIB),
            name="assemble",
        )(ids_of(core, block), own, *mine, *other)
    out = jnp.zeros((width, span * count), own.dtype)
    out = lax.dynamic_update_slice(out, own, (0, block * span))
    for offset, (near_half, far_half, at) in pieces.items():
        col = (block ^ offset) * span
        for array, which in ((near_half, core), (far_half, 1 - core)):
            part = array[:, at : at + span]
            out = lax.dynamic_update_slice(out, part, (which * (width // 2), col))
    return out


def after(value, *others):
    return lax.optimization_barrier((value, *others))[0]


class MapGather:
    def __init__(self, blocks, core, sub_index):
        self.blocks, self.core, self.sub_index = blocks, core, sub_index
        self.depth = len(blocks)
        self.spans = [block[0].shape[1] for block in blocks]
        self.held = [{0: (block[1], 0)} for block in blocks]
        self.first = partner(blocks[0][2], "sub", 1)
        self.early = [self.send([(level, 0) for level in range(1, self.depth)], 0)]

    def send(self, picks, stage, extra=None, gate=None):
        pieces = [(*self.held[level][offset], self.spans[level]) for level, offset in picks]
        picks = list(picks)
        if extra is not None:
            pieces.append((self.blocks[extra][2], 0, self.spans[extra]))
            picks.append((extra, 0))
        if gate is not None:
            pieces[-1] = (after(pieces[-1][0], gate), *pieces[-1][1:])
        value = pieces[0][0] if len(pieces) == 1 else pack(pieces)
        got = partner(value, "sub", 1 << stage)
        at = 0
        for level, offset in picks:
            self.held[level][offset ^ (1 << stage)] = (got, at)
            at += self.spans[level]
        return got

    def stage(self, stage, gate=None):
        picks = [
            (level, offset)
            for level in range(stage + 1, self.depth)
            for offset in self.held[level]
            if offset % (2 << stage) == 0
        ]
        self.early.append(self.send(picks, stage, stage, gate))

    def last(self, gate):
        picks = [
            (level, offset)
            for level in range(1, self.depth)
            for offset in self.held[level]
            if offset % 2 == 0 and offset > 0
        ]
        self.late = self.send(picks, 0, None, gate)

    def weight(self, level, exchanged):
        pieces = {}
        if level == 0:
            pieces[1] = (self.first, exchanged[0], 0)
        else:
            for offset, (array, at) in self.held[level].items():
                if offset == 0:
                    continue
                if array is self.late:
                    pieces[offset] = (array, exchanged[2], at)
                    continue
                pieces[offset] = (self.packed_early, exchanged[1], at + self.early_at(array))
        return assemble(
            self.blocks[level][0], pieces, self.core, self.sub_index % (2 << level)
        )

    def early_at(self, array):
        at = 0
        for known in self.early:
            if known is array:
                return at
            at += known.shape[1]

    def pack_early(self):
        self.packed_early = pack([(array, 0, array.shape[1]) for array in self.early])
        return self.packed_early


class View:
    def __init__(self, array, rows=None, cols=None):
        self.array = array
        self.rows = (0, array.shape[0]) if rows is None else rows
        self.cols = (0, array.shape[1]) if cols is None else cols
        self.shape = (self.rows[1] - self.rows[0], self.cols[1] - self.cols[0])

    def value(self):
        return self.array[slice(*self.rows), slice(*self.cols)]

    def part(self, first, last):
        return View(self.array, (self.rows[0] + first, self.rows[0] + last), self.cols)

    def aligned(self):
        edges = (*self.rows, *self.cols)
        return all(edge % unit == 0 for edge, unit in zip(edges, (16, 16, 128, 128)))


def spots_of(views):
    arrays, spots = [], []
    for view in views:
        known = [i for i, array in enumerate(arrays) if array is view.array]
        if not known:
            arrays.append(view.array)
            known = [len(arrays) - 1]
        spots.append((known[0], view.rows, view.cols))
    return arrays, spots


def stack_rows(views):
    if len(views) == 1 and views[0].shape == views[0].array.shape:
        return views[0].array
    if not all(view.aligned() for view in views):
        return join_all([view.value() for view in views])
    arrays, spots = spots_of(views)

    def body(*values):
        parts = [values[i][slice(*rows), slice(*cols)] for i, rows, cols in spots]
        return (jnp.concatenate(parts, axis=0),)

    return fused(body, "stack_rows", *arrays, limit=6)[0]


def join_all(pieces):
    if all(piece.shape[0] % 16 == 0 for piece in pieces):
        return jnp.concatenate(pieces, axis=0)
    wide = lax.optimization_barrier(tuple(f32(piece) for piece in pieces))
    return bf16(lax.optimization_barrier(jnp.concatenate(wide, axis=0)))


def halve_kernel(groups, count, ids_ref, *refs):
    outs = refs[count:]
    send_ref = outs[-1]
    col = 0
    for spots, keep_ref in zip(groups, outs):
        half = keep_ref.shape[1]
        at = 0
        for index, (first, last), (left, _) in spots:
            where = slice(at, at + last - first)
            for bit, out, here in ((ids_ref[0], keep_ref, 0), (1 - ids_ref[0], send_ref, col)):
                lanes = pl.ds(pl.multiple_of(left + bit * half, 128), half)
                out[where, here : here + half] = refs[index][first:last, lanes]
            at += last - first
        col += half


def halve(groups, bit):
    views = [view for group in groups for view in group]
    if all(view.aligned() and view.shape[1] % 256 == 0 for view in views):
        arrays, spots = spots_of(views)
        by_group, out_shapes = [], []
        for group in groups:
            by_group.append([spots.pop(0) for _ in group])
            out_shapes.append((sum(view.shape[0] for view in group), group[0].shape[1] // 2))
        out_shapes.append((out_shapes[0][0], sum(shape[1] for shape in out_shapes)))
        outs = pl.pallas_call(
            functools.partial(halve_kernel, by_group, len(arrays)),
            out_shape=[jax.ShapeDtypeStruct(shape, jnp.bfloat16) for shape in out_shapes],
            in_specs=[smem_block()] + [whole_block()] * len(arrays),
            out_specs=[whole_block()] * len(out_shapes),
            compiler_params=pltpu.CompilerParams(vmem_limit_bytes=6 * MIB),
            name="halve",
        )(ids_of(bit), *arrays)
        return outs[:-1], outs[-1]
    keeps, sends = [], []
    for group in groups:
        full = join_all([view.value() for view in group])
        half = full.shape[1] // 2
        keeps.append(lax.dynamic_slice_in_dim(full, bit * half, half, 1))
        sends.append(lax.dynamic_slice_in_dim(full, (1 - bit) * half, half, 1))
    return keeps, jnp.concatenate(sends, axis=1)


def upper_grads_kernel(entries, count, ids_ref, *refs):
    own_ref, far_ref, give_ref = refs[count:]
    quarter = own_ref.shape[1]
    col = 0
    for index, turns in enumerate(entries):
        for turn, (inputs, grads) in enumerate(turns):
            grad = jnp.concatenate(
                [refs[i][slice(*rows), slice(*cols)] for i, rows, cols in grads], axis=0
            )
            span = grad.shape[1]
            side = jnp.bitwise_xor(ids_ref[2 + index], turn)
            for far in range(2):
                for core in range(2):
                    which = jnp.bitwise_xor(ids_ref[1], far) * 2 + jnp.bitwise_xor(ids_ref[0], core)
                    lanes = pl.ds(pl.multiple_of(which * quarter, quarter), quarter)
                    rows = jnp.concatenate(
                        [refs[i][slice(*edges), lanes] for i, edges, _ in inputs], axis=0
                    )
                    value = inner_t(rows, grad)
                    if core == 1:
                        give_ref[side, far, :, col : col + span] = bf16(value)
                    elif far == 1:
                        far_ref[side, :, col : col + span] = value
                    else:
                        own_ref[side, :, col : col + span] = value
        col += span


def upper_grads(entries, core, far):
    width = entries[0][1][0][0].shape[1]
    spans = [entry[1][1][0].shape[1] for entry in entries]
    quarter = width // 4
    views = []
    for _, *turns in entries:
        for inputs, grads in turns:
            views += inputs + grads
    if all(view.aligned() for view in views):
        total = sum(spans)
        arrays, spots = spots_of(views)
        by_entry = []
        for _, *turns in entries:
            by_entry.append(
                [
                    ([spots.pop(0) for _ in inputs], [spots.pop(0) for _ in grads])
                    for inputs, grads in turns
                ]
            )
        return pl.pallas_call(
            functools.partial(upper_grads_kernel, by_entry, len(arrays)),
            out_shape=[
                jax.ShapeDtypeStruct((2, quarter, total), jnp.float32),
                jax.ShapeDtypeStruct((2, quarter, total), jnp.float32),
                jax.ShapeDtypeStruct((2, 2, quarter, total), jnp.bfloat16),
            ],
            in_specs=[smem_block()] + [whole_block()] * len(arrays),
            out_specs=[whole_block()] * 3,
            compiler_params=pltpu.CompilerParams(vmem_limit_bytes=12 * MIB),
            name="upper_grads",
        )(ids_of(core, far, *[entry[0] for entry in entries]), *arrays)
    owns, fars, gives = [], [], []
    for first, *turns in entries:
        both = [
            inner_t(join_all([v.value() for v in inputs]), join_all([v.value() for v in grads]))
            for inputs, grads in turns
        ]
        pair = jnp.stack([jnp.where(first == 1, both[1 - i], both[i]) for i in range(2)])
        pair = pair.reshape(2, 2, 2, quarter, -1)
        pair = jnp.where(far == 1, pair[:, ::-1], pair)
        pair = jnp.where(core == 1, pair[:, :, ::-1], pair)
        owns.append(pair[:, 0, 0])
        fars.append(pair[:, 1, 0])
        gives.append(bf16(pair[:, :, 1]))
    return [jnp.concatenate(parts, axis=-1) for parts in (owns, fars, gives)]


def far_sum(far_part, got):
    return (bf16(far_part + f32(got[:, 1])),)


def last_sum(*args):
    parts = []
    for own, got, last in (args[:3], args[3:]):
        parts.append(bf16(own + f32(got[:, 0]) + f32(last)))
    return (jnp.swapaxes(jnp.concatenate(parts, axis=2), 0, 1),)


def mid_forward(term, near, far, weight):
    product = (1.0 + f32(term)) * (1.0 + f32(near)) * f32(far)
    return up_product(bf16(product * rms_factor(product)), weight)


def up_product(message, weight):
    up = matmul(message, weight)
    keep = up.shape[0] // 2
    return message, up[:keep], bf16(up[keep:])


def up_forward(own_up, other_up, weight):
    joined = (1.0 + own_up) * (1.0 + f32(other_up))
    return up_product(bf16(joined * rms_factor(joined)), weight)


def top_forward(own_up, other_up):
    joined = (1.0 + own_up) * (1.0 + f32(other_up))
    return (bf16(joined * rms_factor(joined)),)


def head_body(cotangent, left, right, low, high):
    root = join([low, high])
    value = matmul(root, left)
    gating = jax.nn.sigmoid(matmul(root, right))
    grad_value = bf16(cotangent * gating)
    grad_gate = bf16(cotangent * value * gating * (1.0 - gating))
    back = matmul_t(grad_value, left) + matmul_t(grad_gate, right)
    half = root.shape[0] // 2
    return root, grad_value, grad_gate, back[:half], bf16(back[half:])


def joined(low, high):
    return (join([low, high]),)


def partial_sum(own, got):
    total = own + f32(got)
    half = total.shape[0] // 2
    return total[:half], bf16(total[half:])


def level_back(grad_msg, own_up, other_up):
    own_up, other_up = 1.0 + own_up, 1.0 + f32(other_up)
    joined = own_up * other_up
    scaling = rms_factor(joined)
    grad = norm_back(grad_msg, joined * scaling, scaling)
    return bf16(grad * other_up), bf16(grad * own_up)


def top_back(own_up, other_up, own_part, got):
    return level_back(own_part + f32(got), own_up, other_up)


def down_back(own_up, other_up, weight, low, high):
    return level_back(matmul_t(join([low, high]), weight), own_up, other_up)


def mid_back(term, near, far, weight, low, high):
    own, near, far = 1.0 + f32(term), 1.0 + f32(near), f32(far)
    pair = own * near
    product = pair * far
    scale = rms_factor(product)
    grad_msg = matmul_t(join([low, high]), weight)
    grad = norm_back(grad_msg, product * scale, scale)
    grad_pair = grad * far
    return bf16(grad_pair * near), bf16(grad_pair * own), bf16(grad * pair)


def far_back(grad_pair, term, near):
    grad_pair = f32(grad_pair)
    return bf16(grad_pair * (1.0 + f32(near))), bf16(grad_pair * (1.0 + f32(term)))


def pair_product(term, near):
    return (bf16((1.0 + f32(term)) * (1.0 + f32(near))),)


def swap_blocks(array, size, axis):
    count = array.shape[axis] // size
    parts = [lax.slice_in_dim(array, i * size, (i + 1) * size, axis=axis) for i in range(count)]
    return jnp.concatenate([parts[i ^ 1] for i in range(count)], axis=axis)


def on_device(regions, leaf_map, leaf_bond_weight, mid_weight, upper_weight, head_cotangent):
    rows = regions.shape[0]
    width = upper_weight.shape[1]
    sub_count = lax.axis_size("sub")
    depth = sub_count.bit_length() - 1
    sub_index = lax.axis_index("sub")
    rep_index = lax.axis_index("rep")
    core = rep_index % 2
    far = rep_index // 2
    bits = [(sub_index >> level) % 2 for level in range(depth)]
    flip = sum(bits[level] * (rows >> (level + 1)) for level in range(depth))
    leaf_w = leaf_bond_weight[0]
    mid_w = mid_weight[0, 0]

    blocks, (head_left, head_right) = cut_maps(upper_weight[0], core, bits)
    gather = MapGather(blocks, core, sub_index)
    gather.stage(depth - 1)

    sent = place(after(regions, head_right), leaf_map, ids_of(rep_index, flip))
    near = partner(sent[1], "rep", 1)
    far_both = partner(sent[3], "rep", 3)
    far_one = partner(sent[2], "rep", 2)
    placed = [sent[0], near, far_one, far_both]
    msg0, msg1, term0, term1 = leaf_forward(placed[:2], leaf_w, mid_w)
    near0 = partner(term1, "rep", 1)
    for stage in reversed(range(1, depth - 1)):
        gather.stage(stage, sent[3])
    far_placed = [after(placed[2], term1), placed[3]]
    msg2, msg3, term2, term3 = leaf_forward(far_placed, leaf_w, mid_w)
    near2 = partner(term3, "rep", 1)
    (pair,) = fused(pair_product, "pair_product", term2, near2)
    far_pair = partner(pair, "rep", 2)
    cotangent = after(head_cotangent, pair)
    for level in range(depth):
        swapped = swap_blocks(cotangent, rows >> (level + 1), 0)
        cotangent = jnp.where(bits[level] == 1, swapped, cotangent)
    gather.last(pair)
    exchanged = [partner(after(gather.first, pair), "rep", 1)]
    exchanged.append(partner(after(gather.pack_early(), pair), "rep", 1))
    exchanged.append(partner(gather.late, "rep", 1))
    weights = [gather.weight(level, exchanged) for level in range(depth)]

    messages, own_ups, other_ups = [], [], []
    for level in range(depth):
        if level == 0:
            step = fused(mid_forward, "mid_forward", term0, near0, far_pair, weights[0])
        else:
            step = fused(up_forward, "up_forward", own_ups[-1], other_ups[-1], weights[level])
        messages.append(step[0])
        own_ups.append(step[1])
        other_ups.append(partner(step[2], "sub", 1 << level))
    (root,) = fused(top_forward, "top_forward", own_ups[-1], other_ups[-1])

    for level in reversed(range(1, depth)):
        (root,) = fused(joined, "joined", root, partner(root, "sub", 1 << level))
    root_high = partner(root, "sub", 1)
    root, grad_value, grad_gate, grad_msg, give = fused(
        head_body, "head", cotangent, head_left, head_right, root, root_high
    )
    gates = [give]
    for level in range(depth - 1):
        got = partner(give, "sub", 1 << level)
        grad_msg, give = fused(partial_sum, "partial_sum", grad_msg, got)
        gates.append(give)
    last_part = partner(give, "sub", 1 << (depth - 1))

    turns = [[[View(message)], []] for message in messages]
    for stage in reversed(range(depth)):
        levels = range(stage, depth)
        views = []
        for level in levels:
            views += turns[level][0] + (turns[level][1] if level > stage else [])
        views[0] = View(
            after(views[0].array, gates[depth - 1 - stage]), views[0].rows, views[0].cols
        )
        got = partner(stack_rows(views), "sub", 1 << stage)
        at = 0
        for level in levels:
            count = sum(view.shape[0] for view in turns[level][0])
            turns[level][0 if level > stage else 1].append(View(got, (at, at + count)))
            at += count
            if level > stage:
                turns[level][1].append(View(got, (at, at + count)))
                at += count

    lows, highs = [None] * depth, [None] * depth
    columns = [None] * depth

    def spread(stage, levels, gate):
        groups = []
        for level in levels:
            if columns[level] is None:
                groups.append([View(lows[level]), View(highs[level])])
            else:
                groups.append(list(columns[level]))
        first = groups[0][0]
        groups[0][0] = View(after(first.array, gate), first.rows, first.cols)
        keeps, send = halve(groups, bits[stage])
        got = partner(send, "sub", 1 << stage)
        at = 0
        for level, keep in zip(levels, keeps):
            span = keep.shape[1]
            columns[level] = [View(keep), View(got, None, (at, at + span))]
            at += span

    def columns_of(level, turn):
        if level == 0:
            return [columns[0][turn]]
        count = rows >> level
        return [
            view.part(i * count, (i + 1) * count)
            for view in columns[level]
            for i in range(turn, view.shape[0] // count, 2)
        ]

    for level in reversed(range(depth)):
        if level == depth - 1:
            low, high = fused(
                top_back, "top_back", own_ups[level], other_ups[level], grad_msg, last_part
            )
        else:
            low, high = fused(
                down_back,
                "down_back",
                own_ups[level],
                other_ups[level],
                weights[level + 1],
                lows[level + 1],
                highs[level + 1],
            )
        lows[level] = low
        highs[level] = partner(high, "sub", 1 << level)
        if level < depth - 1:
            spread(level + 1, list(range(level + 1, depth)), low)

    back0, back1, pair_back = fused(
        mid_back, "mid_back", term0, near0, far_pair, weights[0], lows[0], highs[0]
    )
    pair_back = partner(pair_back, "rep", 2)
    back1 = partner(back1, "rep", 1)
    first = leaf_first(placed[:2], [back0, back1], leaf_w, mid_w)
    back2, back3 = fused(far_back, "far_back", after(pair_back, first), term2, near2)
    back3 = partner(back3, "rep", 1)
    spread(0, list(range(1, depth)), back0)
    spread(0, [0], back0)

    def entry(level):
        return (bits[level], *[(turns[level][i], columns_of(level, i)) for i in range(2)])

    groups = [
        [entry(0)],
        [entry(level) for level in range(1, depth)]
        + [(0, ([View(root)], [View(grad_value)]), ([View(root)], [View(grad_gate)]))],
    ]
    sums = [None, None]
    for index, gate in ((1, back1), (0, back2)):
        views = groups[index][0][1][1]
        views[0] = View(after(views[0].array, gate), views[0].rows, views[0].cols)
        own, far_part, give = upper_grads(groups[index], core, far)
        got = partner(give, "rep", 1)
        (far_part,) = fused(far_sum, "far_sum", far_part, got)
        sums[index] = [own, got, partner(far_part, "rep", 2)]
    leaf_grad, mid_grad = leaf_backward(
        placed,
        [msg0, msg1, msg2, msg3],
        [back0, back1, after(back2, far_part), back3],
        leaf_w,
        mid_w,
        first,
    )
    (upper,) = fused(last_sum, "last_sum", *sums[0], *sums[1], limit=16)
    return leaf_grad[None], mid_grad[None, None], upper[None]


def solution(mesh):
    placed = (
        P("rep", "sub", None),
        P("sub"),
        P(("sub", "rep"), None, None, None),
        P("sub", "rep", None, None),
        P("sub", None, None, None),
        P("rep", "sub"),
    )
    return jax.shard_map(
        on_device,
        mesh=mesh,
        in_specs=placed,
        out_specs=(
            P(("sub", "rep"), None, None, None),
            P("sub", "rep", None, None),
            P("sub", "rep", None, None),
        ),
        check_vma=False,
    )
```

time: 261 us -> 197 us (0.75)
  local copies, waits for them, and re-layouts: 65.1 us -> 27.6 us
  starting transfers between devices: 81.1 us -> 49.5 us
  waiting for transfers between devices: 56.6 us -> 77.9 us
  other arithmetic: 9.47 us -> 1.32 us
  Pallas kernels: 45.8 us -> 38.7 us
    unnamed x223 -> x139, local copies, waits for them, and re-layouts: 63.1 us -> 26.7 us
    ppermute x77 -> x40, starting transfers between devices: 81.1 us -> 49.5 us  [partner(): lax.ppermute(value, axis, [(i, i ^ offset) for i in range(lax.axis_size(a...]
    ppermute x77 -> x40, waiting for transfers between devices: 56.6 us -> 77.9 us  [partner(): lax.ppermute(value, axis, [(i, i ^ offset) for i in range(lax.axis_size(a...]
    convert_element_type x4 -> x0, other arithmetic: 7.11 us -> none  [bf16(): return value.astype(jnp.bfloat16)]
    pallas_call x8 -> x10, Pallas kernels: 15.2 us -> 11.5 us  [the longest x3 3.18 us: assemble(): pl.pallas_call(functools.partial(assemble_kernel, spots, len(mine)), out_...]
    pallas_call x11 -> x24, Pallas kernels: 12.1 us -> 11.5 us  [fused(): pl.pallas_call(kernel, out_shape=shapes, in_specs=[whole_block()] * len(a...]
  transfers between devices with their start and end apart: 77 -> 40, of which waited for: 23 -> 22; matrix products, arithmetic and copies ran while one was open for 6% -> 1% of each run, Pallas kernels for 17% -> 15%
where the time goes in v3:
time: 197 us; the launch traced here: 196 us
  waiting for transfers between devices  77.9 us (40%)
  starting transfers between devices  49.5 us (25%)
  Pallas kernels  38.7 us (20%)
  local copies, waits for them, and re-layouts  27.6 us (14%)
    ppermute x40, waiting for transfers between devices, partner(): lax.ppermute(value, axis, [(i, i ^ offset) for i in range(lax.axis_size(a...  77.9 us
    ppermute x40, starting transfers between devices, partner(): lax.ppermute(value, axis, [(i, i ^ offset) for i in range(lax.axis_size(a...  49.5 us
    unnamed x139, local copies, waits for them, and re-layouts  26.7 us
    pallas_call x24, Pallas kernels, fused(): pl.pallas_call(kernel, out_shape=shapes, in_specs=[whole_block()] * len(a...  11.5 us
    pallas_call x1, Pallas kernels, leaf_backward(): pl.pallas_call(leaf_backward_kernel, out_shape=[jax.ShapeDtypeStruct(leaf...  6.77 us
  transfers between devices with their start and end apart: 40, of which 22 were waited for; matrix products, arithmetic and copies ran while one was open for 1% of the time, Pallas kernels for 15%

profile of v3, /device:TPU:0, one launch (start us, length us, event | category | flops | bytes accessed | tf_op | source)
XLA Modules:
  0.0 196.5 jit_solution(2813976279278306295)
XLA Ops:
  0.7 2.2 %copy-done.4 = bf16[1,1024,2,1024]{3,2,1,0:T(2,128)(2,1)S(1)} copy-done((bf16[1,1024,2,1024]{3,2,1,0:T(2,128)(2,1)S(1)}, bf16[1,1024,2,1024]{3,2,1,0:T(2,128)(2,1)}, u32[]{:S(2)}) %copy-start.4) | copy-done | bytes 4194328
  2.9 2.5 %cut_maps.1 = (bf16[1024,512]{1,0:T(8,128)(2,1)S(1)}, bf16[512,512]{1,0:T(8,128)(2,1)}, bf16[512,512]{1,0:T(8,128)(2,1)S(1)}, bf16[1024,256]{1,0:T(8,128)(2,1)S(...) custom-call(s32[4]{0:T(128)S(1)} %pad_add_fusion.1.ids_ref, ...), custom_call_target="tpu_custom_call" | custom-call | tf_op jit(solution)/shard_map/cut_maps/pallas_call | solution.py:271
  12.9 2.8 %place.1 = (bf16[4,128,256]{2,1,0:T(8,128)(2,1)S(1)}, bf16[4,128,256]{2,1,0:T(8,128)(2,1)}, bf16[4,128,256]{2,1,0:T(8,128)(2,1)}, bf16[4,128,256]{2,1,0:T(8,128)(2,1)}) custom-call(s32[2]{0:T(128)S(1)} %pad_add_fusion.ids_ref, s32[16]{0:T(128)S(1)} %copy-done.63, bf16[2048,256]{1,0:T(8,128)(2,1)S(1)} %bitcast.26), custom_call_target="tpu_custom_call" | custom-call | tf_op jit(solution)/shard_map/place/pallas_call | solution.py:79
  16.2 2.5 %collective-permute-start.1 = (bf16[4,128,256]{2,1,0:T(8,128)(2,1)}, bf16[4,128,256]{2,1,0:T(8,128)(2,1)S(1)}, u32[]{:S(2)}, u32[]{:S(2)}) collective-permute-start(bf16[4,128,256]{2,1,0:T(8,128)(2,1)} %get-tuple-element.94), channel_id=1, source_target_pairs={{0,2},{1,3},{2,0},{3,1},{4,6},{5,7},{6,4},{7,5},{8,10},{9,11},{10,... | collective-permute-start | bytes 786440 | tf_op jit(solution)/shard_map/ppermute | solution.py:16
  20.6 2.6 %collective-permute-start.10 = (bf16[512,128]{1,0:T(8,128)(2,1)S(1)}, bf16[512,128]{1,0:T(8,128)(2,1)S(1)}, u32[]{:S(2)}, u32[]{:S(2)}) collective-permute-start(bf16[512,128]{1,0:T(8,128)(2,1)S(1)} %get-tuple-element.113), channel_id=1, source_target_pairs={{0,16},{4,20},{8,24},{12,28},{16,0},{20,4},{24,8},{28,12},{1,17},{... | collective-permute-start | bytes 393224 | tf_op jit(solution)/shard_map/ppermute | solution.py:16
  31.3 2.2 %leaf_forward.3 = (bf16[128,1024]{1,0:T(8,128)(2,1)S(1)}, bf16[128,1024]{1,0:T(8,128)(2,1)S(1)}, bf16[128,1024]{1,0:T(8,128)(2,1)S(1)}, bf16[128,1024]{1,0:T(8,128)(2,1)}) custom-call(bf16[4,128,256]{2,1,0:T(8,128)(2,1)S(1)} %collective-permute-done.1.refs_0_.refs_2_, bf16[4,128,256]{2,1,0:T(8,128)(2,1)S(1)} %collective-permute-done.2.refs_1_.refs_3_, ...), custom_call_target="tpu_custom_call" | custom-call | tf_op jit(solution)/shard_map/leaf_forward/pallas_call | solution.py:110
  43.7 7.5 %collective-permute-done.11.refs_2_.refs_0_ = bf16[512,512]{1,0:T(8,128)(2,1)S(1)} collective-permute-done((bf16[512,512]{1,0:T(8,128)(2,1)S(1)}, bf16[512,512]{1,0:T(8,128)(2,1)S(1)}, u32[]{:S(2)}, u32[]{:S(2)}) %collective-permute-start.11) | collective-permute-done | bytes 524320 | tf_op jit(solution)/shard_map/ppermute | solution.py:16
  54.2 13.0 %collective-permute-done.12.refs_1_ = bf16[512,640]{1,0:T(8,128)(2,1)S(1)} collective-permute-done((bf16[512,640]{1,0:T(8,128)(2,1)S(1)}, bf16[512,640]{1,0:T(8,128)(2,1)S(1)}, u32[]{:S(2)}, u32[]{:S(2)}) %collective-permute-start.12) | collective-permute-done | bytes 655392 | tf_op jit(solution)/shard_map/ppermute | solution.py:16
  71.6 3.5 %collective-permute-done.8.refs_1_ = bf16[64,1024]{1,0:T(8,128)(2,1)S(1)} collective-permute-done((bf16[64,1024]{1,0:T(8,128)(2,1)S(1)}, bf16[64,1024]{1,0:T(8,128)(2,1)S(1)}, u32[]{:S(2)}, u32[]{:S(2)}) %collective-permute-start.8) | collective-permute-done | bytes 131104 | tf_op jit(solution)/shard_map/ppermute | solution.py:16
  80.6 2.7 %collective-permute-start.16 = (bf16[16,1024]{1,0:T(8,128)(2,1)S(1)}, bf16[16,1024]{1,0:T(8,128)(2,1)S(1)}, u32[]{:S(2)}, u32[]{:S(2)}) collective-permute-start(bf16[16,1024]{1,0:T(8,128)(2,1)S(1)} %get-tuple-element.122), channel_id=1, source_target_pairs={{0,16},{4,20},{8,24},{12,28},{16,0},{20,4},{24,8},{28,12},{1,17},{... | collective-permute-start | bytes 98312 | tf_op jit(solution)/shard_map/ppermute | solution.py:16
  83.2 2.2 %collective-permute-done.16.refs_1_ = bf16[16,1024]{1,0:T(8,128)(2,1)S(1)} collective-permute-done((bf16[16,1024]{1,0:T(8,128)(2,1)S(1)}, bf16[16,1024]{1,0:T(8,128)(2,1)S(1)}, u32[]{:S(2)}, u32[]{:S(2)}) %collective-permute-start.16) | collective-permute-done | bytes 32800 | tf_op jit(solution)/shard_map/ppermute | solution.py:16
  85.5 2.7 %collective-permute-start.17 = (bf16[16,1024]{1,0:T(8,128)(2,1)S(1)}, bf16[16,1024]{1,0:T(8,128)(2,1)S(1)}, u32[]{:S(2)}, u32[]{:S(2)}) collective-permute-start(bf16[16,1024]{1,0:T(8,128)(2,1)S(1)} %top_forward.1.refs_0_), channel_id=1, source_target_pairs={{0,16},{4,20},{8,24},{12,28},{16,0},{20,4},{24,8},{28,12},{1,17},{... | collective-permute-start | bytes 98312 | tf_op jit(solution)/shard_map/ppermute | solution.py:16
  88.3 2.2 %collective-permute-done.17.refs_1_ = bf16[16,1024]{1,0:T(8,128)(2,1)S(1)} collective-permute-done((bf16[16,1024]{1,0:T(8,128)(2,1)S(1)}, bf16[16,1024]{1,0:T(8,128)(2,1)S(1)}, u32[]{:S(2)}, u32[]{:S(2)}) %collective-permute-start.17) | collective-permute-done | bytes 32800 | tf_op jit(solution)/shard_map/ppermute | solution.py:16
  92.1 2.6 %collective-permute-done.18.refs_1_ = bf16[32,1024]{1,0:T(8,128)(2,1)S(1)} collective-permute-done((bf16[32,1024]{1,0:T(8,128)(2,1)S(1)}, bf16[32,1024]{1,0:T(8,128)(2,1)S(1)}, u32[]{:S(2)}, u32[]{:S(2)}) %collective-permute-start.18) | collective-permute-done | bytes 65568 | tf_op jit(solution)/shard_map/ppermute | solution.py:16
  96.3 4.7 %collective-permute-done.19.refs_4_ = bf16[64,1024]{1,0:T(8,128)(2,1)S(1)} collective-permute-done((bf16[64,1024]{1,0:T(8,128)(2,1)S(1)}, bf16[64,1024]{1,0:T(8,128)(2,1)S(1)}, u32[]{:S(2)}, u32[]{:S(2)}) %collective-permute-start.19) | collective-permute-done | bytes 131104 | tf_op jit(solution)/shard_map/ppermute | solution.py:16
  103.8 2.7 %collective-permute-start.28 = (bf16[32,1024]{1,0:T(8,128)(2,1)S(1)}, bf16[32,1024]{1,0:T(8,128)(2,1)S(1)}, u32[]{:S(2)}, u32[]{:S(2)}) collective-permute-start(bf16[32,1024]{1,0:T(8,128)(2,1)S(1)} %get-tuple-element.150.refs_1_.refs_3_.refs_6_), channel_id=1, source_target_pairs={{0,16},{4,20},{8,24},{12,28},{16,0},{20,4},{24,8},{28,12},{1,17},{... | collective-permute-start | bytes 196616 | tf_op jit(solution)/shard_map/ppermute | solution.py:16
  111.1 5.4 %collective-permute-done.21.refs_1_ = bf16[32,1024]{1,0:T(8,128)(2,1)S(1)} collective-permute-done((bf16[32,1024]{1,0:T(8,128)(2,1)S(1)}, bf16[32,1024]{1,0:T(8,128)(2,1)S(1)}, u32[]{:S(2)}, u32[]{:S(2)}) %collective-permute-start.21) | collective-permute-done | bytes 65568 | tf_op jit(solution)/shard_map/ppermute | solution.py:16
  118.5 2.1 %collective-permute-start.22 = (bf16[16,1024]{1,0:T(8,128)(2,1)S(1)}, bf16[16,1024]{1,0:T(8,128)(2,1)S(1)}, u32[]{:S(2)}, u32[]{:S(2)}) collective-permute-start(bf16[16,1024]{1,0:T(8,128)(2,1)S(1)} %get-tuple-element.130), channel_id=1, source_target_pairs={{0,16},{4,20},{8,24},{12,28},{16,0},{20,4},{24,8},{28,12},{1,17},{... | collective-permute-start | bytes 98312 | tf_op jit(solution)/shard_map/ppermute | solution.py:16
  120.6 2.7 %collective-permute-done.22.refs_3_ = bf16[16,1024]{1,0:T(8,128)(2,1)S(1)} collective-permute-done((bf16[16,1024]{1,0:T(8,128)(2,1)S(1)}, bf16[16,1024]{1,0:T(8,128)(2,1)S(1)}, u32[]{:S(2)}, u32[]{:S(2)}) %collective-permute-start.22) | collective-permute-done | bytes 32800 | tf_op jit(solution)/shard_map/ppermute | solution.py:16
  123.5 2.2 %collective-permute-start.23 = (bf16[16,1024]{1,0:T(8,128)(2,1)S(1)}, bf16[16,1024]{1,0:T(8,128)(2,1)S(1)}, u32[]{:S(2)}, u32[]{:S(2)}) collective-permute-start(bf16[16,1024]{1,0:T(8,128)(2,1)S(1)} %get-tuple-element.132), channel_id=1, source_target_pairs={{0,16},{4,20},{8,24},{12,28},{16,0},{20,4},{24,8},{28,12},{1,17},{... | collective-permute-start | bytes 98312 | tf_op jit(solution)/shard_map/ppermute | solution.py:16
  125.7 2.7 %collective-permute-done.23.refs_4_.refs_1_ = bf16[16,1024]{1,0:T(8,128)(2,1)S(1)} collective-permute-done((bf16[16,1024]{1,0:T(8,128)(2,1)S(1)}, bf16[16,1024]{1,0:T(8,128)(2,1)S(1)}, u32[]{:S(2)}, u32[]{:S(2)}) %collective-permute-start.23) | collective-permute-done | bytes 32800 | tf_op jit(solution)/shard_map/ppermute | solution.py:16
  129.3 2.3 %collective-permute-start.24 = (bf16[32,1024]{1,0:T(8,128)(2,1)S(1)}, bf16[32,1024]{1,0:T(8,128)(2,1)S(1)}, u32[]{:S(2)}, u32[]{:S(2)}) collective-permute-start(bf16[32,1024]{1,0:T(8,128)(2,1)S(1)} %get-tuple-element.134), channel_id=1, source_target_pairs={{0,8},{4,12},{8,0},{12,4},{16,24},{20,28},{24,16},{28,20},{1,9},{5... | collective-permute-start | bytes 196616 | tf_op jit(solution)/shard_map/ppermute | solution.py:16
  131.6 2.2 %collective-permute-done.24.refs_4_.refs_1_ = bf16[32,1024]{1,0:T(8,128)(2,1)S(1)} collective-permute-done((bf16[32,1024]{1,0:T(8,128)(2,1)S(1)}, bf16[32,1024]{1,0:T(8,128)(2,1)S(1)}, u32[]{:S(2)}, u32[]{:S(2)}) %collective-permute-start.24) | collective-permute-done | bytes 65568 | tf_op jit(solution)/shard_map/ppermute | solution.py:16
  135.6 4.2 %collective-permute-done.25.refs_5_.refs_1_ = bf16[64,1024]{1,0:T(8,128)(2,1)S(1)} collective-permute-done((bf16[64,1024]{1,0:T(8,128)(2,1)S(1)}, bf16[64,1024]{1,0:T(8,128)(2,1)S(1)}, u32[]{:S(2)}, u32[]{:S(2)}) %collective-permute-start.25) | collective-permute-done | bytes 131104 | tf_op jit(solution)/shard_map/ppermute | solution.py:16
  139.8 2.1 %mid_back.1 = (bf16[128,1024]{1,0:T(8,128)(2,1)S(1)}, bf16[128,1024]{1,0:T(8,128)(2,1)}, bf16[128,1024]{1,0:T(8,128)(2,1)}) custom-call(bf16[128,1024]{1,0:T(8,128)(2,1)S(1)} %copy-done.23, bf16[128,1024]{1,0:T(8,128)(2,1)S(1)} %collective-permute-done.3.refs_1_, bf16[128,1024]{1,0:T(8,128)(2,1)S(1)} %collective-permute-done.5.refs_2_, ...), custom_call_target="tpu_custom_call" | custom-call | tf_op jit(solution)/shard_map/mid_back/pallas_call | solution.py:195
  144.1 2.2 %collective-permute-start.35 = (bf16[32,512]{1,0:T(8,128)(2,1)S(1)}, bf16[32,512]{1,0:T(8,128)(2,1)S(1)}, u32[]{:S(2)}, u32[]{:S(2)}) collective-permute-start(bf16[32,512]{1,0:T(8,128)(2,1)S(1)} %get-tuple-element.162), channel_id=1, source_target_pairs={{0,16},{4,20},{8,24},{12,28},{16,0},{20,4},{24,8},{28,12},{1,17},{... | collective-permute-start | bytes 98312 | tf_op jit(solution)/shard_map/ppermute | solution.py:16
  146.2 2.7 %collective-permute-done.35.refs_3_ = bf16[32,512]{1,0:T(8,128)(2,1)S(1)} collective-permute-done((bf16[32,512]{1,0:T(8,128)(2,1)S(1)}, bf16[32,512]{1,0:T(8,128)(2,1)S(1)}, u32[]{:S(2)}, u32[]{:S(2)}) %collective-permute-start.35) | collective-permute-done | bytes 32800 | tf_op jit(solution)/shard_map/ppermute | solution.py:16
  150.1 2.0 %collective-permute-start.36 = (bf16[64,768]{1,0:T(8,128)(2,1)}, bf16[64,768]{1,0:T(8,128)(2,1)}, u32[]{:S(2)}, u32[]{:S(2)}) collective-permute-start(bf16[64,768]{1,0:T(8,128)(2,1)} %get-tuple-element.165), channel_id=1, source_target_pairs={{0,8},{4,12},{8,0},{12,4},{16,24},{20,28},{24,16},{28,20},{1,9},{5... | collective-permute-start | bytes 294920 | tf_op jit(solution)/shard_map/ppermute | solution.py:16
  161.1 3.1 %leaf_first.1.refs_14_ = bf16[4,256,1024]{2,1,0:T(8,128)(2,1)S(1)} custom-call(bf16[4,128,256]{2,1,0:T(8,128)(2,1)S(1)} %get-tuple-element.92.refs_0_, bf16[4,128,256]{2,1,0:T(8,128)(2,1)S(1)} %collective-permute-done.refs_1_, bf16[128,1024]{1,0:T(8,128)(2,1)S(1)} %copy-done.17, bf16[128,1024]{1,0:T(8,128)(2,1)} %collective-permute-done.26.refs_3_.refs_9_, ...), custom_call_target="tpu_custom_call" | custom-call | tf_op jit(solution)/shard_map/leaf_first/pallas_call | solution.py:148
  173.7 6.8 %leaf_backward.1 = (bf16[4,256,1024]{2,1,0:T(8,128)(2,1)}, bf16[1024,1024]{1,0:T(8,128)(2,1)}) custom-call(bf16[4,128,256]{2,1,0:T(8,128)(2,1)S(1)} %get-tuple-element.92.refs_0_, bf16[4,128,256]{2,1,0:T(8,128)(2,1)S(1)} %collective-permute-done.refs_1_, bf16[4,128,256]{2,1,0:T(8,128)(2,1)S(1)} %copy-done.8, bf16[4,128,256]{2,1,0:T(8,128)(2,1)S(1)} %copy-done.10, ...), custom_call_target="tpu_custom_call" | custom-call | tf_op jit(solution)/shard_map/leaf_backward/pallas_call | solution.py:172
  180.5 4.0 %collective-permute-done.39.refs_5_ = bf16[2,256,512]{2,1,0:T(8,128)(2,1)S(1)} collective-permute-done((bf16[2,256,512]{2,1,0:T(8,128)(2,1)S(1)}, bf16[2,256,512]{2,1,0:T(8,128)(2,1)S(1)}, u32[]{:S(2)}, u32[]{:S(2)}) %collective-permute-start.39) | collective-permute-done | bytes 524320 | tf_op jit(solution)/shard_map/ppermute | solution.py:16
  184.6 10.4 %collective-permute-done.34.refs_2_ = bf16[2,256,512]{2,1,0:T(8,128)(2,1)S(1)} collective-permute-done((bf16[2,256,512]{2,1,0:T(8,128)(2,1)S(1)}, bf16[2,256,512]{2,1,0:T(8,128)(2,1)S(1)}, u32[]{:S(2)}, u32[]{:S(2)}) %collective-permute-start.34) | collective-permute-done | bytes 524320 | tf_op jit(solution)/shard_map/ppermute | solution.py:16
  (239 shorter events, 79.4 us)
Async XLA Ops:
  15.7 9.2 %collective-permute-start = (bf16[4,128,256]{2,1,0:T(8,128)(2,1)}, bf16[4,128,256]{2,1,0:T(8,128)(2,1)S(1)}, u32[]{:S(2)}, u32[]{:S(2)}) collective-permute-start(bf16[4,128,256]{2,1,0:T(8,128)(2,1)} %get-tuple-element.93), channel_id=1, source_target_pairs={{0,1},{1,0},{2,3},{3,2},{4,5},{5,4},{6,7},{7,6},{8,9},{9,8},{10,11... | collective-permute-start | bytes 786440 | tf_op jit(solution)/shard_map/ppermute | solution.py:16
  16.2 15.1 %collective-permute-start.1 = (bf16[4,128,256]{2,1,0:T(8,128)(2,1)}, bf16[4,128,256]{2,1,0:T(8,128)(2,1)S(1)}, u32[]{:S(2)}, u32[]{:S(2)}) collective-permute-start(bf16[4,128,256]{2,1,0:T(8,128)(2,1)} %get-tuple-element.94), channel_id=1, source_target_pairs={{0,2},{1,3},{2,0},{3,1},{4,6},{5,7},{6,4},{7,5},{8,10},{9,11},{10,... | collective-permute-start | bytes 786440 | tf_op jit(solution)/shard_map/ppermute | solution.py:16
  18.7 12.6 %collective-permute-start.2 = (bf16[4,128,256]{2,1,0:T(8,128)(2,1)}, bf16[4,128,256]{2,1,0:T(8,128)(2,1)S(1)}, u32[]{:S(2)}, u32[]{:S(2)}) collective-permute-start(bf16[4,128,256]{2,1,0:T(8,128)(2,1)} %get-tuple-element.95), channel_id=1, source_target_pairs={{0,3},{1,2},{2,1},{3,0},{4,7},{5,6},{6,5},{7,4},{8,11},{9,10},{10,... | collective-permute-start | bytes 786440 | tf_op jit(solution)/shard_map/ppermute | solution.py:16
  18.8 23.0 %collective-permute-start.6 = (bf16[512,512]{1,0:T(8,128)(2,1)}, bf16[512,512]{1,0:T(8,128)(2,1)}, u32[]{:S(2)}, u32[]{:S(2)}) collective-permute-start(bf16[512,512]{1,0:T(8,128)(2,1)} %copy-done.64), channel_id=1, source_target_pairs={{0,4},{4,0},{8,12},{12,8},{16,20},{20,16},{24,28},{28,24},{1,5},{5... | collective-permute-start | bytes 1572872 | tf_op jit(solution)/shard_map/ppermute | solution.py:16
  20.6 15.6 %collective-permute-start.10 = (bf16[512,128]{1,0:T(8,128)(2,1)S(1)}, bf16[512,128]{1,0:T(8,128)(2,1)S(1)}, u32[]{:S(2)}, u32[]{:S(2)}) collective-permute-start(bf16[512,128]{1,0:T(8,128)(2,1)S(1)} %get-tuple-element.113), channel_id=1, source_target_pairs={{0,16},{4,20},{8,24},{12,28},{16,0},{20,4},{24,8},{28,12},{1,17},{... | collective-permute-start | bytes 393224 | tf_op jit(solution)/shard_map/ppermute | solution.py:16
  24.9 28.1 %collective-permute-start.9 = (bf16[512,384]{1,0:T(8,128)(2,1)}, bf16[512,384]{1,0:T(8,128)(2,1)}, u32[]{:S(2)}, u32[]{:S(2)}) collective-permute-start(bf16[512,384]{1,0:T(8,128)(2,1)} %copy-done.32), channel_id=1, source_target_pairs={{0,4},{4,0},{8,12},{12,8},{16,20},{20,16},{24,28},{28,24},{1,5},{5... | collective-permute-start | bytes 1179656 | tf_op jit(solution)/shard_map/ppermute | solution.py:16
  37.1 14.0 %collective-permute-start.11 = (bf16[512,512]{1,0:T(8,128)(2,1)S(1)}, bf16[512,512]{1,0:T(8,128)(2,1)S(1)}, u32[]{:S(2)}, u32[]{:S(2)}) collective-permute-start(bf16[512,512]{1,0:T(8,128)(2,1)S(1)} %pack.5), channel_id=1, source_target_pairs={{0,8},{4,12},{8,0},{12,4},{16,24},{20,28},{24,16},{28,20},{1,9},{5... | collective-permute-start | bytes 1572872 | tf_op jit(solution)/shard_map/ppermute | solution.py:16
  39.1 29.4 %collective-permute-start.3 = (bf16[128,1024]{1,0:T(8,128)(2,1)}, bf16[128,1024]{1,0:T(8,128)(2,1)S(1)}, u32[]{:S(2)}, u32[]{:S(2)}) collective-permute-start(bf16[128,1024]{1,0:T(8,128)(2,1)} %copy-done.65), channel_id=1, source_target_pairs={{0,1},{1,0},{2,3},{3,2},{4,5},{5,4},{6,7},{7,6},{8,9},{9,8},{10,11... | collective-permute-start | bytes 786440 | tf_op jit(solution)/shard_map/ppermute | solution.py:16
  40.3 28.2 %collective-permute-start.5 = (bf16[128,1024]{1,0:T(8,128)(2,1)S(1)}, bf16[128,1024]{1,0:T(8,128)(2,1)S(1)}, u32[]{:S(2)}, u32[]{:S(2)}) collective-permute-start(bf16[128,1024]{1,0:T(8,128)(2,1)S(1)} %pair_product.1), channel_id=1, source_target_pairs={{0,2},{1,3},{2,0},{3,1},{4,6},{5,7},{6,4},{7,5},{8,10},{9,11},{10,... | collective-permute-start | bytes 786440 | tf_op jit(solution)/shard_map/ppermute | solution.py:16
  41.8 25.4 %collective-permute-start.7 = (bf16[512,512]{1,0:T(8,128)(2,1)}, bf16[512,512]{1,0:T(8,128)(2,1)S(1)}, u32[]{:S(2)}, u32[]{:S(2)}) collective-permute-start(bf16[512,512]{1,0:T(8,128)(2,1)} %collective-permute-done.6.refs_0_), channel_id=1, source_target_pairs={{0,1},{1,0},{2,3},{3,2},{4,5},{5,4},{6,7},{7,6},{8,9},{9,8},{10,11... | collective-permute-start | bytes 1572872 | tf_op jit(solution)/shard_map/ppermute | solution.py:16
  51.2 16.0 %collective-permute-start.12 = (bf16[512,640]{1,0:T(8,128)(2,1)S(1)}, bf16[512,640]{1,0:T(8,128)(2,1)S(1)}, u32[]{:S(2)}, u32[]{:S(2)}) collective-permute-start(bf16[512,640]{1,0:T(8,128)(2,1)S(1)} %pack.7), channel_id=1, source_target_pairs={{0,4},{4,0},{8,12},{12,8},{16,20},{20,16},{24,28},{28,24},{1,5},{5... | collective-permute-start | bytes 1966088 | tf_op jit(solution)/shard_map/ppermute | solution.py:16
  54.1 16.7 %collective-permute-start.13 = (bf16[512,1024]{1,0:T(8,128)(2,1)S(1)}, bf16[512,1024]{1,0:T(8,128)(2,1)S(1)}, u32[]{:S(2)}, u32[]{:S(2)}) collective-permute-start(bf16[512,1024]{1,0:T(8,128)(2,1)S(1)} %pack.6.refs_0_), channel_id=1, source_target_pairs={{0,1},{1,0},{2,3},{3,2},{4,5},{5,4},{6,7},{7,6},{8,9},{9,8},{10,11... | collective-permute-start | bytes 3145736 | tf_op jit(solution)/shard_map/ppermute | solution.py:16
  69.2 6.0 %collective-permute-start.8 = (bf16[64,1024]{1,0:T(8,128)(2,1)S(1)}, bf16[64,1024]{1,0:T(8,128)(2,1)S(1)}, u32[]{:S(2)}, u32[]{:S(2)}) collective-permute-start(bf16[64,1024]{1,0:T(8,128)(2,1)S(1)} %get-tuple-element.109), channel_id=1, source_target_pairs={{0,4},{4,0},{8,12},{12,8},{16,20},{20,16},{24,28},{28,24},{1,5},{5... | collective-permute-start | bytes 393224 | tf_op jit(solution)/shard_map/ppermute | solution.py:16
  80.6 4.9 %collective-permute-start.16 = (bf16[16,1024]{1,0:T(8,128)(2,1)S(1)}, bf16[16,1024]{1,0:T(8,128)(2,1)S(1)}, u32[]{:S(2)}, u32[]{:S(2)}) collective-permute-start(bf16[16,1024]{1,0:T(8,128)(2,1)S(1)} %get-tuple-element.122), channel_id=1, source_target_pairs={{0,16},{4,20},{8,24},{12,28},{16,0},{20,4},{24,8},{28,12},{1,17},{... | collective-permute-start | bytes 98312 | tf_op jit(solution)/shard_map/ppermute | solution.py:16
  85.5 4.9 %collective-permute-start.17 = (bf16[16,1024]{1,0:T(8,128)(2,1)S(1)}, bf16[16,1024]{1,0:T(8,128)(2,1)S(1)}, u32[]{:S(2)}, u32[]{:S(2)}) collective-permute-start(bf16[16,1024]{1,0:T(8,128)(2,1)S(1)} %top_forward.1.refs_0_), channel_id=1, source_target_pairs={{0,16},{4,20},{8,24},{12,28},{16,0},{20,4},{24,8},{28,12},{1,17},{... | collective-permute-start | bytes 98312 | tf_op jit(solution)/shard_map/ppermute | solution.py:16
  94.7 6.3 %collective-permute-start.19 = (bf16[64,1024]{1,0:T(8,128)(2,1)S(1)}, bf16[64,1024]{1,0:T(8,128)(2,1)S(1)}, u32[]{:S(2)}, u32[]{:S(2)}) collective-permute-start(bf16[64,1024]{1,0:T(8,128)(2,1)S(1)} %joined.3.refs_3_), channel_id=1, source_target_pairs={{0,4},{4,0},{8,12},{12,8},{16,20},{20,16},{24,28},{28,24},{1,5},{5... | collective-permute-start | bytes 393224 | tf_op jit(solution)/shard_map/ppermute | solution.py:16
  102.3 5.0 %collective-permute-start.20 = (bf16[64,1024]{1,0:T(8,128)(2,1)S(1)}, bf16[64,1024]{1,0:T(8,128)(2,1)S(1)}, u32[]{:S(2)}, u32[]{:S(2)}) collective-permute-start(bf16[64,1024]{1,0:T(8,128)(2,1)S(1)} %get-tuple-element.126), channel_id=1, source_target_pairs={{0,4},{4,0},{8,12},{12,8},{16,20},{20,16},{24,28},{28,24},{1,5},{5... | collective-permute-start | bytes 393224 | tf_op jit(solution)/shard_map/ppermute | solution.py:16
  103.8 5.2 %collective-permute-start.28 = (bf16[32,1024]{1,0:T(8,128)(2,1)S(1)}, bf16[32,1024]{1,0:T(8,128)(2,1)S(1)}, u32[]{:S(2)}, u32[]{:S(2)}) collective-permute-start(bf16[32,1024]{1,0:T(8,128)(2,1)S(1)} %get-tuple-element.150.refs_1_.refs_3_.refs_6_), channel_id=1, source_target_pairs={{0,16},{4,20},{8,24},{12,28},{16,0},{20,4},{24,8},{28,12},{1,17},{... | collective-permute-start | bytes 196616 | tf_op jit(solution)/shard_map/ppermute | solution.py:16
  109.0 7.5 %collective-permute-start.29 = (bf16[128,1024]{1,0:T(8,128)(2,1)S(1)}, bf16[128,1024]{1,0:T(8,128)(2,1)S(1)}, u32[]{:S(2)}, u32[]{:S(2)}) collective-permute-start(bf16[128,1024]{1,0:T(8,128)(2,1)S(1)} %stack_rows.2), channel_id=1, source_target_pairs={{0,8},{4,12},{8,0},{12,4},{16,24},{20,28},{24,16},{28,20},{1,9},{5... | collective-permute-start | bytes 786440 | tf_op jit(solution)/shard_map/ppermute | solution.py:16
  111.0 5.5 %collective-permute-start.21 = (bf16[32,1024]{1,0:T(8,128)(2,1)S(1)}, bf16[32,1024]{1,0:T(8,128)(2,1)S(1)}, u32[]{:S(2)}, u32[]{:S(2)}) collective-permute-start(bf16[32,1024]{1,0:T(8,128)(2,1)S(1)} %get-tuple-element.128), channel_id=1, source_target_pairs={{0,8},{4,12},{8,0},{12,4},{16,24},{20,28},{24,16},{28,20},{1,9},{5... | collective-permute-start | bytes 196616 | tf_op jit(solution)/shard_map/ppermute | solution.py:16
  117.5 48.0 %collective-permute-start.30 = (bf16[384,1024]{1,0:T(8,128)(2,1)}, bf16[384,1024]{1,0:T(8,128)(2,1)S(1)}, u32[]{:S(2)}, u32[]{:S(2)}) collective-permute-start(bf16[384,1024]{1,0:T(8,128)(2,1)} %stack_rows.3), channel_id=1, source_target_pairs={{0,4},{4,0},{8,12},{12,8},{16,20},{20,16},{24,28},{28,24},{1,5},{5... | collective-permute-start | bytes 2359304 | tf_op jit(solution)/shard_map/ppermute | solution.py:16
  118.5 4.8 %collective-permute-start.22 = (bf16[16,1024]{1,0:T(8,128)(2,1)S(1)}, bf16[16,1024]{1,0:T(8,128)(2,1)S(1)}, u32[]{:S(2)}, u32[]{:S(2)}) collective-permute-start(bf16[16,1024]{1,0:T(8,128)(2,1)S(1)} %get-tuple-element.130), channel_id=1, source_target_pairs={{0,16},{4,20},{8,24},{12,28},{16,0},{20,4},{24,8},{28,12},{1,17},{... | collective-permute-start | bytes 98312 | tf_op jit(solution)/shard_map/ppermute | solution.py:16
  123.5 4.9 %collective-permute-start.23 = (bf16[16,1024]{1,0:T(8,128)(2,1)S(1)}, bf16[16,1024]{1,0:T(8,128)(2,1)S(1)}, u32[]{:S(2)}, u32[]{:S(2)}) collective-permute-start(bf16[16,1024]{1,0:T(8,128)(2,1)S(1)} %get-tuple-element.132), channel_id=1, source_target_pairs={{0,16},{4,20},{8,24},{12,28},{16,0},{20,4},{24,8},{28,12},{1,17},{... | collective-permute-start | bytes 98312 | tf_op jit(solution)/shard_map/ppermute | solution.py:16
  134.8 5.0 %collective-permute-start.25 = (bf16[64,1024]{1,0:T(8,128)(2,1)S(1)}, bf16[64,1024]{1,0:T(8,128)(2,1)S(1)}, u32[]{:S(2)}, u32[]{:S(2)}) collective-permute-start(bf16[64,1024]{1,0:T(8,128)(2,1)S(1)} %get-tuple-element.136), channel_id=1, source_target_pairs={{0,4},{4,0},{8,12},{12,8},{16,20},{20,16},{24,28},{28,24},{1,5},{5... | collective-permute-start | bytes 393224 | tf_op jit(solution)/shard_map/ppermute | solution.py:16
  142.6 15.9 %collective-permute-start.26 = (bf16[128,1024]{1,0:T(8,128)(2,1)}, bf16[128,1024]{1,0:T(8,128)(2,1)}, u32[]{:S(2)}, u32[]{:S(2)}) collective-permute-start(bf16[128,1024]{1,0:T(8,128)(2,1)} %get-tuple-element.138), channel_id=1, source_target_pairs={{0,1},{1,0},{2,3},{3,2},{4,5},{5,4},{6,7},{7,6},{8,9},{9,8},{10,11... | collective-permute-start | bytes 786440 | tf_op jit(solution)/shard_map/ppermute | solution.py:16
  142.6 21.7 %collective-permute-start.27 = (bf16[128,1024]{1,0:T(8,128)(2,1)}, bf16[128,1024]{1,0:T(8,128)(2,1)}, u32[]{:S(2)}, u32[]{:S(2)}) collective-permute-start(bf16[128,1024]{1,0:T(8,128)(2,1)} %get-tuple-element.139), channel_id=1, source_target_pairs={{0,2},{1,3},{2,0},{3,1},{4,6},{5,7},{6,4},{7,5},{8,10},{9,11},{10,... | collective-permute-start | bytes 786440 | tf_op jit(solution)/shard_map/ppermute | solution.py:16
  144.1 4.8 %collective-permute-start.35 = (bf16[32,512]{1,0:T(8,128)(2,1)S(1)}, bf16[32,512]{1,0:T(8,128)(2,1)S(1)}, u32[]{:S(2)}, u32[]{:S(2)}) collective-permute-start(bf16[32,512]{1,0:T(8,128)(2,1)S(1)} %get-tuple-element.162), channel_id=1, source_target_pairs={{0,16},{4,20},{8,24},{12,28},{16,0},{20,4},{24,8},{28,12},{1,17},{... | collective-permute-start | bytes 98312 | tf_op jit(solution)/shard_map/ppermute | solution.py:16
  150.1 4.9 %collective-permute-start.36 = (bf16[64,768]{1,0:T(8,128)(2,1)}, bf16[64,768]{1,0:T(8,128)(2,1)}, u32[]{:S(2)}, u32[]{:S(2)}) collective-permute-start(bf16[64,768]{1,0:T(8,128)(2,1)} %get-tuple-element.165), channel_id=1, source_target_pairs={{0,8},{4,12},{8,0},{12,4},{16,24},{20,28},{24,16},{28,20},{1,9},{5... | collective-permute-start | bytes 294920 | tf_op jit(solution)/shard_map/ppermute | solution.py:16
  153.5 13.4 %collective-permute-start.31 = (bf16[128,512]{1,0:T(8,128)(2,1)}, bf16[128,512]{1,0:T(8,128)(2,1)}, u32[]{:S(2)}, u32[]{:S(2)}) collective-permute-start(bf16[128,512]{1,0:T(8,128)(2,1)} %get-tuple-element.151), channel_id=1, source_target_pairs={{0,4},{4,0},{8,12},{12,8},{16,20},{20,16},{24,28},{28,24},{1,5},{5... | collective-permute-start | bytes 393224 | tf_op jit(solution)/shard_map/ppermute | solution.py:16
  157.6 7.9 %collective-permute-start.37 = (bf16[128,384]{1,0:T(8,128)(2,1)S(1)}, bf16[128,384]{1,0:T(8,128)(2,1)S(1)}, u32[]{:S(2)}, u32[]{:S(2)}) collective-permute-start(bf16[128,384]{1,0:T(8,128)(2,1)S(1)} %get-tuple-element.169), channel_id=1, source_target_pairs={{0,4},{4,0},{8,12},{12,8},{16,20},{20,16},{24,28},{28,24},{1,5},{5... | collective-permute-start | bytes 294920 | tf_op jit(solution)/shard_map/ppermute | solution.py:16
  169.7 14.8 %collective-permute-start.39 = (bf16[2,256,512]{2,1,0:T(8,128)(2,1)S(1)}, bf16[2,256,512]{2,1,0:T(8,128)(2,1)S(1)}, u32[]{:S(2)}, u32[]{:S(2)}) collective-permute-start(bf16[2,256,512]{2,1,0:T(8,128)(2,1)S(1)} %far_sum.3), channel_id=1, source_target_pairs={{0,2},{1,3},{2,0},{3,1},{4,6},{5,7},{6,4},{7,5},{8,10},{9,11},{10,... | collective-permute-start | bytes 1572872 | tf_op jit(solution)/shard_map/ppermute | solution.py:16
  171.5 23.4 %collective-permute-start.34 = (bf16[2,256,512]{2,1,0:T(8,128)(2,1)S(1)}, bf16[2,256,512]{2,1,0:T(8,128)(2,1)S(1)}, u32[]{:S(2)}, u32[]{:S(2)}) collective-permute-start(bf16[2,256,512]{2,1,0:T(8,128)(2,1)S(1)} %far_sum.2), channel_id=1, source_target_pairs={{0,2},{1,3},{2,0},{3,1},{4,6},{5,7},{6,4},{7,5},{8,10},{9,11},{10,... | collective-permute-start | bytes 1572872 | tf_op jit(solution)/shard_map/ppermute | solution.py:16
  (74 other events, 433.3 us)

commit v4 on v3

v4 whole, which is shorter than its diff:
```python
import functools

import jax
import jax.numpy as jnp
from jax import lax
from jax.experimental import pallas as pl
from jax.experimental.pallas import tpu as pltpu
from jax.sharding import PartitionSpec as P

EPSILON = 1e-06
CHILDREN = 4
MIB = 1024 * 1024


def partner(value, axis, offset):
    return lax.ppermute(value, axis, [(i, i ^ offset) for i in range(lax.axis_size(axis))])


def rms_factor(values):
    return lax.rsqrt(jnp.mean(values * values, axis=-1, keepdims=True) + EPSILON)


def norm_back(gradient, normed, factor):
    return factor * (gradient - normed * jnp.mean(gradient * normed, axis=-1, keepdims=True))


def matmul(left_arr, right_arr):
    return jnp.dot(left_arr, right_arr, preferred_element_type=jnp.float32)


def matmul_t(left_arr, right_arr):
    return lax.dot_general(
        left_arr, right_arr, (((1,), (1,)), ((), ())), preferred_element_type=jnp.float32
    )


def inner_t(left_arr, right_arr):
    return lax.dot_general(
        left_arr, right_arr, (((0,), (0,)), ((), ())), preferred_element_type=jnp.float32
    )


def bf16(value):
    return value.astype(jnp.bfloat16)


def f32(value):
    return value.astype(jnp.float32)


def whole_block():
    return pl.BlockSpec(memory_space=pltpu.VMEM)


def smem_block():
    return pl.BlockSpec(memory_space=pltpu.SMEM)


def bit_of(value, level):
    return jnp.bitwise_and(jnp.right_shift(value, level), 1)


def place_kernel(slots, depth, ids_ref, map_ref, regions_ref, cotangent_ref, *rest):
    outs, cotangent_out, wide = rest[:CHILDREN], rest[CHILDREN], rest[CHILDREN + 1]
    rows = regions_ref.shape[0] // slots
    parts = wide.shape[0]
    for part in range(parts):
        wide[part] = regions_ref[:, part * 128 : (part + 1) * 128].astype(jnp.float32)
    flip = 0
    for level in range(depth):
        flip = flip + bit_of(ids_ref[0], level) * (rows >> (level + 1))
    row = lax.broadcasted_iota(jnp.int32, (rows, rows), 0)
    col = lax.broadcasted_iota(jnp.int32, (rows, rows), 1)
    select = bf16(jnp.bitwise_xor(row, flip) == col)
    left = cotangent_ref[...]
    picked = 0.0
    for _ in range(3):
        top = bf16(left)
        left = left - f32(top)
        picked = picked + matmul(select, top)
    cotangent_out[...] = picked
    for offset in range(CHILDREN):
        node = jnp.bitwise_xor(ids_ref[1], offset)
        for child in range(CHILDREN):
            region = map_ref[node * CHILDREN + child]
            for part in range(parts):
                values = bf16(wide[part, pl.ds(region, rows, stride=slots), :])
                outs[offset][child, :, part * 128 : (part + 1) * 128] = bf16(
                    matmul(select, values)
                )


def place(regions, leaf_map, cotangent, ids, depth):
    rows, slots, feats = regions.shape
    flat = regions.reshape(rows * slots, feats)
    return pl.pallas_call(
        functools.partial(place_kernel, slots, depth),
        out_shape=[jax.ShapeDtypeStruct((CHILDREN, rows, feats), jnp.bfloat16)] * CHILDREN
        + [jax.ShapeDtypeStruct(cotangent.shape, cotangent.dtype)],
        in_specs=[smem_block(), smem_block(), whole_block(), whole_block()],
        out_specs=[whole_block()] * (CHILDREN + 1),
        scratch_shapes=[pltpu.VMEM((feats // 128, rows * slots, 128), jnp.float32)],
        compiler_params=pltpu.CompilerParams(vmem_limit_bytes=7 * MIB),
        name="place",
    )(ids, leaf_map, flat, cotangent)


def leaf_forward_kernel(count, *refs):
    placed, leaf_w, mid_w = refs[:count], refs[count], refs[count + 1]
    msgs, terms = refs[count + 2 : 2 * count + 2], refs[2 * count + 2 :]
    rows = placed[0].shape[1]
    product = None
    for child in range(CHILDREN):
        values = jnp.concatenate([ref[child] for ref in placed], axis=0)
        factor = 1.0 + matmul(values, leaf_w[child])
        product = factor if product is None else product * factor
    message = bf16(product * rms_factor(product))
    out = bf16(matmul(message, mid_w[...]))
    for i in range(count):
        msgs[i][...] = message[i * rows : (i + 1) * rows]
        terms[i][...] = out[i * rows : (i + 1) * rows]


def leaf_forward(placed, leaf_w, mid_w):
    count = len(placed)
    rows = placed[0].shape[1]
    width = mid_w.shape[0]
    return pl.pallas_call(
        functools.partial(leaf_forward_kernel, count),
        out_shape=[jax.ShapeDtypeStruct((rows, width), jnp.bfloat16)] * (2 * count),
        in_specs=[whole_block()] * (count + 2),
        out_specs=[whole_block()] * (2 * count),
        compiler_params=pltpu.CompilerParams(vmem_limit_bytes=14 * MIB),
        name="leaf_forward",
    )(*placed, leaf_w, mid_w)


def leaf_cotangents(placed, grads, leaf_w, mid_w):
    factors = [
        1.0 + matmul(jnp.concatenate([ref[child] for ref in placed], axis=0), leaf_w[child])
        for child in range(CHILDREN)
    ]
    low = factors[0] * factors[1]
    high = factors[2] * factors[3]
    product = low * high
    scale = rms_factor(product)
    back = matmul_t(jnp.concatenate([ref[...] for ref in grads], axis=0), mid_w[...])
    node = norm_back(back, product * scale, scale)
    high, low = node * high, node * low
    return [
        bf16(high * factors[1]),
        bf16(high * factors[0]),
        bf16(low * factors[3]),
        bf16(low * factors[2]),
    ]


def leaf_first_kernel(*refs):
    placed, grads, leaf_w, mid_w, out = refs[0:2], refs[2:4], refs[4], refs[5], refs[6]
    for child, value in enumerate(leaf_cotangents(placed, grads, leaf_w, mid_w)):
        out[child] = value


def leaf_first(placed, grads, leaf_w, mid_w):
    rows = placed[0].shape[1]
    return pl.pallas_call(
        leaf_first_kernel,
        out_shape=jax.ShapeDtypeStruct((CHILDREN, 2 * rows, mid_w.shape[0]), jnp.bfloat16),
        in_specs=[whole_block()] * 6,
        out_specs=whole_block(),
        compiler_params=pltpu.CompilerParams(vmem_limit_bytes=18 * MIB),
        name="leaf_first",
    )(*placed, *grads, leaf_w, mid_w)


def leaf_backward_kernel(*refs):
    placed, msgs, grads = refs[0:4], refs[4:8], refs[8:12]
    leaf_w, mid_w, first, leaf_out, mid_out = refs[12:17]
    all_grads = jnp.concatenate([ref[...] for ref in grads], axis=0)
    all_msgs = jnp.concatenate([ref[...] for ref in msgs], axis=0)
    mid_out[...] = bf16(inner_t(all_msgs, all_grads))
    second = leaf_cotangents(placed[2:], grads[2:], leaf_w, mid_w)
    for child in range(CHILDREN):
        values = jnp.concatenate([ref[child] for ref in placed], axis=0)
        cot = jnp.concatenate([first[child], second[child]], axis=0)
        leaf_out[child] = bf16(inner_t(values, cot))


def leaf_backward(placed, msgs, grads, leaf_w, mid_w, first):
    return pl.pallas_call(
        leaf_backward_kernel,
        out_shape=[
            jax.ShapeDtypeStruct(leaf_w.shape, jnp.bfloat16),
            jax.ShapeDtypeStruct(mid_w.shape, jnp.bfloat16),
        ],
        in_specs=[whole_block()] * 15,
        out_specs=[whole_block()] * 2,
        compiler_params=pltpu.CompilerParams(vmem_limit_bytes=30 * MIB),
        name="leaf_backward",
    )(*placed, *msgs, *grads, leaf_w, mid_w, first)


def fused(body, name, *args, limit=8, ids=None, plain=False):
    if plain or any(arg.shape[-2] % 16 or arg.shape[-1] % 128 for arg in args):
        return body(*args) if ids is None else body(ids, *args)
    count = len(args)
    if ids is None:
        shapes = jax.eval_shape(body, *args)
    else:
        shapes = jax.eval_shape(body, ids, *args)
        args = (ids, *args)

    def kernel(*refs):
        outs = refs[len(args) :]
        values = [ref[...] for ref in refs[len(args) - count : len(args)]]
        results = body(*values) if ids is None else body(refs[0], *values)
        for ref, result in zip(outs, results):
            ref[...] = result

    return pl.pallas_call(
        kernel,
        out_shape=shapes,
        in_specs=[smem_block()] * (len(args) - count) + [whole_block()] * count,
        out_specs=[whole_block()] * len(shapes),
        compiler_params=pltpu.CompilerParams(vmem_limit_bytes=limit * MIB),
        name=name,
    )(*args)


def join(pieces):
    if pieces[0].shape[0] % 16 == 0:
        return jnp.concatenate(pieces, axis=0)
    wide = lax.optimization_barrier(tuple(f32(piece) for piece in pieces))
    return bf16(lax.optimization_barrier(jnp.concatenate(wide, axis=0)))


def pack(pieces):
    arrays = []
    for array, _, _ in pieces:
        if not any(array is known for known in arrays):
            arrays.append(array)
    spots = [next(i for i, known in enumerate(arrays) if known is piece[0]) for piece in pieces]

    def body(*values):
        parts = [values[i][:, at : at + span] for i, (_, at, span) in zip(spots, pieces)]
        return (jnp.concatenate(parts, axis=1),)

    if any(piece[2] % 128 for piece in pieces):
        return body(*arrays)[0]
    return fused(body, "pack", *arrays, limit=6)[0]


def cut_kernel(depth, ids_ref, maps_ref, *refs):
    outs, split = refs[:-1], refs[-1]
    split[...] = jnp.swapaxes(maps_ref[...], 0, 1)
    width = maps_ref.shape[0]
    half = width // 2
    rows = pl.ds(pl.multiple_of(bit_of(ids_ref[1], 0) * half, half), half)
    for level in range(depth):
        span = width >> (level + 1)
        cols = pl.ds(width - 2 * span, span)
        side = bit_of(ids_ref[0], level)
        outs[3 * level][...] = split[side, :, cols]
        outs[3 * level + 1][...] = split[side, rows, cols]
        outs[3 * level + 2][...] = split[1 - side, rows, cols]
    span = width >> depth
    for side in range(2):
        outs[3 * depth + side][...] = split[side, :, width - span :]


def cut_maps(maps, ids, depth):
    width = maps.shape[0]
    half = width // 2
    spans = [width >> (level + 1) for level in range(depth)]
    if spans[-1] % 128 == 0:
        shapes = []
        for span in spans:
            shapes += [(width, span), (half, span), (half, span)]
        shapes += [(width, spans[-1])] * 2
        outs = pl.pallas_call(
            functools.partial(cut_kernel, depth),
            out_shape=[jax.ShapeDtypeStruct(shape, maps.dtype) for shape in shapes],
            in_specs=[smem_block(), whole_block()],
            out_specs=[whole_block()] * len(shapes),
            scratch_shapes=[pltpu.VMEM((2, width, width), maps.dtype)],
            compiler_params=pltpu.CompilerParams(vmem_limit_bytes=18 * MIB),
            name="cut_maps",
        )(ids, maps)
    else:
        maps = jnp.transpose(maps, (1, 0, 2))
        outs = []
        core = bit_of(ids[1], 0)
        for level, span in enumerate(spans):
            side = bit_of(ids[0], level)
            first = width - 2 * span
            outs.append(lax.dynamic_slice(maps, (side, 0, first), (1, width, span))[0])
            for which in (side, 1 - side):
                outs.append(lax.dynamic_slice(maps, (which, core * half, first), (1, half, span))[0])
        outs += [maps[0, :, width - spans[-1] :], maps[1, :, width - spans[-1] :]]
    return [outs[3 * i : 3 * i + 3] for i in range(depth)], outs[3 * depth :]


def assemble_kernel(spots, count, ids_ref, own_ref, *refs):
    out_ref = refs[-1]
    width, span = own_ref.shape
    half = width // 2
    block = jnp.bitwise_and(ids_ref[0], out_ref.shape[1] // span - 1)
    own_core = bit_of(ids_ref[1], 0)
    out_ref[:, pl.ds(pl.multiple_of(block * span, span), span)] = own_ref[...]
    for offset, index, at in spots:
        col = jnp.bitwise_xor(block, offset) * span
        for ref, core in ((refs[index], own_core), (refs[count + index], 1 - own_core)):
            out_ref[
                pl.ds(pl.multiple_of(core * half, half), half),
                pl.ds(pl.multiple_of(col, span), span),
            ] = ref[:, at : at + span]


def assemble(own, pieces, ids):
    width, span = own.shape
    count = len(pieces) + 1
    if span % 128 == 0:
        mine, other, spots = [], [], []
        for offset, (near_half, far_half, at) in pieces.items():
            known = [i for i, array in enumerate(mine) if array is near_half]
            if not known:
                mine.append(near_half)
                other.append(far_half)
                known = [len(mine) - 1]
            spots.append((offset, known[0], at))
        return pl.pallas_call(
            functools.partial(assemble_kernel, spots, len(mine)),
            out_shape=jax.ShapeDtypeStruct((width, span * count), own.dtype),
            in_specs=[smem_block()] + [whole_block()] * (2 * len(mine) + 1),
            out_specs=whole_block(),
            compiler_params=pltpu.CompilerParams(vmem_limit_bytes=8 * MIB),
            name="assemble",
        )(ids, own, *mine, *other)
    block = jnp.bitwise_and(ids[0], count - 1)
    core = bit_of(ids[1], 0)
    out = jnp.zeros((width, span * count), own.dtype)
    out = lax.dynamic_update_slice(out, own, (0, block * span))
    for offset, (near_half, far_half, at) in pieces.items():
        col = (block ^ offset) * span
        for array, which in ((near_half, core), (far_half, 1 - core)):
            part = array[:, at : at + span]
            out = lax.dynamic_update_slice(out, part, (which * (width // 2), col))
    return out


def after(value, *others):
    return lax.optimization_barrier((value, *others))[0]


class MapGather:
    def __init__(self, blocks, ids):
        self.blocks, self.ids = blocks, ids
        self.depth = len(blocks)
        self.spans = [block[0].shape[1] for block in blocks]
        self.held = [{0: (block[1], 0)} for block in blocks]
        self.first = partner(blocks[0][2], "sub", 1)
        self.early = [self.send([(level, 0) for level in range(1, self.depth)], 0)]

    def send(self, picks, stage, extra=None, gate=None):
        pieces = [(*self.held[level][offset], self.spans[level]) for level, offset in picks]
        picks = list(picks)
        if extra is not None:
            pieces.append((self.blocks[extra][2], 0, self.spans[extra]))
            picks.append((extra, 0))
        if gate is not None:
            pieces[-1] = (after(pieces[-1][0], gate), *pieces[-1][1:])
        value = pieces[0][0] if len(pieces) == 1 else pack(pieces)
        self.packed = value
        got = partner(value, "sub", 1 << stage)
        at = 0
        for level, offset in picks:
            self.held[level][offset ^ (1 << stage)] = (got, at)
            at += self.spans[level]
        return got

    def stage(self, stage, gate=None):
        picks = [
            (level, offset)
            for level in range(stage + 1, self.depth)
            for offset in self.held[level]
            if offset % (2 << stage) == 0
        ]
        self.early.append(self.send(picks, stage, stage, gate))

    def last(self, gate):
        picks = [
            (level, offset)
            for level in range(1, self.depth)
            for offset in self.held[level]
            if offset % 2 == 0 and offset > 0
        ]
        self.late = self.send(picks, 0, None, gate)

    def weight(self, level, exchanged):
        pieces = {}
        if level == 0:
            pieces[1] = (self.first, exchanged[0], 0)
        else:
            for offset, (array, at) in self.held[level].items():
                if offset == 0:
                    continue
                if array is self.late:
                    pieces[offset] = (array, exchanged[2], at)
                    continue
                pieces[offset] = (self.packed_early, exchanged[1], at + self.early_at(array))
        return assemble(self.blocks[level][0], pieces, self.ids)

    def early_at(self, array):
        at = 0
        for known in self.early:
            if known is array:
                return at
            at += known.shape[1]

    def pack_early(self, gate):
        pieces = [(array, 0, array.shape[1]) for array in self.early]
        pieces[0] = (after(self.early[0], gate), *pieces[0][1:])
        self.packed_early = pack(pieces)
        return self.packed_early


class View:
    def __init__(self, array, rows=None, cols=None):
        self.array = array
        self.rows = (0, array.shape[0]) if rows is None else rows
        self.cols = (0, array.shape[1]) if cols is None else cols
        self.shape = (self.rows[1] - self.rows[0], self.cols[1] - self.cols[0])

    def value(self):
        return self.array[slice(*self.rows), slice(*self.cols)]

    def part(self, first, last):
        return View(self.array, (self.rows[0] + first, self.rows[0] + last), self.cols)

    def gated(self, *gates):
        return View(after(self.array, *gates), self.rows, self.cols)

    def aligned(self):
        edges = (*self.rows, *self.cols)
        return all(edge % unit == 0 for edge, unit in zip(edges, (16, 16, 128, 128)))


def spots_of(views):
    arrays, spots = [], []
    for view in views:
        known = [i for i, array in enumerate(arrays) if array is view.array]
        if not known:
            arrays.append(view.array)
            known = [len(arrays) - 1]
        spots.append((known[0], view.rows, view.cols))
    return arrays, spots


def join_all(pieces):
    if all(piece.shape[0] % 16 == 0 for piece in pieces):
        return jnp.concatenate(pieces, axis=0)
    wide = lax.optimization_barrier(tuple(f32(piece) for piece in pieces))
    return bf16(lax.optimization_barrier(jnp.concatenate(wide, axis=0)))


def step(body, name, args, stacks=(), halves=(), level=0, far=None, ids=None, limit=8):
    groups = [list(stacks)] + [list(group) for group in halves] + [list(far or ())]
    views = [view for group in groups for view in group]
    arrays = list(args)
    for view in views:
        if not any(array is view.array for array in arrays):
            arrays.append(view.array)

    def cut(values, group):
        parts = []
        for view in group:
            index = next(i for i, array in enumerate(arrays) if array is view.array)
            parts.append(values[index][slice(*view.rows), slice(*view.cols)])
        return join_all(parts)

    def whole(ids, *values):
        results = list(body(*values[: len(args)]))
        if stacks:
            results.append(cut(values, groups[0]))
        if halves:
            own = bit_of(ids[0], level) == 1
            sends = []
            for group in groups[1:-1]:
                full = cut(values, group)
                half = full.shape[1] // 2
                low, high = full[:, :half], full[:, half:]
                results.append(jnp.where(own, high, low))
                sends.append(jnp.where(own, low, high))
            results.append(jnp.concatenate(sends, axis=1))
        if far:
            full = cut(values, groups[-1])
            half = full.shape[1] // 2
            results.append(jnp.where(bit_of(ids[1], 1) == 1, full[:, :half], full[:, half:]))
        return results

    plain = not all(view.aligned() for view in views)
    return fused(whole, name, *arrays, limit=limit, ids=ids, plain=plain)


def near_inputs_kernel(spots, ids_ref, far_ref, *refs):
    out_ref = refs[-1]
    quarter = out_ref.shape[1]
    other = 1 - bit_of(ids_ref[1], 0)
    lanes = pl.ds(pl.multiple_of((bit_of(ids_ref[1], 1) * 2 + other) * quarter, quarter), quarter)
    at = 0
    for index, (first, last), _ in spots:
        out_ref[at : at + last - first] = refs[index][first:last, lanes]
        at += last - first
    out_ref[at:] = far_ref[:, pl.ds(pl.multiple_of(other * quarter, quarter), quarter)]


def near_inputs(views, got, ids):
    quarter = views[0].shape[1] // 4
    if not all(view.aligned() for view in views):
        full = join_all([view.value() for view in views])
        other = 1 - bit_of(ids[1], 0)
        where = (bit_of(ids[1], 1) * 2 + other) * quarter
        own = lax.dynamic_slice_in_dim(full, where, quarter, 1)
        return jnp.concatenate(
            [own, lax.dynamic_slice_in_dim(got, other * quarter, quarter, 1)], axis=0
        )
    arrays, spots = spots_of(views)
    return pl.pallas_call(
        functools.partial(near_inputs_kernel, spots),
        out_shape=jax.ShapeDtypeStruct((2 * got.shape[0], quarter), jnp.bfloat16),
        in_specs=[smem_block()] + [whole_block()] * (len(arrays) + 1),
        out_specs=whole_block(),
        compiler_params=pltpu.CompilerParams(vmem_limit_bytes=8 * MIB),
        name="near_inputs",
    )(ids, got, *arrays)


def side_by_side_kernel(groups, *refs):
    out_ref = refs[-1]
    col = 0
    for spots in groups:
        at = 0
        for index, rows, cols in spots:
            span = cols[1] - cols[0]
            count = rows[1] - rows[0]
            out_ref[at : at + count, col : col + span] = refs[index][slice(*rows), slice(*cols)]
            at += count
        col += span


def side_by_side(groups):
    views = [view for group in groups for view in group]
    if not all(view.aligned() for view in views):
        return jnp.concatenate(
            [join_all([view.value() for view in group]) for group in groups], axis=1
        )
    arrays, spots = spots_of(views)
    by_group = [[spots.pop(0) for _ in group] for group in groups]
    shape = (
        sum(view.shape[0] for view in groups[0]),
        sum(group[0].shape[1] for group in groups),
    )
    return pl.pallas_call(
        functools.partial(side_by_side_kernel, by_group),
        out_shape=jax.ShapeDtypeStruct(shape, jnp.bfloat16),
        in_specs=[whole_block()] * len(arrays),
        out_specs=whole_block(),
        compiler_params=pltpu.CompilerParams(vmem_limit_bytes=6 * MIB),
        name="side_by_side",
    )(*arrays)


def upper_grads_kernel(spots, spans, rows, ids_ref, far_ref, near_ref, *refs):
    grads, inputs, out_ref, both = refs[:4], refs[4:-2], refs[-2], refs[-1]
    quarter = out_ref.shape[0]
    core, far = bit_of(ids_ref[1], 0), bit_of(ids_ref[1], 1)
    lanes = pl.ds(pl.multiple_of((far * 2 + core) * quarter, quarter), quarter)
    far_lanes = pl.ds(pl.multiple_of(core * quarter, quarter), quarter)
    total = far_ref.shape[0]
    col = 0
    for level, span in enumerate(spans):
        for turn in range(2):
            here, at = spots[level][turn]
            pieces = [inputs[i][slice(*edges), lanes] for i, edges, _ in here]
            pieces.append(far_ref[at : at + rows, far_lanes])
            pieces.append(near_ref[at : at + rows])
            pieces.append(near_ref[total + at : total + at + rows])
            grad = jnp.concatenate(
                [ref[turn * rows : (turn + 1) * rows, col : col + span] for ref in grads], axis=0
            )
            value = bf16(inner_t(jnp.concatenate(pieces, axis=0), grad))
            side = turn
            if level < len(spans) - 1:
                side = jnp.bitwise_xor(bit_of(ids_ref[0], level), turn)
            both[side, :, col : col + span] = value
        col += span
    out_ref[...] = jnp.swapaxes(both[...], 0, 1)


def upper_grads(entries, far_got, near_got, grads, ids):
    depth = len(entries) - 1
    width = entries[0][0][0].shape[1]
    rows = sum(view.shape[0] for view in entries[0][0])
    spans = [width >> (level + 1) for level in range(depth)] + [width >> depth]
    views = [view for entry in entries for turn in entry for view in turn]
    starts, at = [], 0
    for level in range(depth + 1):
        starts.append([at, at + rows if level < depth else at])
        at += 2 * rows
    if all(view.aligned() for view in views) and spans[-1] % 128 == 0:
        arrays, flat = spots_of(views)
        spots = [
            [([flat.pop(0) for _ in entry[turn]], starts[level][turn]) for turn in range(2)]
            for level, entry in enumerate(entries)
        ]
        return pl.pallas_call(
            functools.partial(upper_grads_kernel, spots, spans, rows),
            out_shape=jax.ShapeDtypeStruct((width // 4, 2, width), jnp.bfloat16),
            in_specs=[smem_block()] + [whole_block()] * (len(arrays) + 6),
            out_specs=whole_block(),
            scratch_shapes=[pltpu.VMEM((2, width // 4, width), jnp.bfloat16)],
            compiler_params=pltpu.CompilerParams(vmem_limit_bytes=16 * MIB),
            name="upper_grads",
        )(ids, far_got, near_got, *grads, *arrays)
    quarter = width // 4
    core, far = bit_of(ids[1], 0), bit_of(ids[1], 1)
    total = far_got.shape[0]
    parts, col = [], 0
    for level, span in enumerate(spans):
        both = []
        for turn in range(2):
            at = starts[level][turn]
            own = join_all([view.value() for view in entries[level][turn]])
            pieces = [
                lax.dynamic_slice_in_dim(own, (far * 2 + core) * quarter, quarter, 1),
                lax.dynamic_slice_in_dim(far_got[at : at + rows], core * quarter, quarter, 1),
                near_got[at : at + rows],
                near_got[total + at : total + at + rows],
            ]
            grad = [part[turn * rows : (turn + 1) * rows, col : col + span] for part in grads]
            both.append(bf16(inner_t(jnp.concatenate(pieces), jnp.concatenate(grad))))
        if level < depth:
            swap = bit_of(ids[0], level) == 1
            both = [jnp.where(swap, both[1 - i], both[i]) for i in range(2)]
        parts.append(jnp.stack(both, axis=1))
        col += span
    return jnp.concatenate(parts, axis=2)


def mid_forward(term, near, far, weight):
    product = (1.0 + f32(term)) * (1.0 + f32(near)) * f32(far)
    return up_product(bf16(product * rms_factor(product)), weight)


def up_product(message, weight):
    up = matmul(message, weight)
    keep = up.shape[0] // 2
    return message, up[:keep], bf16(up[keep:])


def up_forward(own_up, other_up, weight):
    joined = (1.0 + own_up) * (1.0 + f32(other_up))
    return up_product(bf16(joined * rms_factor(joined)), weight)


def top_forward(own_up, other_up):
    joined = (1.0 + own_up) * (1.0 + f32(other_up))
    return (bf16(joined * rms_factor(joined)),)


def head_body(cotangent, left, right, low, high):
    root = join([low, high])
    value = matmul(root, left)
    gating = jax.nn.sigmoid(matmul(root, right))
    grad_value = bf16(cotangent * gating)
    grad_gate = bf16(cotangent * value * gating * (1.0 - gating))
    back = matmul_t(grad_value, left) + matmul_t(grad_gate, right)
    half = root.shape[0] // 2
    return root, grad_value, grad_gate, back[:half], bf16(back[half:])


def joined(low, high):
    return (join([low, high]),)


def partial_sum(own, got):
    total = own + f32(got)
    half = total.shape[0] // 2
    return total[:half], bf16(total[half:])


def level_back(grad_msg, own_up, other_up):
    own_up, other_up = 1.0 + own_up, 1.0 + f32(other_up)
    joined = own_up * other_up
    scaling = rms_factor(joined)
    grad = norm_back(grad_msg, joined * scaling, scaling)
    return bf16(grad * other_up), bf16(grad * own_up)


def top_back(own_up, other_up, own_part, got):
    return level_back(own_part + f32(got), own_up, other_up)


def down_back(own_up, other_up, weight, low, high):
    return level_back(matmul_t(join([low, high]), weight), own_up, other_up)


def mid_back(term, near, far, weight, low, high):
    own, near, far = 1.0 + f32(term), 1.0 + f32(near), f32(far)
    pair = own * near
    product = pair * far
    scale = rms_factor(product)
    grad_msg = matmul_t(join([low, high]), weight)
    grad = norm_back(grad_msg, product * scale, scale)
    grad_pair = grad * far
    return bf16(grad_pair * near), bf16(grad_pair * own), bf16(grad * pair)


def far_back(grad_pair, term, near):
    grad_pair = f32(grad_pair)
    return bf16(grad_pair * (1.0 + f32(near))), bf16(grad_pair * (1.0 + f32(term)))


def pair_product(term, near):
    return (bf16((1.0 + f32(term)) * (1.0 + f32(near))),)


def on_device(regions, leaf_map, leaf_bond_weight, mid_weight, upper_weight, head_cotangent):
    rows = regions.shape[0]
    sub_count = lax.axis_size("sub")
    depth = sub_count.bit_length() - 1
    ids = jnp.stack([lax.axis_index("sub"), lax.axis_index("rep")]).astype(jnp.int32)
    leaf_w = leaf_bond_weight[0]
    mid_w = mid_weight[0, 0]

    blocks, (head_left, head_right) = cut_maps(upper_weight[0], ids, depth)
    gather = MapGather(blocks, ids)

    *sent, cotangent = place(after(regions, gather.packed), leaf_map, head_cotangent, ids, depth)
    near = partner(sent[1], "rep", 1)
    far_both = partner(sent[3], "rep", 3)
    far_one = partner(sent[2], "rep", 2)
    placed = [sent[0], near, far_one, far_both]
    for stage in reversed(range(1, depth)):
        gather.stage(stage, sent[3] if stage < depth - 1 else None)

    near_placed = [sent[0], after(near, gather.packed)]
    msg0, msg1, term0, term1 = leaf_forward(near_placed, leaf_w, mid_w)
    near0 = partner(term1, "rep", 1)
    far_placed = [after(far_one, term1), far_both]
    msg2, msg3, term2, term3 = leaf_forward(far_placed, leaf_w, mid_w)
    near2 = partner(term3, "rep", 1)
    (pair,) = fused(pair_product, "pair_product", term2, near2)
    far_pair = partner(pair, "rep", 2)
    exchanged = [partner(after(gather.first, term1), "rep", 1)]
    gather.last(pair)

    weights, messages, own_ups, other_ups = [], [], [], []
    for level in range(depth):
        if level == 1:
            exchanged.append(partner(gather.pack_early(other_ups[0]), "rep", 1))
            exchanged.append(partner(after(gather.late, other_ups[0]), "rep", 1))
        weights.append(gather.weight(level, exchanged))
        if level == 0:
            outs = fused(mid_forward, "mid_forward", term0, near0, far_pair, weights[0])
        else:
            outs = fused(up_forward, "up_forward", own_ups[-1], other_ups[-1], weights[level])
        messages.append(outs[0])
        own_ups.append(outs[1])
        other_ups.append(partner(outs[2], "sub", 1 << level))
    (root,) = fused(top_forward, "top_forward", own_ups[-1], other_ups[-1])

    turns = [[[View(message)], []] for message in messages]

    def gather_turns(stage, value):
        got = partner(value, "sub", 1 << stage)
        at = 0
        for level in range(stage, depth):
            count = sum(view.shape[0] for view in turns[level][0])
            turns[level][0 if level > stage else 1].append(View(got, (at, at + count)))
            at += count
            if level > stage:
                turns[level][1].append(View(got, (at, at + count)))
                at += count

    gather_turns(depth - 1, messages[-1])
    for stage in reversed(range(1, depth)):
        views = []
        for level in range(stage - 1, depth):
            views += turns[level][0] + (turns[level][1] if level > stage - 1 else [])
        got = partner(root, "sub", 1 << stage)
        root, stack = step(joined, "joined", [root, got], stacks=views, ids=ids)
        gather_turns(stage - 1, stack)
    root_high = partner(root, "sub", 1)
    root, grad_value, grad_gate, grad_msg, give = fused(
        head_body, "head", cotangent, head_left, head_right, root, root_high
    )
    for level in range(depth - 1):
        got = partner(give, "sub", 1 << level)
        grad_msg, give = fused(partial_sum, "partial_sum", grad_msg, got)
    last_part = partner(give, "sub", 1 << (depth - 1))
    turns.append([[View(root)], [View(root)]])
    inputs = [view for entry in turns[:depth] for turn in entry for view in turn] + turns[depth][0]

    lows, highs = [None] * depth, [None] * depth
    columns = [None] * depth

    def groups_of(stage):
        return [
            [View(lows[level]), View(highs[level])] if columns[level] is None else columns[level]
            for level in range(stage, depth)
        ]

    def spread(stage, keeps, send):
        got = partner(send, "sub", 1 << stage)
        at = 0
        for level, keep in zip(range(stage, depth), keeps):
            span = keep.shape[1]
            columns[level] = [View(keep), View(got, None, (at, at + span))]
            at += span

    def columns_of(level, turn):
        if level == depth:
            return [View(grad_gate if turn else grad_value)]
        if level == 0:
            return [columns[0][turn]]
        count = rows >> level
        return [
            view.part(i * count, (i + 1) * count)
            for view in columns[level]
            for i in range(turn, view.shape[0] // count, 2)
        ]

    far_got = None
    for level in reversed(range(depth)):
        if level == depth - 1:
            low, high = fused(
                top_back, "top_back", own_ups[level], other_ups[level], grad_msg, last_part
            )
        else:
            above = level + 1
            low, high, *rest = step(
                down_back,
                "down_back",
                [own_ups[level], other_ups[level], weights[above], lows[above], highs[above]],
                halves=groups_of(above),
                level=above,
                far=inputs if above == depth - 1 else None,
                ids=ids,
                limit=12,
            )
            if above == depth - 1:
                far_got = partner(rest.pop(), "rep", 2)
            spread(above, rest[:-1], rest[-1])
        lows[level] = low
        highs[level] = partner(high, "sub", 1 << level)

    back0, back1, pair_back, *rest = step(
        mid_back,
        "mid_back",
        [term0, near0, far_pair, weights[0], lows[0], highs[0]],
        halves=groups_of(0),
        level=0,
        ids=ids,
        limit=12,
    )
    back1 = partner(back1, "rep", 1)
    pair_back = partner(pair_back, "rep", 2)
    spread(0, rest[:-1], rest[-1])
    first = leaf_first(placed[:2], [back0, back1], leaf_w, mid_w)
    groups = [
        [view for turn in range(2) for view in columns_of(level, turn)]
        for level in range(depth + 1)
    ]
    groups[0][0] = groups[0][0].gated(first)
    own_grads = side_by_side(groups)
    far_grads = partner(own_grads, "rep", 2)
    near_grads = partner(own_grads, "rep", 1)
    back2, back3 = fused(far_back, "far_back", after(pair_back, own_grads), term2, near2)
    back3 = partner(back3, "rep", 1)
    near_got = partner(near_inputs([inputs[0].gated(back2)] + inputs[1:], far_got, ids), "rep", 1)
    leaf_grad, mid_grad = leaf_backward(
        placed, [msg0, msg1, msg2, msg3], [back0, back1, back2, back3], leaf_w, mid_w, first
    )
    grads = [own_grads, far_grads, near_grads]
    grads.append(partner(after(far_grads, leaf_grad), "rep", 1))
    upper = upper_grads(turns, far_got, near_got, grads, ids)
    return leaf_grad[None], mid_grad[None, None], upper[None]


def solution(mesh):
    placed = (
        P("rep", "sub", None),
        P("sub"),
        P(("sub", "rep"), None, None, None),
        P("sub", "rep", None, None),
        P("sub", None, None, None),
        P("rep", "sub"),
    )
    return jax.shard_map(
        on_device,
        mesh=mesh,
        in_specs=placed,
        out_specs=(
            P(("sub", "rep"), None, None, None),
            P("sub", "rep", None, None),
            P("sub", "rep", None, None),
        ),
        check_vma=False,
    )
```

time: 197 us -> 170 us (0.86)
  local copies, waits for them, and re-layouts: 27.6 us -> 2.21 us
  waiting for transfers between devices: 77.9 us -> 93.1 us
  Pallas kernels: 38.7 us -> 30.4 us
  starting transfers between devices: 49.5 us -> 43.3 us
    unnamed x139 -> x12, local copies, waits for them, and re-layouts: 26.7 us -> 2.21 us
    ppermute x40, waiting for transfers between devices: 77.9 us -> 93.1 us  [partner(): lax.ppermute(value, axis, [(i, i ^ offset) for i in range(lax.axis_size(a...]
    ppermute x40, starting transfers between devices: 49.5 us -> 43.3 us  [partner(): lax.ppermute(value, axis, [(i, i ^ offset) for i in range(lax.axis_size(a...]
    pallas_call x31 -> x23, Pallas kernels: 19.5 us -> 14.5 us  [the longest x19 9.11 us: fused(): pl.pallas_call(kernel, out_shape=shapes, in_specs=[smem_block()] * (len(a...]
  transfers between devices with their start and end apart: 40 -> 40, of which waited for: 22 -> 24; matrix products, arithmetic and copies ran while one was open for 1% -> 0% of each run, Pallas kernels for 15% -> 12%
where the time goes in v4:
time: 170 us
  waiting for transfers between devices  93.1 us (55%)
  starting transfers between devices  43.3 us (25%)
  Pallas kernels  30.4 us (18%)
  local copies, waits for them, and re-layouts  2.21 us (1%)
    ppermute x40, waiting for transfers between devices, partner(): lax.ppermute(value, axis, [(i, i ^ offset) for i in range(lax.axis_size(a...  93.1 us
    ppermute x40, starting transfers between devices, partner(): lax.ppermute(value, axis, [(i, i ^ offset) for i in range(lax.axis_size(a...  43.3 us
    pallas_call x19, Pallas kernels, fused(): pl.pallas_call(kernel, out_shape=shapes, in_specs=[smem_block()] * (len(a...  9.11 us
    pallas_call x1, Pallas kernels, leaf_backward(): pl.pallas_call(leaf_backward_kernel, out_shape=[jax.ShapeDtypeStruct(leaf...  5.8 us
  transfers between devices with their start and end apart: 40, of which 24 were waited for; matrix products, arithmetic and copies ran while one was open for 0% of the time, Pallas kernels for 12%

profile of v4, /device:TPU:0, one launch (start us, length us, event | category | flops | bytes accessed | tf_op | source)
XLA Modules:
  0.0 170.1 jit_solution(13959319579636888883)
XLA Ops:
  0.7 2.2 %copy-done.2 = bf16[1,1024,2,1024]{3,2,1,0:T(2,128)(2,1)S(1)} copy-done((bf16[1,1024,2,1024]{3,2,1,0:T(2,128)(2,1)S(1)}, bf16[1,1024,2,1024]{3,2,1,0:T(2,128)(2,1)}, u32[]{:S(2)}) %copy-start.2) | copy-done | bytes 4194328
  2.9 2.6 %cut_maps.1 = (bf16[1024,512]{1,0:T(8,128)(2,1)S(1)}, bf16[512,512]{1,0:T(8,128)(2,1)}, bf16[512,512]{1,0:T(8,128)(2,1)S(1)}, bf16[1024,256]{1,0:T(8,128)(2,1)S(...) custom-call(s32[2]{0:T(128)S(1)} %pad_add_fusion.ids_ref.refs_0_, ...), custom_call_target="tpu_custom_call" | custom-call | tf_op jit(solution)/shard_map/cut_maps/pallas_call | solution.py:280
  5.5 3.0 %collective-permute-start.7 = (bf16[512,512]{1,0:T(8,128)(2,1)S(1)}, bf16[512,512]{1,0:T(8,128)(2,1)S(1)}, u32[]{:S(2)}, u32[]{:S(2)}) collective-permute-start(bf16[512,512]{1,0:T(8,128)(2,1)S(1)} %get-tuple-element.104), channel_id=1, source_target_pairs={{0,4},{4,0},{8,12},{12,8},{16,20},{20,16},{24,28},{28,24},{1,5},{5... | collective-permute-start | bytes 1572872 | tf_op jit(solution)/shard_map/ppermute | solution.py:16
  8.6 2.1 %place.1 = (bf16[4,128,256]{2,1,0:T(8,128)(2,1)S(1)}, bf16[4,128,256]{2,1,0:T(8,128)(2,1)S(1)}, bf16[4,128,256]{2,1,0:T(8,128)(2,1)S(1)}, bf16[4,128,256]{2,1,0:T(8,128)(2,1)S(1)}, f32[128,128]{1,0:T(8,128)S(1)}) custom-call(s32[2]{0:T(128)S(1)} %pad_add_fusion.ids_ref.refs_0_, s32[16]{0:T(128)S(1)} %copy-done.5, bf16[2048,256]{1,0:T(8,128)(2,1)S(1)} %bitcast.18, ...), custom_call_target="tpu_custom_call" | custom-call | tf_op jit(solution)/shard_map/place/pallas_call | solution.py:96
  12.6 2.6 %collective-permute-start.3 = (bf16[512,128]{1,0:T(8,128)(2,1)S(1)}, bf16[512,128]{1,0:T(8,128)(2,1)S(1)}, u32[]{:S(2)}, u32[]{:S(2)}) collective-permute-start(bf16[512,128]{1,0:T(8,128)(2,1)S(1)} %get-tuple-element.90), channel_id=1, source_target_pairs={{0,16},{4,20},{8,24},{12,28},{16,0},{20,4},{24,8},{28,12},{1,17},{... | collective-permute-start | bytes 393224 | tf_op jit(solution)/shard_map/ppermute | solution.py:16
  15.1 6.9 %collective-permute-done.3.refs_1_ = bf16[512,128]{1,0:T(8,128)(2,1)S(1)} collective-permute-done((bf16[512,128]{1,0:T(8,128)(2,1)S(1)}, bf16[512,128]{1,0:T(8,128)(2,1)S(1)}, u32[]{:S(2)}, u32[]{:S(2)}) %collective-permute-start.3) | collective-permute-done | bytes 131104 | tf_op jit(solution)/shard_map/ppermute | solution.py:16
  30.6 5.0 %collective-permute-done.11.refs_2_.refs_0_ = bf16[512,512]{1,0:T(8,128)(2,1)S(1)} collective-permute-done((bf16[512,512]{1,0:T(8,128)(2,1)S(1)}, bf16[512,512]{1,0:T(8,128)(2,1)S(1)}, u32[]{:S(2)}, u32[]{:S(2)}) %collective-permute-start.11) | collective-permute-done | bytes 524320 | tf_op jit(solution)/shard_map/ppermute | solution.py:16
  39.1 2.9 %collective-permute-done.10.refs_0_ = bf16[512,384]{1,0:T(8,128)(2,1)S(1)} collective-permute-done((bf16[512,384]{1,0:T(8,128)(2,1)S(1)}, bf16[512,384]{1,0:T(8,128)(2,1)S(1)}, u32[]{:S(2)}, u32[]{:S(2)}) %collective-permute-start.10) | collective-permute-done | bytes 393248 | tf_op jit(solution)/shard_map/ppermute | solution.py:16
  42.0 15.9 %collective-permute-done.9.refs_1_.refs_2_ = bf16[64,1024]{1,0:T(8,128)(2,1)S(1)} collective-permute-done((bf16[64,1024]{1,0:T(8,128)(2,1)S(1)}, bf16[64,1024]{1,0:T(8,128)(2,1)S(1)}, u32[]{:S(2)}, u32[]{:S(2)}) %collective-permute-start.9) | collective-permute-done | bytes 131104 | tf_op jit(solution)/shard_map/ppermute | solution.py:16
  58.6 3.1 %collective-permute-done.14.refs_3_ = bf16[512,640]{1,0:T(8,128)(2,1)S(1)} collective-permute-done((bf16[512,640]{1,0:T(8,128)(2,1)S(1)}, bf16[512,640]{1,0:T(8,128)(2,1)S(1)}, u32[]{:S(2)}, u32[]{:S(2)}) %collective-permute-start.14) | collective-permute-done | bytes 655392 | tf_op jit(solution)/shard_map/ppermute | solution.py:16
  63.0 1.9 %collective-permute-start.15 = (bf16[32,1024]{1,0:T(8,128)(2,1)S(1)}, bf16[32,1024]{1,0:T(8,128)(2,1)S(1)}, u32[]{:S(2)}, u32[]{:S(2)}) collective-permute-start(bf16[32,1024]{1,0:T(8,128)(2,1)S(1)} %get-tuple-element.113), channel_id=1, source_target_pairs={{0,8},{4,12},{8,0},{12,4},{16,24},{20,28},{24,16},{28,20},{1,9},{5... | collective-permute-start | bytes 196616 | tf_op jit(solution)/shard_map/ppermute | solution.py:16
  67.9 3.0 %collective-permute-start.16 = (bf16[16,1024]{1,0:T(8,128)(2,1)S(1)}, bf16[16,1024]{1,0:T(8,128)(2,1)S(1)}, u32[]{:S(2)}, u32[]{:S(2)}) collective-permute-start(bf16[16,1024]{1,0:T(8,128)(2,1)S(1)} %get-tuple-element.116), channel_id=1, source_target_pairs={{0,16},{4,20},{8,24},{12,28},{16,0},{20,4},{24,8},{28,12},{1,17},{... | collective-permute-start | bytes 98312 | tf_op jit(solution)/shard_map/ppermute | solution.py:16
  72.9 3.1 %collective-permute-start.17 = (bf16[16,1024]{1,0:T(8,128)(2,1)S(1)}, bf16[16,1024]{1,0:T(8,128)(2,1)S(1)}, u32[]{:S(2)}, u32[]{:S(2)}) collective-permute-start(bf16[16,1024]{1,0:T(8,128)(2,1)S(1)} %top_forward.1.refs_1_), channel_id=1, source_target_pairs={{0,16},{4,20},{8,24},{12,28},{16,0},{20,4},{24,8},{28,12},{1,17},{... | collective-permute-start | bytes 98312 | tf_op jit(solution)/shard_map/ppermute | solution.py:16
  78.4 2.4 %collective-permute-start.20 = (bf16[128,1024]{1,0:T(8,128)(2,1)S(1)}, bf16[128,1024]{1,0:T(8,128)(2,1)S(1)}, u32[]{:S(2)}, u32[]{:S(2)}) collective-permute-start(bf16[128,1024]{1,0:T(8,128)(2,1)S(1)} %get-tuple-element.124), channel_id=1, source_target_pairs={{0,8},{4,12},{8,0},{12,4},{16,24},{20,28},{24,16},{28,20},{1,9},{5... | collective-permute-start | bytes 786440 | tf_op jit(solution)/shard_map/ppermute | solution.py:16
  80.9 5.3 %collective-permute-done.19.refs_2_ = bf16[32,1024]{1,0:T(8,128)(2,1)S(1)} collective-permute-done((bf16[32,1024]{1,0:T(8,128)(2,1)S(1)}, bf16[32,1024]{1,0:T(8,128)(2,1)S(1)}, u32[]{:S(2)}, u32[]{:S(2)}) %collective-permute-start.19) | collective-permute-done | bytes 65568 | tf_op jit(solution)/shard_map/ppermute | solution.py:16
  88.8 17.9 %collective-permute-done.21.refs_4_ = bf16[64,1024]{1,0:T(8,128)(2,1)S(1)} collective-permute-done((bf16[64,1024]{1,0:T(8,128)(2,1)S(1)}, bf16[64,1024]{1,0:T(8,128)(2,1)S(1)}, u32[]{:S(2)}, u32[]{:S(2)}) %collective-permute-start.21) | collective-permute-done | bytes 131104 | tf_op jit(solution)/shard_map/ppermute | solution.py:16
  107.5 4.8 %collective-permute-done.22.refs_1_ = bf16[64,1024]{1,0:T(8,128)(2,1)S(1)} collective-permute-done((bf16[64,1024]{1,0:T(8,128)(2,1)S(1)}, bf16[64,1024]{1,0:T(8,128)(2,1)S(1)}, u32[]{:S(2)}, u32[]{:S(2)}) %collective-permute-start.22) | collective-permute-done | bytes 131104 | tf_op jit(solution)/shard_map/ppermute | solution.py:16
  114.1 2.5 %collective-permute-done.23.refs_1_ = bf16[32,1024]{1,0:T(8,128)(2,1)S(1)} collective-permute-done((bf16[32,1024]{1,0:T(8,128)(2,1)S(1)}, bf16[32,1024]{1,0:T(8,128)(2,1)S(1)}, u32[]{:S(2)}, u32[]{:S(2)}) %collective-permute-start.23) | collective-permute-done | bytes 65568 | tf_op jit(solution)/shard_map/ppermute | solution.py:16
  116.7 2.1 %collective-permute-start.24 = (bf16[16,1024]{1,0:T(8,128)(2,1)S(1)}, bf16[16,1024]{1,0:T(8,128)(2,1)S(1)}, u32[]{:S(2)}, u32[]{:S(2)}) collective-permute-start(bf16[16,1024]{1,0:T(8,128)(2,1)S(1)} %get-tuple-element.131), channel_id=1, source_target_pairs={{0,16},{4,20},{8,24},{12,28},{16,0},{20,4},{24,8},{28,12},{1,17},{... | collective-permute-start | bytes 98312 | tf_op jit(solution)/shard_map/ppermute | solution.py:16
  118.8 2.8 %collective-permute-done.24.refs_3_ = bf16[16,1024]{1,0:T(8,128)(2,1)S(1)} collective-permute-done((bf16[16,1024]{1,0:T(8,128)(2,1)S(1)}, bf16[16,1024]{1,0:T(8,128)(2,1)S(1)}, u32[]{:S(2)}, u32[]{:S(2)}) %collective-permute-start.24) | collective-permute-done | bytes 32800 | tf_op jit(solution)/shard_map/ppermute | solution.py:16
  121.8 2.1 %collective-permute-start.25 = (bf16[16,1024]{1,0:T(8,128)(2,1)S(1)}, bf16[16,1024]{1,0:T(8,128)(2,1)S(1)}, u32[]{:S(2)}, u32[]{:S(2)}) collective-permute-start(bf16[16,1024]{1,0:T(8,128)(2,1)S(1)} %get-tuple-element.133), channel_id=1, source_target_pairs={{0,16},{4,20},{8,24},{12,28},{16,0},{20,4},{24,8},{28,12},{1,17},{... | collective-permute-start | bytes 98312 | tf_op jit(solution)/shard_map/ppermute | solution.py:16
  123.9 2.8 %collective-permute-done.25.refs_5_ = bf16[16,1024]{1,0:T(8,128)(2,1)S(1)} collective-permute-done((bf16[16,1024]{1,0:T(8,128)(2,1)S(1)}, bf16[16,1024]{1,0:T(8,128)(2,1)S(1)}, u32[]{:S(2)}, u32[]{:S(2)}) %collective-permute-start.25) | collective-permute-done | bytes 32800 | tf_op jit(solution)/shard_map/ppermute | solution.py:16
  128.8 1.9 %collective-permute-start.27 = (bf16[32,1024]{1,0:T(8,128)(2,1)S(1)}, bf16[32,1024]{1,0:T(8,128)(2,1)S(1)}, u32[]{:S(2)}, u32[]{:S(2)}) collective-permute-start(bf16[32,1024]{1,0:T(8,128)(2,1)S(1)} %get-tuple-element.137), channel_id=1, source_target_pairs={{0,8},{4,12},{8,0},{12,4},{16,24},{20,28},{24,16},{28,20},{1,9},{5... | collective-permute-start | bytes 196616 | tf_op jit(solution)/shard_map/ppermute | solution.py:16
  130.7 2.1 %collective-permute-start.28 = (bf16[32,512]{1,0:T(8,128)(2,1)S(1)}, bf16[32,512]{1,0:T(8,128)(2,1)S(1)}, u32[]{:S(2)}, u32[]{:S(2)}) collective-permute-start(bf16[32,512]{1,0:T(8,128)(2,1)S(1)} %get-tuple-element.139), channel_id=1, source_target_pairs={{0,16},{4,20},{8,24},{12,28},{16,0},{20,4},{24,8},{28,12},{1,17},{... | collective-permute-start | bytes 98312 | tf_op jit(solution)/shard_map/ppermute | solution.py:16
  132.8 2.7 %collective-permute-done.28.refs_7_ = bf16[32,512]{1,0:T(8,128)(2,1)S(1)} collective-permute-done((bf16[32,512]{1,0:T(8,128)(2,1)S(1)}, bf16[32,512]{1,0:T(8,128)(2,1)S(1)}, u32[]{:S(2)}, u32[]{:S(2)}) %collective-permute-start.28) | collective-permute-done | bytes 32800 | tf_op jit(solution)/shard_map/ppermute | solution.py:16
  137.4 4.4 %collective-permute-done.30.refs_8_ = bf16[64,768]{1,0:T(8,128)(2,1)S(1)} collective-permute-done((bf16[64,768]{1,0:T(8,128)(2,1)S(1)}, bf16[64,768]{1,0:T(8,128)(2,1)S(1)}, u32[]{:S(2)}, u32[]{:S(2)}) %collective-permute-start.30) | collective-permute-done | bytes 98336 | tf_op jit(solution)/shard_map/ppermute | solution.py:16
  147.2 2.1 %leaf_first.1.refs_14_ = bf16[4,256,1024]{2,1,0:T(8,128)(2,1)S(1)} custom-call(bf16[4,128,256]{2,1,0:T(8,128)(2,1)S(1)} %get-tuple-element.86.refs_0_, bf16[4,128,256]{2,1,0:T(8,128)(2,1)S(1)} %collective-permute-done.refs_1_, bf16[128,1024]{1,0:T(8,128)(2,1)S(1)} %get-tuple-element.145.refs_2_.refs_8_, ...), custom_call_target="tpu_custom_call" | custom-call | tf_op jit(solution)/shard_map/leaf_first/pallas_call | solution.py:166
  149.3 2.7 %collective-permute-done.33.refs_1_ = bf16[128,896]{1,0:T(8,128)(2,1)S(1)} collective-permute-done((bf16[128,896]{1,0:T(8,128)(2,1)S(1)}, bf16[128,896]{1,0:T(8,128)(2,1)S(1)}, u32[]{:S(2)}, u32[]{:S(2)}) %collective-permute-start.33) | collective-permute-done | bytes 229408 | tf_op jit(solution)/shard_map/ppermute | solution.py:16
  155.6 2.3 %collective-permute-done.34.refs_11_ = bf16[128,1024]{1,0:T(8,128)(2,1)S(1)} collective-permute-done((bf16[128,1024]{1,0:T(8,128)(2,1)S(1)}, bf16[128,1024]{1,0:T(8,128)(2,1)S(1)}, u32[]{:S(2)}, u32[]{:S(2)}) %collective-permute-start.34) | collective-permute-done | bytes 262176 | tf_op jit(solution)/shard_map/ppermute | solution.py:16
  157.8 5.8 %leaf_backward.1 = (bf16[4,256,1024]{2,1,0:T(8,128)(2,1)}, bf16[1024,1024]{1,0:T(8,128)(2,1)}) custom-call(bf16[4,128,256]{2,1,0:T(8,128)(2,1)S(1)} %get-tuple-element.86.refs_0_, bf16[4,128,256]{2,1,0:T(8,128)(2,1)S(1)} %collective-permute-done.refs_1_, bf16[4,128,256]{2,1,0:T(8,128)(2,1)S(1)} %collective-permute-done.1.refs_0_.refs_2_, ...), custom_call_target="tpu_custom_call" | custom-call | tf_op jit(solution)/shard_map/leaf_backward/pallas_call | solution.py:190
  163.6 2.0 %collective-permute-done.37.refs_1_ = bf16[256,1024]{1,0:T(8,128)(2,1)S(1)} collective-permute-done((bf16[256,1024]{1,0:T(8,128)(2,1)S(1)}, bf16[256,1024]{1,0:T(8,128)(2,1)S(1)}, u32[]{:S(2)}, u32[]{:S(2)}) %collective-permute-start.37) | collective-permute-done | bytes 524320 | tf_op jit(solution)/shard_map/ppermute | solution.py:16
  167.5 2.6 %upper_grads.1 = bf16[256,2,1024]{2,1,0:T(2,128)(2,1)} custom-call(s32[2]{0:T(128)S(1)} %pad_add_fusion.ids_ref.refs_0_, bf16[896,512]{1,0:T(8,128)(2,1)S(1)} %collective-permute-done.35.far_ref, bf16[1792,256]{1,0:T(8,128)(2,1)S(1)} %collective-permute-done.36.near_ref, bf16[256,1024]{1,0:T(8,128)(2,1)S(1)} %side_by_side.1.refs_0_, ...), custom_call_target="tpu_custom_call" | custom-call | tf_op jit(solution)/shard_map/upper_grads/pallas_call | solution.py:616
  (92 shorter events, 44.0 us)
Async XLA Ops:
  5.5 20.5 %collective-permute-start.7 = (bf16[512,512]{1,0:T(8,128)(2,1)S(1)}, bf16[512,512]{1,0:T(8,128)(2,1)S(1)}, u32[]{:S(2)}, u32[]{:S(2)}) collective-permute-start(bf16[512,512]{1,0:T(8,128)(2,1)S(1)} %get-tuple-element.104), channel_id=1, source_target_pairs={{0,4},{4,0},{8,12},{12,8},{16,20},{20,16},{24,28},{28,24},{1,5},{5... | collective-permute-start | bytes 1572872 | tf_op jit(solution)/shard_map/ppermute | solution.py:16
  10.6 12.2 %collective-permute-start = (bf16[4,128,256]{2,1,0:T(8,128)(2,1)S(1)}, bf16[4,128,256]{2,1,0:T(8,128)(2,1)S(1)}, u32[]{:S(2)}, u32[]{:S(2)}) collective-permute-start(bf16[4,128,256]{2,1,0:T(8,128)(2,1)S(1)} %get-tuple-element.87), channel_id=1, source_target_pairs={{0,1},{1,0},{2,3},{3,2},{4,5},{5,4},{6,7},{7,6},{8,9},{9,8},{10,11... | collective-permute-start | bytes 786440 | tf_op jit(solution)/shard_map/ppermute | solution.py:16
  10.7 13.6 %collective-permute-start.1 = (bf16[4,128,256]{2,1,0:T(8,128)(2,1)S(1)}, bf16[4,128,256]{2,1,0:T(8,128)(2,1)S(1)}, u32[]{:S(2)}, u32[]{:S(2)}) collective-permute-start(bf16[4,128,256]{2,1,0:T(8,128)(2,1)S(1)} %get-tuple-element.88), channel_id=1, source_target_pairs={{0,2},{1,3},{2,0},{3,1},{4,6},{5,7},{6,4},{7,5},{8,10},{9,11},{10,... | collective-permute-start | bytes 786440 | tf_op jit(solution)/shard_map/ppermute | solution.py:16
  12.3 12.3 %collective-permute-start.2 = (bf16[4,128,256]{2,1,0:T(8,128)(2,1)S(1)}, bf16[4,128,256]{2,1,0:T(8,128)(2,1)S(1)}, u32[]{:S(2)}, u32[]{:S(2)}) collective-permute-start(bf16[4,128,256]{2,1,0:T(8,128)(2,1)S(1)} %get-tuple-element.89), channel_id=1, source_target_pairs={{0,3},{1,2},{2,1},{3,0},{4,7},{5,6},{6,5},{7,4},{8,11},{9,10},{10,... | collective-permute-start | bytes 786440 | tf_op jit(solution)/shard_map/ppermute | solution.py:16
  12.6 9.5 %collective-permute-start.3 = (bf16[512,128]{1,0:T(8,128)(2,1)S(1)}, bf16[512,128]{1,0:T(8,128)(2,1)S(1)}, u32[]{:S(2)}, u32[]{:S(2)}) collective-permute-start(bf16[512,128]{1,0:T(8,128)(2,1)S(1)} %get-tuple-element.90), channel_id=1, source_target_pairs={{0,16},{4,20},{8,24},{12,28},{16,0},{20,4},{24,8},{28,12},{1,17},{... | collective-permute-start | bytes 393224 | tf_op jit(solution)/shard_map/ppermute | solution.py:16
  22.1 13.4 %collective-permute-start.11 = (bf16[512,512]{1,0:T(8,128)(2,1)S(1)}, bf16[512,512]{1,0:T(8,128)(2,1)S(1)}, u32[]{:S(2)}, u32[]{:S(2)}) collective-permute-start(bf16[512,512]{1,0:T(8,128)(2,1)S(1)} %pack.5), channel_id=1, source_target_pairs={{0,8},{4,12},{8,0},{12,4},{16,24},{20,28},{24,16},{28,20},{1,9},{5... | collective-permute-start | bytes 1572872 | tf_op jit(solution)/shard_map/ppermute | solution.py:16
  26.0 10.3 %collective-permute-start.8 = (bf16[512,512]{1,0:T(8,128)(2,1)S(1)}, bf16[512,512]{1,0:T(8,128)(2,1)S(1)}, u32[]{:S(2)}, u32[]{:S(2)}) collective-permute-start(bf16[512,512]{1,0:T(8,128)(2,1)S(1)} %collective-permute-done.7.refs_0_), channel_id=1, source_target_pairs={{0,1},{1,0},{2,3},{3,2},{4,5},{5,4},{6,7},{7,6},{8,9},{9,8},{10,11... | collective-permute-start | bytes 1572872 | tf_op jit(solution)/shard_map/ppermute | solution.py:16
  26.6 10.4 %collective-permute-start.4 = (bf16[128,1024]{1,0:T(8,128)(2,1)S(1)}, bf16[128,1024]{1,0:T(8,128)(2,1)S(1)}, u32[]{:S(2)}, u32[]{:S(2)}) collective-permute-start(bf16[128,1024]{1,0:T(8,128)(2,1)S(1)} %get-tuple-element.96), channel_id=1, source_target_pairs={{0,1},{1,0},{2,3},{3,2},{4,5},{5,4},{6,7},{7,6},{8,9},{9,8},{10,11... | collective-permute-start | bytes 786440 | tf_op jit(solution)/shard_map/ppermute | solution.py:16
  28.5 8.6 %collective-permute-start.6 = (bf16[128,1024]{1,0:T(8,128)(2,1)S(1)}, bf16[128,1024]{1,0:T(8,128)(2,1)S(1)}, u32[]{:S(2)}, u32[]{:S(2)}) collective-permute-start(bf16[128,1024]{1,0:T(8,128)(2,1)S(1)} %pair_product.1), channel_id=1, source_target_pairs={{0,2},{1,3},{2,0},{3,1},{4,6},{5,7},{6,4},{7,5},{8,10},{9,11},{10,... | collective-permute-start | bytes 786440 | tf_op jit(solution)/shard_map/ppermute | solution.py:16
  30.0 12.0 %collective-permute-start.10 = (bf16[512,384]{1,0:T(8,128)(2,1)S(1)}, bf16[512,384]{1,0:T(8,128)(2,1)S(1)}, u32[]{:S(2)}, u32[]{:S(2)}) collective-permute-start(bf16[512,384]{1,0:T(8,128)(2,1)S(1)} %pack.4), channel_id=1, source_target_pairs={{0,4},{4,0},{8,12},{12,8},{16,20},{20,16},{24,28},{28,24},{1,5},{5... | collective-permute-start | bytes 1179656 | tf_op jit(solution)/shard_map/ppermute | solution.py:16
  35.6 22.5 %collective-permute-start.12 = (bf16[512,640]{1,0:T(8,128)(2,1)S(1)}, bf16[512,640]{1,0:T(8,128)(2,1)S(1)}, u32[]{:S(2)}, u32[]{:S(2)}) collective-permute-start(bf16[512,640]{1,0:T(8,128)(2,1)S(1)} %pack.7), channel_id=1, source_target_pairs={{0,4},{4,0},{8,12},{12,8},{16,20},{20,16},{24,28},{28,24},{1,5},{5... | collective-permute-start | bytes 1966088 | tf_op jit(solution)/shard_map/ppermute | solution.py:16
  37.7 20.2 %collective-permute-start.9 = (bf16[64,1024]{1,0:T(8,128)(2,1)S(1)}, bf16[64,1024]{1,0:T(8,128)(2,1)S(1)}, u32[]{:S(2)}, u32[]{:S(2)}) collective-permute-start(bf16[64,1024]{1,0:T(8,128)(2,1)S(1)} %get-tuple-element.107), channel_id=1, source_target_pairs={{0,4},{4,0},{8,12},{12,8},{16,20},{20,16},{24,28},{28,24},{1,5},{5... | collective-permute-start | bytes 393224 | tf_op jit(solution)/shard_map/ppermute | solution.py:16
  67.9 4.8 %collective-permute-start.16 = (bf16[16,1024]{1,0:T(8,128)(2,1)S(1)}, bf16[16,1024]{1,0:T(8,128)(2,1)S(1)}, u32[]{:S(2)}, u32[]{:S(2)}) collective-permute-start(bf16[16,1024]{1,0:T(8,128)(2,1)S(1)} %get-tuple-element.116), channel_id=1, source_target_pairs={{0,16},{4,20},{8,24},{12,28},{16,0},{20,4},{24,8},{28,12},{1,17},{... | collective-permute-start | bytes 98312 | tf_op jit(solution)/shard_map/ppermute | solution.py:16
  70.9 7.0 %collective-permute-start.18 = (bf16[32,1024]{1,0:T(8,128)(2,1)S(1)}, bf16[32,1024]{1,0:T(8,128)(2,1)S(1)}, u32[]{:S(2)}, u32[]{:S(2)}) collective-permute-start(bf16[32,1024]{1,0:T(8,128)(2,1)S(1)} %get-tuple-element.121.refs_4_.refs_6_.refs_10_.refs_8_), channel_id=1, source_target_pairs={{0,16},{4,20},{8,24},{12,28},{16,0},{20,4},{24,8},{28,12},{1,17},{... | collective-permute-start | bytes 196616 | tf_op jit(solution)/shard_map/ppermute | solution.py:16
  72.9 5.0 %collective-permute-start.17 = (bf16[16,1024]{1,0:T(8,128)(2,1)S(1)}, bf16[16,1024]{1,0:T(8,128)(2,1)S(1)}, u32[]{:S(2)}, u32[]{:S(2)}) collective-permute-start(bf16[16,1024]{1,0:T(8,128)(2,1)S(1)} %top_forward.1.refs_1_), channel_id=1, source_target_pairs={{0,16},{4,20},{8,24},{12,28},{16,0},{20,4},{24,8},{28,12},{1,17},{... | collective-permute-start | bytes 98312 | tf_op jit(solution)/shard_map/ppermute | solution.py:16
  78.4 7.7 %collective-permute-start.20 = (bf16[128,1024]{1,0:T(8,128)(2,1)S(1)}, bf16[128,1024]{1,0:T(8,128)(2,1)S(1)}, u32[]{:S(2)}, u32[]{:S(2)}) collective-permute-start(bf16[128,1024]{1,0:T(8,128)(2,1)S(1)} %get-tuple-element.124), channel_id=1, source_target_pairs={{0,8},{4,12},{8,0},{12,4},{16,24},{20,28},{24,16},{28,20},{1,9},{5... | collective-permute-start | bytes 786440 | tf_op jit(solution)/shard_map/ppermute | solution.py:16
  80.8 5.4 %collective-permute-start.19 = (bf16[32,1024]{1,0:T(8,128)(2,1)S(1)}, bf16[32,1024]{1,0:T(8,128)(2,1)S(1)}, u32[]{:S(2)}, u32[]{:S(2)}) collective-permute-start(bf16[32,1024]{1,0:T(8,128)(2,1)S(1)} %get-tuple-element.122.refs_1_), channel_id=1, source_target_pairs={{0,8},{4,12},{8,0},{12,4},{16,24},{20,28},{24,16},{28,20},{1,9},{5... | collective-permute-start | bytes 196616 | tf_op jit(solution)/shard_map/ppermute | solution.py:16
  86.8 39.9 %collective-permute-start.26 = (bf16[384,1024]{1,0:T(8,128)(2,1)S(1)}, bf16[384,1024]{1,0:T(8,128)(2,1)S(1)}, u32[]{:S(2)}, u32[]{:S(2)}) collective-permute-start(bf16[384,1024]{1,0:T(8,128)(2,1)S(1)} %get-tuple-element.134), channel_id=1, source_target_pairs={{0,4},{4,0},{8,12},{12,8},{16,20},{20,16},{24,28},{28,24},{1,5},{5... | collective-permute-start | bytes 2359304 | tf_op jit(solution)/shard_map/ppermute | solution.py:16
  87.0 19.7 %collective-permute-start.21 = (bf16[64,1024]{1,0:T(8,128)(2,1)S(1)}, bf16[64,1024]{1,0:T(8,128)(2,1)S(1)}, u32[]{:S(2)}, u32[]{:S(2)}) collective-permute-start(bf16[64,1024]{1,0:T(8,128)(2,1)S(1)} %get-tuple-element.125.refs_3_), channel_id=1, source_target_pairs={{0,4},{4,0},{8,12},{12,8},{16,20},{20,16},{24,28},{28,24},{1,5},{5... | collective-permute-start | bytes 393224 | tf_op jit(solution)/shard_map/ppermute | solution.py:16
  107.3 5.0 %collective-permute-start.22 = (bf16[64,1024]{1,0:T(8,128)(2,1)S(1)}, bf16[64,1024]{1,0:T(8,128)(2,1)S(1)}, u32[]{:S(2)}, u32[]{:S(2)}) collective-permute-start(bf16[64,1024]{1,0:T(8,128)(2,1)S(1)} %get-tuple-element.127), channel_id=1, source_target_pairs={{0,4},{4,0},{8,12},{12,8},{16,20},{20,16},{24,28},{28,24},{1,5},{5... | collective-permute-start | bytes 393224 | tf_op jit(solution)/shard_map/ppermute | solution.py:16
  116.7 4.9 %collective-permute-start.24 = (bf16[16,1024]{1,0:T(8,128)(2,1)S(1)}, bf16[16,1024]{1,0:T(8,128)(2,1)S(1)}, u32[]{:S(2)}, u32[]{:S(2)}) collective-permute-start(bf16[16,1024]{1,0:T(8,128)(2,1)S(1)} %get-tuple-element.131), channel_id=1, source_target_pairs={{0,16},{4,20},{8,24},{12,28},{16,0},{20,4},{24,8},{28,12},{1,17},{... | collective-permute-start | bytes 98312 | tf_op jit(solution)/shard_map/ppermute | solution.py:16
  121.8 4.9 %collective-permute-start.25 = (bf16[16,1024]{1,0:T(8,128)(2,1)S(1)}, bf16[16,1024]{1,0:T(8,128)(2,1)S(1)}, u32[]{:S(2)}, u32[]{:S(2)}) collective-permute-start(bf16[16,1024]{1,0:T(8,128)(2,1)S(1)} %get-tuple-element.133), channel_id=1, source_target_pairs={{0,16},{4,20},{8,24},{12,28},{16,0},{20,4},{24,8},{28,12},{1,17},{... | collective-permute-start | bytes 98312 | tf_op jit(solution)/shard_map/ppermute | solution.py:16
  128.2 26.0 %collective-permute-start.35 = (bf16[896,512]{1,0:T(8,128)(2,1)S(1)}, bf16[896,512]{1,0:T(8,128)(2,1)S(1)}, u32[]{:S(2)}, u32[]{:S(2)}) collective-permute-start(bf16[896,512]{1,0:T(8,128)(2,1)S(1)} %get-tuple-element.160), channel_id=1, source_target_pairs={{0,2},{1,3},{2,0},{3,1},{4,6},{5,7},{6,4},{7,5},{8,10},{9,11},{10,... | collective-permute-start | bytes 2752520 | tf_op jit(solution)/shard_map/ppermute | solution.py:16
  128.8 6.7 %collective-permute-start.27 = (bf16[32,1024]{1,0:T(8,128)(2,1)S(1)}, bf16[32,1024]{1,0:T(8,128)(2,1)S(1)}, u32[]{:S(2)}, u32[]{:S(2)}) collective-permute-start(bf16[32,1024]{1,0:T(8,128)(2,1)S(1)} %get-tuple-element.137), channel_id=1, source_target_pairs={{0,8},{4,12},{8,0},{12,4},{16,24},{20,28},{24,16},{28,20},{1,9},{5... | collective-permute-start | bytes 196616 | tf_op jit(solution)/shard_map/ppermute | solution.py:16
  130.7 4.8 %collective-permute-start.28 = (bf16[32,512]{1,0:T(8,128)(2,1)S(1)}, bf16[32,512]{1,0:T(8,128)(2,1)S(1)}, u32[]{:S(2)}, u32[]{:S(2)}) collective-permute-start(bf16[32,512]{1,0:T(8,128)(2,1)S(1)} %get-tuple-element.139), channel_id=1, source_target_pairs={{0,16},{4,20},{8,24},{12,28},{16,0},{20,4},{24,8},{28,12},{1,17},{... | collective-permute-start | bytes 98312 | tf_op jit(solution)/shard_map/ppermute | solution.py:16
  137.0 5.0 %collective-permute-start.29 = (bf16[64,1024]{1,0:T(8,128)(2,1)S(1)}, bf16[64,1024]{1,0:T(8,128)(2,1)S(1)}, u32[]{:S(2)}, u32[]{:S(2)}) collective-permute-start(bf16[64,1024]{1,0:T(8,128)(2,1)S(1)} %get-tuple-element.141), channel_id=1, source_target_pairs={{0,4},{4,0},{8,12},{12,8},{16,20},{20,16},{24,28},{28,24},{1,5},{5... | collective-permute-start | bytes 393224 | tf_op jit(solution)/shard_map/ppermute | solution.py:16
  137.2 4.6 %collective-permute-start.30 = (bf16[64,768]{1,0:T(8,128)(2,1)S(1)}, bf16[64,768]{1,0:T(8,128)(2,1)S(1)}, u32[]{:S(2)}, u32[]{:S(2)}) collective-permute-start(bf16[64,768]{1,0:T(8,128)(2,1)S(1)} %get-tuple-element.143), channel_id=1, source_target_pairs={{0,8},{4,12},{8,0},{12,4},{16,24},{20,28},{24,16},{28,20},{1,9},{5... | collective-permute-start | bytes 294920 | tf_op jit(solution)/shard_map/ppermute | solution.py:16
  144.0 8.0 %collective-permute-start.33 = (bf16[128,896]{1,0:T(8,128)(2,1)S(1)}, bf16[128,896]{1,0:T(8,128)(2,1)S(1)}, u32[]{:S(2)}, u32[]{:S(2)}) collective-permute-start(bf16[128,896]{1,0:T(8,128)(2,1)S(1)} %get-tuple-element.150), channel_id=1, source_target_pairs={{0,4},{4,0},{8,12},{12,8},{16,20},{20,16},{24,28},{28,24},{1,5},{5... | collective-permute-start | bytes 688136 | tf_op jit(solution)/shard_map/ppermute | solution.py:16
  145.7 8.4 %collective-permute-start.32 = (bf16[128,1024]{1,0:T(8,128)(2,1)S(1)}, bf16[128,1024]{1,0:T(8,128)(2,1)S(1)}, u32[]{:S(2)}, u32[]{:S(2)}) collective-permute-start(bf16[128,1024]{1,0:T(8,128)(2,1)S(1)} %get-tuple-element.147), channel_id=1, source_target_pairs={{0,2},{1,3},{2,0},{3,1},{4,6},{5,7},{6,4},{7,5},{8,10},{9,11},{10,... | collective-permute-start | bytes 786440 | tf_op jit(solution)/shard_map/ppermute | solution.py:16
  152.1 13.6 %collective-permute-start.37 = (bf16[256,1024]{1,0:T(8,128)(2,1)S(1)}, bf16[256,1024]{1,0:T(8,128)(2,1)S(1)}, u32[]{:S(2)}, u32[]{:S(2)}) collective-permute-start(bf16[256,1024]{1,0:T(8,128)(2,1)S(1)} %side_by_side.1.refs_0_), channel_id=1, source_target_pairs={{0,2},{1,3},{2,0},{3,1},{4,6},{5,7},{6,4},{7,5},{8,10},{9,11},{10,... | collective-permute-start | bytes 1572872 | tf_op jit(solution)/shard_map/ppermute | solution.py:16
  154.9 12.6 %collective-permute-start.36 = (bf16[1792,256]{1,0:T(8,128)(2,1)S(1)}, bf16[1792,256]{1,0:T(8,128)(2,1)S(1)}, u32[]{:S(2)}, u32[]{:S(2)}) collective-permute-start(bf16[1792,256]{1,0:T(8,128)(2,1)S(1)} %near_inputs.1), channel_id=1, source_target_pairs={{0,1},{1,0},{2,3},{3,2},{4,5},{5,4},{6,7},{7,6},{8,9},{9,8},{10,11... | collective-permute-start | bytes 2752520 | tf_op jit(solution)/shard_map/ppermute | solution.py:16
  155.5 10.1 %collective-permute-start.38 = (bf16[256,1024]{1,0:T(8,128)(2,1)S(1)}, bf16[256,1024]{1,0:T(8,128)(2,1)S(1)}, u32[]{:S(2)}, u32[]{:S(2)}) collective-permute-start(bf16[256,1024]{1,0:T(8,128)(2,1)S(1)} %side_by_side.1.refs_0_), channel_id=1, source_target_pairs={{0,1},{1,0},{2,3},{3,2},{4,5},{5,4},{6,7},{7,6},{8,9},{9,8},{10,11... | collective-permute-start | bytes 1572872 | tf_op jit(solution)/shard_map/ppermute | solution.py:16
  (14 other events, 82.3 us)

commit v5 on v4

--- a/solution.py
+++ b/solution.py
@@ -358,70 +358,52 @@
         self.depth = len(blocks)
         self.spans = [block[0].shape[1] for block in blocks]
         self.held = [{0: (block[1], 0)} for block in blocks]
-        self.first = partner(blocks[0][2], "sub", 1)
-        self.early = [self.send([(level, 0) for level in range(1, self.depth)], 0)]
-
-    def send(self, picks, stage, extra=None, gate=None):
-        pieces = [(*self.held[level][offset], self.spans[level]) for level, offset in picks]
-        picks = list(picks)
-        if extra is not None:
-            pieces.append((self.blocks[extra][2], 0, self.spans[extra]))
-            picks.append((extra, 0))
-        if gate is not None:
-            pieces[-1] = (after(pieces[-1][0], gate), *pieces[-1][1:])
-        value = pieces[0][0] if len(pieces) == 1 else pack(pieces)
-        self.packed = value
+        self.other = {}
+        pieces = [(blocks[0][2], 0, self.spans[0])]
+        pieces += [(blocks[i][1], 0, self.spans[i]) for i in range(1, self.depth)]
+        self.first = pack(pieces)
+        got = partner(self.first, "sub", 1)
+        self.received = got
+        at = 0
+        for level in range(self.depth):
+            self.held[level][1] = (got, at)
+            at += self.spans[level]
+
+    def relay(self, level, stage, gate=None):
+        if stage == level:
+            offsets, value = [0], self.blocks[level][2]
+            if gate is not None:
+                value = after(value, gate)
+        else:
+            offsets = [i for i in self.held[level] if i % (2 << stage) == 0]
+            if stage == 0:
+                offsets = [i for i in offsets if i > 0]
+            pieces = [(*self.held[level][i], self.spans[level]) for i in offsets]
+            if gate is not None:
+                pieces[-1] = (after(pieces[-1][0], gate), *pieces[-1][1:])
+            if len(pieces) == 1 and pieces[0][0].shape[1] == pieces[0][2]:
+                value = pieces[0][0]
+            else:
+                value = pack(pieces)
+            for place, offset in enumerate(offsets):
+                if offset > 0:
+                    self.held[level][offset] = (value, place * self.spans[level])
         got = partner(value, "sub", 1 << stage)
-        at = 0
-        for level, offset in picks:
-            self.held[level][offset ^ (1 << stage)] = (got, at)
-            at += self.spans[level]
-        return got
-
-    def stage(self, stage, gate=None):
-        picks = [
-            (level, offset)
-            for level in range(stage + 1, self.depth)
-            for offset in self.held[level]
-            if offset % (2 << stage) == 0
-        ]
-        self.early.append(self.send(picks, stage, stage, gate))
-
-    def last(self, gate):
-        picks = [
-            (level, offset)
-            for level in range(1, self.depth)
-            for offset in self.held[level]
-            if offset % 2 == 0 and offset > 0
-        ]
-        self.late = self.send(picks, 0, None, gate)
-
-    def weight(self, level, exchanged):
+        for place, offset in enumerate(offsets):
+            self.held[level][offset ^ (1 << stage)] = (got, place * self.spans[level])
+        return value
+
+    def exchange(self, level, gate):
+        for offset, (array, _) in self.held[level].items():
+            if offset > 0 and id(array) not in self.other:
+                self.other[id(array)] = (array, partner(after(array, gate), "rep", 1))
+
+    def weight(self, level):
         pieces = {}
-        if level == 0:
-            pieces[1] = (self.first, exchanged[0], 0)
-        else:
-            for offset, (array, at) in self.held[level].items():
-                if offset == 0:
-                    continue
-                if array is self.late:
-                    pieces[offset] = (array, exchanged[2], at)
-                    continue
-                pieces[offset] = (self.packed_early, exchanged[1], at + self.early_at(array))
+        for offset, (array, at) in self.held[level].items():
+            if offset > 0:
+                pieces[offset] = (array, self.other[id(array)][1], at)
         return assemble(self.blocks[level][0], pieces, self.ids)
-
-    def early_at(self, array):
-        at = 0
-        for known in self.early:
-            if known is array:
-                return at
-            at += known.shape[1]
-
-    def pack_early(self, gate):
-        pieces = [(array, 0, array.shape[1]) for array in self.early]
-        pieces[0] = (after(self.early[0], gate), *pieces[0][1:])
-        self.packed_early = pack(pieces)
-        return self.packed_early
 
 
 class View:
@@ -736,31 +718,34 @@
     blocks, (head_left, head_right) = cut_maps(upper_weight[0], ids, depth)
     gather = MapGather(blocks, ids)
 
-    *sent, cotangent = place(after(regions, gather.packed), leaf_map, head_cotangent, ids, depth)
+    *sent, cotangent = place(after(regions, gather.first), leaf_map, head_cotangent, ids, depth)
     near = partner(sent[1], "rep", 1)
     far_both = partner(sent[3], "rep", 3)
     far_one = partner(sent[2], "rep", 2)
     placed = [sent[0], near, far_one, far_both]
-    for stage in reversed(range(1, depth)):
-        gather.stage(stage, sent[3] if stage < depth - 1 else None)
-
-    near_placed = [sent[0], after(near, gather.packed)]
-    msg0, msg1, term0, term1 = leaf_forward(near_placed, leaf_w, mid_w)
+    for level in reversed(range(1, depth)):
+        value = gather.relay(level, level, sent[3] if level < depth - 1 else None)
+    gather.got = gather.held[1][2][0]
+    for level in range(2, depth):
+        for stage in reversed(range(1, level)):
+            value = gather.relay(level, stage, sent[3])
+
+    msg0, msg1, term0, term1 = leaf_forward(placed[:2], leaf_w, mid_w)
     near0 = partner(term1, "rep", 1)
-    far_placed = [after(far_one, term1), far_both]
+    far_placed = [after(far_one, term1, value, gather.got), far_both]
     msg2, msg3, term2, term3 = leaf_forward(far_placed, leaf_w, mid_w)
     near2 = partner(term3, "rep", 1)
+    for level in range(1, depth):
+        gather.relay(level, 0, term3)
+    gather.exchange(0, term3)
     (pair,) = fused(pair_product, "pair_product", term2, near2)
     far_pair = partner(pair, "rep", 2)
-    exchanged = [partner(after(gather.first, term1), "rep", 1)]
-    gather.last(pair)
+    for level in range(1, depth):
+        gather.exchange(level, pair)
 
     weights, messages, own_ups, other_ups = [], [], [], []
     for level in range(depth):
-        if level == 1:
-            exchanged.append(partner(gather.pack_early(other_ups[0]), "rep", 1))
-            exchanged.append(partner(after(gather.late, other_ups[0]), "rep", 1))
-        weights.append(gather.weight(level, exchanged))
+        weights.append(gather.weight(level))
         if level == 0:
             outs = fused(mid_forward, "mid_forward", term0, near0, far_pair, weights[0])
         else:
@@ -772,10 +757,10 @@
 
     turns = [[[View(message)], []] for message in messages]
 
-    def gather_turns(stage, value):
+    def gather_turns(stage, value, levels):
         got = partner(value, "sub", 1 << stage)
         at = 0
-        for level in range(stage, depth):
+        for level in levels:
             count = sum(view.shape[0] for view in turns[level][0])
             turns[level][0 if level > stage else 1].append(View(got, (at, at + count)))
             at += count
@@ -783,14 +768,18 @@
                 turns[level][1].append(View(got, (at, at + count)))
                 at += count
 
-    gather_turns(depth - 1, messages[-1])
+    gather_turns(0, after(messages[0], other_ups[0]), [0])
+    gather_turns(depth - 1, messages[-1], [depth - 1])
     for stage in reversed(range(1, depth)):
         views = []
-        for level in range(stage - 1, depth):
+        for level in range(max(stage - 1, 1), depth):
             views += turns[level][0] + (turns[level][1] if level > stage - 1 else [])
         got = partner(root, "sub", 1 << stage)
+        if stage == depth - 1:
+            root = after(root, turns[0][1][0].array)
         root, stack = step(joined, "joined", [root, got], stacks=views, ids=ids)
-        gather_turns(stage - 1, stack)
+        if stage > 1:
+            gather_turns(stage - 1, stack, range(stage - 1, depth))
     root_high = partner(root, "sub", 1)
     root, grad_value, grad_gate, grad_msg, give = fused(
         head_body, "head", cotangent, head_left, head_right, root, root_high
@@ -798,6 +787,8 @@
     for level in range(depth - 1):
         got = partner(give, "sub", 1 << level)
         grad_msg, give = fused(partial_sum, "partial_sum", grad_msg, got)
+        if level == 0:
+            gather_turns(0, after(stack, give), range(1, depth))
     last_part = partner(give, "sub", 1 << (depth - 1))
     turns.append([[View(root)], [View(root)]])
     inputs = [view for entry in turns[:depth] for turn in entry for view in turn] + turns[depth][0]

time: 170 us -> 162 us (0.953)
  waiting for transfers between devices: 93.1 us -> 83.2 us
  starting transfers between devices: 43.3 us -> 45.7 us
    ppermute x40 -> x44, waiting for transfers between devices: 93.1 us -> 83.2 us  [partner(): lax.ppermute(value, axis, [(i, i ^ offset) for i in range(lax.axis_size(a...]
    ppermute x40 -> x44, starting transfers between devices: 43.3 us -> 45.7 us  [partner(): lax.ppermute(value, axis, [(i, i ^ offset) for i in range(lax.axis_size(a...]
    pallas_call x19 -> x18, Pallas kernels: 9.11 us -> 8.84 us  [fused(): pl.pallas_call(kernel, out_shape=shapes, in_specs=[smem_block()] * (len(a...]
  transfers between devices with their start and end apart: 40 -> 44, of which waited for: 24 -> 25; matrix products, arithmetic and copies ran while one was open for 0% -> 0% of each run, Pallas kernels for 12% -> 13%
where the time goes in v5:
time: 162 us
  waiting for transfers between devices  83.2 us (51%)
  starting transfers between devices  45.7 us (28%)
  Pallas kernels  30.2 us (19%)
  local copies, waits for them, and re-layouts  2.21 us (1%)
    ppermute x44, waiting for transfers between devices, partner(): lax.ppermute(value, axis, [(i, i ^ offset) for i in range(lax.axis_size(a...  83.2 us
    ppermute x44, starting transfers between devices, partner(): lax.ppermute(value, axis, [(i, i ^ offset) for i in range(lax.axis_size(a...  45.7 us
    pallas_call x18, Pallas kernels, fused(): pl.pallas_call(kernel, out_shape=shapes, in_specs=[smem_block()] * (len(a...  8.84 us
    pallas_call x1, Pallas kernels, leaf_backward(): pl.pallas_call(leaf_backward_kernel, out_shape=[jax.ShapeDtypeStruct(leaf...  5.8 us
  transfers between devices with their start and end apart: 44, of which 25 were waited for; matrix products, arithmetic and copies ran while one was open for 0% of the time, Pallas kernels for 13%

profile of v5, /device:TPU:0, one launch (start us, length us, event | category | flops | bytes accessed | tf_op | source)
XLA Modules:
  0.0 162.3 jit_solution(10635082239696242443)
XLA Ops:
  0.7 2.2 %copy-done.2 = bf16[1,1024,2,1024]{3,2,1,0:T(2,128)(2,1)S(1)} copy-done((bf16[1,1024,2,1024]{3,2,1,0:T(2,128)(2,1)S(1)}, bf16[1,1024,2,1024]{3,2,1,0:T(2,128)(2,1)}, u32[]{:S(2)}) %copy-start.2) | copy-done | bytes 4194328
  2.9 2.6 %cut_maps.1 = (bf16[1024,512]{1,0:T(8,128)(2,1)S(1)}, bf16[512,512]{1,0:T(8,128)(2,1)}, bf16[512,512]{1,0:T(8,128)(2,1)S(1)}, bf16[1024,256]{1,0:T(8,128)(2,1)S(...) custom-call(s32[2]{0:T(128)S(1)} %pad_add_fusion.ids_ref.refs_0_, ...), custom_call_target="tpu_custom_call" | custom-call | tf_op jit(solution)/shard_map/cut_maps/pallas_call | solution.py:280
  5.6 3.0 %collective-permute-start.8 = (bf16[512,896]{1,0:T(8,128)(2,1)S(1)}, bf16[512,896]{1,0:T(8,128)(2,1)S(1)}, u32[]{:S(2)}, u32[]{:S(2)}) collective-permute-start(bf16[512,896]{1,0:T(8,128)(2,1)S(1)} %pack.3), channel_id=1, source_target_pairs={{0,4},{4,0},{8,12},{12,8},{16,20},{20,16},{24,28},{28,24},{1,5},{5... | collective-permute-start | bytes 2752520 | tf_op jit(solution)/shard_map/ppermute | solution.py:16
  8.6 2.6 %collective-permute-start.3 = (bf16[512,128]{1,0:T(8,128)(2,1)S(1)}, bf16[512,128]{1,0:T(8,128)(2,1)S(1)}, u32[]{:S(2)}, u32[]{:S(2)}) collective-permute-start(bf16[512,128]{1,0:T(8,128)(2,1)S(1)} %get-tuple-element.100), channel_id=1, source_target_pairs={{0,16},{4,20},{8,24},{12,28},{16,0},{20,4},{24,8},{28,12},{1,17},{... | collective-permute-start | bytes 393224 | tf_op jit(solution)/shard_map/ppermute | solution.py:16
  11.2 2.1 %place.1 = (bf16[4,128,256]{2,1,0:T(8,128)(2,1)S(1)}, bf16[4,128,256]{2,1,0:T(8,128)(2,1)S(1)}, bf16[4,128,256]{2,1,0:T(8,128)(2,1)S(1)}, bf16[4,128,256]{2,1,0:T(8,128)(2,1)S(1)}, f32[128,128]{1,0:T(8,128)S(1)}) custom-call(s32[2]{0:T(128)S(1)} %pad_add_fusion.ids_ref.refs_0_, s32[16]{0:T(128)S(1)} %copy-done.5, bf16[2048,256]{1,0:T(8,128)(2,1)S(1)} %bitcast.18, ...), custom_call_target="tpu_custom_call" | custom-call | tf_op jit(solution)/shard_map/place/pallas_call | solution.py:96
  18.9 4.0 %collective-permute-done.4.refs_1_ = bf16[512,256]{1,0:T(8,128)(2,1)S(1)} collective-permute-done((bf16[512,256]{1,0:T(8,128)(2,1)S(1)}, bf16[512,256]{1,0:T(8,128)(2,1)S(1)}, u32[]{:S(2)}, u32[]{:S(2)}) %collective-permute-start.4) | collective-permute-done | bytes 262176 | tf_op jit(solution)/shard_map/ppermute | solution.py:16
  24.2 4.1 %collective-permute-done.2.refs_1_.refs_3_ = bf16[4,128,256]{2,1,0:T(8,128)(2,1)S(1)} collective-permute-done((bf16[4,128,256]{2,1,0:T(8,128)(2,1)S(1)}, bf16[4,128,256]{2,1,0:T(8,128)(2,1)S(1)}, u32[]{:S(2)}, u32[]{:S(2)}) %collective-permute-start.2) | collective-permute-done | bytes 262176 | tf_op jit(solution)/shard_map/ppermute | solution.py:16
  31.1 7.8 %collective-permute-done.15.refs_1_.refs_2_ = bf16[512,256]{1,0:T(8,128)(2,1)S(1)} collective-permute-done((bf16[512,256]{1,0:T(8,128)(2,1)S(1)}, bf16[512,256]{1,0:T(8,128)(2,1)S(1)}, u32[]{:S(2)}, u32[]{:S(2)}) %collective-permute-start.15) | collective-permute-done | bytes 262176 | tf_op jit(solution)/shard_map/ppermute | solution.py:16
  42.7 8.3 %collective-permute-done.16.refs_2_ = bf16[512,384]{1,0:T(8,128)(2,1)S(1)} collective-permute-done((bf16[512,384]{1,0:T(8,128)(2,1)S(1)}, bf16[512,384]{1,0:T(8,128)(2,1)S(1)}, u32[]{:S(2)}, u32[]{:S(2)}) %collective-permute-start.16) | collective-permute-done | bytes 393248 | tf_op jit(solution)/shard_map/ppermute | solution.py:16
  51.1 3.8 %collective-permute-done.11.refs_2_ = bf16[512,256]{1,0:T(8,128)(2,1)S(1)} collective-permute-done((bf16[512,256]{1,0:T(8,128)(2,1)S(1)}, bf16[512,256]{1,0:T(8,128)(2,1)S(1)}, u32[]{:S(2)}, u32[]{:S(2)}) %collective-permute-start.11) | collective-permute-done | bytes 262176 | tf_op jit(solution)/shard_map/ppermute | solution.py:16
  57.5 5.3 %collective-permute-done.10.refs_1_.refs_2_ = bf16[64,1024]{1,0:T(8,128)(2,1)S(1)} collective-permute-done((bf16[64,1024]{1,0:T(8,128)(2,1)S(1)}, bf16[64,1024]{1,0:T(8,128)(2,1)S(1)}, u32[]{:S(2)}, u32[]{:S(2)}) %collective-permute-start.10) | collective-permute-done | bytes 131104 | tf_op jit(solution)/shard_map/ppermute | solution.py:16
  64.7 2.1 %collective-permute-start.14 = (bf16[32,1024]{1,0:T(8,128)(2,1)S(1)}, bf16[32,1024]{1,0:T(8,128)(2,1)S(1)}, u32[]{:S(2)}, u32[]{:S(2)}) collective-permute-start(bf16[32,1024]{1,0:T(8,128)(2,1)S(1)} %get-tuple-element.119), channel_id=1, source_target_pairs={{0,8},{4,12},{8,0},{12,4},{16,24},{20,28},{24,16},{28,20},{1,9},{5... | collective-permute-start | bytes 196616 | tf_op jit(solution)/shard_map/ppermute | solution.py:16
  69.6 3.0 %collective-permute-start.19 = (bf16[16,1024]{1,0:T(8,128)(2,1)S(1)}, bf16[16,1024]{1,0:T(8,128)(2,1)S(1)}, u32[]{:S(2)}, u32[]{:S(2)}) collective-permute-start(bf16[16,1024]{1,0:T(8,128)(2,1)S(1)} %get-tuple-element.125), channel_id=1, source_target_pairs={{0,16},{4,20},{8,24},{12,28},{16,0},{20,4},{24,8},{28,12},{1,17},{... | collective-permute-start | bytes 98312 | tf_op jit(solution)/shard_map/ppermute | solution.py:16
  74.8 2.9 %collective-permute-start.21 = (bf16[16,1024]{1,0:T(8,128)(2,1)S(1)}, bf16[16,1024]{1,0:T(8,128)(2,1)S(1)}, u32[]{:S(2)}, u32[]{:S(2)}) collective-permute-start(bf16[16,1024]{1,0:T(8,128)(2,1)S(1)} %top_forward.1.refs_1_), channel_id=1, source_target_pairs={{0,16},{4,20},{8,24},{12,28},{16,0},{20,4},{24,8},{28,12},{1,17},{... | collective-permute-start | bytes 98312 | tf_op jit(solution)/shard_map/ppermute | solution.py:16
  80.2 2.4 %collective-permute-start.24 = (bf16[128,1024]{1,0:T(8,128)(2,1)S(1)}, bf16[128,1024]{1,0:T(8,128)(2,1)S(1)}, u32[]{:S(2)}, u32[]{:S(2)}) collective-permute-start(bf16[128,1024]{1,0:T(8,128)(2,1)S(1)} %get-tuple-element.135), channel_id=1, source_target_pairs={{0,8},{4,12},{8,0},{12,4},{16,24},{20,28},{24,16},{28,20},{1,9},{5... | collective-permute-start | bytes 786440 | tf_op jit(solution)/shard_map/ppermute | solution.py:16
  82.8 5.0 %collective-permute-done.23.refs_2_ = bf16[32,1024]{1,0:T(8,128)(2,1)S(1)} collective-permute-done((bf16[32,1024]{1,0:T(8,128)(2,1)S(1)}, bf16[32,1024]{1,0:T(8,128)(2,1)S(1)}, u32[]{:S(2)}, u32[]{:S(2)}) %collective-permute-start.23) | collective-permute-done | bytes 65568 | tf_op jit(solution)/shard_map/ppermute | solution.py:16
  88.3 2.1 %collective-permute-start.25 = (bf16[64,1024]{1,0:T(8,128)(2,1)S(1)}, bf16[64,1024]{1,0:T(8,128)(2,1)S(1)}, u32[]{:S(2)}, u32[]{:S(2)}) collective-permute-start(bf16[64,1024]{1,0:T(8,128)(2,1)S(1)} %get-tuple-element.136.refs_3_), channel_id=1, source_target_pairs={{0,4},{4,0},{8,12},{12,8},{16,20},{20,16},{24,28},{28,24},{1,5},{5... | collective-permute-start | bytes 393224 | tf_op jit(solution)/shard_map/ppermute | solution.py:16
  90.5 3.8 %collective-permute-done.25.refs_4_ = bf16[64,1024]{1,0:T(8,128)(2,1)S(1)} collective-permute-done((bf16[64,1024]{1,0:T(8,128)(2,1)S(1)}, bf16[64,1024]{1,0:T(8,128)(2,1)S(1)}, u32[]{:S(2)}, u32[]{:S(2)}) %collective-permute-start.25) | collective-permute-done | bytes 131104 | tf_op jit(solution)/shard_map/ppermute | solution.py:16
  96.0 5.2 %collective-permute-done.26.refs_1_ = bf16[64,1024]{1,0:T(8,128)(2,1)S(1)} collective-permute-done((bf16[64,1024]{1,0:T(8,128)(2,1)S(1)}, bf16[64,1024]{1,0:T(8,128)(2,1)S(1)}, u32[]{:S(2)}, u32[]{:S(2)}) %collective-permute-start.26) | collective-permute-done | bytes 131104 | tf_op jit(solution)/shard_map/ppermute | solution.py:16
  103.6 3.3 %collective-permute-done.27.refs_1_ = bf16[32,1024]{1,0:T(8,128)(2,1)S(1)} collective-permute-done((bf16[32,1024]{1,0:T(8,128)(2,1)S(1)}, bf16[32,1024]{1,0:T(8,128)(2,1)S(1)}, u32[]{:S(2)}, u32[]{:S(2)}) %collective-permute-start.27) | collective-permute-done | bytes 65568 | tf_op jit(solution)/shard_map/ppermute | solution.py:16
  108.7 3.1 %collective-permute-done.28.refs_3_ = bf16[16,1024]{1,0:T(8,128)(2,1)S(1)} collective-permute-done((bf16[16,1024]{1,0:T(8,128)(2,1)S(1)}, bf16[16,1024]{1,0:T(8,128)(2,1)S(1)}, u32[]{:S(2)}, u32[]{:S(2)}) %collective-permute-start.28) | collective-permute-done | bytes 32800 | tf_op jit(solution)/shard_map/ppermute | solution.py:16
  111.9 2.2 %collective-permute-start.29 = (bf16[16,1024]{1,0:T(8,128)(2,1)S(1)}, bf16[16,1024]{1,0:T(8,128)(2,1)S(1)}, u32[]{:S(2)}, u32[]{:S(2)}) collective-permute-start(bf16[16,1024]{1,0:T(8,128)(2,1)S(1)} %get-tuple-element.144), channel_id=1, source_target_pairs={{0,16},{4,20},{8,24},{12,28},{16,0},{20,4},{24,8},{28,12},{1,17},{... | collective-permute-start | bytes 98312 | tf_op jit(solution)/shard_map/ppermute | solution.py:16
  114.1 2.7 %collective-permute-done.29.refs_5_ = bf16[16,1024]{1,0:T(8,128)(2,1)S(1)} collective-permute-done((bf16[16,1024]{1,0:T(8,128)(2,1)S(1)}, bf16[16,1024]{1,0:T(8,128)(2,1)S(1)}, u32[]{:S(2)}, u32[]{:S(2)}) %collective-permute-start.29) | collective-permute-done | bytes 32800 | tf_op jit(solution)/shard_map/ppermute | solution.py:16
  121.4 2.5 %collective-permute-start.32 = (bf16[32,512]{1,0:T(8,128)(2,1)S(1)}, bf16[32,512]{1,0:T(8,128)(2,1)S(1)}, u32[]{:S(2)}, u32[]{:S(2)}) collective-permute-start(bf16[32,512]{1,0:T(8,128)(2,1)S(1)} %get-tuple-element.151), channel_id=1, source_target_pairs={{0,16},{4,20},{8,24},{12,28},{16,0},{20,4},{24,8},{28,12},{1,17},{... | collective-permute-start | bytes 98312 | tf_op jit(solution)/shard_map/ppermute | solution.py:16
  123.9 2.7 %collective-permute-done.32.refs_7_ = bf16[32,512]{1,0:T(8,128)(2,1)S(1)} collective-permute-done((bf16[32,512]{1,0:T(8,128)(2,1)S(1)}, bf16[32,512]{1,0:T(8,128)(2,1)S(1)}, u32[]{:S(2)}, u32[]{:S(2)}) %collective-permute-start.32) | collective-permute-done | bytes 32800 | tf_op jit(solution)/shard_map/ppermute | solution.py:16
  130.0 4.4 %collective-permute-done.34.refs_8_ = bf16[64,768]{1,0:T(8,128)(2,1)S(1)} collective-permute-done((bf16[64,768]{1,0:T(8,128)(2,1)S(1)}, bf16[64,768]{1,0:T(8,128)(2,1)S(1)}, u32[]{:S(2)}, u32[]{:S(2)}) %collective-permute-start.34) | collective-permute-done | bytes 98336 | tf_op jit(solution)/shard_map/ppermute | solution.py:16
  137.7 2.1 %leaf_first.1.refs_14_ = bf16[4,256,1024]{2,1,0:T(8,128)(2,1)S(1)} custom-call(bf16[4,128,256]{2,1,0:T(8,128)(2,1)S(1)} %get-tuple-element.93.refs_0_, bf16[4,128,256]{2,1,0:T(8,128)(2,1)S(1)} %collective-permute-done.refs_1_, bf16[128,1024]{1,0:T(8,128)(2,1)S(1)} %get-tuple-element.157.refs_2_.refs_8_, ...), custom_call_target="tpu_custom_call" | custom-call | tf_op jit(solution)/shard_map/leaf_first/pallas_call | solution.py:166
  139.7 4.4 %collective-permute-done.37.refs_1_ = bf16[128,896]{1,0:T(8,128)(2,1)S(1)} collective-permute-done((bf16[128,896]{1,0:T(8,128)(2,1)S(1)}, bf16[128,896]{1,0:T(8,128)(2,1)S(1)}, u32[]{:S(2)}, u32[]{:S(2)}) %collective-permute-start.37) | collective-permute-done | bytes 229408 | tf_op jit(solution)/shard_map/ppermute | solution.py:16
  146.5 2.3 %collective-permute-done.38.refs_11_ = bf16[128,1024]{1,0:T(8,128)(2,1)S(1)} collective-permute-done((bf16[128,1024]{1,0:T(8,128)(2,1)S(1)}, bf16[128,1024]{1,0:T(8,128)(2,1)S(1)}, u32[]{:S(2)}, u32[]{:S(2)}) %collective-permute-start.38) | collective-permute-done | bytes 262176 | tf_op jit(solution)/shard_map/ppermute | solution.py:16
  148.8 5.8 %leaf_backward.1 = (bf16[4,256,1024]{2,1,0:T(8,128)(2,1)}, bf16[1024,1024]{1,0:T(8,128)(2,1)}) custom-call(bf16[4,128,256]{2,1,0:T(8,128)(2,1)S(1)} %get-tuple-element.93.refs_0_, bf16[4,128,256]{2,1,0:T(8,128)(2,1)S(1)} %collective-permute-done.refs_1_, bf16[4,128,256]{2,1,0:T(8,128)(2,1)S(1)} %collective-permute-done.1.refs_0_.refs_2_, ...), custom_call_target="tpu_custom_call" | custom-call | tf_op jit(solution)/shard_map/leaf_backward/pallas_call | solution.py:190
  154.6 3.2 %collective-permute-done.41.refs_1_ = bf16[256,1024]{1,0:T(8,128)(2,1)S(1)} collective-permute-done((bf16[256,1024]{1,0:T(8,128)(2,1)S(1)}, bf16[256,1024]{1,0:T(8,128)(2,1)S(1)}, u32[]{:S(2)}, u32[]{:S(2)}) %collective-permute-start.41) | collective-permute-done | bytes 524320 | tf_op jit(solution)/shard_map/ppermute | solution.py:16
  159.7 2.6 %upper_grads.1 = bf16[256,2,1024]{2,1,0:T(2,128)(2,1)} custom-call(s32[2]{0:T(128)S(1)} %pad_add_fusion.ids_ref.refs_0_, bf16[896,512]{1,0:T(8,128)(2,1)S(1)} %collective-permute-done.39.far_ref, bf16[1792,256]{1,0:T(8,128)(2,1)S(1)} %collective-permute-done.40.near_ref, bf16[256,1024]{1,0:T(8,128)(2,1)S(1)} %side_by_side.1.refs_0_, ...), custom_call_target="tpu_custom_call" | custom-call | tf_op jit(solution)/shard_map/upper_grads/pallas_call | solution.py:598
  (99 shorter events, 47.9 us)
Async XLA Ops:
  5.6 24.1 %collective-permute-start.8 = (bf16[512,896]{1,0:T(8,128)(2,1)S(1)}, bf16[512,896]{1,0:T(8,128)(2,1)S(1)}, u32[]{:S(2)}, u32[]{:S(2)}) collective-permute-start(bf16[512,896]{1,0:T(8,128)(2,1)S(1)} %pack.3), channel_id=1, source_target_pairs={{0,4},{4,0},{8,12},{12,8},{16,20},{20,16},{24,28},{28,24},{1,5},{5... | collective-permute-start | bytes 2752520 | tf_op jit(solution)/shard_map/ppermute | solution.py:16
  8.6 8.8 %collective-permute-start.3 = (bf16[512,128]{1,0:T(8,128)(2,1)S(1)}, bf16[512,128]{1,0:T(8,128)(2,1)S(1)}, u32[]{:S(2)}, u32[]{:S(2)}) collective-permute-start(bf16[512,128]{1,0:T(8,128)(2,1)S(1)} %get-tuple-element.100), channel_id=1, source_target_pairs={{0,16},{4,20},{8,24},{12,28},{16,0},{20,4},{24,8},{28,12},{1,17},{... | collective-permute-start | bytes 393224 | tf_op jit(solution)/shard_map/ppermute | solution.py:16
  13.4 9.5 %collective-permute-start.4 = (bf16[512,256]{1,0:T(8,128)(2,1)S(1)}, bf16[512,256]{1,0:T(8,128)(2,1)S(1)}, u32[]{:S(2)}, u32[]{:S(2)}) collective-permute-start(bf16[512,256]{1,0:T(8,128)(2,1)S(1)} %get-tuple-element.103), channel_id=1, source_target_pairs={{0,8},{4,12},{8,0},{12,4},{16,24},{20,28},{24,16},{28,20},{1,9},{5... | collective-permute-start | bytes 786440 | tf_op jit(solution)/shard_map/ppermute | solution.py:16
  15.0 9.2 %collective-permute-start.1 = (bf16[4,128,256]{2,1,0:T(8,128)(2,1)S(1)}, bf16[4,128,256]{2,1,0:T(8,128)(2,1)S(1)}, u32[]{:S(2)}, u32[]{:S(2)}) collective-permute-start(bf16[4,128,256]{2,1,0:T(8,128)(2,1)S(1)} %get-tuple-element.95), channel_id=1, source_target_pairs={{0,2},{1,3},{2,0},{3,1},{4,6},{5,7},{6,4},{7,5},{8,10},{9,11},{10,... | collective-permute-start | bytes 786440 | tf_op jit(solution)/shard_map/ppermute | solution.py:16
  17.4 10.8 %collective-permute-start.2 = (bf16[4,128,256]{2,1,0:T(8,128)(2,1)S(1)}, bf16[4,128,256]{2,1,0:T(8,128)(2,1)S(1)}, u32[]{:S(2)}, u32[]{:S(2)}) collective-permute-start(bf16[4,128,256]{2,1,0:T(8,128)(2,1)S(1)} %get-tuple-element.96), channel_id=1, source_target_pairs={{0,3},{1,2},{2,1},{3,0},{4,7},{5,6},{6,5},{7,4},{8,11},{9,10},{10,... | collective-permute-start | bytes 786440 | tf_op jit(solution)/shard_map/ppermute | solution.py:16
  29.7 25.7 %collective-permute-start.9 = (bf16[512,896]{1,0:T(8,128)(2,1)S(1)}, bf16[512,896]{1,0:T(8,128)(2,1)S(1)}, u32[]{:S(2)}, u32[]{:S(2)}) collective-permute-start(bf16[512,896]{1,0:T(8,128)(2,1)S(1)} %collective-permute-done.8.refs_0_), channel_id=1, source_target_pairs={{0,1},{1,0},{2,3},{3,2},{4,5},{5,4},{6,7},{7,6},{8,9},{9,8},{10,11... | collective-permute-start | bytes 2752520 | tf_op jit(solution)/shard_map/ppermute | solution.py:16
  30.6 8.3 %collective-permute-start.15 = (bf16[512,256]{1,0:T(8,128)(2,1)S(1)}, bf16[512,256]{1,0:T(8,128)(2,1)S(1)}, u32[]{:S(2)}, u32[]{:S(2)}) collective-permute-start(bf16[512,256]{1,0:T(8,128)(2,1)S(1)} %pack.4.refs_0_), channel_id=1, source_target_pairs={{0,8},{4,12},{8,0},{12,4},{16,24},{20,28},{24,16},{28,20},{1,9},{5... | collective-permute-start | bytes 786440 | tf_op jit(solution)/shard_map/ppermute | solution.py:16
  31.1 10.0 %collective-permute-start.6 = (bf16[128,1024]{1,0:T(8,128)(2,1)S(1)}, bf16[128,1024]{1,0:T(8,128)(2,1)S(1)}, u32[]{:S(2)}, u32[]{:S(2)}) collective-permute-start(bf16[128,1024]{1,0:T(8,128)(2,1)S(1)} %get-tuple-element.109), channel_id=1, source_target_pairs={{0,1},{1,0},{2,3},{3,2},{4,5},{5,4},{6,7},{7,6},{8,9},{9,8},{10,11... | collective-permute-start | bytes 786440 | tf_op jit(solution)/shard_map/ppermute | solution.py:16
  39.0 12.1 %collective-permute-start.16 = (bf16[512,384]{1,0:T(8,128)(2,1)S(1)}, bf16[512,384]{1,0:T(8,128)(2,1)S(1)}, u32[]{:S(2)}, u32[]{:S(2)}) collective-permute-start(bf16[512,384]{1,0:T(8,128)(2,1)S(1)} %pack.5.refs_1_), channel_id=1, source_target_pairs={{0,4},{4,0},{8,12},{12,8},{16,20},{20,16},{24,28},{28,24},{1,5},{5... | collective-permute-start | bytes 1179656 | tf_op jit(solution)/shard_map/ppermute | solution.py:16
  39.6 15.3 %collective-permute-start.11 = (bf16[512,256]{1,0:T(8,128)(2,1)S(1)}, bf16[512,256]{1,0:T(8,128)(2,1)S(1)}, u32[]{:S(2)}, u32[]{:S(2)}) collective-permute-start(bf16[512,256]{1,0:T(8,128)(2,1)S(1)} %collective-permute-done.4.refs_1_), channel_id=1, source_target_pairs={{0,4},{4,0},{8,12},{12,8},{16,20},{20,16},{24,28},{28,24},{1,5},{5... | collective-permute-start | bytes 786440 | tf_op jit(solution)/shard_map/ppermute | solution.py:16
  41.0 13.9 %collective-permute-start.5 = (bf16[128,1024]{1,0:T(8,128)(2,1)S(1)}, bf16[128,1024]{1,0:T(8,128)(2,1)S(1)}, u32[]{:S(2)}, u32[]{:S(2)}) collective-permute-start(bf16[128,1024]{1,0:T(8,128)(2,1)S(1)} %get-tuple-element.99), channel_id=1, source_target_pairs={{0,1},{1,0},{2,3},{3,2},{4,5},{5,4},{6,7},{7,6},{8,9},{9,8},{10,11... | collective-permute-start | bytes 786440 | tf_op jit(solution)/shard_map/ppermute | solution.py:16
  41.2 15.0 %collective-permute-start.7 = (bf16[128,1024]{1,0:T(8,128)(2,1)S(1)}, bf16[128,1024]{1,0:T(8,128)(2,1)S(1)}, u32[]{:S(2)}, u32[]{:S(2)}) collective-permute-start(bf16[128,1024]{1,0:T(8,128)(2,1)S(1)} %pair_product.1), channel_id=1, source_target_pairs={{0,2},{1,3},{2,0},{3,1},{4,6},{5,7},{6,4},{7,5},{8,10},{9,11},{10,... | collective-permute-start | bytes 786440 | tf_op jit(solution)/shard_map/ppermute | solution.py:16
  51.1 15.8 %collective-permute-start.17 = (bf16[512,384]{1,0:T(8,128)(2,1)S(1)}, bf16[512,384]{1,0:T(8,128)(2,1)S(1)}, u32[]{:S(2)}, u32[]{:S(2)}) collective-permute-start(bf16[512,384]{1,0:T(8,128)(2,1)S(1)} %pack.5.refs_1_), channel_id=1, source_target_pairs={{0,1},{1,0},{2,3},{3,2},{4,5},{5,4},{6,7},{7,6},{8,9},{9,8},{10,11... | collective-permute-start | bytes 1179656 | tf_op jit(solution)/shard_map/ppermute | solution.py:16
  54.9 11.9 %collective-permute-start.18 = (bf16[512,384]{1,0:T(8,128)(2,1)S(1)}, bf16[512,384]{1,0:T(8,128)(2,1)S(1)}, u32[]{:S(2)}, u32[]{:S(2)}) collective-permute-start(bf16[512,384]{1,0:T(8,128)(2,1)S(1)} %collective-permute-done.16.refs_2_), channel_id=1, source_target_pairs={{0,1},{1,0},{2,3},{3,2},{4,5},{5,4},{6,7},{7,6},{8,9},{9,8},{10,11... | collective-permute-start | bytes 1179656 | tf_op jit(solution)/shard_map/ppermute | solution.py:16
  54.9 8.4 %collective-permute-start.12 = (bf16[512,256]{1,0:T(8,128)(2,1)S(1)}, bf16[512,256]{1,0:T(8,128)(2,1)S(1)}, u32[]{:S(2)}, u32[]{:S(2)}) collective-permute-start(bf16[512,256]{1,0:T(8,128)(2,1)S(1)} %collective-permute-done.4.refs_1_), channel_id=1, source_target_pairs={{0,1},{1,0},{2,3},{3,2},{4,5},{5,4},{6,7},{7,6},{8,9},{9,8},{10,11... | collective-permute-start | bytes 786440 | tf_op jit(solution)/shard_map/ppermute | solution.py:16
  55.4 7.9 %collective-permute-start.13 = (bf16[512,256]{1,0:T(8,128)(2,1)S(1)}, bf16[512,256]{1,0:T(8,128)(2,1)S(1)}, u32[]{:S(2)}, u32[]{:S(2)}) collective-permute-start(bf16[512,256]{1,0:T(8,128)(2,1)S(1)} %collective-permute-done.11.refs_2_), channel_id=1, source_target_pairs={{0,1},{1,0},{2,3},{3,2},{4,5},{5,4},{6,7},{7,6},{8,9},{9,8},{10,11... | collective-permute-start | bytes 786440 | tf_op jit(solution)/shard_map/ppermute | solution.py:16
  56.8 5.9 %collective-permute-start.10 = (bf16[64,1024]{1,0:T(8,128)(2,1)S(1)}, bf16[64,1024]{1,0:T(8,128)(2,1)S(1)}, u32[]{:S(2)}, u32[]{:S(2)}) collective-permute-start(bf16[64,1024]{1,0:T(8,128)(2,1)S(1)} %get-tuple-element.113), channel_id=1, source_target_pairs={{0,4},{4,0},{8,12},{12,8},{16,20},{20,16},{24,28},{28,24},{1,5},{5... | collective-permute-start | bytes 393224 | tf_op jit(solution)/shard_map/ppermute | solution.py:16
  62.8 14.9 %collective-permute-start.20 = (bf16[128,1024]{1,0:T(8,128)(2,1)S(1)}, bf16[128,1024]{1,0:T(8,128)(2,1)S(1)}, u32[]{:S(2)}, u32[]{:S(2)}) collective-permute-start(bf16[128,1024]{1,0:T(8,128)(2,1)S(1)} %get-tuple-element.173.refs_6_.refs_0_.refs_4_), channel_id=1, source_target_pairs={{0,4},{4,0},{8,12},{12,8},{16,20},{20,16},{24,28},{28,24},{1,5},{5... | collective-permute-start | bytes 786440 | tf_op jit(solution)/shard_map/ppermute | solution.py:16
  72.6 7.0 %collective-permute-start.22 = (bf16[32,1024]{1,0:T(8,128)(2,1)S(1)}, bf16[32,1024]{1,0:T(8,128)(2,1)S(1)}, u32[]{:S(2)}, u32[]{:S(2)}) collective-permute-start(bf16[32,1024]{1,0:T(8,128)(2,1)S(1)} %get-tuple-element.133.refs_4_.refs_5_.refs_11_.refs_9_), channel_id=1, source_target_pairs={{0,16},{4,20},{8,24},{12,28},{16,0},{20,4},{24,8},{28,12},{1,17},{... | collective-permute-start | bytes 196616 | tf_op jit(solution)/shard_map/ppermute | solution.py:16
  80.2 7.5 %collective-permute-start.24 = (bf16[128,1024]{1,0:T(8,128)(2,1)S(1)}, bf16[128,1024]{1,0:T(8,128)(2,1)S(1)}, u32[]{:S(2)}, u32[]{:S(2)}) collective-permute-start(bf16[128,1024]{1,0:T(8,128)(2,1)S(1)} %get-tuple-element.135), channel_id=1, source_target_pairs={{0,8},{4,12},{8,0},{12,4},{16,24},{20,28},{24,16},{28,20},{1,9},{5... | collective-permute-start | bytes 786440 | tf_op jit(solution)/shard_map/ppermute | solution.py:16
  88.3 5.9 %collective-permute-start.25 = (bf16[64,1024]{1,0:T(8,128)(2,1)S(1)}, bf16[64,1024]{1,0:T(8,128)(2,1)S(1)}, u32[]{:S(2)}, u32[]{:S(2)}) collective-permute-start(bf16[64,1024]{1,0:T(8,128)(2,1)S(1)} %get-tuple-element.136.refs_3_), channel_id=1, source_target_pairs={{0,4},{4,0},{8,12},{12,8},{16,20},{20,16},{24,28},{28,24},{1,5},{5... | collective-permute-start | bytes 393224 | tf_op jit(solution)/shard_map/ppermute | solution.py:16
  94.8 6.5 %collective-permute-start.26 = (bf16[64,1024]{1,0:T(8,128)(2,1)S(1)}, bf16[64,1024]{1,0:T(8,128)(2,1)S(1)}, u32[]{:S(2)}, u32[]{:S(2)}) collective-permute-start(bf16[64,1024]{1,0:T(8,128)(2,1)S(1)} %get-tuple-element.138), channel_id=1, source_target_pairs={{0,4},{4,0},{8,12},{12,8},{16,20},{20,16},{24,28},{28,24},{1,5},{5... | collective-permute-start | bytes 393224 | tf_op jit(solution)/shard_map/ppermute | solution.py:16
  101.3 15.5 %collective-permute-start.30 = (bf16[256,1024]{1,0:T(8,128)(2,1)S(1)}, bf16[256,1024]{1,0:T(8,128)(2,1)S(1)}, u32[]{:S(2)}, u32[]{:S(2)}) collective-permute-start(bf16[256,1024]{1,0:T(8,128)(2,1)S(1)} %get-tuple-element.146), channel_id=1, source_target_pairs={{0,4},{4,0},{8,12},{12,8},{16,20},{20,16},{24,28},{28,24},{1,5},{5... | collective-permute-start | bytes 1572872 | tf_op jit(solution)/shard_map/ppermute | solution.py:16
  118.4 26.8 %collective-permute-start.39 = (bf16[896,512]{1,0:T(8,128)(2,1)S(1)}, bf16[896,512]{1,0:T(8,128)(2,1)S(1)}, u32[]{:S(2)}, u32[]{:S(2)}) collective-permute-start(bf16[896,512]{1,0:T(8,128)(2,1)S(1)} %get-tuple-element.172), channel_id=1, source_target_pairs={{0,2},{1,3},{2,0},{3,1},{4,6},{5,7},{6,4},{7,5},{8,10},{9,11},{10,... | collective-permute-start | bytes 2752520 | tf_op jit(solution)/shard_map/ppermute | solution.py:16
  120.0 6.6 %collective-permute-start.31 = (bf16[32,1024]{1,0:T(8,128)(2,1)S(1)}, bf16[32,1024]{1,0:T(8,128)(2,1)S(1)}, u32[]{:S(2)}, u32[]{:S(2)}) collective-permute-start(bf16[32,1024]{1,0:T(8,128)(2,1)S(1)} %get-tuple-element.149), channel_id=1, source_target_pairs={{0,8},{4,12},{8,0},{12,4},{16,24},{20,28},{24,16},{28,20},{1,9},{5... | collective-permute-start | bytes 196616 | tf_op jit(solution)/shard_map/ppermute | solution.py:16
  121.4 5.2 %collective-permute-start.32 = (bf16[32,512]{1,0:T(8,128)(2,1)S(1)}, bf16[32,512]{1,0:T(8,128)(2,1)S(1)}, u32[]{:S(2)}, u32[]{:S(2)}) collective-permute-start(bf16[32,512]{1,0:T(8,128)(2,1)S(1)} %get-tuple-element.151), channel_id=1, source_target_pairs={{0,16},{4,20},{8,24},{12,28},{16,0},{20,4},{24,8},{28,12},{1,17},{... | collective-permute-start | bytes 98312 | tf_op jit(solution)/shard_map/ppermute | solution.py:16
  128.0 6.4 %collective-permute-start.33 = (bf16[64,1024]{1,0:T(8,128)(2,1)S(1)}, bf16[64,1024]{1,0:T(8,128)(2,1)S(1)}, u32[]{:S(2)}, u32[]{:S(2)}) collective-permute-start(bf16[64,1024]{1,0:T(8,128)(2,1)S(1)} %get-tuple-element.153), channel_id=1, source_target_pairs={{0,4},{4,0},{8,12},{12,8},{16,20},{20,16},{24,28},{28,24},{1,5},{5... | collective-permute-start | bytes 393224 | tf_op jit(solution)/shard_map/ppermute | solution.py:16
  136.2 8.0 %collective-permute-start.37 = (bf16[128,896]{1,0:T(8,128)(2,1)S(1)}, bf16[128,896]{1,0:T(8,128)(2,1)S(1)}, u32[]{:S(2)}, u32[]{:S(2)}) collective-permute-start(bf16[128,896]{1,0:T(8,128)(2,1)S(1)} %get-tuple-element.162), channel_id=1, source_target_pairs={{0,4},{4,0},{8,12},{12,8},{16,20},{20,16},{24,28},{28,24},{1,5},{5... | collective-permute-start | bytes 688136 | tf_op jit(solution)/shard_map/ppermute | solution.py:16
  136.7 8.4 %collective-permute-start.36 = (bf16[128,1024]{1,0:T(8,128)(2,1)S(1)}, bf16[128,1024]{1,0:T(8,128)(2,1)S(1)}, u32[]{:S(2)}, u32[]{:S(2)}) collective-permute-start(bf16[128,1024]{1,0:T(8,128)(2,1)S(1)} %get-tuple-element.159), channel_id=1, source_target_pairs={{0,2},{1,3},{2,0},{3,1},{4,6},{5,7},{6,4},{7,5},{8,10},{9,11},{10,... | collective-permute-start | bytes 786440 | tf_op jit(solution)/shard_map/ppermute | solution.py:16
  144.2 13.6 %collective-permute-start.41 = (bf16[256,1024]{1,0:T(8,128)(2,1)S(1)}, bf16[256,1024]{1,0:T(8,128)(2,1)S(1)}, u32[]{:S(2)}, u32[]{:S(2)}) collective-permute-start(bf16[256,1024]{1,0:T(8,128)(2,1)S(1)} %side_by_side.1.refs_0_), channel_id=1, source_target_pairs={{0,2},{1,3},{2,0},{3,1},{4,6},{5,7},{6,4},{7,5},{8,10},{9,11},{10,... | collective-permute-start | bytes 1572872 | tf_op jit(solution)/shard_map/ppermute | solution.py:16
  145.9 13.8 %collective-permute-start.40 = (bf16[1792,256]{1,0:T(8,128)(2,1)S(1)}, bf16[1792,256]{1,0:T(8,128)(2,1)S(1)}, u32[]{:S(2)}, u32[]{:S(2)}) collective-permute-start(bf16[1792,256]{1,0:T(8,128)(2,1)S(1)} %near_inputs.1), channel_id=1, source_target_pairs={{0,1},{1,0},{2,3},{3,2},{4,5},{5,4},{6,7},{7,6},{8,9},{9,8},{10,11... | collective-permute-start | bytes 2752520 | tf_op jit(solution)/shard_map/ppermute | solution.py:16
  146.5 11.3 %collective-permute-start.42 = (bf16[256,1024]{1,0:T(8,128)(2,1)S(1)}, bf16[256,1024]{1,0:T(8,128)(2,1)S(1)}, u32[]{:S(2)}, u32[]{:S(2)}) collective-permute-start(bf16[256,1024]{1,0:T(8,128)(2,1)S(1)} %side_by_side.1.refs_0_), channel_id=1, source_target_pairs={{0,1},{1,0},{2,3},{3,2},{4,5},{5,4},{6,7},{7,6},{8,9},{9,8},{10,11... | collective-permute-start | bytes 1572872 | tf_op jit(solution)/shard_map/ppermute | solution.py:16
  (18 other events, 102.1 us)

commit v6 on v5

--- a/solution.py
+++ b/solution.py
@@ -61,7 +61,7 @@
 
 
 def place_kernel(slots, depth, ids_ref, map_ref, regions_ref, cotangent_ref, *rest):
-    outs, cotangent_out, wide = rest[:CHILDREN], rest[CHILDREN], rest[CHILDREN + 1]
+    outs, keep_ref, send_ref, wide = rest[:CHILDREN], *rest[CHILDREN:]
     rows = regions_ref.shape[0] // slots
     parts = wide.shape[0]
     for part in range(parts):
@@ -72,13 +72,19 @@
     row = lax.broadcasted_iota(jnp.int32, (rows, rows), 0)
     col = lax.broadcasted_iota(jnp.int32, (rows, rows), 1)
     select = bf16(jnp.bitwise_xor(row, flip) == col)
+    block = rows >> depth
+    wanted = jnp.bitwise_and(row, block - 1)
+    for level in range(depth):
+        wanted = wanted + bit_of(row // block, level) * (block << (depth - 1 - level))
+    pick = bf16(jnp.bitwise_xor(wanted, flip) == col)
     left = cotangent_ref[...]
     picked = 0.0
     for _ in range(3):
         top = bf16(left)
         left = left - f32(top)
-        picked = picked + matmul(select, top)
-    cotangent_out[...] = picked
+        picked = picked + matmul(pick, top)
+    keep_ref[...] = picked[: rows // 2]
+    send_ref[...] = picked[rows // 2 :]
     for offset in range(CHILDREN):
         node = jnp.bitwise_xor(ids_ref[1], offset)
         for child in range(CHILDREN):
@@ -96,9 +102,9 @@
     return pl.pallas_call(
         functools.partial(place_kernel, slots, depth),
         out_shape=[jax.ShapeDtypeStruct((CHILDREN, rows, feats), jnp.bfloat16)] * CHILDREN
-        + [jax.ShapeDtypeStruct(cotangent.shape, cotangent.dtype)],
+        + [jax.ShapeDtypeStruct((rows // 2, cotangent.shape[1]), cotangent.dtype)] * 2,
         in_specs=[smem_block(), smem_block(), whole_block(), whole_block()],
-        out_specs=[whole_block()] * (CHILDREN + 1),
+        out_specs=[whole_block()] * (CHILDREN + 2),
         scratch_shapes=[pltpu.VMEM((feats // 128, rows * slots, 128), jnp.float32)],
         compiler_params=pltpu.CompilerParams(vmem_limit_bytes=7 * MIB),
         name="place",
@@ -266,6 +272,7 @@
     span = width >> depth
     for side in range(2):
         outs[3 * depth + side][...] = split[side, :, width - span :]
+        outs[3 * depth + 2][:, side * span : (side + 1) * span] = split[side, rows, width - span :]
 
 
 def cut_maps(maps, ids, depth):
@@ -276,7 +283,7 @@
         shapes = []
         for span in spans:
             shapes += [(width, span), (half, span), (half, span)]
-        shapes += [(width, spans[-1])] * 2
+        shapes += [(width, spans[-1])] * 2 + [(half, 2 * spans[-1])]
         outs = pl.pallas_call(
             functools.partial(cut_kernel, depth),
             out_shape=[jax.ShapeDtypeStruct(shape, maps.dtype) for shape in shapes],
@@ -297,6 +304,8 @@
             for which in (side, 1 - side):
                 outs.append(lax.dynamic_slice(maps, (which, core * half, first), (1, half, span))[0])
         outs += [maps[0, :, width - spans[-1] :], maps[1, :, width - spans[-1] :]]
+        both = jnp.concatenate(outs[-2:], axis=1)
+        outs.append(lax.dynamic_slice_in_dim(both, core * half, half, 0))
     return [outs[3 * i : 3 * i + 3] for i in range(depth)], outs[3 * depth :]
 
 
@@ -348,15 +357,64 @@
     return out
 
 
+def assemble_head_kernel(spots, count, ids_ref, left_ref, right_ref, *refs):
+    out_ref = refs[-1]
+    width, span = left_ref.shape
+    half, total = width // 2, out_ref.shape[1] // 2
+    out_ref[:, :span] = left_ref[...]
+    out_ref[:, total : total + span] = right_ref[...]
+    own_core = bit_of(ids_ref[1], 0)
+    for offset, index, at in spots:
+        for ref, core in ((refs[index], own_core), (refs[count + index], 1 - own_core)):
+            rows = pl.ds(pl.multiple_of(core * half, half), half)
+            for side in range(2):
+                col = side * total + (offset // 2) * span
+                out_ref[rows, col : col + span] = ref[:, at + side * span : at + (side + 1) * span]
+
+
+def assemble_head(left, right, pieces, ids):
+    width, span = left.shape
+    total = span * (len(pieces) + 1)
+    mine, other, spots = [], [], []
+    for offset, (near_half, far_half, at) in pieces.items():
+        known = [i for i, array in enumerate(mine) if array is near_half]
+        if not known:
+            mine.append(near_half)
+            other.append(far_half)
+            known = [len(mine) - 1]
+        spots.append((offset, known[0], at))
+    if span % 128 == 0:
+        return pl.pallas_call(
+            functools.partial(assemble_head_kernel, spots, len(mine)),
+            out_shape=jax.ShapeDtypeStruct((width, 2 * total), left.dtype),
+            in_specs=[smem_block()] + [whole_block()] * (2 * len(mine) + 2),
+            out_specs=whole_block(),
+            compiler_params=pltpu.CompilerParams(vmem_limit_bytes=8 * MIB),
+            name="assemble_head",
+        )(ids, left, right, *mine, *other)
+    core = bit_of(ids[1], 0)
+    out = jnp.zeros((width, 2 * total), left.dtype)
+    out = lax.dynamic_update_slice(out, left, (0, 0))
+    out = lax.dynamic_update_slice(out, right, (0, total))
+    for offset, index, at in spots:
+        for array, which in ((mine[index], core), (other[index], 1 - core)):
+            for side in range(2):
+                part = array[:, at + side * span : at + (side + 1) * span]
+                col = side * total + (offset // 2) * span
+                out = lax.dynamic_update_slice(out, part, (which * (width // 2), col))
+    return out
+
+
 def after(value, *others):
     return lax.optimization_barrier((value, *others))[0]
 
 
 class MapGather:
-    def __init__(self, blocks, ids):
-        self.blocks, self.ids = blocks, ids
+    def __init__(self, blocks, head_half, ids):
+        self.blocks, self.ids = blocks + [(None, head_half, None)], ids
         self.depth = len(blocks)
-        self.spans = [block[0].shape[1] for block in blocks]
+        blocks = self.blocks
+        self.spans = [block[1].shape[1] for block in blocks]
         self.held = [{0: (block[1], 0)} for block in blocks]
         self.other = {}
         pieces = [(blocks[0][2], 0, self.spans[0])]
@@ -385,8 +443,8 @@
                 value = pieces[0][0]
             else:
                 value = pack(pieces)
-            for place, offset in enumerate(offsets):
-                if offset > 0:
+            if 0 not in offsets:
+                for place, offset in enumerate(offsets):
                     self.held[level][offset] = (value, place * self.spans[level])
         got = partner(value, "sub", 1 << stage)
         for place, offset in enumerate(offsets):
@@ -398,12 +456,18 @@
             if offset > 0 and id(array) not in self.other:
                 self.other[id(array)] = (array, partner(after(array, gate), "rep", 1))
 
+    def head(self, left, right):
+        return assemble_head(left, right, self.pieces(self.depth), self.ids)
+
     def weight(self, level):
+        return assemble(self.blocks[level][0], self.pieces(level), self.ids)
+
+    def pieces(self, level):
         pieces = {}
         for offset, (array, at) in self.held[level].items():
             if offset > 0:
                 pieces[offset] = (array, self.other[id(array)][1], at)
-        return assemble(self.blocks[level][0], pieces, self.ids)
+        return pieces
 
 
 class View:
@@ -439,52 +503,57 @@
 
 
 def join_all(pieces):
-    if all(piece.shape[0] % 16 == 0 for piece in pieces):
+    if len(pieces) == 1:
+        return pieces[0]
+    if pieces[0].dtype == jnp.float32 or all(piece.shape[0] % 16 == 0 for piece in pieces):
         return jnp.concatenate(pieces, axis=0)
     wide = lax.optimization_barrier(tuple(f32(piece) for piece in pieces))
     return bf16(lax.optimization_barrier(jnp.concatenate(wide, axis=0)))
 
 
-def step(body, name, args, stacks=(), halves=(), level=0, far=None, ids=None, limit=8):
-    groups = [list(stacks)] + [list(group) for group in halves] + [list(far or ())]
-    views = [view for group in groups for view in group]
+def step(body, name, args, parts=(), stacks=(), halves=(), fixed=(), level=0, far=None, **options):
+    groups = [[view] for view in parts] + [list(group) for group in stacks]
+    halved = [list(group) for group in (*halves, *fixed)]
+    views = [view for group in (*groups, *halved, far or ()) for view in group]
     arrays = list(args)
     for view in views:
         if not any(array is view.array for array in arrays):
             arrays.append(view.array)
 
     def cut(values, group):
-        parts = []
+        pieces = []
         for view in group:
             index = next(i for i, array in enumerate(arrays) if array is view.array)
-            parts.append(values[index][slice(*view.rows), slice(*view.cols)])
-        return join_all(parts)
+            pieces.append(values[index][slice(*view.rows), slice(*view.cols)])
+        return join_all(pieces)
 
     def whole(ids, *values):
-        results = list(body(*values[: len(args)]))
-        if stacks:
-            results.append(cut(values, groups[0]))
-        if halves:
-            own = bit_of(ids[0], level) == 1
-            sends = []
-            for group in groups[1:-1]:
-                full = cut(values, group)
-                half = full.shape[1] // 2
-                low, high = full[:, :half], full[:, half:]
-                results.append(jnp.where(own, high, low))
-                sends.append(jnp.where(own, low, high))
+        given = [cut(values, group) for group in groups[: len(parts)]]
+        results = list(body(*values[: len(args)], *given))
+        results += [cut(values, group) for group in groups[len(parts) :]]
+        sends = []
+        for index, group in enumerate(halved):
+            full = cut(values, group)
+            half = full.shape[1] // 2
+            low, high = full[:, :half], full[:, half:]
+            if index < len(halves):
+                own = bit_of(ids[0], level) == 1
+                low, high = jnp.where(own, high, low), jnp.where(own, low, high)
+            results.append(low)
+            sends.append(high)
+        if sends:
             results.append(jnp.concatenate(sends, axis=1))
         if far:
-            full = cut(values, groups[-1])
+            full = cut(values, far)
             half = full.shape[1] // 2
             results.append(jnp.where(bit_of(ids[1], 1) == 1, full[:, :half], full[:, half:]))
         return results
 
     plain = not all(view.aligned() for view in views)
-    return fused(whole, name, *arrays, limit=limit, ids=ids, plain=plain)
-
-
-def near_inputs_kernel(spots, ids_ref, far_ref, *refs):
+    return fused(whole, name, *arrays, plain=plain, **options)
+
+
+def near_inputs_kernel(spots, ids_ref, first_ref, second_ref, *refs):
     out_ref = refs[-1]
     quarter = out_ref.shape[1]
     other = 1 - bit_of(ids_ref[1], 0)
@@ -493,7 +562,11 @@
     for index, (first, last), _ in spots:
         out_ref[at : at + last - first] = refs[index][first:last, lanes]
         at += last - first
-    out_ref[at:] = far_ref[:, pl.ds(pl.multiple_of(other * quarter, quarter), quarter)]
+    for ref in (first_ref, second_ref):
+        count = ref.shape[0]
+        lanes = pl.ds(pl.multiple_of(other * quarter, quarter), quarter)
+        out_ref[at : at + count] = ref[:, lanes]
+        at += count
 
 
 def near_inputs(views, got, ids):
@@ -503,18 +576,21 @@
         other = 1 - bit_of(ids[1], 0)
         where = (bit_of(ids[1], 1) * 2 + other) * quarter
         own = lax.dynamic_slice_in_dim(full, where, quarter, 1)
+        far = jnp.concatenate(got, axis=0)
         return jnp.concatenate(
-            [own, lax.dynamic_slice_in_dim(got, other * quarter, quarter, 1)], axis=0
+            [own, lax.dynamic_slice_in_dim(far, other * quarter, quarter, 1)], axis=0
         )
     arrays, spots = spots_of(views)
     return pl.pallas_call(
         functools.partial(near_inputs_kernel, spots),
-        out_shape=jax.ShapeDtypeStruct((2 * got.shape[0], quarter), jnp.bfloat16),
-        in_specs=[smem_block()] + [whole_block()] * (len(arrays) + 1),
+        out_shape=jax.ShapeDtypeStruct(
+            (2 * sum(array.shape[0] for array in got), quarter), jnp.bfloat16
+        ),
+        in_specs=[smem_block()] + [whole_block()] * (len(arrays) + 2),
         out_specs=whole_block(),
         compiler_params=pltpu.CompilerParams(vmem_limit_bytes=8 * MIB),
         name="near_inputs",
-    )(ids, got, *arrays)
+    )(ids, *got, *arrays)
 
 
 def side_by_side_kernel(groups, *refs):
@@ -552,19 +628,23 @@
     )(*arrays)
 
 
-def upper_grads_kernel(spots, spans, rows, ids_ref, far_ref, near_ref, *refs):
+def upper_grads_kernel(spots, spans, rows, ids_ref, first_ref, second_ref, near_ref, *refs):
     grads, inputs, out_ref, both = refs[:4], refs[4:-2], refs[-2], refs[-1]
     quarter = out_ref.shape[0]
     core, far = bit_of(ids_ref[1], 0), bit_of(ids_ref[1], 1)
     lanes = pl.ds(pl.multiple_of((far * 2 + core) * quarter, quarter), quarter)
     far_lanes = pl.ds(pl.multiple_of(core * quarter, quarter), quarter)
-    total = far_ref.shape[0]
+    total = first_ref.shape[0] + second_ref.shape[0]
     col = 0
     for level, span in enumerate(spans):
         for turn in range(2):
             here, at = spots[level][turn]
             pieces = [inputs[i][slice(*edges), lanes] for i, edges, _ in here]
-            pieces.append(far_ref[at : at + rows, far_lanes])
+            if at < first_ref.shape[0]:
+                pieces.append(first_ref[at : at + rows, far_lanes])
+            else:
+                there = at - first_ref.shape[0]
+                pieces.append(second_ref[there : there + rows, far_lanes])
             pieces.append(near_ref[at : at + rows])
             pieces.append(near_ref[total + at : total + at + rows])
             grad = jnp.concatenate(
@@ -585,10 +665,9 @@
     rows = sum(view.shape[0] for view in entries[0][0])
     spans = [width >> (level + 1) for level in range(depth)] + [width >> depth]
     views = [view for entry in entries for turn in entry for view in turn]
-    starts, at = [], 0
-    for level in range(depth + 1):
-        starts.append([at, at + rows if level < depth else at])
-        at += 2 * rows
+    starts = [[0, rows]]
+    starts += [[(2 * level + 1) * rows, (2 * level + 2) * rows] for level in range(1, depth)]
+    starts.append([2 * rows, 2 * rows])
     if all(view.aligned() for view in views) and spans[-1] % 128 == 0:
         arrays, flat = spots_of(views)
         spots = [
@@ -598,14 +677,15 @@
         return pl.pallas_call(
             functools.partial(upper_grads_kernel, spots, spans, rows),
             out_shape=jax.ShapeDtypeStruct((width // 4, 2, width), jnp.bfloat16),
-            in_specs=[smem_block()] + [whole_block()] * (len(arrays) + 6),
+            in_specs=[smem_block()] + [whole_block()] * (len(arrays) + 7),
             out_specs=whole_block(),
             scratch_shapes=[pltpu.VMEM((2, width // 4, width), jnp.bfloat16)],
             compiler_params=pltpu.CompilerParams(vmem_limit_bytes=16 * MIB),
             name="upper_grads",
-        )(ids, far_got, near_got, *grads, *arrays)
+        )(ids, *far_got, near_got, *grads, *arrays)
     quarter = width // 4
     core, far = bit_of(ids[1], 0), bit_of(ids[1], 1)
+    far_got = jnp.concatenate(far_got, axis=0)
     total = far_got.shape[0]
     parts, col = [], 0
     for level, span in enumerate(spans):
@@ -650,25 +730,17 @@
     return (bf16(joined * rms_factor(joined)),)
 
 
-def head_body(cotangent, left, right, low, high):
+def head_body(low, high, maps, *cotangents):
     root = join([low, high])
-    value = matmul(root, left)
-    gating = jax.nn.sigmoid(matmul(root, right))
+    cotangent = jnp.concatenate(cotangents, axis=1)
+    half = maps.shape[1] // 2
+    both = matmul(root, maps)
+    value, gating = both[:, :half], jax.nn.sigmoid(both[:, half:])
     grad_value = bf16(cotangent * gating)
     grad_gate = bf16(cotangent * value * gating * (1.0 - gating))
-    back = matmul_t(grad_value, left) + matmul_t(grad_gate, right)
-    half = root.shape[0] // 2
-    return root, grad_value, grad_gate, back[:half], bf16(back[half:])
-
-
-def joined(low, high):
-    return (join([low, high]),)
-
-
-def partial_sum(own, got):
-    total = own + f32(got)
-    half = total.shape[0] // 2
-    return total[:half], bf16(total[half:])
+    back = matmul_t(grad_value, maps[:, :half]) + matmul_t(grad_gate, maps[:, half:])
+    rows = root.shape[0] // 2
+    return root, grad_value, grad_gate, back[:rows], bf16(back[rows:])
 
 
 def level_back(grad_msg, own_up, other_up):
@@ -715,38 +787,65 @@
     leaf_w = leaf_bond_weight[0]
     mid_w = mid_weight[0, 0]
 
-    blocks, (head_left, head_right) = cut_maps(upper_weight[0], ids, depth)
-    gather = MapGather(blocks, ids)
-
-    *sent, cotangent = place(after(regions, gather.first), leaf_map, head_cotangent, ids, depth)
+    blocks, (head_left, head_right, head_half) = cut_maps(upper_weight[0], ids, depth)
+    gather = MapGather(blocks, head_half, ids)
+
+    *sent, cotangent, cotangent_sent = place(after(regions, head_right), leaf_map, head_cotangent, ids, depth)
     near = partner(sent[1], "rep", 1)
     far_both = partner(sent[3], "rep", 3)
     far_one = partner(sent[2], "rep", 2)
     placed = [sent[0], near, far_one, far_both]
     for level in reversed(range(1, depth)):
-        value = gather.relay(level, level, sent[3] if level < depth - 1 else None)
-    gather.got = gather.held[1][2][0]
+        value = gather.relay(level, level, near)
+    msg0, msg1, term0, term1 = leaf_forward(placed[:2], leaf_w, mid_w)
+    near0 = partner(term1, "rep", 1)
     for level in range(2, depth):
         for stage in reversed(range(1, level)):
-            value = gather.relay(level, stage, sent[3])
-
-    msg0, msg1, term0, term1 = leaf_forward(placed[:2], leaf_w, mid_w)
-    near0 = partner(term1, "rep", 1)
-    far_placed = [after(far_one, term1, value, gather.got), far_both]
+            value = gather.relay(level, stage, term1)
+    far_placed = [after(far_one, term1, value), far_both]
     msg2, msg3, term2, term3 = leaf_forward(far_placed, leaf_w, mid_w)
     near2 = partner(term3, "rep", 1)
-    for level in range(1, depth):
-        gather.relay(level, 0, term3)
+    gather.relay(1, 0, term3)
+    for level in range(2, depth):
+        value = gather.relay(level, 0, term1)
     gather.exchange(0, term3)
-    (pair,) = fused(pair_product, "pair_product", term2, near2)
+    gather.relay(depth, depth - 1, term1)
+    (pair,) = fused(pair_product, "pair_product", term2, after(near2, value))
     far_pair = partner(pair, "rep", 2)
-    for level in range(1, depth):
-        gather.exchange(level, pair)
+    gather.exchange(1, pair)
+
+    cotangents = {0: View(cotangent)}
+    for stage in reversed(range(1, depth)):
+        if stage == depth - 1:
+            value = after(cotangent_sent, pair)
+        else:
+            half = next(iter(cotangents.values())).shape[0] // 2
+            (value,) = step(
+                lambda: (),
+                "stack",
+                [],
+                stacks=[[view.part(half, 2 * half) for view in cotangents.values()]],
+                ids=ids,
+            )
+            cotangents = {key: view.part(0, half) for key, view in cotangents.items()}
+        got = partner(value, "sub", 1 << stage)
+        half = cotangents[0].shape[0]
+        for place_at, key in enumerate(list(cotangents)):
+            cotangents[key ^ (1 << stage)] = View(got, (place_at * half, (place_at + 1) * half))
 
     weights, messages, own_ups, other_ups = [], [], [], []
     for level in range(depth):
-        weights.append(gather.weight(level))
+        if level == 1:
+            for later in range(2, depth):
+                gather.exchange(later, own_ups[0])
+            weights += [gather.weight(later) for later in range(1, depth)]
+            weights[1] = after(weights[1], weights[2])
+        if level == 2:
+            gather.exchange(depth, other_ups[1])
         if level == 0:
+            weights.append(gather.weight(0))
+            for stage in reversed(range(1, depth - 1)):
+                far_pair = after(far_pair, gather.relay(depth, stage, weights[0]))
             outs = fused(mid_forward, "mid_forward", term0, near0, far_pair, weights[0])
         else:
             outs = fused(up_forward, "up_forward", own_ups[-1], other_ups[-1], weights[level])
@@ -764,37 +863,60 @@
             count = sum(view.shape[0] for view in turns[level][0])
             turns[level][0 if level > stage else 1].append(View(got, (at, at + count)))
             at += count
-            if level > stage:
+            if stage < level < depth:
                 turns[level][1].append(View(got, (at, at + count)))
                 at += count
 
+    def to_stack(stage, levels):
+        return [
+            view
+            for level in levels
+            for view in turns[level][0] + (turns[level][1] if stage < level < depth else [])
+        ]
+
+    def stack_turns(stage, levels):
+        (value,) = step(lambda: (), "stack", [], stacks=[to_stack(stage, levels)], ids=ids)
+        gather_turns(stage, value, levels)
+
     gather_turns(0, after(messages[0], other_ups[0]), [0])
-    gather_turns(depth - 1, messages[-1], [depth - 1])
-    for stage in reversed(range(1, depth)):
-        views = []
-        for level in range(max(stage - 1, 1), depth):
-            views += turns[level][0] + (turns[level][1] if level > stage - 1 else [])
-        got = partner(root, "sub", 1 << stage)
-        if stage == depth - 1:
-            root = after(root, turns[0][1][0].array)
-        root, stack = step(joined, "joined", [root, got], stacks=views, ids=ids)
-        if stage > 1:
-            gather_turns(stage - 1, stack, range(stage - 1, depth))
+    for level in range(1, depth):
+        gather_turns(level, after(messages[level], own_ups[level]), [level])
+    for stage in reversed(range(2, depth - 1)):
+        stack_turns(stage, range(stage + 1, depth))
+
+    head_maps = gather.head(head_left, head_right)
     root_high = partner(root, "sub", 1)
-    root, grad_value, grad_gate, grad_msg, give = fused(
-        head_body, "head", cotangent, head_left, head_right, root, root_high
+    root, grad_value, grad_gate, grad_msg, give, value = step(
+        head_body,
+        "head",
+        [after(root, turns[0][1][0].array), root_high, head_maps],
+        parts=[cotangents[2 * i] for i in range(sub_count // 2)],
+        stacks=[to_stack(1, range(2, depth))],
+        ids=ids,
+        limit=12,
     )
-    for level in range(depth - 1):
-        got = partner(give, "sub", 1 << level)
-        grad_msg, give = fused(partial_sum, "partial_sum", grad_msg, got)
-        if level == 0:
-            gather_turns(0, after(stack, give), range(1, depth))
-    last_part = partner(give, "sub", 1 << (depth - 1))
-    turns.append([[View(root)], [View(root)]])
-    inputs = [view for entry in turns[:depth] for turn in entry for view in turn] + turns[depth][0]
+    got = partner(give, "sub", 1)
+    gather_turns(1, value, range(2, depth))
+    turns.append([[View(root)], []])
+    gather_turns(depth - 1, root, [depth])
+    low, high, value, root_value = step(
+        top_back,
+        "top_back",
+        [own_ups[-1], other_ups[-1], grad_msg, got],
+        stacks=[to_stack(0, range(1, depth)), to_stack(depth - 2, [depth])],
+        ids=ids,
+    )
+    gather_turns(0, value, range(1, depth))
+    gather_turns(depth - 2, root_value, [depth])
+    for stage in reversed(range(1, depth - 2)):
+        stack_turns(stage, [depth])
+    turns[depth][1] = turns[depth][0]
+    first_inputs = turns[0][0] + turns[0][1] + turns[depth][0]
+    second_inputs = [view for entry in turns[1:depth] for turn in entry for view in turn]
 
     lows, highs = [None] * depth, [None] * depth
-    columns = [None] * depth
+    lows[-1], highs[-1] = low, partner(high, "sub", 1 << (depth - 1))
+    columns = [None] * depth + [[View(grad_value)], [View(grad_gate)]]
 
     def groups_of(stage):
         return [
@@ -805,14 +927,14 @@
     def spread(stage, keeps, send):
         got = partner(send, "sub", 1 << stage)
         at = 0
-        for level, keep in zip(range(stage, depth), keeps):
+        for level, keep in zip(range(stage, depth + 2), keeps):
             span = keep.shape[1]
             columns[level] = [View(keep), View(got, None, (at, at + span))]
             at += span
 
     def columns_of(level, turn):
         if level == depth:
-            return [View(grad_gate if turn else grad_value)]
+            return columns[depth + turn]
         if level == 0:
             return [columns[0][turn]]
         count = rows >> level
@@ -822,30 +944,28 @@
             for i in range(turn, view.shape[0] // count, 2)
         ]
 
-    far_got = None
-    for level in reversed(range(depth)):
-        if level == depth - 1:
-            low, high = fused(
-                top_back, "top_back", own_ups[level], other_ups[level], grad_msg, last_part
-            )
-        else:
-            above = level + 1
-            low, high, *rest = step(
-                down_back,
-                "down_back",
-                [own_ups[level], other_ups[level], weights[above], lows[above], highs[above]],
-                halves=groups_of(above),
-                level=above,
-                far=inputs if above == depth - 1 else None,
-                ids=ids,
-                limit=12,
-            )
-            if above == depth - 1:
-                far_got = partner(rest.pop(), "rep", 2)
-            spread(above, rest[:-1], rest[-1])
+    far_got = []
+    for level in reversed(range(depth - 1)):
+        above = level + 1
+        far = {depth - 2: first_inputs, 0: second_inputs}.get(level)
+        low, high, *rest = step(
+            down_back,
+            "down_back",
+            [own_ups[level], other_ups[level], weights[above], lows[above], highs[above]],
+            halves=groups_of(above),
+            fixed=columns[depth:],
+            level=above,
+            far=far,
+            ids=ids,
+            limit=12,
+        )
         lows[level] = low
         highs[level] = partner(high, "sub", 1 << level)
-
+        if far:
+            far_got.append(partner(rest.pop(), "rep", 2))
+        spread(above, rest[:-1], rest[-1])
+
+    lows[0] = after(lows[0], far_got[0])
     back0, back1, pair_back, *rest = step(
         mid_back,
         "mid_back",
@@ -869,6 +989,7 @@
     near_grads = partner(own_grads, "rep", 1)
     back2, back3 = fused(far_back, "far_back", after(pair_back, own_grads), term2, near2)
     back3 = partner(back3, "rep", 1)
+    inputs = first_inputs + second_inputs
     near_got = partner(near_inputs([inputs[0].gated(back2)] + inputs[1:], far_got, ids), "rep", 1)
     leaf_grad, mid_grad = leaf_backward(
         placed, [msg0, msg1, msg2, msg3], [back0, back1, back2, back3], leaf_w, mid_w, first

time: 162 us -> 147 us (0.907)
  waiting for transfers between devices: 83.2 us -> 62.7 us
  starting transfers between devices: 45.7 us -> 48.2 us
  Pallas kernels: 30.2 us -> 32.6 us
    ppermute x44 -> x50, waiting for transfers between devices: 83.2 us -> 62.7 us  [partner(): lax.ppermute(value, axis, [(i, i ^ offset) for i in range(lax.axis_size(a...]
    ppermute x44 -> x50, starting transfers between devices: 45.7 us -> 48.2 us  [partner(): lax.ppermute(value, axis, [(i, i ^ offset) for i in range(lax.axis_size(a...]
    pallas_call x18 -> x16, Pallas kernels: 8.84 us -> 10 us  [fused(): pl.pallas_call(kernel, out_shape=shapes, in_specs=[smem_block()] * (len(a...]
  transfers between devices with their start and end apart: 44 -> 50, of which waited for: 25 -> 26; matrix products, arithmetic and copies ran while one was open for 0% -> 0% of each run, Pallas kernels for 13% -> 18%
where the time goes in v6:
time: 147 us
  waiting for transfers between devices  62.7 us (43%)
  starting transfers between devices  48.2 us (33%)
  Pallas kernels  32.6 us (22%)
  local copies, waits for them, and re-layouts  2.21 us (2%)
    ppermute x50, waiting for transfers between devices, partner(): lax.ppermute(value, axis, [(i, i ^ offset) for i in range(lax.axis_size(a...  62.7 us
    ppermute x50, starting transfers between devices, partner(): lax.ppermute(value, axis, [(i, i ^ offset) for i in range(lax.axis_size(a...  48.2 us
    pallas_call x16, Pallas kernels, fused(): pl.pallas_call(kernel, out_shape=shapes, in_specs=[smem_block()] * (len(a...  10 us
    pallas_call x1, Pallas kernels, leaf_backward(): pl.pallas_call(leaf_backward_kernel, out_shape=[jax.ShapeDtypeStruct(leaf...  5.8 us
  transfers between devices with their start and end apart: 50, of which 26 were waited for; matrix products, arithmetic and copies ran while one was open for 0% of the time, Pallas kernels for 18%

profile of v6, /device:TPU:0, one launch (start us, length us, event | category | flops | bytes accessed | tf_op | source)
XLA Modules:
  0.0 146.7 jit_solution(8375328633050847909)
XLA Ops:
  0.7 2.2 %copy-done.2 = bf16[1,1024,2,1024]{3,2,1,0:T(2,128)(2,1)S(1)} copy-done((bf16[1,1024,2,1024]{3,2,1,0:T(2,128)(2,1)S(1)}, bf16[1,1024,2,1024]{3,2,1,0:T(2,128)(2,1)}, u32[]{:S(2)}) %copy-start.2) | copy-done | bytes 4194328
  2.9 2.7 %cut_maps.1 = (bf16[1024,512]{1,0:T(8,128)(2,1)S(1)}, bf16[512,512]{1,0:T(8,128)(2,1)}, bf16[512,512]{1,0:T(8,128)(2,1)S(1)}, bf16[1024,256]{1,0:T(8,128)(2,1)S(...) custom-call(s32[2]{0:T(128)S(1)} %pad_add_fusion.ids_ref.refs_0_, ...), custom_call_target="tpu_custom_call" | custom-call | tf_op jit(solution)/shard_map/cut_maps/pallas_call | solution.py:287
  5.7 3.0 %collective-permute-start.9 = (bf16[512,896]{1,0:T(8,128)(2,1)S(1)}, bf16[512,896]{1,0:T(8,128)(2,1)S(1)}, u32[]{:S(2)}, u32[]{:S(2)}) collective-permute-start(bf16[512,896]{1,0:T(8,128)(2,1)S(1)} %pack.6), channel_id=1, source_target_pairs={{0,4},{4,0},{8,12},{12,8},{16,20},{20,16},{24,28},{28,24},{1,5},{5... | collective-permute-start | bytes 2752520 | tf_op jit(solution)/shard_map/ppermute | solution.py:16
  8.7 2.1 %place.1 = (bf16[4,128,256]{2,1,0:T(8,128)(2,1)S(1)}, bf16[4,128,256]{2,1,0:T(8,128)(2,1)S(1)}, bf16[4,128,256]{2,1,0:T(8,128)(2,1)S(1)}, bf16[4,128,256]{2,1,0:...) custom-call(s32[2]{0:T(128)S(1)} %pad_add_fusion.ids_ref.refs_0_, s32[16]{0:T(128)S(1)} %copy-done.5, ...), custom_call_target="tpu_custom_call" | custom-call | tf_op jit(solution)/shard_map/place/pallas_call | solution.py:102
  12.7 2.6 %collective-permute-start.3 = (bf16[512,128]{1,0:T(8,128)(2,1)S(1)}, bf16[512,128]{1,0:T(8,128)(2,1)S(1)}, u32[]{:S(2)}, u32[]{:S(2)}) collective-permute-start(bf16[512,128]{1,0:T(8,128)(2,1)S(1)} %get-tuple-element.113), channel_id=1, source_target_pairs={{0,16},{4,20},{8,24},{12,28},{16,0},{20,4},{24,8},{28,12},{1,17},{... | collective-permute-start | bytes 393224 | tf_op jit(solution)/shard_map/ppermute | solution.py:16
  16.7 5.4 %collective-permute-done.3.refs_1_.refs_0_ = bf16[512,128]{1,0:T(8,128)(2,1)S(1)} collective-permute-done((bf16[512,128]{1,0:T(8,128)(2,1)S(1)}, bf16[512,128]{1,0:T(8,128)(2,1)S(1)}, u32[]{:S(2)}, u32[]{:S(2)}) %collective-permute-start.3) | collective-permute-done | bytes 131104 | tf_op jit(solution)/shard_map/ppermute | solution.py:16
  22.2 2.5 %collective-permute-done.2.refs_1_.refs_3_ = bf16[4,128,256]{2,1,0:T(8,128)(2,1)S(1)} collective-permute-done((bf16[4,128,256]{2,1,0:T(8,128)(2,1)S(1)}, bf16[4,128,256]{2,1,0:T(8,128)(2,1)S(1)}, u32[]{:S(2)}, u32[]{:S(2)}) %collective-permute-start.2) | collective-permute-done | bytes 262176 | tf_op jit(solution)/shard_map/ppermute | solution.py:16
  26.2 2.9 %collective-permute-done.9.refs_0_ = bf16[512,896]{1,0:T(8,128)(2,1)S(1)} collective-permute-done((bf16[512,896]{1,0:T(8,128)(2,1)S(1)}, bf16[512,896]{1,0:T(8,128)(2,1)S(1)}, u32[]{:S(2)}, u32[]{:S(2)}) %collective-permute-start.9) | collective-permute-done | bytes 917536 | tf_op jit(solution)/shard_map/ppermute | solution.py:16
  31.3 6.8 %collective-permute-done.6.refs_1_.refs_2_ = bf16[512,256]{1,0:T(8,128)(2,1)S(1)} collective-permute-done((bf16[512,256]{1,0:T(8,128)(2,1)S(1)}, bf16[512,256]{1,0:T(8,128)(2,1)S(1)}, u32[]{:S(2)}, u32[]{:S(2)}) %collective-permute-start.6) | collective-permute-done | bytes 262176 | tf_op jit(solution)/shard_map/ppermute | solution.py:16
  40.0 2.6 %collective-permute-start.8 = (bf16[512,256]{1,0:T(8,128)(2,1)S(1)}, bf16[512,256]{1,0:T(8,128)(2,1)S(1)}, u32[]{:S(2)}, u32[]{:S(2)}) collective-permute-start(bf16[512,256]{1,0:T(8,128)(2,1)S(1)} %get-tuple-element.124.refs_0_), channel_id=1, source_target_pairs={{0,16},{4,20},{8,24},{12,28},{16,0},{20,4},{24,8},{28,12},{1,17},{... | collective-permute-start | bytes 786440 | tf_op jit(solution)/shard_map/ppermute | solution.py:16
  44.3 2.3 %collective-permute-done.12.refs_1_ = bf16[512,256]{1,0:T(8,128)(2,1)S(1)} collective-permute-done((bf16[512,256]{1,0:T(8,128)(2,1)S(1)}, bf16[512,256]{1,0:T(8,128)(2,1)S(1)}, u32[]{:S(2)}, u32[]{:S(2)}) %collective-permute-start.12) | collective-permute-done | bytes 262176 | tf_op jit(solution)/shard_map/ppermute | solution.py:16
  46.6 2.8 %collective-permute-start.13 = (bf16[512,256]{1,0:T(8,128)(2,1)S(1)}, bf16[512,256]{1,0:T(8,128)(2,1)S(1)}, u32[]{:S(2)}, u32[]{:S(2)}) collective-permute-start(bf16[512,256]{1,0:T(8,128)(2,1)S(1)} %collective-permute-done.12.refs_1_), channel_id=1, source_target_pairs={{0,4},{4,0},{8,12},{12,8},{16,20},{20,16},{24,28},{28,24},{1,5},{5... | collective-permute-start | bytes 786440 | tf_op jit(solution)/shard_map/ppermute | solution.py:16
  50.0 3.8 %collective-permute-done.8.refs_1_.refs_0_ = bf16[512,256]{1,0:T(8,128)(2,1)S(1)} collective-permute-done((bf16[512,256]{1,0:T(8,128)(2,1)S(1)}, bf16[512,256]{1,0:T(8,128)(2,1)S(1)}, u32[]{:S(2)}, u32[]{:S(2)}) %collective-permute-start.8) | collective-permute-done | bytes 262176 | tf_op jit(solution)/shard_map/ppermute | solution.py:16
  60.6 3.0 %collective-permute-done.11.refs_1_.refs_2_ = bf16[64,1024]{1,0:T(8,128)(2,1)S(1)} collective-permute-done((bf16[64,1024]{1,0:T(8,128)(2,1)S(1)}, bf16[64,1024]{1,0:T(8,128)(2,1)S(1)}, u32[]{:S(2)}, u32[]{:S(2)}) %collective-permute-start.11) | collective-permute-done | bytes 131104 | tf_op jit(solution)/shard_map/ppermute | solution.py:16
  65.5 3.0 %collective-permute-done.19.refs_1_.refs_2_ = bf16[32,1024]{1,0:T(8,128)(2,1)S(1)} collective-permute-done((bf16[32,1024]{1,0:T(8,128)(2,1)S(1)}, bf16[32,1024]{1,0:T(8,128)(2,1)S(1)}, u32[]{:S(2)}, u32[]{:S(2)}) %collective-permute-start.19) | collective-permute-done | bytes 65568 | tf_op jit(solution)/shard_map/ppermute | solution.py:16
  69.3 3.4 %collective-permute-start.26 = (f32[64,128]{1,0:T(8,128)S(1)}, f32[64,128]{1,0:T(8,128)S(1)}, u32[]{:S(2)}, u32[]{:S(2)}) collective-permute-start(f32[64,128]{1,0:T(8,128)S(1)} %get-tuple-element.155), channel_id=1, source_target_pairs={{0,16},{4,20},{8,24},{12,28},{16,0},{20,4},{24,8},{28,12},{1,17},{... | collective-permute-start | bytes 98312 | tf_op jit(solution)/shard_map/ppermute | solution.py:16
  75.1 2.6 %collective-permute-start.28 = (bf16[32,1024]{1,0:T(8,128)(2,1)S(1)}, bf16[32,1024]{1,0:T(8,128)(2,1)S(1)}, u32[]{:S(2)}, u32[]{:S(2)}) collective-permute-start(bf16[32,1024]{1,0:T(8,128)(2,1)S(1)} %get-tuple-element.157.refs_7_.refs_13_.refs_8_.refs_9_), channel_id=1, source_target_pairs={{0,16},{4,20},{8,24},{12,28},{16,0},{20,4},{24,8},{28,12},{1,17},{... | collective-permute-start | bytes 196616 | tf_op jit(solution)/shard_map/ppermute | solution.py:16
  90.7 1.9 %collective-permute-done.32.refs_11_.refs_3_.refs_13_ = bf16[32,1024]{1,0:T(8,128)(2,1)S(1)} collective-permute-done((bf16[32,1024]{1,0:T(8,128)(2,1)S(1)}, bf16[32,1024]{1,0:T(8,128)(2,1)S(1)}, u32[]{:S(2)}, u32[]{:S(2)}) %collective-permute-start.32) | collective-permute-done | bytes 65568 | tf_op jit(solution)/shard_map/ppermute | solution.py:16
  95.6 2.0 %collective-permute-start.33 = (bf16[16,1024]{1,0:T(8,128)(2,1)S(1)}, bf16[16,1024]{1,0:T(8,128)(2,1)S(1)}, u32[]{:S(2)}, u32[]{:S(2)}) collective-permute-start(bf16[16,1024]{1,0:T(8,128)(2,1)S(1)} %get-tuple-element.165), channel_id=1, source_target_pairs={{0,16},{4,20},{8,24},{12,28},{16,0},{20,4},{24,8},{28,12},{1,17},{... | collective-permute-start | bytes 98312 | tf_op jit(solution)/shard_map/ppermute | solution.py:16
  97.6 2.9 %collective-permute-done.33.refs_5_ = bf16[16,1024]{1,0:T(8,128)(2,1)S(1)} collective-permute-done((bf16[16,1024]{1,0:T(8,128)(2,1)S(1)}, bf16[16,1024]{1,0:T(8,128)(2,1)S(1)}, u32[]{:S(2)}, u32[]{:S(2)}) %collective-permute-start.33) | collective-permute-done | bytes 32800 | tf_op jit(solution)/shard_map/ppermute | solution.py:16
  103.5 2.5 %collective-permute-start.35 = (bf16[32,1024]{1,0:T(8,128)(2,1)S(1)}, bf16[32,1024]{1,0:T(8,128)(2,1)S(1)}, u32[]{:S(2)}, u32[]{:S(2)}) collective-permute-start(bf16[32,1024]{1,0:T(8,128)(2,1)S(1)} %get-tuple-element.170), channel_id=1, source_target_pairs={{0,8},{4,12},{8,0},{12,4},{16,24},{20,28},{24,16},{28,20},{1,9},{5... | collective-permute-start | bytes 196616 | tf_op jit(solution)/shard_map/ppermute | solution.py:16
  108.3 3.5 %collective-permute-done.36.refs_7_ = bf16[32,1024]{1,0:T(8,128)(2,1)S(1)} collective-permute-done((bf16[32,1024]{1,0:T(8,128)(2,1)S(1)}, bf16[32,1024]{1,0:T(8,128)(2,1)S(1)}, u32[]{:S(2)}, u32[]{:S(2)}) %collective-permute-start.36) | collective-permute-done | bytes 65568 | tf_op jit(solution)/shard_map/ppermute | solution.py:16
  114.5 3.9 %collective-permute-done.39.refs_6_ = bf16[64,1024]{1,0:T(8,128)(2,1)S(1)} collective-permute-done((bf16[64,1024]{1,0:T(8,128)(2,1)S(1)}, bf16[64,1024]{1,0:T(8,128)(2,1)S(1)}, u32[]{:S(2)}, u32[]{:S(2)}) %collective-permute-start.39) | collective-permute-done | bytes 131104 | tf_op jit(solution)/shard_map/ppermute | solution.py:16
  120.2 2.0 %collective-permute-start.43 = (bf16[128,896]{1,0:T(8,128)(2,1)S(1)}, bf16[128,896]{1,0:T(8,128)(2,1)S(1)}, u32[]{:S(2)}, u32[]{:S(2)}) collective-permute-start(bf16[128,896]{1,0:T(8,128)(2,1)S(1)} %get-tuple-element.188), channel_id=1, source_target_pairs={{0,4},{4,0},{8,12},{12,8},{16,20},{20,16},{24,28},{28,24},{1,5},{5... | collective-permute-start | bytes 688136 | tf_op jit(solution)/shard_map/ppermute | solution.py:16
  122.3 2.1 %leaf_first.1.refs_14_ = bf16[4,256,1024]{2,1,0:T(8,128)(2,1)S(1)} custom-call(bf16[4,128,256]{2,1,0:T(8,128)(2,1)S(1)} %get-tuple-element.104.refs_0_, bf16[4,128,256]{2,1,0:T(8,128)(2,1)S(1)} %collective-permute-done.refs_1_, bf16[128,1024]{1,0:T(8,128)(2,1)S(1)} %get-tuple-element.183.refs_2_.refs_8_, ...), custom_call_target="tpu_custom_call" | custom-call | tf_op jit(solution)/shard_map/leaf_first/pallas_call | solution.py:172
  124.3 4.1 %collective-permute-done.43.refs_1_ = bf16[128,896]{1,0:T(8,128)(2,1)S(1)} collective-permute-done((bf16[128,896]{1,0:T(8,128)(2,1)S(1)}, bf16[128,896]{1,0:T(8,128)(2,1)S(1)}, u32[]{:S(2)}, u32[]{:S(2)}) %collective-permute-start.43) | collective-permute-done | bytes 229408 | tf_op jit(solution)/shard_map/ppermute | solution.py:16
  128.6 2.0 %collective-permute-done.42.refs_0_ = bf16[128,1024]{1,0:T(8,128)(2,1)S(1)} collective-permute-done((bf16[128,1024]{1,0:T(8,128)(2,1)S(1)}, bf16[128,1024]{1,0:T(8,128)(2,1)S(1)}, u32[]{:S(2)}, u32[]{:S(2)}) %collective-permute-start.42) | collective-permute-done | bytes 262176 | tf_op jit(solution)/shard_map/ppermute | solution.py:16
  132.1 2.3 %collective-permute-done.44.refs_11_ = bf16[128,1024]{1,0:T(8,128)(2,1)S(1)} collective-permute-done((bf16[128,1024]{1,0:T(8,128)(2,1)S(1)}, bf16[128,1024]{1,0:T(8,128)(2,1)S(1)}, u32[]{:S(2)}, u32[]{:S(2)}) %collective-permute-start.44) | collective-permute-done | bytes 262176 | tf_op jit(solution)/shard_map/ppermute | solution.py:16
  134.4 5.8 %leaf_backward.1 = (bf16[4,256,1024]{2,1,0:T(8,128)(2,1)}, bf16[1024,1024]{1,0:T(8,128)(2,1)}) custom-call(bf16[4,128,256]{2,1,0:T(8,128)(2,1)S(1)} %get-tuple-element.104.refs_0_, bf16[4,128,256]{2,1,0:T(8,128)(2,1)S(1)} %collective-permute-done.refs_1_, bf16[4,128,256]{2,1,0:T(8,128)(2,1)S(1)} %collective-permute-done.1.refs_0_.refs_2_, ...), custom_call_target="tpu_custom_call" | custom-call | tf_op jit(solution)/shard_map/leaf_backward/pallas_call | solution.py:196
  140.2 2.0 %collective-permute-done.47.refs_1_ = bf16[256,1024]{1,0:T(8,128)(2,1)S(1)} collective-permute-done((bf16[256,1024]{1,0:T(8,128)(2,1)S(1)}, bf16[256,1024]{1,0:T(8,128)(2,1)S(1)}, u32[]{:S(2)}, u32[]{:S(2)}) %collective-permute-start.47) | collective-permute-done | bytes 524320 | tf_op jit(solution)/shard_map/ppermute | solution.py:16
  142.2 1.9 %collective-permute-done.49.refs_3_ = bf16[256,1024]{1,0:T(8,128)(2,1)S(1)} collective-permute-done((bf16[256,1024]{1,0:T(8,128)(2,1)S(1)}, bf16[256,1024]{1,0:T(8,128)(2,1)S(1)}, u32[]{:S(2)}, u32[]{:S(2)}) %collective-permute-start.49) | collective-permute-done | bytes 524320 | tf_op jit(solution)/shard_map/ppermute | solution.py:16
  144.1 2.6 %upper_grads.1 = bf16[256,2,1024]{2,1,0:T(2,128)(2,1)} custom-call(s32[2]{0:T(128)S(1)} %pad_add_fusion.ids_ref.refs_0_, bf16[384,512]{1,0:T(8,128)(2,1)S(1)} %collective-permute-done.38.first_ref, bf16[512,512]{1,0:T(8,128)(2,1)S(1)} %collective-permute-done.45.second_ref, bf16[1792,256]{1,0:T(8,128)(2,1)S(1)} %collective-permute-done.46.near_ref, ...), custom_call_target="tpu_custom_call" | custom-call | tf_op jit(solution)/shard_map/upper_grads/pallas_call | solution.py:677
  (110 shorter events, 50.6 us)
Async XLA Ops:
  5.7 23.4 %collective-permute-start.9 = (bf16[512,896]{1,0:T(8,128)(2,1)S(1)}, bf16[512,896]{1,0:T(8,128)(2,1)S(1)}, u32[]{:S(2)}, u32[]{:S(2)}) collective-permute-start(bf16[512,896]{1,0:T(8,128)(2,1)S(1)} %pack.6), channel_id=1, source_target_pairs={{0,4},{4,0},{8,12},{12,8},{16,20},{20,16},{24,28},{28,24},{1,5},{5... | collective-permute-start | bytes 2752520 | tf_op jit(solution)/shard_map/ppermute | solution.py:16
  10.8 11.4 %collective-permute-start.1 = (bf16[4,128,256]{2,1,0:T(8,128)(2,1)S(1)}, bf16[4,128,256]{2,1,0:T(8,128)(2,1)S(1)}, u32[]{:S(2)}, u32[]{:S(2)}) collective-permute-start(bf16[4,128,256]{2,1,0:T(8,128)(2,1)S(1)} %get-tuple-element.106), channel_id=1, source_target_pairs={{0,2},{1,3},{2,0},{3,1},{4,6},{5,7},{6,4},{7,5},{8,10},{9,11},{10,... | collective-permute-start | bytes 786440 | tf_op jit(solution)/shard_map/ppermute | solution.py:16
  12.4 12.3 %collective-permute-start.2 = (bf16[4,128,256]{2,1,0:T(8,128)(2,1)S(1)}, bf16[4,128,256]{2,1,0:T(8,128)(2,1)S(1)}, u32[]{:S(2)}, u32[]{:S(2)}) collective-permute-start(bf16[4,128,256]{2,1,0:T(8,128)(2,1)S(1)} %get-tuple-element.107), channel_id=1, source_target_pairs={{0,3},{1,2},{2,1},{3,0},{4,7},{5,6},{6,5},{7,4},{8,11},{9,10},{10,... | collective-permute-start | bytes 786440 | tf_op jit(solution)/shard_map/ppermute | solution.py:16
  12.7 9.5 %collective-permute-start.3 = (bf16[512,128]{1,0:T(8,128)(2,1)S(1)}, bf16[512,128]{1,0:T(8,128)(2,1)S(1)}, u32[]{:S(2)}, u32[]{:S(2)}) collective-permute-start(bf16[512,128]{1,0:T(8,128)(2,1)S(1)} %get-tuple-element.113), channel_id=1, source_target_pairs={{0,16},{4,20},{8,24},{12,28},{16,0},{20,4},{24,8},{28,12},{1,17},{... | collective-permute-start | bytes 393224 | tf_op jit(solution)/shard_map/ppermute | solution.py:16
  29.0 17.5 %collective-permute-start.10 = (bf16[512,896]{1,0:T(8,128)(2,1)S(1)}, bf16[512,896]{1,0:T(8,128)(2,1)S(1)}, u32[]{:S(2)}, u32[]{:S(2)}) collective-permute-start(bf16[512,896]{1,0:T(8,128)(2,1)S(1)} %collective-permute-done.9.refs_0_), channel_id=1, source_target_pairs={{0,1},{1,0},{2,3},{3,2},{4,5},{5,4},{6,7},{7,6},{8,9},{9,8},{10,11... | collective-permute-start | bytes 2752520 | tf_op jit(solution)/shard_map/ppermute | solution.py:16
  29.0 9.1 %collective-permute-start.6 = (bf16[512,256]{1,0:T(8,128)(2,1)S(1)}, bf16[512,256]{1,0:T(8,128)(2,1)S(1)}, u32[]{:S(2)}, u32[]{:S(2)}) collective-permute-start(bf16[512,256]{1,0:T(8,128)(2,1)S(1)} %pack.4), channel_id=1, source_target_pairs={{0,8},{4,12},{8,0},{12,4},{16,24},{20,28},{24,16},{28,20},{1,9},{5... | collective-permute-start | bytes 786440 | tf_op jit(solution)/shard_map/ppermute | solution.py:16
  30.8 11.8 %collective-permute-start.5 = (bf16[128,1024]{1,0:T(8,128)(2,1)S(1)}, bf16[128,1024]{1,0:T(8,128)(2,1)S(1)}, u32[]{:S(2)}, u32[]{:S(2)}) collective-permute-start(bf16[128,1024]{1,0:T(8,128)(2,1)S(1)} %get-tuple-element.120), channel_id=1, source_target_pairs={{0,1},{1,0},{2,3},{3,2},{4,5},{5,4},{6,7},{7,6},{8,9},{9,8},{10,11... | collective-permute-start | bytes 786440 | tf_op jit(solution)/shard_map/ppermute | solution.py:16
  31.1 15.5 %collective-permute-start.12 = (bf16[512,256]{1,0:T(8,128)(2,1)S(1)}, bf16[512,256]{1,0:T(8,128)(2,1)S(1)}, u32[]{:S(2)}, u32[]{:S(2)}) collective-permute-start(bf16[512,256]{1,0:T(8,128)(2,1)S(1)} %get-tuple-element.135), channel_id=1, source_target_pairs={{0,8},{4,12},{8,0},{12,4},{16,24},{20,28},{24,16},{28,20},{1,9},{5... | collective-permute-start | bytes 786440 | tf_op jit(solution)/shard_map/ppermute | solution.py:16
  38.2 17.2 %collective-permute-start.16 = (bf16[512,384]{1,0:T(8,128)(2,1)S(1)}, bf16[512,384]{1,0:T(8,128)(2,1)S(1)}, u32[]{:S(2)}, u32[]{:S(2)}) collective-permute-start(bf16[512,384]{1,0:T(8,128)(2,1)S(1)} %pack.5.refs_1_), channel_id=1, source_target_pairs={{0,4},{4,0},{8,12},{12,8},{16,20},{20,16},{24,28},{28,24},{1,5},{5... | collective-permute-start | bytes 1179656 | tf_op jit(solution)/shard_map/ppermute | solution.py:16
  40.0 13.8 %collective-permute-start.8 = (bf16[512,256]{1,0:T(8,128)(2,1)S(1)}, bf16[512,256]{1,0:T(8,128)(2,1)S(1)}, u32[]{:S(2)}, u32[]{:S(2)}) collective-permute-start(bf16[512,256]{1,0:T(8,128)(2,1)S(1)} %get-tuple-element.124.refs_0_), channel_id=1, source_target_pairs={{0,16},{4,20},{8,24},{12,28},{16,0},{20,4},{24,8},{28,12},{1,17},{... | collective-permute-start | bytes 786440 | tf_op jit(solution)/shard_map/ppermute | solution.py:16
  42.7 12.0 %collective-permute-start.7 = (bf16[128,1024]{1,0:T(8,128)(2,1)S(1)}, bf16[128,1024]{1,0:T(8,128)(2,1)S(1)}, u32[]{:S(2)}, u32[]{:S(2)}) collective-permute-start(bf16[128,1024]{1,0:T(8,128)(2,1)S(1)} %pair_product.1), channel_id=1, source_target_pairs={{0,2},{1,3},{2,0},{3,1},{4,6},{5,7},{6,4},{7,5},{8,10},{9,11},{10,... | collective-permute-start | bytes 786440 | tf_op jit(solution)/shard_map/ppermute | solution.py:16
  46.5 8.1 %collective-permute-start.4 = (bf16[128,1024]{1,0:T(8,128)(2,1)S(1)}, bf16[128,1024]{1,0:T(8,128)(2,1)S(1)}, u32[]{:S(2)}, u32[]{:S(2)}) collective-permute-start(bf16[128,1024]{1,0:T(8,128)(2,1)S(1)} %get-tuple-element.110), channel_id=1, source_target_pairs={{0,1},{1,0},{2,3},{3,2},{4,5},{5,4},{6,7},{7,6},{8,9},{9,8},{10,11... | collective-permute-start | bytes 786440 | tf_op jit(solution)/shard_map/ppermute | solution.py:16
  46.6 9.7 %collective-permute-start.13 = (bf16[512,256]{1,0:T(8,128)(2,1)S(1)}, bf16[512,256]{1,0:T(8,128)(2,1)S(1)}, u32[]{:S(2)}, u32[]{:S(2)}) collective-permute-start(bf16[512,256]{1,0:T(8,128)(2,1)S(1)} %collective-permute-done.12.refs_1_), channel_id=1, source_target_pairs={{0,4},{4,0},{8,12},{12,8},{16,20},{20,16},{24,28},{28,24},{1,5},{5... | collective-permute-start | bytes 786440 | tf_op jit(solution)/shard_map/ppermute | solution.py:16
  53.9 14.6 %collective-permute-start.23 = (bf16[512,512]{1,0:T(8,128)(2,1)S(1)}, bf16[512,512]{1,0:T(8,128)(2,1)S(1)}, u32[]{:S(2)}, u32[]{:S(2)}) collective-permute-start(bf16[512,512]{1,0:T(8,128)(2,1)S(1)} %pack.7), channel_id=1, source_target_pairs={{0,8},{4,12},{8,0},{12,4},{16,24},{20,28},{24,16},{28,20},{1,9},{5... | collective-permute-start | bytes 1572872 | tf_op jit(solution)/shard_map/ppermute | solution.py:16
  68.5 14.2 %collective-permute-start.25 = (bf16[512,512]{1,0:T(8,128)(2,1)S(1)}, bf16[512,512]{1,0:T(8,128)(2,1)S(1)}, u32[]{:S(2)}, u32[]{:S(2)}) collective-permute-start(bf16[512,512]{1,0:T(8,128)(2,1)S(1)} %collective-permute-done.23.refs_1_), channel_id=1, source_target_pairs={{0,1},{1,0},{2,3},{3,2},{4,5},{5,4},{6,7},{7,6},{8,9},{9,8},{10,11... | collective-permute-start | bytes 1572872 | tf_op jit(solution)/shard_map/ppermute | solution.py:16
  68.5 11.7 %collective-permute-start.21 = (bf16[128,1024]{1,0:T(8,128)(2,1)S(1)}, bf16[128,1024]{1,0:T(8,128)(2,1)S(1)}, u32[]{:S(2)}, u32[]{:S(2)}) collective-permute-start(bf16[128,1024]{1,0:T(8,128)(2,1)S(1)} %get-tuple-element.199.refs_8_.refs_0_.refs_4_), channel_id=1, source_target_pairs={{0,4},{4,0},{8,12},{12,8},{16,20},{20,16},{24,28},{28,24},{1,5},{5... | collective-permute-start | bytes 786440 | tf_op jit(solution)/shard_map/ppermute | solution.py:16
  69.1 12.9 %collective-permute-start.24 = (bf16[512,256]{1,0:T(8,128)(2,1)S(1)}, bf16[512,256]{1,0:T(8,128)(2,1)S(1)}, u32[]{:S(2)}, u32[]{:S(2)}) collective-permute-start(bf16[512,256]{1,0:T(8,128)(2,1)S(1)} %collective-permute-done.8.refs_1_.refs_0_), channel_id=1, source_target_pairs={{0,1},{1,0},{2,3},{3,2},{4,5},{5,4},{6,7},{7,6},{8,9},{9,8},{10,11... | collective-permute-start | bytes 786440 | tf_op jit(solution)/shard_map/ppermute | solution.py:16
  69.3 5.8 %collective-permute-start.26 = (f32[64,128]{1,0:T(8,128)S(1)}, f32[64,128]{1,0:T(8,128)S(1)}, u32[]{:S(2)}, u32[]{:S(2)}) collective-permute-start(f32[64,128]{1,0:T(8,128)S(1)} %get-tuple-element.155), channel_id=1, source_target_pairs={{0,16},{4,20},{8,24},{12,28},{16,0},{20,4},{24,8},{28,12},{1,17},{... | collective-permute-start | bytes 98312 | tf_op jit(solution)/shard_map/ppermute | solution.py:16
  73.2 5.8 %collective-permute-start.20 = (bf16[16,1024]{1,0:T(8,128)(2,1)S(1)}, bf16[16,1024]{1,0:T(8,128)(2,1)S(1)}, u32[]{:S(2)}, u32[]{:S(2)}) collective-permute-start(bf16[16,1024]{1,0:T(8,128)(2,1)S(1)} %get-tuple-element.146), channel_id=1, source_target_pairs={{0,16},{4,20},{8,24},{12,28},{16,0},{20,4},{24,8},{28,12},{1,17},{... | collective-permute-start | bytes 98312 | tf_op jit(solution)/shard_map/ppermute | solution.py:16
  75.1 8.8 %collective-permute-start.28 = (bf16[32,1024]{1,0:T(8,128)(2,1)S(1)}, bf16[32,1024]{1,0:T(8,128)(2,1)S(1)}, u32[]{:S(2)}, u32[]{:S(2)}) collective-permute-start(bf16[32,1024]{1,0:T(8,128)(2,1)S(1)} %get-tuple-element.157.refs_7_.refs_13_.refs_8_.refs_9_), channel_id=1, source_target_pairs={{0,16},{4,20},{8,24},{12,28},{16,0},{20,4},{24,8},{28,12},{1,17},{... | collective-permute-start | bytes 196616 | tf_op jit(solution)/shard_map/ppermute | solution.py:16
  81.9 7.1 %collective-permute-start.30 = (bf16[64,1024]{1,0:T(8,128)(2,1)S(1)}, bf16[64,1024]{1,0:T(8,128)(2,1)S(1)}, u32[]{:S(2)}, u32[]{:S(2)}) collective-permute-start(bf16[64,1024]{1,0:T(8,128)(2,1)S(1)} %get-tuple-element.161.refs_5_.refs_10_.refs_6_), channel_id=1, source_target_pairs={{0,8},{4,12},{8,0},{12,4},{16,24},{20,28},{24,16},{28,20},{1,9},{5... | collective-permute-start | bytes 393224 | tf_op jit(solution)/shard_map/ppermute | solution.py:16
  85.9 6.8 %collective-permute-start.31 = (bf16[64,1024]{1,0:T(8,128)(2,1)S(1)}, bf16[64,1024]{1,0:T(8,128)(2,1)S(1)}, u32[]{:S(2)}, u32[]{:S(2)}) collective-permute-start(bf16[64,1024]{1,0:T(8,128)(2,1)S(1)} %get-tuple-element.162), channel_id=1, source_target_pairs={{0,8},{4,12},{8,0},{12,4},{16,24},{20,28},{24,16},{28,20},{1,9},{5... | collective-permute-start | bytes 393224 | tf_op jit(solution)/shard_map/ppermute | solution.py:16
  86.8 5.9 %collective-permute-start.32 = (bf16[32,1024]{1,0:T(8,128)(2,1)S(1)}, bf16[32,1024]{1,0:T(8,128)(2,1)S(1)}, u32[]{:S(2)}, u32[]{:S(2)}) collective-permute-start(bf16[32,1024]{1,0:T(8,128)(2,1)S(1)} %get-tuple-element.163.refs_10_.refs_2_.refs_12_), channel_id=1, source_target_pairs={{0,16},{4,20},{8,24},{12,28},{16,0},{20,4},{24,8},{28,12},{1,17},{... | collective-permute-start | bytes 196616 | tf_op jit(solution)/shard_map/ppermute | solution.py:16
  93.4 18.3 %collective-permute-start.37 = (bf16[256,1024]{1,0:T(8,128)(2,1)S(1)}, bf16[256,1024]{1,0:T(8,128)(2,1)S(1)}, u32[]{:S(2)}, u32[]{:S(2)}) collective-permute-start(bf16[256,1024]{1,0:T(8,128)(2,1)S(1)} %get-tuple-element.175), channel_id=1, source_target_pairs={{0,4},{4,0},{8,12},{12,8},{16,20},{20,16},{24,28},{28,24},{1,5},{5... | collective-permute-start | bytes 1572872 | tf_op jit(solution)/shard_map/ppermute | solution.py:16
  94.3 6.2 %collective-permute-start.34 = (bf16[64,1024]{1,0:T(8,128)(2,1)S(1)}, bf16[64,1024]{1,0:T(8,128)(2,1)S(1)}, u32[]{:S(2)}, u32[]{:S(2)}) collective-permute-start(bf16[64,1024]{1,0:T(8,128)(2,1)S(1)} %get-tuple-element.168), channel_id=1, source_target_pairs={{0,8},{4,12},{8,0},{12,4},{16,24},{20,28},{24,16},{28,20},{1,9},{5... | collective-permute-start | bytes 393224 | tf_op jit(solution)/shard_map/ppermute | solution.py:16
  102.1 12.4 %collective-permute-start.38 = (bf16[384,512]{1,0:T(8,128)(2,1)S(1)}, bf16[384,512]{1,0:T(8,128)(2,1)S(1)}, u32[]{:S(2)}, u32[]{:S(2)}) collective-permute-start(bf16[384,512]{1,0:T(8,128)(2,1)S(1)} %get-tuple-element.177), channel_id=1, source_target_pairs={{0,2},{1,3},{2,0},{3,1},{4,6},{5,7},{6,4},{7,5},{8,10},{9,11},{10,... | collective-permute-start | bytes 1179656 | tf_op jit(solution)/shard_map/ppermute | solution.py:16
  113.7 17.1 %collective-permute-start.45 = (bf16[512,512]{1,0:T(8,128)(2,1)S(1)}, bf16[512,512]{1,0:T(8,128)(2,1)S(1)}, u32[]{:S(2)}, u32[]{:S(2)}) collective-permute-start(bf16[512,512]{1,0:T(8,128)(2,1)S(1)} %get-tuple-element.198), channel_id=1, source_target_pairs={{0,2},{1,3},{2,0},{3,1},{4,6},{5,7},{6,4},{7,5},{8,10},{9,11},{10,... | collective-permute-start | bytes 1572872 | tf_op jit(solution)/shard_map/ppermute | solution.py:16
  120.2 8.2 %collective-permute-start.43 = (bf16[128,896]{1,0:T(8,128)(2,1)S(1)}, bf16[128,896]{1,0:T(8,128)(2,1)S(1)}, u32[]{:S(2)}, u32[]{:S(2)}) collective-permute-start(bf16[128,896]{1,0:T(8,128)(2,1)S(1)} %get-tuple-element.188), channel_id=1, source_target_pairs={{0,4},{4,0},{8,12},{12,8},{16,20},{20,16},{24,28},{28,24},{1,5},{5... | collective-permute-start | bytes 688136 | tf_op jit(solution)/shard_map/ppermute | solution.py:16
  122.2 8.4 %collective-permute-start.42 = (bf16[128,1024]{1,0:T(8,128)(2,1)S(1)}, bf16[128,1024]{1,0:T(8,128)(2,1)S(1)}, u32[]{:S(2)}, u32[]{:S(2)}) collective-permute-start(bf16[128,1024]{1,0:T(8,128)(2,1)S(1)} %get-tuple-element.185), channel_id=1, source_target_pairs={{0,2},{1,3},{2,0},{3,1},{4,6},{5,7},{6,4},{7,5},{8,10},{9,11},{10,... | collective-permute-start | bytes 786440 | tf_op jit(solution)/shard_map/ppermute | solution.py:16
  128.5 13.7 %collective-permute-start.47 = (bf16[256,1024]{1,0:T(8,128)(2,1)S(1)}, bf16[256,1024]{1,0:T(8,128)(2,1)S(1)}, u32[]{:S(2)}, u32[]{:S(2)}) collective-permute-start(bf16[256,1024]{1,0:T(8,128)(2,1)S(1)} %side_by_side.1.refs_0_), channel_id=1, source_target_pairs={{0,2},{1,3},{2,0},{3,1},{4,6},{5,7},{6,4},{7,5},{8,10},{9,11},{10,... | collective-permute-start | bytes 1572872 | tf_op jit(solution)/shard_map/ppermute | solution.py:16
  131.4 12.7 %collective-permute-start.46 = (bf16[1792,256]{1,0:T(8,128)(2,1)S(1)}, bf16[1792,256]{1,0:T(8,128)(2,1)S(1)}, u32[]{:S(2)}, u32[]{:S(2)}) collective-permute-start(bf16[1792,256]{1,0:T(8,128)(2,1)S(1)} %near_inputs.1), channel_id=1, source_target_pairs={{0,1},{1,0},{2,3},{3,2},{4,5},{5,4},{6,7},{7,6},{8,9},{9,8},{10,11... | collective-permute-start | bytes 2752520 | tf_op jit(solution)/shard_map/ppermute | solution.py:16
  132.0 10.2 %collective-permute-start.48 = (bf16[256,1024]{1,0:T(8,128)(2,1)S(1)}, bf16[256,1024]{1,0:T(8,128)(2,1)S(1)}, u32[]{:S(2)}, u32[]{:S(2)}) collective-permute-start(bf16[256,1024]{1,0:T(8,128)(2,1)S(1)} %side_by_side.1.refs_0_), channel_id=1, source_target_pairs={{0,1},{1,0},{2,3},{3,2},{4,5},{5,4},{6,7},{7,6},{8,9},{9,8},{10,11... | collective-permute-start | bytes 1572872 | tf_op jit(solution)/shard_map/ppermute | solution.py:16
  (24 other events, 111.2 us)

commit v7 on v6

--- a/solution.py
+++ b/solution.py
@@ -450,6 +450,16 @@
         for place, offset in enumerate(offsets):
             self.held[level][offset ^ (1 << stage)] = (got, place * self.spans[level])
         return value
+
+    def top_relay(self, gate):
+        level, stage = self.depth - 1, self.depth - 1
+        pieces = [
+            (after(self.blocks[level][2], gate), 0, self.spans[level]),
+            (self.blocks[self.depth][1], 0, self.spans[self.depth]),
+        ]
+        got = partner(pack(pieces), "sub", 1 << stage)
+        self.held[level][1 << stage] = (got, 0)
+        self.held[self.depth][1 << stage] = (got, self.spans[level])
 
     def exchange(self, level, gate):
         for offset, (array, _) in self.held[level].items():
@@ -795,24 +805,26 @@
     far_both = partner(sent[3], "rep", 3)
     far_one = partner(sent[2], "rep", 2)
     placed = [sent[0], near, far_one, far_both]
-    for level in reversed(range(1, depth)):
-        value = gather.relay(level, level, near)
+    gather.top_relay(near)
+    for level in reversed(range(1, depth - 1)):
+        gather.relay(level, level, near)
     msg0, msg1, term0, term1 = leaf_forward(placed[:2], leaf_w, mid_w)
     near0 = partner(term1, "rep", 1)
+    packed = []
     for level in range(2, depth):
-        for stage in reversed(range(1, level)):
-            value = gather.relay(level, stage, term1)
-    far_placed = [after(far_one, term1, value), far_both]
+        packed += [gather.relay(level, stage, term1) for stage in reversed(range(1, level))]
+    packed += [gather.relay(depth, stage, term1) for stage in reversed(range(1, depth - 1))]
+    gather.relay(1, 0, term1)
+    far_placed = [after(far_one, term1, gather.held[1][3][0], *packed), far_both]
     msg2, msg3, term2, term3 = leaf_forward(far_placed, leaf_w, mid_w)
     near2 = partner(term3, "rep", 1)
-    gather.relay(1, 0, term3)
-    for level in range(2, depth):
-        value = gather.relay(level, 0, term1)
-    gather.exchange(0, term3)
-    gather.relay(depth, depth - 1, term1)
-    (pair,) = fused(pair_product, "pair_product", term2, after(near2, value))
+    near2 = after(near2, gather.held[depth - 1][2][0])
+    gather.exchange(0, near2)
+    first_map = gather.weight(0)
+    (pair,) = fused(pair_product, "pair_product", term2, near2)
     far_pair = partner(pair, "rep", 2)
-    gather.exchange(1, pair)
+    packed = [gather.relay(level, 0, pair) for level in range(2, depth)]
+    far_pair = after(far_pair, *packed)
 
     cotangents = {0: View(cotangent)}
     for stage in reversed(range(1, depth)):
@@ -827,6 +839,7 @@
                 stacks=[[view.part(half, 2 * half) for view in cotangents.values()]],
                 ids=ids,
             )
+            far_pair = after(far_pair, value)
             cotangents = {key: view.part(0, half) for key, view in cotangents.items()}
         got = partner(value, "sub", 1 << stage)
         half = cotangents[0].shape[0]
@@ -836,22 +849,23 @@
     weights, messages, own_ups, other_ups = [], [], [], []
     for level in range(depth):
         if level == 1:
-            for later in range(2, depth):
+            for later in range(1, depth):
                 gather.exchange(later, own_ups[0])
             weights += [gather.weight(later) for later in range(1, depth)]
             weights[1] = after(weights[1], weights[2])
-        if level == 2:
-            gather.exchange(depth, other_ups[1])
         if level == 0:
-            weights.append(gather.weight(0))
-            for stage in reversed(range(1, depth - 1)):
-                far_pair = after(far_pair, gather.relay(depth, stage, weights[0]))
+            weights.append(first_map)
             outs = fused(mid_forward, "mid_forward", term0, near0, far_pair, weights[0])
         else:
             outs = fused(up_forward, "up_forward", own_ups[-1], other_ups[-1], weights[level])
         messages.append(outs[0])
         own_ups.append(outs[1])
         other_ups.append(partner(outs[2], "sub", 1 << level))
+        if level == 0:
+            early = partner(after(messages[0], other_ups[0]), "sub", 1)
+        if level == 1:
+            other_ups[1] = after(other_ups[1], early)
+    gather.exchange(depth, other_ups[-1])
     (root,) = fused(top_forward, "top_forward", own_ups[-1], other_ups[-1])
 
     turns = [[[View(message)], []] for message in messages]
@@ -878,7 +892,7 @@
         (value,) = step(lambda: (), "stack", [], stacks=[to_stack(stage, levels)], ids=ids)
         gather_turns(stage, value, levels)
 
-    gather_turns(0, after(messages[0], other_ups[0]), [0])
+    turns[0][1].append(View(early))
     for level in range(1, depth):
         gather_turns(level, after(messages[level], own_ups[level]), [level])
     for stage in reversed(range(2, depth - 1)):
@@ -889,7 +903,7 @@
     root, grad_value, grad_gate, grad_msg, give, value = step(
         head_body,
         "head",
-        [after(root, turns[0][1][0].array), root_high, head_maps],
+        [root, root_high, head_maps],
         parts=[cotangents[2 * i] for i in range(sub_count // 2)],
         stacks=[to_stack(1, range(2, depth))],
         ids=ids,

time: 147 us -> 144 us (0.980)
  starting transfers between devices: 48.2 us -> 43.9 us
    ppermute x50 -> x49, starting transfers between devices: 48.2 us -> 43.9 us  [partner(): lax.ppermute(value, axis, [(i, i ^ offset) for i in range(lax.axis_size(a...]
    ppermute x50 -> x49, waiting for transfers between devices: 62.7 us -> 64.1 us  [partner(): lax.ppermute(value, axis, [(i, i ^ offset) for i in range(lax.axis_size(a...]
    pallas_call x16 -> x17, Pallas kernels: 10 us -> 9.88 us  [fused(): pl.pallas_call(kernel, out_shape=shapes, in_specs=[smem_block()] * (len(a...]
  transfers between devices with their start and end apart: 50 -> 49, of which waited for: 26 -> 24; matrix products, arithmetic and copies ran while one was open for 0% -> 0% of each run, Pallas kernels for 18% -> 17%
where the time goes in v7:
time: 144 us
  waiting for transfers between devices  64.1 us (45%)
  starting transfers between devices  43.9 us (30%)
  Pallas kernels  32.4 us (22%)
  local copies, waits for them, and re-layouts  2.21 us (2%)
    ppermute x49, waiting for transfers between devices, partner(): lax.ppermute(value, axis, [(i, i ^ offset) for i in range(lax.axis_size(a...  64.1 us
    ppermute x49, starting transfers between devices, partner(): lax.ppermute(value, axis, [(i, i ^ offset) for i in range(lax.axis_size(a...  43.9 us
    pallas_call x17, Pallas kernels, fused(): pl.pallas_call(kernel, out_shape=shapes, in_specs=[smem_block()] * (len(a...  9.88 us
    pallas_call x1, Pallas kernels, leaf_backward(): pl.pallas_call(leaf_backward_kernel, out_shape=[jax.ShapeDtypeStruct(leaf...  5.8 us
  transfers between devices with their start and end apart: 49, of which 24 were waited for; matrix products, arithmetic and copies ran while one was open for 0% of the time, Pallas kernels for 17%

profile of v7, /device:TPU:0, one launch (start us, length us, event | category | flops | bytes accessed | tf_op | source)
XLA Modules:
  0.0 143.7 jit_solution(13677379365655706582)
XLA Ops:
  0.7 2.2 %copy-done.2 = bf16[1,1024,2,1024]{3,2,1,0:T(2,128)(2,1)S(1)} copy-done((bf16[1,1024,2,1024]{3,2,1,0:T(2,128)(2,1)S(1)}, bf16[1,1024,2,1024]{3,2,1,0:T(2,128)(2,1)}, u32[]{:S(2)}) %copy-start.2) | copy-done | bytes 4194328
  2.9 2.7 %cut_maps.1 = (bf16[1024,512]{1,0:T(8,128)(2,1)S(1)}, bf16[512,512]{1,0:T(8,128)(2,1)}, bf16[512,512]{1,0:T(8,128)(2,1)S(1)}, bf16[1024,256]{1,0:T(8,128)(2,1)S(...) custom-call(s32[2]{0:T(128)S(1)} %pad_add_fusion.ids_ref.refs_0_, ...), custom_call_target="tpu_custom_call" | custom-call | tf_op jit(solution)/shard_map/cut_maps/pallas_call | solution.py:287
  5.6 2.1 %place.1 = (bf16[4,128,256]{2,1,0:T(8,128)(2,1)S(1)}, bf16[4,128,256]{2,1,0:T(8,128)(2,1)S(1)}, bf16[4,128,256]{2,1,0:T(8,128)(2,1)S(1)}, bf16[4,128,256]{2,1,0:...) custom-call(s32[2]{0:T(128)S(1)} %pad_add_fusion.ids_ref.refs_0_, s32[16]{0:T(128)S(1)} %copy-done.5, ...), custom_call_target="tpu_custom_call" | custom-call | tf_op jit(solution)/shard_map/place/pallas_call | solution.py:102
  8.2 2.6 %collective-permute-start.11 = (bf16[512,896]{1,0:T(8,128)(2,1)S(1)}, bf16[512,896]{1,0:T(8,128)(2,1)S(1)}, u32[]{:S(2)}, u32[]{:S(2)}) collective-permute-start(bf16[512,896]{1,0:T(8,128)(2,1)S(1)} %pack.9), channel_id=1, source_target_pairs={{0,4},{4,0},{8,12},{12,8},{16,20},{20,16},{24,28},{28,24},{1,5},{5... | collective-permute-start | bytes 2752520 | tf_op jit(solution)/shard_map/ppermute | solution.py:16
  12.5 2.7 %collective-permute-start.5 = (bf16[512,384]{1,0:T(8,128)(2,1)S(1)}, bf16[512,384]{1,0:T(8,128)(2,1)S(1)}, u32[]{:S(2)}, u32[]{:S(2)}) collective-permute-start(bf16[512,384]{1,0:T(8,128)(2,1)S(1)} %pack.5), channel_id=1, source_target_pairs={{0,16},{4,20},{8,24},{12,28},{16,0},{20,4},{24,8},{28,12},{1,17},{... | collective-permute-start | bytes 1179656 | tf_op jit(solution)/shard_map/ppermute | solution.py:16
  18.1 6.6 %collective-permute-done.3.refs_1_ = bf16[512,256]{1,0:T(8,128)(2,1)S(1)} collective-permute-done((bf16[512,256]{1,0:T(8,128)(2,1)S(1)}, bf16[512,256]{1,0:T(8,128)(2,1)S(1)}, u32[]{:S(2)}, u32[]{:S(2)}) %collective-permute-start.3) | collective-permute-done | bytes 262176 | tf_op jit(solution)/shard_map/ppermute | solution.py:16
  26.1 6.8 %collective-permute-done.5.refs_1_.refs_0_ = bf16[512,384]{1,0:T(8,128)(2,1)S(1)} collective-permute-done((bf16[512,384]{1,0:T(8,128)(2,1)S(1)}, bf16[512,384]{1,0:T(8,128)(2,1)S(1)}, u32[]{:S(2)}, u32[]{:S(2)}) %collective-permute-start.5) | collective-permute-done | bytes 393248 | tf_op jit(solution)/shard_map/ppermute | solution.py:16
  33.0 4.4 %collective-permute-done.4.refs_2_ = bf16[512,256]{1,0:T(8,128)(2,1)S(1)} collective-permute-done((bf16[512,256]{1,0:T(8,128)(2,1)S(1)}, bf16[512,256]{1,0:T(8,128)(2,1)S(1)}, u32[]{:S(2)}, u32[]{:S(2)}) %collective-permute-start.4) | collective-permute-done | bytes 262176 | tf_op jit(solution)/shard_map/ppermute | solution.py:16
  40.8 1.8 %collective-permute-start.16 = (bf16[512,384]{1,0:T(8,128)(2,1)S(1)}, bf16[512,384]{1,0:T(8,128)(2,1)S(1)}, u32[]{:S(2)}, u32[]{:S(2)}) collective-permute-start(bf16[512,384]{1,0:T(8,128)(2,1)S(1)} %pack.8.refs_1_), channel_id=1, source_target_pairs={{0,4},{4,0},{8,12},{12,8},{16,20},{20,16},{24,28},{28,24},{1,5},{5... | collective-permute-start | bytes 1179656 | tf_op jit(solution)/shard_map/ppermute | solution.py:16
  44.1 2.6 %collective-permute-start.10 = (f32[64,128]{1,0:T(8,128)S(1)}, f32[64,128]{1,0:T(8,128)S(1)}, u32[]{:S(2)}, u32[]{:S(2)}) collective-permute-start(f32[64,128]{1,0:T(8,128)S(1)} %get-tuple-element.129), channel_id=1, source_target_pairs={{0,16},{4,20},{8,24},{12,28},{16,0},{20,4},{24,8},{28,12},{1,17},{... | collective-permute-start | bytes 98312 | tf_op jit(solution)/shard_map/ppermute | solution.py:16
  46.7 2.2 %collective-permute-done.10.refs_2_.refs_6_ = f32[64,128]{1,0:T(8,128)S(1)} collective-permute-done((f32[64,128]{1,0:T(8,128)S(1)}, f32[64,128]{1,0:T(8,128)S(1)}, u32[]{:S(2)}, u32[]{:S(2)}) %collective-permute-start.10) | collective-permute-done | bytes 32800 | tf_op jit(solution)/shard_map/ppermute | solution.py:16
  52.4 1.6 %collective-permute-start.23 = (bf16[512,512]{1,0:T(8,128)(2,1)S(1)}, bf16[512,512]{1,0:T(8,128)(2,1)S(1)}, u32[]{:S(2)}, u32[]{:S(2)}) collective-permute-start(bf16[512,512]{1,0:T(8,128)(2,1)S(1)} %pack.7), channel_id=1, source_target_pairs={{0,8},{4,12},{8,0},{12,4},{16,24},{20,28},{24,16},{28,20},{1,9},{5... | collective-permute-start | bytes 1572872 | tf_op jit(solution)/shard_map/ppermute | solution.py:16
  55.0 4.5 %collective-permute-done.13.refs_1_.refs_2_ = bf16[64,1024]{1,0:T(8,128)(2,1)S(1)} collective-permute-done((bf16[64,1024]{1,0:T(8,128)(2,1)S(1)}, bf16[64,1024]{1,0:T(8,128)(2,1)S(1)}, u32[]{:S(2)}, u32[]{:S(2)}) %collective-permute-start.13) | collective-permute-done | bytes 131104 | tf_op jit(solution)/shard_map/ppermute | solution.py:16
  64.2 4.1 %collective-permute-done.20.refs_9_.refs_1_.refs_5_ = bf16[128,1024]{1,0:T(8,128)(2,1)S(1)} collective-permute-done((bf16[128,1024]{1,0:T(8,128)(2,1)S(1)}, bf16[128,1024]{1,0:T(8,128)(2,1)S(1)}, u32[]{:S(2)}, u32[]{:S(2)}) %collective-permute-start.20) | collective-permute-done | bytes 262176 | tf_op jit(solution)/shard_map/ppermute | solution.py:16
  68.8 2.6 %collective-permute-start.21 = (bf16[16,1024]{1,0:T(8,128)(2,1)S(1)}, bf16[16,1024]{1,0:T(8,128)(2,1)S(1)}, u32[]{:S(2)}, u32[]{:S(2)}) collective-permute-start(bf16[16,1024]{1,0:T(8,128)(2,1)S(1)} %get-tuple-element.150), channel_id=1, source_target_pairs={{0,16},{4,20},{8,24},{12,28},{16,0},{20,4},{24,8},{28,12},{1,17},{... | collective-permute-start | bytes 98312 | tf_op jit(solution)/shard_map/ppermute | solution.py:16
  71.5 2.2 %collective-permute-done.21.refs_1_.refs_2_ = bf16[16,1024]{1,0:T(8,128)(2,1)S(1)} collective-permute-done((bf16[16,1024]{1,0:T(8,128)(2,1)S(1)}, bf16[16,1024]{1,0:T(8,128)(2,1)S(1)}, u32[]{:S(2)}, u32[]{:S(2)}) %collective-permute-start.21) | collective-permute-done | bytes 32800 | tf_op jit(solution)/shard_map/ppermute | solution.py:16
  74.2 2.7 %collective-permute-start.27 = (bf16[32,1024]{1,0:T(8,128)(2,1)S(1)}, bf16[32,1024]{1,0:T(8,128)(2,1)S(1)}, u32[]{:S(2)}, u32[]{:S(2)}) collective-permute-start(bf16[32,1024]{1,0:T(8,128)(2,1)S(1)} %get-tuple-element.155.refs_7_.refs_13_.refs_8_.refs_9_), channel_id=1, source_target_pairs={{0,16},{4,20},{8,24},{12,28},{16,0},{20,4},{24,8},{28,12},{1,17},{... | collective-permute-start | bytes 196616 | tf_op jit(solution)/shard_map/ppermute | solution.py:16
  82.6 1.7 %head.1 = (bf16[32,1024]{1,0:T(8,128)(2,1)S(1)}, bf16[32,512]{1,0:T(8,128)(2,1)S(1)}, bf16[32,512]{1,0:T(8,128)(2,1)S(1)}, f32[16,1024]{1,0:T(8,128)S(1)}, bf16[...) custom-call(s32[2]{0:T(128)S(1)} %pad_add_fusion.ids_ref.refs_0_, bf16[16,1024]{1,0:T(8,128)(2,1)S(1)} %top_forward.1.refs_1_, ...), custom_call_target="tpu_custom_call" | custom-call | tf_op jit(solution)/shard_map/head/pallas_call | solution.py:226
  84.7 1.7 %collective-permute-start.31 = (bf16[32,1024]{1,0:T(8,128)(2,1)S(1)}, bf16[32,1024]{1,0:T(8,128)(2,1)S(1)}, u32[]{:S(2)}, u32[]{:S(2)}) collective-permute-start(bf16[32,1024]{1,0:T(8,128)(2,1)S(1)} %get-tuple-element.161.refs_10_.refs_2_.refs_12_), channel_id=1, source_target_pairs={{0,16},{4,20},{8,24},{12,28},{16,0},{20,4},{24,8},{28,12},{1,17},{... | collective-permute-start | bytes 196616 | tf_op jit(solution)/shard_map/ppermute | solution.py:16
  86.9 3.4 %collective-permute-done.28.refs_4_ = bf16[16,1024]{1,0:T(8,128)(2,1)S(1)} collective-permute-done((bf16[16,1024]{1,0:T(8,128)(2,1)S(1)}, bf16[16,1024]{1,0:T(8,128)(2,1)S(1)}, u32[]{:S(2)}, u32[]{:S(2)}) %collective-permute-start.28) | collective-permute-done | bytes 32800 | tf_op jit(solution)/shard_map/ppermute | solution.py:16
  94.4 3.2 %collective-permute-done.32.refs_5_ = bf16[16,1024]{1,0:T(8,128)(2,1)S(1)} collective-permute-done((bf16[16,1024]{1,0:T(8,128)(2,1)S(1)}, bf16[16,1024]{1,0:T(8,128)(2,1)S(1)}, u32[]{:S(2)}, u32[]{:S(2)}) %collective-permute-start.32) | collective-permute-done | bytes 32800 | tf_op jit(solution)/shard_map/ppermute | solution.py:16
  99.1 1.7 %collective-permute-start.37 = (bf16[384,512]{1,0:T(8,128)(2,1)S(1)}, bf16[384,512]{1,0:T(8,128)(2,1)S(1)}, u32[]{:S(2)}, u32[]{:S(2)}) collective-permute-start(bf16[384,512]{1,0:T(8,128)(2,1)S(1)} %get-tuple-element.175), channel_id=1, source_target_pairs={{0,2},{1,3},{2,0},{3,1},{4,6},{5,7},{6,4},{7,5},{8,10},{9,11},{10,... | collective-permute-start | bytes 1179656 | tf_op jit(solution)/shard_map/ppermute | solution.py:16
  105.1 3.1 %collective-permute-done.35.refs_7_ = bf16[32,1024]{1,0:T(8,128)(2,1)S(1)} collective-permute-done((bf16[32,1024]{1,0:T(8,128)(2,1)S(1)}, bf16[32,1024]{1,0:T(8,128)(2,1)S(1)}, u32[]{:S(2)}, u32[]{:S(2)}) %collective-permute-start.35) | collective-permute-done | bytes 65568 | tf_op jit(solution)/shard_map/ppermute | solution.py:16
  111.7 3.0 %collective-permute-done.38.refs_6_ = bf16[64,1024]{1,0:T(8,128)(2,1)S(1)} collective-permute-done((bf16[64,1024]{1,0:T(8,128)(2,1)S(1)}, bf16[64,1024]{1,0:T(8,128)(2,1)S(1)}, u32[]{:S(2)}, u32[]{:S(2)}) %collective-permute-start.38) | collective-permute-done | bytes 131104 | tf_op jit(solution)/shard_map/ppermute | solution.py:16
  115.8 1.7 %mid_back.1 = (bf16[128,1024]{1,0:T(8,128)(2,1)S(1)}, bf16[128,1024]{1,0:T(8,128)(2,1)S(1)}, bf16[128,1024]{1,0:T(8,128)(2,1)S(1)}, bf16[128,512]{1,0:T(8,128)(2...) custom-call(s32[2]{0:T(128)S(1)} %pad_add_fusion.ids_ref.refs_0_, ...), custom_call_target="tpu_custom_call" | custom-call | tf_op jit(solution)/shard_map/mid_back/pallas_call | solution.py:226
  119.2 2.1 %leaf_first.1.refs_14_ = bf16[4,256,1024]{2,1,0:T(8,128)(2,1)S(1)} custom-call(bf16[4,128,256]{2,1,0:T(8,128)(2,1)S(1)} %get-tuple-element.103.refs_0_, bf16[4,128,256]{2,1,0:T(8,128)(2,1)S(1)} %collective-permute-done.refs_1_, bf16[128,1024]{1,0:T(8,128)(2,1)S(1)} %get-tuple-element.181.refs_2_.refs_8_, ...), custom_call_target="tpu_custom_call" | custom-call | tf_op jit(solution)/shard_map/leaf_first/pallas_call | solution.py:172
  121.2 4.4 %collective-permute-done.42.refs_1_ = bf16[128,896]{1,0:T(8,128)(2,1)S(1)} collective-permute-done((bf16[128,896]{1,0:T(8,128)(2,1)S(1)}, bf16[128,896]{1,0:T(8,128)(2,1)S(1)}, u32[]{:S(2)}, u32[]{:S(2)}) %collective-permute-start.42) | collective-permute-done | bytes 229408 | tf_op jit(solution)/shard_map/ppermute | solution.py:16
  128.5 2.3 %collective-permute-done.43.refs_11_ = bf16[128,1024]{1,0:T(8,128)(2,1)S(1)} collective-permute-done((bf16[128,1024]{1,0:T(8,128)(2,1)S(1)}, bf16[128,1024]{1,0:T(8,128)(2,1)S(1)}, u32[]{:S(2)}, u32[]{:S(2)}) %collective-permute-start.43) | collective-permute-done | bytes 262176 | tf_op jit(solution)/shard_map/ppermute | solution.py:16
  130.7 5.8 %leaf_backward.1 = (bf16[4,256,1024]{2,1,0:T(8,128)(2,1)}, bf16[1024,1024]{1,0:T(8,128)(2,1)}) custom-call(bf16[4,128,256]{2,1,0:T(8,128)(2,1)S(1)} %get-tuple-element.103.refs_0_, bf16[4,128,256]{2,1,0:T(8,128)(2,1)S(1)} %collective-permute-done.refs_1_, bf16[4,128,256]{2,1,0:T(8,128)(2,1)S(1)} %collective-permute-done.1.refs_0_.refs_2_, ...), custom_call_target="tpu_custom_call" | custom-call | tf_op jit(solution)/shard_map/leaf_backward/pallas_call | solution.py:196
  136.5 2.7 %collective-permute-done.46.refs_1_ = bf16[256,1024]{1,0:T(8,128)(2,1)S(1)} collective-permute-done((bf16[256,1024]{1,0:T(8,128)(2,1)S(1)}, bf16[256,1024]{1,0:T(8,128)(2,1)S(1)}, u32[]{:S(2)}, u32[]{:S(2)}) %collective-permute-start.46) | collective-permute-done | bytes 524320 | tf_op jit(solution)/shard_map/ppermute | solution.py:16
  139.2 1.9 %collective-permute-done.48.refs_3_ = bf16[256,1024]{1,0:T(8,128)(2,1)S(1)} collective-permute-done((bf16[256,1024]{1,0:T(8,128)(2,1)S(1)}, bf16[256,1024]{1,0:T(8,128)(2,1)S(1)}, u32[]{:S(2)}, u32[]{:S(2)}) %collective-permute-start.48) | collective-permute-done | bytes 524320 | tf_op jit(solution)/shard_map/ppermute | solution.py:16
  141.1 2.6 %upper_grads.1 = bf16[256,2,1024]{2,1,0:T(2,128)(2,1)} custom-call(s32[2]{0:T(128)S(1)} %pad_add_fusion.ids_ref.refs_0_, bf16[384,512]{1,0:T(8,128)(2,1)S(1)} %collective-permute-done.37.first_ref, bf16[512,512]{1,0:T(8,128)(2,1)S(1)} %collective-permute-done.44.second_ref, bf16[1792,256]{1,0:T(8,128)(2,1)S(1)} %collective-permute-done.45.near_ref, ...), custom_call_target="tpu_custom_call" | custom-call | tf_op jit(solution)/shard_map/upper_grads/pallas_call | solution.py:687
  (109 shorter events, 47.2 us)
Async XLA Ops:
  8.2 32.3 %collective-permute-start.11 = (bf16[512,896]{1,0:T(8,128)(2,1)S(1)}, bf16[512,896]{1,0:T(8,128)(2,1)S(1)}, u32[]{:S(2)}, u32[]{:S(2)}) collective-permute-start(bf16[512,896]{1,0:T(8,128)(2,1)S(1)} %pack.9), channel_id=1, source_target_pairs={{0,4},{4,0},{8,12},{12,8},{16,20},{20,16},{24,28},{28,24},{1,5},{5... | collective-permute-start | bytes 2752520 | tf_op jit(solution)/shard_map/ppermute | solution.py:16
  10.9 13.8 %collective-permute-start.3 = (bf16[512,256]{1,0:T(8,128)(2,1)S(1)}, bf16[512,256]{1,0:T(8,128)(2,1)S(1)}, u32[]{:S(2)}, u32[]{:S(2)}) collective-permute-start(bf16[512,256]{1,0:T(8,128)(2,1)S(1)} %get-tuple-element.111), channel_id=1, source_target_pairs={{0,8},{4,12},{8,0},{12,4},{16,24},{20,28},{24,16},{28,20},{1,9},{5... | collective-permute-start | bytes 786440 | tf_op jit(solution)/shard_map/ppermute | solution.py:16
  12.5 20.4 %collective-permute-start.5 = (bf16[512,384]{1,0:T(8,128)(2,1)S(1)}, bf16[512,384]{1,0:T(8,128)(2,1)S(1)}, u32[]{:S(2)}, u32[]{:S(2)}) collective-permute-start(bf16[512,384]{1,0:T(8,128)(2,1)S(1)} %pack.5), channel_id=1, source_target_pairs={{0,16},{4,20},{8,24},{12,28},{16,0},{20,4},{24,8},{28,12},{1,17},{... | collective-permute-start | bytes 1179656 | tf_op jit(solution)/shard_map/ppermute | solution.py:16
  15.1 17.9 %collective-permute-start.1 = (bf16[4,128,256]{2,1,0:T(8,128)(2,1)S(1)}, bf16[4,128,256]{2,1,0:T(8,128)(2,1)S(1)}, u32[]{:S(2)}, u32[]{:S(2)}) collective-permute-start(bf16[4,128,256]{2,1,0:T(8,128)(2,1)S(1)} %get-tuple-element.105), channel_id=1, source_target_pairs={{0,2},{1,3},{2,0},{3,1},{4,6},{5,7},{6,4},{7,5},{8,10},{9,11},{10,... | collective-permute-start | bytes 786440 | tf_op jit(solution)/shard_map/ppermute | solution.py:16
  24.7 12.8 %collective-permute-start.4 = (bf16[512,256]{1,0:T(8,128)(2,1)S(1)}, bf16[512,256]{1,0:T(8,128)(2,1)S(1)}, u32[]{:S(2)}, u32[]{:S(2)}) collective-permute-start(bf16[512,256]{1,0:T(8,128)(2,1)S(1)} %collective-permute-done.3.refs_1_), channel_id=1, source_target_pairs={{0,4},{4,0},{8,12},{12,8},{16,20},{20,16},{24,28},{28,24},{1,5},{5... | collective-permute-start | bytes 786440 | tf_op jit(solution)/shard_map/ppermute | solution.py:16
  26.0 11.5 %collective-permute-start.2 = (bf16[4,128,256]{2,1,0:T(8,128)(2,1)S(1)}, bf16[4,128,256]{2,1,0:T(8,128)(2,1)S(1)}, u32[]{:S(2)}, u32[]{:S(2)}) collective-permute-start(bf16[4,128,256]{2,1,0:T(8,128)(2,1)S(1)} %get-tuple-element.106), channel_id=1, source_target_pairs={{0,3},{1,2},{2,1},{3,0},{4,7},{5,6},{6,5},{7,4},{8,11},{9,10},{10,... | collective-permute-start | bytes 786440 | tf_op jit(solution)/shard_map/ppermute | solution.py:16
  32.9 7.4 %collective-permute-start.8 = (bf16[512,256]{1,0:T(8,128)(2,1)S(1)}, bf16[512,256]{1,0:T(8,128)(2,1)S(1)}, u32[]{:S(2)}, u32[]{:S(2)}) collective-permute-start(bf16[512,256]{1,0:T(8,128)(2,1)S(1)} %pack.6), channel_id=1, source_target_pairs={{0,8},{4,12},{8,0},{12,4},{16,24},{20,28},{24,16},{28,20},{1,9},{5... | collective-permute-start | bytes 786440 | tf_op jit(solution)/shard_map/ppermute | solution.py:16
  40.5 10.4 %collective-permute-start.12 = (bf16[512,896]{1,0:T(8,128)(2,1)S(1)}, bf16[512,896]{1,0:T(8,128)(2,1)S(1)}, u32[]{:S(2)}, u32[]{:S(2)}) collective-permute-start(bf16[512,896]{1,0:T(8,128)(2,1)S(1)} %collective-permute-done.11.refs_0_), channel_id=1, source_target_pairs={{0,1},{1,0},{2,3},{3,2},{4,5},{5,4},{6,7},{7,6},{8,9},{9,8},{10,11... | collective-permute-start | bytes 2752520 | tf_op jit(solution)/shard_map/ppermute | solution.py:16
  40.8 13.7 %collective-permute-start.16 = (bf16[512,384]{1,0:T(8,128)(2,1)S(1)}, bf16[512,384]{1,0:T(8,128)(2,1)S(1)}, u32[]{:S(2)}, u32[]{:S(2)}) collective-permute-start(bf16[512,384]{1,0:T(8,128)(2,1)S(1)} %pack.8.refs_1_), channel_id=1, source_target_pairs={{0,4},{4,0},{8,12},{12,8},{16,20},{20,16},{24,28},{28,24},{1,5},{5... | collective-permute-start | bytes 1179656 | tf_op jit(solution)/shard_map/ppermute | solution.py:16
  42.6 8.3 %collective-permute-start.9 = (bf16[128,1024]{1,0:T(8,128)(2,1)S(1)}, bf16[128,1024]{1,0:T(8,128)(2,1)S(1)}, u32[]{:S(2)}, u32[]{:S(2)}) collective-permute-start(bf16[128,1024]{1,0:T(8,128)(2,1)S(1)} %pair_product.1), channel_id=1, source_target_pairs={{0,2},{1,3},{2,0},{3,1},{4,6},{5,7},{6,4},{7,5},{8,10},{9,11},{10,... | collective-permute-start | bytes 786440 | tf_op jit(solution)/shard_map/ppermute | solution.py:16
  44.1 7.5 %collective-permute-start.6 = (bf16[128,1024]{1,0:T(8,128)(2,1)S(1)}, bf16[128,1024]{1,0:T(8,128)(2,1)S(1)}, u32[]{:S(2)}, u32[]{:S(2)}) collective-permute-start(bf16[128,1024]{1,0:T(8,128)(2,1)S(1)} %get-tuple-element.109), channel_id=1, source_target_pairs={{0,1},{1,0},{2,3},{3,2},{4,5},{5,4},{6,7},{7,6},{8,9},{9,8},{10,11... | collective-permute-start | bytes 786440 | tf_op jit(solution)/shard_map/ppermute | solution.py:16
  52.3 7.3 %collective-permute-start.14 = (bf16[512,256]{1,0:T(8,128)(2,1)S(1)}, bf16[512,256]{1,0:T(8,128)(2,1)S(1)}, u32[]{:S(2)}, u32[]{:S(2)}) collective-permute-start(bf16[512,256]{1,0:T(8,128)(2,1)S(1)} %collective-permute-done.3.refs_1_), channel_id=1, source_target_pairs={{0,1},{1,0},{2,3},{3,2},{4,5},{5,4},{6,7},{7,6},{8,9},{9,8},{10,11... | collective-permute-start | bytes 786440 | tf_op jit(solution)/shard_map/ppermute | solution.py:16
  52.4 19.1 %collective-permute-start.23 = (bf16[512,512]{1,0:T(8,128)(2,1)S(1)}, bf16[512,512]{1,0:T(8,128)(2,1)S(1)}, u32[]{:S(2)}, u32[]{:S(2)}) collective-permute-start(bf16[512,512]{1,0:T(8,128)(2,1)S(1)} %pack.7), channel_id=1, source_target_pairs={{0,8},{4,12},{8,0},{12,4},{16,24},{20,28},{24,16},{28,20},{1,9},{5... | collective-permute-start | bytes 1572872 | tf_op jit(solution)/shard_map/ppermute | solution.py:16
  54.0 5.6 %collective-permute-start.13 = (bf16[64,1024]{1,0:T(8,128)(2,1)S(1)}, bf16[64,1024]{1,0:T(8,128)(2,1)S(1)}, u32[]{:S(2)}, u32[]{:S(2)}) collective-permute-start(bf16[64,1024]{1,0:T(8,128)(2,1)S(1)} %get-tuple-element.136), channel_id=1, source_target_pairs={{0,4},{4,0},{8,12},{12,8},{16,20},{20,16},{24,28},{28,24},{1,5},{5... | collective-permute-start | bytes 393224 | tf_op jit(solution)/shard_map/ppermute | solution.py:16
  54.5 7.4 %collective-permute-start.17 = (bf16[512,384]{1,0:T(8,128)(2,1)S(1)}, bf16[512,384]{1,0:T(8,128)(2,1)S(1)}, u32[]{:S(2)}, u32[]{:S(2)}) collective-permute-start(bf16[512,384]{1,0:T(8,128)(2,1)S(1)} %pack.8.refs_1_), channel_id=1, source_target_pairs={{0,1},{1,0},{2,3},{3,2},{4,5},{5,4},{6,7},{7,6},{8,9},{9,8},{10,11... | collective-permute-start | bytes 1179656 | tf_op jit(solution)/shard_map/ppermute | solution.py:16
  54.5 7.4 %collective-permute-start.18 = (bf16[512,384]{1,0:T(8,128)(2,1)S(1)}, bf16[512,384]{1,0:T(8,128)(2,1)S(1)}, u32[]{:S(2)}, u32[]{:S(2)}) collective-permute-start(bf16[512,384]{1,0:T(8,128)(2,1)S(1)} %collective-permute-done.16.refs_2_), channel_id=1, source_target_pairs={{0,1},{1,0},{2,3},{3,2},{4,5},{5,4},{6,7},{7,6},{8,9},{9,8},{10,11... | collective-permute-start | bytes 1179656 | tf_op jit(solution)/shard_map/ppermute | solution.py:16
  59.6 8.7 %collective-permute-start.20 = (bf16[128,1024]{1,0:T(8,128)(2,1)S(1)}, bf16[128,1024]{1,0:T(8,128)(2,1)S(1)}, u32[]{:S(2)}, u32[]{:S(2)}) collective-permute-start(bf16[128,1024]{1,0:T(8,128)(2,1)S(1)} %get-tuple-element.197.refs_8_.refs_0_.refs_4_), channel_id=1, source_target_pairs={{0,4},{4,0},{8,12},{12,8},{16,20},{20,16},{24,28},{28,24},{1,5},{5... | collective-permute-start | bytes 786440 | tf_op jit(solution)/shard_map/ppermute | solution.py:16
  73.7 5.9 %collective-permute-start.25 = (bf16[512,512]{1,0:T(8,128)(2,1)S(1)}, bf16[512,512]{1,0:T(8,128)(2,1)S(1)}, u32[]{:S(2)}, u32[]{:S(2)}) collective-permute-start(bf16[512,512]{1,0:T(8,128)(2,1)S(1)} %collective-permute-done.23.refs_1_), channel_id=1, source_target_pairs={{0,1},{1,0},{2,3},{3,2},{4,5},{5,4},{6,7},{7,6},{8,9},{9,8},{10,11... | collective-permute-start | bytes 1572872 | tf_op jit(solution)/shard_map/ppermute | solution.py:16
  73.7 5.5 %collective-permute-start.24 = (bf16[512,384]{1,0:T(8,128)(2,1)S(1)}, bf16[512,384]{1,0:T(8,128)(2,1)S(1)}, u32[]{:S(2)}, u32[]{:S(2)}) collective-permute-start(bf16[512,384]{1,0:T(8,128)(2,1)S(1)} %collective-permute-done.5.refs_1_.refs_0_), channel_id=1, source_target_pairs={{0,1},{1,0},{2,3},{3,2},{4,5},{5,4},{6,7},{7,6},{8,9},{9,8},{10,11... | collective-permute-start | bytes 1179656 | tf_op jit(solution)/shard_map/ppermute | solution.py:16
  74.2 8.4 %collective-permute-start.27 = (bf16[32,1024]{1,0:T(8,128)(2,1)S(1)}, bf16[32,1024]{1,0:T(8,128)(2,1)S(1)}, u32[]{:S(2)}, u32[]{:S(2)}) collective-permute-start(bf16[32,1024]{1,0:T(8,128)(2,1)S(1)} %get-tuple-element.155.refs_7_.refs_13_.refs_8_.refs_9_), channel_id=1, source_target_pairs={{0,16},{4,20},{8,24},{12,28},{16,0},{20,4},{24,8},{28,12},{1,17},{... | collective-permute-start | bytes 196616 | tf_op jit(solution)/shard_map/ppermute | solution.py:16
  79.2 7.7 %collective-permute-start.29 = (bf16[64,1024]{1,0:T(8,128)(2,1)S(1)}, bf16[64,1024]{1,0:T(8,128)(2,1)S(1)}, u32[]{:S(2)}, u32[]{:S(2)}) collective-permute-start(bf16[64,1024]{1,0:T(8,128)(2,1)S(1)} %get-tuple-element.159.refs_5_.refs_10_.refs_6_), channel_id=1, source_target_pairs={{0,8},{4,12},{8,0},{12,4},{16,24},{20,28},{24,16},{28,20},{1,9},{5... | collective-permute-start | bytes 393224 | tf_op jit(solution)/shard_map/ppermute | solution.py:16
  84.2 6.1 %collective-permute-start.30 = (bf16[64,1024]{1,0:T(8,128)(2,1)S(1)}, bf16[64,1024]{1,0:T(8,128)(2,1)S(1)}, u32[]{:S(2)}, u32[]{:S(2)}) collective-permute-start(bf16[64,1024]{1,0:T(8,128)(2,1)S(1)} %get-tuple-element.160), channel_id=1, source_target_pairs={{0,8},{4,12},{8,0},{12,4},{16,24},{20,28},{24,16},{28,20},{1,9},{5... | collective-permute-start | bytes 393224 | tf_op jit(solution)/shard_map/ppermute | solution.py:16
  84.7 5.6 %collective-permute-start.31 = (bf16[32,1024]{1,0:T(8,128)(2,1)S(1)}, bf16[32,1024]{1,0:T(8,128)(2,1)S(1)}, u32[]{:S(2)}, u32[]{:S(2)}) collective-permute-start(bf16[32,1024]{1,0:T(8,128)(2,1)S(1)} %get-tuple-element.161.refs_10_.refs_2_.refs_12_), channel_id=1, source_target_pairs={{0,16},{4,20},{8,24},{12,28},{16,0},{20,4},{24,8},{28,12},{1,17},{... | collective-permute-start | bytes 196616 | tf_op jit(solution)/shard_map/ppermute | solution.py:16
  91.0 17.1 %collective-permute-start.36 = (bf16[256,1024]{1,0:T(8,128)(2,1)S(1)}, bf16[256,1024]{1,0:T(8,128)(2,1)S(1)}, u32[]{:S(2)}, u32[]{:S(2)}) collective-permute-start(bf16[256,1024]{1,0:T(8,128)(2,1)S(1)} %get-tuple-element.173), channel_id=1, source_target_pairs={{0,4},{4,0},{8,12},{12,8},{16,20},{20,16},{24,28},{28,24},{1,5},{5... | collective-permute-start | bytes 1572872 | tf_op jit(solution)/shard_map/ppermute | solution.py:16
  99.1 12.6 %collective-permute-start.37 = (bf16[384,512]{1,0:T(8,128)(2,1)S(1)}, bf16[384,512]{1,0:T(8,128)(2,1)S(1)}, u32[]{:S(2)}, u32[]{:S(2)}) collective-permute-start(bf16[384,512]{1,0:T(8,128)(2,1)S(1)} %get-tuple-element.175), channel_id=1, source_target_pairs={{0,2},{1,3},{2,0},{3,1},{4,6},{5,7},{6,4},{7,5},{8,10},{9,11},{10,... | collective-permute-start | bytes 1179656 | tf_op jit(solution)/shard_map/ppermute | solution.py:16
  102.3 5.8 %collective-permute-start.35 = (bf16[32,1024]{1,0:T(8,128)(2,1)S(1)}, bf16[32,1024]{1,0:T(8,128)(2,1)S(1)}, u32[]{:S(2)}, u32[]{:S(2)}) collective-permute-start(bf16[32,1024]{1,0:T(8,128)(2,1)S(1)} %get-tuple-element.170), channel_id=1, source_target_pairs={{0,16},{4,20},{8,24},{12,28},{16,0},{20,4},{24,8},{28,12},{1,17},{... | collective-permute-start | bytes 196616 | tf_op jit(solution)/shard_map/ppermute | solution.py:16
  111.2 16.0 %collective-permute-start.44 = (bf16[512,512]{1,0:T(8,128)(2,1)S(1)}, bf16[512,512]{1,0:T(8,128)(2,1)S(1)}, u32[]{:S(2)}, u32[]{:S(2)}) collective-permute-start(bf16[512,512]{1,0:T(8,128)(2,1)S(1)} %get-tuple-element.196), channel_id=1, source_target_pairs={{0,2},{1,3},{2,0},{3,1},{4,6},{5,7},{6,4},{7,5},{8,10},{9,11},{10,... | collective-permute-start | bytes 1572872 | tf_op jit(solution)/shard_map/ppermute | solution.py:16
  117.6 8.0 %collective-permute-start.42 = (bf16[128,896]{1,0:T(8,128)(2,1)S(1)}, bf16[128,896]{1,0:T(8,128)(2,1)S(1)}, u32[]{:S(2)}, u32[]{:S(2)}) collective-permute-start(bf16[128,896]{1,0:T(8,128)(2,1)S(1)} %get-tuple-element.186), channel_id=1, source_target_pairs={{0,4},{4,0},{8,12},{12,8},{16,20},{20,16},{24,28},{28,24},{1,5},{5... | collective-permute-start | bytes 688136 | tf_op jit(solution)/shard_map/ppermute | solution.py:16
  118.6 8.4 %collective-permute-start.41 = (bf16[128,1024]{1,0:T(8,128)(2,1)S(1)}, bf16[128,1024]{1,0:T(8,128)(2,1)S(1)}, u32[]{:S(2)}, u32[]{:S(2)}) collective-permute-start(bf16[128,1024]{1,0:T(8,128)(2,1)S(1)} %get-tuple-element.183), channel_id=1, source_target_pairs={{0,2},{1,3},{2,0},{3,1},{4,6},{5,7},{6,4},{7,5},{8,10},{9,11},{10,... | collective-permute-start | bytes 786440 | tf_op jit(solution)/shard_map/ppermute | solution.py:16
  125.7 13.6 %collective-permute-start.46 = (bf16[256,1024]{1,0:T(8,128)(2,1)S(1)}, bf16[256,1024]{1,0:T(8,128)(2,1)S(1)}, u32[]{:S(2)}, u32[]{:S(2)}) collective-permute-start(bf16[256,1024]{1,0:T(8,128)(2,1)S(1)} %side_by_side.1.refs_0_), channel_id=1, source_target_pairs={{0,2},{1,3},{2,0},{3,1},{4,6},{5,7},{6,4},{7,5},{8,10},{9,11},{10,... | collective-permute-start | bytes 1572872 | tf_op jit(solution)/shard_map/ppermute | solution.py:16
  127.8 11.4 %collective-permute-start.45 = (bf16[1792,256]{1,0:T(8,128)(2,1)S(1)}, bf16[1792,256]{1,0:T(8,128)(2,1)S(1)}, u32[]{:S(2)}, u32[]{:S(2)}) collective-permute-start(bf16[1792,256]{1,0:T(8,128)(2,1)S(1)} %near_inputs.1), channel_id=1, source_target_pairs={{0,1},{1,0},{2,3},{3,2},{4,5},{5,4},{6,7},{7,6},{8,9},{9,8},{10,11... | collective-permute-start | bytes 2752520 | tf_op jit(solution)/shard_map/ppermute | solution.py:16
  128.4 10.8 %collective-permute-start.47 = (bf16[256,1024]{1,0:T(8,128)(2,1)S(1)}, bf16[256,1024]{1,0:T(8,128)(2,1)S(1)}, u32[]{:S(2)}, u32[]{:S(2)}) collective-permute-start(bf16[256,1024]{1,0:T(8,128)(2,1)S(1)} %side_by_side.1.refs_0_), channel_id=1, source_target_pairs={{0,1},{1,0},{2,3},{3,2},{4,5},{5,4},{6,7},{7,6},{8,9},{9,8},{10,11... | collective-permute-start | bytes 1572872 | tf_op jit(solution)/shard_map/ppermute | solution.py:16
  (23 other events, 98.5 us)

commit v8 on v7

--- a/solution.py
+++ b/solution.py
@@ -450,16 +450,6 @@
         for place, offset in enumerate(offsets):
             self.held[level][offset ^ (1 << stage)] = (got, place * self.spans[level])
         return value
-
-    def top_relay(self, gate):
-        level, stage = self.depth - 1, self.depth - 1
-        pieces = [
-            (after(self.blocks[level][2], gate), 0, self.spans[level]),
-            (self.blocks[self.depth][1], 0, self.spans[self.depth]),
-        ]
-        got = partner(pack(pieces), "sub", 1 << stage)
-        self.held[level][1 << stage] = (got, 0)
-        self.held[self.depth][1 << stage] = (got, self.spans[level])
 
     def exchange(self, level, gate):
         for offset, (array, _) in self.held[level].items():
@@ -805,31 +795,30 @@
     far_both = partner(sent[3], "rep", 3)
     far_one = partner(sent[2], "rep", 2)
     placed = [sent[0], near, far_one, far_both]
-    gather.top_relay(near)
-    for level in reversed(range(1, depth - 1)):
+    for level in reversed(range(1, depth)):
         gather.relay(level, level, near)
     msg0, msg1, term0, term1 = leaf_forward(placed[:2], leaf_w, mid_w)
     near0 = partner(term1, "rep", 1)
     packed = []
     for level in range(2, depth):
         packed += [gather.relay(level, stage, term1) for stage in reversed(range(1, level))]
-    packed += [gather.relay(depth, stage, term1) for stage in reversed(range(1, depth - 1))]
-    gather.relay(1, 0, term1)
-    far_placed = [after(far_one, term1, gather.held[1][3][0], *packed), far_both]
+    far_placed = [after(far_one, term1, gather.held[1][2][0], *packed), far_both]
     msg2, msg3, term2, term3 = leaf_forward(far_placed, leaf_w, mid_w)
     near2 = partner(term3, "rep", 1)
-    near2 = after(near2, gather.held[depth - 1][2][0])
+    gather.relay(1, 0, term3)
+    near2 = after(near2, *[gather.relay(level, 0, term1) for level in range(2, depth)])
     gather.exchange(0, near2)
-    first_map = gather.weight(0)
+    gather.relay(depth, depth - 1, term1)
     (pair,) = fused(pair_product, "pair_product", term2, near2)
     far_pair = partner(pair, "rep", 2)
-    packed = [gather.relay(level, 0, pair) for level in range(2, depth)]
-    far_pair = after(far_pair, *packed)
+    first_map = gather.weight(0)
+    packed = [gather.relay(depth, stage, first_map) for stage in reversed(range(1, depth - 1))]
+    far_pair = after(far_pair, gather.held[1][3][0], *packed)
 
     cotangents = {0: View(cotangent)}
     for stage in reversed(range(1, depth)):
         if stage == depth - 1:
-            value = after(cotangent_sent, pair)
+            value = after(cotangent_sent, first_map)
         else:
             half = next(iter(cotangents.values())).shape[0] // 2
             (value,) = step(

time: 144 us -> 144 us (level)
  waiting for transfers between devices: 64.1 us -> 60.9 us
  starting transfers between devices: 43.9 us -> 46.8 us
    ppermute x49 -> x50, waiting for transfers between devices: 64.1 us -> 60.9 us  [partner(): lax.ppermute(value, axis, [(i, i ^ offset) for i in range(lax.axis_size(a...]
    ppermute x49 -> x50, starting transfers between devices: 43.9 us -> 46.8 us  [partner(): lax.ppermute(value, axis, [(i, i ^ offset) for i in range(lax.axis_size(a...]
    pallas_call x17 -> x16, Pallas kernels: 9.88 us -> 10 us  [fused(): pl.pallas_call(kernel, out_shape=shapes, in_specs=[smem_block()] * (len(a...]
  transfers between devices with their start and end apart: 49 -> 50, of which waited for: 24 -> 21; matrix products, arithmetic and copies ran while one was open for 0% -> 0% of each run, Pallas kernels for 17% -> 18%
where the time goes in v8:
time: 144 us
  waiting for transfers between devices  60.9 us (42%)
  starting transfers between devices  46.8 us (32%)
  Pallas kernels  32.6 us (23%)
  local copies, waits for them, and re-layouts  2.21 us (2%)
    ppermute x50, waiting for transfers between devices, partner(): lax.ppermute(value, axis, [(i, i ^ offset) for i in range(lax.axis_size(a...  60.9 us
    ppermute x50, starting transfers between devices, partner(): lax.ppermute(value, axis, [(i, i ^ offset) for i in range(lax.axis_size(a...  46.8 us
    pallas_call x16, Pallas kernels, fused(): pl.pallas_call(kernel, out_shape=shapes, in_specs=[smem_block()] * (len(a...  10 us
    pallas_call x1, Pallas kernels, leaf_backward(): pl.pallas_call(leaf_backward_kernel, out_shape=[jax.ShapeDtypeStruct(leaf...  5.8 us
  transfers between devices with their start and end apart: 50, of which 21 were waited for; matrix products, arithmetic and copies ran while one was open for 0% of the time, Pallas kernels for 18%

profile of v8, /device:TPU:0, one launch (start us, length us, event | category | flops | bytes accessed | tf_op | source)
XLA Modules:
  0.0 143.5 jit_solution(11150947520025316393)
XLA Ops:
  0.7 2.2 %copy-done.2 = bf16[1,1024,2,1024]{3,2,1,0:T(2,128)(2,1)S(1)} copy-done((bf16[1,1024,2,1024]{3,2,1,0:T(2,128)(2,1)S(1)}, bf16[1,1024,2,1024]{3,2,1,0:T(2,128)(2,1)}, u32[]{:S(2)}) %copy-start.2) | copy-done | bytes 4194328
  2.9 2.7 %cut_maps.1 = (bf16[1024,512]{1,0:T(8,128)(2,1)S(1)}, bf16[512,512]{1,0:T(8,128)(2,1)}, bf16[512,512]{1,0:T(8,128)(2,1)S(1)}, bf16[1024,256]{1,0:T(8,128)(2,1)S(...) custom-call(s32[2]{0:T(128)S(1)} %pad_add_fusion.ids_ref.refs_0_, ...), custom_call_target="tpu_custom_call" | custom-call | tf_op jit(solution)/shard_map/cut_maps/pallas_call | solution.py:287
  5.7 3.0 %collective-permute-start.11 = (bf16[512,896]{1,0:T(8,128)(2,1)S(1)}, bf16[512,896]{1,0:T(8,128)(2,1)S(1)}, u32[]{:S(2)}, u32[]{:S(2)}) collective-permute-start(bf16[512,896]{1,0:T(8,128)(2,1)S(1)} %pack.6), channel_id=1, source_target_pairs={{0,4},{4,0},{8,12},{12,8},{16,20},{20,16},{24,28},{28,24},{1,5},{5... | collective-permute-start | bytes 2752520 | tf_op jit(solution)/shard_map/ppermute | solution.py:16
  8.7 2.1 %place.1 = (bf16[4,128,256]{2,1,0:T(8,128)(2,1)S(1)}, bf16[4,128,256]{2,1,0:T(8,128)(2,1)S(1)}, bf16[4,128,256]{2,1,0:T(8,128)(2,1)S(1)}, bf16[4,128,256]{2,1,0:...) custom-call(s32[2]{0:T(128)S(1)} %pad_add_fusion.ids_ref.refs_0_, s32[16]{0:T(128)S(1)} %copy-done.5, ...), custom_call_target="tpu_custom_call" | custom-call | tf_op jit(solution)/shard_map/place/pallas_call | solution.py:102
  14.9 2.6 %collective-permute-start.4 = (bf16[512,128]{1,0:T(8,128)(2,1)S(1)}, bf16[512,128]{1,0:T(8,128)(2,1)S(1)}, u32[]{:S(2)}, u32[]{:S(2)}) collective-permute-start(bf16[512,128]{1,0:T(8,128)(2,1)S(1)} %get-tuple-element.116), channel_id=1, source_target_pairs={{0,16},{4,20},{8,24},{12,28},{16,0},{20,4},{24,8},{28,12},{1,17},{... | collective-permute-start | bytes 393224 | tf_op jit(solution)/shard_map/ppermute | solution.py:16
  18.9 3.8 %collective-permute-done.4.refs_1_.refs_0_ = bf16[512,128]{1,0:T(8,128)(2,1)S(1)} collective-permute-done((bf16[512,128]{1,0:T(8,128)(2,1)S(1)}, bf16[512,128]{1,0:T(8,128)(2,1)S(1)}, u32[]{:S(2)}, u32[]{:S(2)}) %collective-permute-start.4) | collective-permute-done | bytes 131104 | tf_op jit(solution)/shard_map/ppermute | solution.py:16
  22.8 3.5 %collective-permute-start.7 = (bf16[512,256]{1,0:T(8,128)(2,1)S(1)}, bf16[512,256]{1,0:T(8,128)(2,1)S(1)}, u32[]{:S(2)}, u32[]{:S(2)}) collective-permute-start(bf16[512,256]{1,0:T(8,128)(2,1)S(1)} %pack.4), channel_id=1, source_target_pairs={{0,8},{4,12},{8,0},{12,4},{16,24},{20,28},{24,16},{28,20},{1,9},{5... | collective-permute-start | bytes 786440 | tf_op jit(solution)/shard_map/ppermute | solution.py:16
  27.8 4.3 %collective-permute-done.7.refs_1_.refs_2_ = bf16[512,256]{1,0:T(8,128)(2,1)S(1)} collective-permute-done((bf16[512,256]{1,0:T(8,128)(2,1)S(1)}, bf16[512,256]{1,0:T(8,128)(2,1)S(1)}, u32[]{:S(2)}, u32[]{:S(2)}) %collective-permute-start.7) | collective-permute-done | bytes 262176 | tf_op jit(solution)/shard_map/ppermute | solution.py:16
  32.8 1.7 %collective-permute-start.10 = (bf16[512,256]{1,0:T(8,128)(2,1)S(1)}, bf16[512,256]{1,0:T(8,128)(2,1)S(1)}, u32[]{:S(2)}, u32[]{:S(2)}) collective-permute-start(bf16[512,256]{1,0:T(8,128)(2,1)S(1)} %get-tuple-element.128.refs_0_), channel_id=1, source_target_pairs={{0,16},{4,20},{8,24},{12,28},{16,0},{20,4},{24,8},{28,12},{1,17},{... | collective-permute-start | bytes 786440 | tf_op jit(solution)/shard_map/ppermute | solution.py:16
  38.2 9.5 %collective-permute-done.10.refs_1_.refs_0_ = bf16[512,256]{1,0:T(8,128)(2,1)S(1)} collective-permute-done((bf16[512,256]{1,0:T(8,128)(2,1)S(1)}, bf16[512,256]{1,0:T(8,128)(2,1)S(1)}, u32[]{:S(2)}, u32[]{:S(2)}) %collective-permute-start.10) | collective-permute-done | bytes 262176 | tf_op jit(solution)/shard_map/ppermute | solution.py:16
  47.7 1.6 %collective-permute-done.9.refs_2_ = bf16[512,256]{1,0:T(8,128)(2,1)S(1)} collective-permute-done((bf16[512,256]{1,0:T(8,128)(2,1)S(1)}, bf16[512,256]{1,0:T(8,128)(2,1)S(1)}, u32[]{:S(2)}, u32[]{:S(2)}) %collective-permute-start.9) | collective-permute-done | bytes 262176 | tf_op jit(solution)/shard_map/ppermute | solution.py:16
  49.4 3.1 %collective-permute-done.13.refs_2_.refs_6_ = f32[64,128]{1,0:T(8,128)S(1)} collective-permute-done((f32[64,128]{1,0:T(8,128)S(1)}, f32[64,128]{1,0:T(8,128)S(1)}, u32[]{:S(2)}, u32[]{:S(2)}) %collective-permute-start.13) | collective-permute-done | bytes 32800 | tf_op jit(solution)/shard_map/ppermute | solution.py:16
  56.0 3.7 %collective-permute-done.14.refs_1_.refs_2_ = bf16[64,1024]{1,0:T(8,128)(2,1)S(1)} collective-permute-done((bf16[64,1024]{1,0:T(8,128)(2,1)S(1)}, bf16[64,1024]{1,0:T(8,128)(2,1)S(1)}, u32[]{:S(2)}, u32[]{:S(2)}) %collective-permute-start.14) | collective-permute-done | bytes 131104 | tf_op jit(solution)/shard_map/ppermute | solution.py:16
  63.8 1.8 %collective-permute-start.20 = (bf16[32,1024]{1,0:T(8,128)(2,1)S(1)}, bf16[32,1024]{1,0:T(8,128)(2,1)S(1)}, u32[]{:S(2)}, u32[]{:S(2)}) collective-permute-start(bf16[32,1024]{1,0:T(8,128)(2,1)S(1)} %get-tuple-element.149), channel_id=1, source_target_pairs={{0,8},{4,12},{8,0},{12,4},{16,24},{20,28},{24,16},{28,20},{1,9},{5... | collective-permute-start | bytes 196616 | tf_op jit(solution)/shard_map/ppermute | solution.py:16
  65.6 2.8 %collective-permute-done.21.refs_9_.refs_1_.refs_5_ = bf16[128,1024]{1,0:T(8,128)(2,1)S(1)} collective-permute-done((bf16[128,1024]{1,0:T(8,128)(2,1)S(1)}, bf16[128,1024]{1,0:T(8,128)(2,1)S(1)}, u32[]{:S(2)}, u32[]{:S(2)}) %collective-permute-start.21) | collective-permute-done | bytes 262176 | tf_op jit(solution)/shard_map/ppermute | solution.py:16
  70.9 4.4 %collective-permute-done.22.refs_1_.refs_2_ = bf16[16,1024]{1,0:T(8,128)(2,1)S(1)} collective-permute-done((bf16[16,1024]{1,0:T(8,128)(2,1)S(1)}, bf16[16,1024]{1,0:T(8,128)(2,1)S(1)}, u32[]{:S(2)}, u32[]{:S(2)}) %collective-permute-start.22) | collective-permute-done | bytes 32800 | tf_op jit(solution)/shard_map/ppermute | solution.py:16
  82.0 1.7 %head.1 = (bf16[32,1024]{1,0:T(8,128)(2,1)S(1)}, bf16[32,512]{1,0:T(8,128)(2,1)S(1)}, bf16[32,512]{1,0:T(8,128)(2,1)S(1)}, f32[16,1024]{1,0:T(8,128)S(1)}, bf16[...) custom-call(s32[2]{0:T(128)S(1)} %pad_add_fusion.ids_ref.refs_0_, bf16[16,1024]{1,0:T(8,128)(2,1)S(1)} %top_forward.1.refs_1_, ...), custom_call_target="tpu_custom_call" | custom-call | tf_op jit(solution)/shard_map/head/pallas_call | solution.py:226
  84.5 2.0 %collective-permute-start.32 = (bf16[32,1024]{1,0:T(8,128)(2,1)S(1)}, bf16[32,1024]{1,0:T(8,128)(2,1)S(1)}, u32[]{:S(2)}, u32[]{:S(2)}) collective-permute-start(bf16[32,1024]{1,0:T(8,128)(2,1)S(1)} %get-tuple-element.165.refs_10_.refs_2_.refs_12_), channel_id=1, source_target_pairs={{0,16},{4,20},{8,24},{12,28},{16,0},{20,4},{24,8},{28,12},{1,17},{... | collective-permute-start | bytes 196616 | tf_op jit(solution)/shard_map/ppermute | solution.py:16
  88.0 2.4 %collective-permute-done.29.refs_4_ = bf16[16,1024]{1,0:T(8,128)(2,1)S(1)} collective-permute-done((bf16[16,1024]{1,0:T(8,128)(2,1)S(1)}, bf16[16,1024]{1,0:T(8,128)(2,1)S(1)}, u32[]{:S(2)}, u32[]{:S(2)}) %collective-permute-start.29) | collective-permute-done | bytes 32800 | tf_op jit(solution)/shard_map/ppermute | solution.py:16
  94.9 3.5 %collective-permute-done.33.refs_5_ = bf16[16,1024]{1,0:T(8,128)(2,1)S(1)} collective-permute-done((bf16[16,1024]{1,0:T(8,128)(2,1)S(1)}, bf16[16,1024]{1,0:T(8,128)(2,1)S(1)}, u32[]{:S(2)}, u32[]{:S(2)}) %collective-permute-start.33) | collective-permute-done | bytes 32800 | tf_op jit(solution)/shard_map/ppermute | solution.py:16
  103.9 1.8 %collective-permute-done.35.refs_5_ = bf16[32,1024]{1,0:T(8,128)(2,1)S(1)} collective-permute-done((bf16[32,1024]{1,0:T(8,128)(2,1)S(1)}, bf16[32,1024]{1,0:T(8,128)(2,1)S(1)}, u32[]{:S(2)}, u32[]{:S(2)}) %collective-permute-start.35) | collective-permute-done | bytes 65568 | tf_op jit(solution)/shard_map/ppermute | solution.py:16
  105.7 2.9 %collective-permute-done.36.refs_7_ = bf16[32,1024]{1,0:T(8,128)(2,1)S(1)} collective-permute-done((bf16[32,1024]{1,0:T(8,128)(2,1)S(1)}, bf16[32,1024]{1,0:T(8,128)(2,1)S(1)}, u32[]{:S(2)}, u32[]{:S(2)}) %collective-permute-start.36) | collective-permute-done | bytes 65568 | tf_op jit(solution)/shard_map/ppermute | solution.py:16
  111.7 3.5 %collective-permute-done.39.refs_6_ = bf16[64,1024]{1,0:T(8,128)(2,1)S(1)} collective-permute-done((bf16[64,1024]{1,0:T(8,128)(2,1)S(1)}, bf16[64,1024]{1,0:T(8,128)(2,1)S(1)}, u32[]{:S(2)}, u32[]{:S(2)}) %collective-permute-start.39) | collective-permute-done | bytes 131104 | tf_op jit(solution)/shard_map/ppermute | solution.py:16
  115.6 1.7 %mid_back.1 = (bf16[128,1024]{1,0:T(8,128)(2,1)S(1)}, bf16[128,1024]{1,0:T(8,128)(2,1)S(1)}, bf16[128,1024]{1,0:T(8,128)(2,1)S(1)}, bf16[128,512]{1,0:T(8,128)(2...) custom-call(s32[2]{0:T(128)S(1)} %pad_add_fusion.ids_ref.refs_0_, ...), custom_call_target="tpu_custom_call" | custom-call | tf_op jit(solution)/shard_map/mid_back/pallas_call | solution.py:226
  117.4 1.7 %collective-permute-start.43 = (bf16[128,896]{1,0:T(8,128)(2,1)S(1)}, bf16[128,896]{1,0:T(8,128)(2,1)S(1)}, u32[]{:S(2)}, u32[]{:S(2)}) collective-permute-start(bf16[128,896]{1,0:T(8,128)(2,1)S(1)} %get-tuple-element.190), channel_id=1, source_target_pairs={{0,4},{4,0},{8,12},{12,8},{16,20},{20,16},{24,28},{28,24},{1,5},{5... | collective-permute-start | bytes 688136 | tf_op jit(solution)/shard_map/ppermute | solution.py:16
  119.7 2.1 %leaf_first.1.refs_14_ = bf16[4,256,1024]{2,1,0:T(8,128)(2,1)S(1)} custom-call(bf16[4,128,256]{2,1,0:T(8,128)(2,1)S(1)} %get-tuple-element.105.refs_0_, bf16[4,128,256]{2,1,0:T(8,128)(2,1)S(1)} %collective-permute-done.refs_1_, bf16[128,1024]{1,0:T(8,128)(2,1)S(1)} %get-tuple-element.185.refs_2_.refs_8_, ...), custom_call_target="tpu_custom_call" | custom-call | tf_op jit(solution)/shard_map/leaf_first/pallas_call | solution.py:172
  121.8 3.6 %collective-permute-done.43.refs_1_ = bf16[128,896]{1,0:T(8,128)(2,1)S(1)} collective-permute-done((bf16[128,896]{1,0:T(8,128)(2,1)S(1)}, bf16[128,896]{1,0:T(8,128)(2,1)S(1)}, u32[]{:S(2)}, u32[]{:S(2)}) %collective-permute-start.43) | collective-permute-done | bytes 229408 | tf_op jit(solution)/shard_map/ppermute | solution.py:16
  128.9 2.3 %collective-permute-done.44.refs_11_ = bf16[128,1024]{1,0:T(8,128)(2,1)S(1)} collective-permute-done((bf16[128,1024]{1,0:T(8,128)(2,1)S(1)}, bf16[128,1024]{1,0:T(8,128)(2,1)S(1)}, u32[]{:S(2)}, u32[]{:S(2)}) %collective-permute-start.44) | collective-permute-done | bytes 262176 | tf_op jit(solution)/shard_map/ppermute | solution.py:16
  131.2 5.8 %leaf_backward.1 = (bf16[4,256,1024]{2,1,0:T(8,128)(2,1)}, bf16[1024,1024]{1,0:T(8,128)(2,1)}) custom-call(bf16[4,128,256]{2,1,0:T(8,128)(2,1)S(1)} %get-tuple-element.105.refs_0_, bf16[4,128,256]{2,1,0:T(8,128)(2,1)S(1)} %collective-permute-done.refs_1_, bf16[4,128,256]{2,1,0:T(8,128)(2,1)S(1)} %collective-permute-done.1.refs_0_.refs_2_, ...), custom_call_target="tpu_custom_call" | custom-call | tf_op jit(solution)/shard_map/leaf_backward/pallas_call | solution.py:196
  137.0 2.1 %collective-permute-done.47.refs_1_ = bf16[256,1024]{1,0:T(8,128)(2,1)S(1)} collective-permute-done((bf16[256,1024]{1,0:T(8,128)(2,1)S(1)}, bf16[256,1024]{1,0:T(8,128)(2,1)S(1)}, u32[]{:S(2)}, u32[]{:S(2)}) %collective-permute-start.47) | collective-permute-done | bytes 524320 | tf_op jit(solution)/shard_map/ppermute | solution.py:16
  139.0 1.9 %collective-permute-done.49.refs_3_ = bf16[256,1024]{1,0:T(8,128)(2,1)S(1)} collective-permute-done((bf16[256,1024]{1,0:T(8,128)(2,1)S(1)}, bf16[256,1024]{1,0:T(8,128)(2,1)S(1)}, u32[]{:S(2)}, u32[]{:S(2)}) %collective-permute-start.49) | collective-permute-done | bytes 524320 | tf_op jit(solution)/shard_map/ppermute | solution.py:16
  140.9 2.6 %upper_grads.1 = bf16[256,2,1024]{2,1,0:T(2,128)(2,1)} custom-call(s32[2]{0:T(128)S(1)} %pad_add_fusion.ids_ref.refs_0_, bf16[384,512]{1,0:T(8,128)(2,1)S(1)} %collective-permute-done.38.first_ref, bf16[512,512]{1,0:T(8,128)(2,1)S(1)} %collective-permute-done.45.second_ref, bf16[1792,256]{1,0:T(8,128)(2,1)S(1)} %collective-permute-done.46.near_ref, ...), custom_call_target="tpu_custom_call" | custom-call | tf_op jit(solution)/shard_map/upper_grads/pallas_call | solution.py:677
  (110 shorter events, 48.4 us)
Async XLA Ops:
  5.7 26.5 %collective-permute-start.11 = (bf16[512,896]{1,0:T(8,128)(2,1)S(1)}, bf16[512,896]{1,0:T(8,128)(2,1)S(1)}, u32[]{:S(2)}, u32[]{:S(2)}) collective-permute-start(bf16[512,896]{1,0:T(8,128)(2,1)S(1)} %pack.6), channel_id=1, source_target_pairs={{0,4},{4,0},{8,12},{12,8},{16,20},{20,16},{24,28},{28,24},{1,5},{5... | collective-permute-start | bytes 2752520 | tf_op jit(solution)/shard_map/ppermute | solution.py:16
  10.8 15.4 %collective-permute-start.1 = (bf16[4,128,256]{2,1,0:T(8,128)(2,1)S(1)}, bf16[4,128,256]{2,1,0:T(8,128)(2,1)S(1)}, u32[]{:S(2)}, u32[]{:S(2)}) collective-permute-start(bf16[4,128,256]{2,1,0:T(8,128)(2,1)S(1)} %get-tuple-element.107), channel_id=1, source_target_pairs={{0,2},{1,3},{2,0},{3,1},{4,6},{5,7},{6,4},{7,5},{8,10},{9,11},{10,... | collective-permute-start | bytes 786440 | tf_op jit(solution)/shard_map/ppermute | solution.py:16
  12.4 13.9 %collective-permute-start.3 = (bf16[512,256]{1,0:T(8,128)(2,1)S(1)}, bf16[512,256]{1,0:T(8,128)(2,1)S(1)}, u32[]{:S(2)}, u32[]{:S(2)}) collective-permute-start(bf16[512,256]{1,0:T(8,128)(2,1)S(1)} %get-tuple-element.113), channel_id=1, source_target_pairs={{0,8},{4,12},{8,0},{12,4},{16,24},{20,28},{24,16},{28,20},{1,9},{5... | collective-permute-start | bytes 786440 | tf_op jit(solution)/shard_map/ppermute | solution.py:16
  14.0 12.3 %collective-permute-start.2 = (bf16[4,128,256]{2,1,0:T(8,128)(2,1)S(1)}, bf16[4,128,256]{2,1,0:T(8,128)(2,1)S(1)}, u32[]{:S(2)}, u32[]{:S(2)}) collective-permute-start(bf16[4,128,256]{2,1,0:T(8,128)(2,1)S(1)} %get-tuple-element.108), channel_id=1, source_target_pairs={{0,3},{1,2},{2,1},{3,0},{4,7},{5,6},{6,5},{7,4},{8,11},{9,10},{10,... | collective-permute-start | bytes 786440 | tf_op jit(solution)/shard_map/ppermute | solution.py:16
  14.9 7.8 %collective-permute-start.4 = (bf16[512,128]{1,0:T(8,128)(2,1)S(1)}, bf16[512,128]{1,0:T(8,128)(2,1)S(1)}, u32[]{:S(2)}, u32[]{:S(2)}) collective-permute-start(bf16[512,128]{1,0:T(8,128)(2,1)S(1)} %get-tuple-element.116), channel_id=1, source_target_pairs={{0,16},{4,20},{8,24},{12,28},{16,0},{20,4},{24,8},{28,12},{1,17},{... | collective-permute-start | bytes 393224 | tf_op jit(solution)/shard_map/ppermute | solution.py:16
  22.8 9.3 %collective-permute-start.7 = (bf16[512,256]{1,0:T(8,128)(2,1)S(1)}, bf16[512,256]{1,0:T(8,128)(2,1)S(1)}, u32[]{:S(2)}, u32[]{:S(2)}) collective-permute-start(bf16[512,256]{1,0:T(8,128)(2,1)S(1)} %pack.4), channel_id=1, source_target_pairs={{0,8},{4,12},{8,0},{12,4},{16,24},{20,28},{24,16},{28,20},{1,9},{5... | collective-permute-start | bytes 786440 | tf_op jit(solution)/shard_map/ppermute | solution.py:16
  32.2 23.3 %collective-permute-start.17 = (bf16[512,384]{1,0:T(8,128)(2,1)S(1)}, bf16[512,384]{1,0:T(8,128)(2,1)S(1)}, u32[]{:S(2)}, u32[]{:S(2)}) collective-permute-start(bf16[512,384]{1,0:T(8,128)(2,1)S(1)} %pack.5.refs_1_), channel_id=1, source_target_pairs={{0,4},{4,0},{8,12},{12,8},{16,20},{20,16},{24,28},{28,24},{1,5},{5... | collective-permute-start | bytes 1179656 | tf_op jit(solution)/shard_map/ppermute | solution.py:16
  32.8 14.9 %collective-permute-start.10 = (bf16[512,256]{1,0:T(8,128)(2,1)S(1)}, bf16[512,256]{1,0:T(8,128)(2,1)S(1)}, u32[]{:S(2)}, u32[]{:S(2)}) collective-permute-start(bf16[512,256]{1,0:T(8,128)(2,1)S(1)} %get-tuple-element.128.refs_0_), channel_id=1, source_target_pairs={{0,16},{4,20},{8,24},{12,28},{16,0},{20,4},{24,8},{28,12},{1,17},{... | collective-permute-start | bytes 786440 | tf_op jit(solution)/shard_map/ppermute | solution.py:16
  34.5 14.9 %collective-permute-start.9 = (bf16[512,256]{1,0:T(8,128)(2,1)S(1)}, bf16[512,256]{1,0:T(8,128)(2,1)S(1)}, u32[]{:S(2)}, u32[]{:S(2)}) collective-permute-start(bf16[512,256]{1,0:T(8,128)(2,1)S(1)} %collective-permute-done.3.refs_1_), channel_id=1, source_target_pairs={{0,4},{4,0},{8,12},{12,8},{16,20},{20,16},{24,28},{28,24},{1,5},{5... | collective-permute-start | bytes 786440 | tf_op jit(solution)/shard_map/ppermute | solution.py:16
  36.1 13.3 %collective-permute-start.8 = (bf16[128,1024]{1,0:T(8,128)(2,1)S(1)}, bf16[128,1024]{1,0:T(8,128)(2,1)S(1)}, u32[]{:S(2)}, u32[]{:S(2)}) collective-permute-start(bf16[128,1024]{1,0:T(8,128)(2,1)S(1)} %pair_product.1), channel_id=1, source_target_pairs={{0,2},{1,3},{2,0},{3,1},{4,6},{5,7},{6,4},{7,5},{8,10},{9,11},{10,... | collective-permute-start | bytes 786440 | tf_op jit(solution)/shard_map/ppermute | solution.py:16
  37.5 15.5 %collective-permute-start.5 = (bf16[128,1024]{1,0:T(8,128)(2,1)S(1)}, bf16[128,1024]{1,0:T(8,128)(2,1)S(1)}, u32[]{:S(2)}, u32[]{:S(2)}) collective-permute-start(bf16[128,1024]{1,0:T(8,128)(2,1)S(1)} %get-tuple-element.111), channel_id=1, source_target_pairs={{0,1},{1,0},{2,3},{3,2},{4,5},{5,4},{6,7},{7,6},{8,9},{9,8},{10,11... | collective-permute-start | bytes 786440 | tf_op jit(solution)/shard_map/ppermute | solution.py:16
  53.7 6.0 %collective-permute-start.15 = (bf16[512,256]{1,0:T(8,128)(2,1)S(1)}, bf16[512,256]{1,0:T(8,128)(2,1)S(1)}, u32[]{:S(2)}, u32[]{:S(2)}) collective-permute-start(bf16[512,256]{1,0:T(8,128)(2,1)S(1)} %collective-permute-done.3.refs_1_), channel_id=1, source_target_pairs={{0,1},{1,0},{2,3},{3,2},{4,5},{5,4},{6,7},{7,6},{8,9},{9,8},{10,11... | collective-permute-start | bytes 786440 | tf_op jit(solution)/shard_map/ppermute | solution.py:16
  53.8 21.4 %collective-permute-start.24 = (bf16[512,512]{1,0:T(8,128)(2,1)S(1)}, bf16[512,512]{1,0:T(8,128)(2,1)S(1)}, u32[]{:S(2)}, u32[]{:S(2)}) collective-permute-start(bf16[512,512]{1,0:T(8,128)(2,1)S(1)} %pack.7), channel_id=1, source_target_pairs={{0,8},{4,12},{8,0},{12,4},{16,24},{20,28},{24,16},{28,20},{1,9},{5... | collective-permute-start | bytes 1572872 | tf_op jit(solution)/shard_map/ppermute | solution.py:16
  53.9 5.8 %collective-permute-start.14 = (bf16[64,1024]{1,0:T(8,128)(2,1)S(1)}, bf16[64,1024]{1,0:T(8,128)(2,1)S(1)}, u32[]{:S(2)}, u32[]{:S(2)}) collective-permute-start(bf16[64,1024]{1,0:T(8,128)(2,1)S(1)} %get-tuple-element.140), channel_id=1, source_target_pairs={{0,4},{4,0},{8,12},{12,8},{16,20},{20,16},{24,28},{28,24},{1,5},{5... | collective-permute-start | bytes 393224 | tf_op jit(solution)/shard_map/ppermute | solution.py:16
  55.5 6.6 %collective-permute-start.18 = (bf16[512,384]{1,0:T(8,128)(2,1)S(1)}, bf16[512,384]{1,0:T(8,128)(2,1)S(1)}, u32[]{:S(2)}, u32[]{:S(2)}) collective-permute-start(bf16[512,384]{1,0:T(8,128)(2,1)S(1)} %pack.5.refs_1_), channel_id=1, source_target_pairs={{0,1},{1,0},{2,3},{3,2},{4,5},{5,4},{6,7},{7,6},{8,9},{9,8},{10,11... | collective-permute-start | bytes 1179656 | tf_op jit(solution)/shard_map/ppermute | solution.py:16
  55.5 6.6 %collective-permute-start.19 = (bf16[512,384]{1,0:T(8,128)(2,1)S(1)}, bf16[512,384]{1,0:T(8,128)(2,1)S(1)}, u32[]{:S(2)}, u32[]{:S(2)}) collective-permute-start(bf16[512,384]{1,0:T(8,128)(2,1)S(1)} %collective-permute-done.17.refs_2_), channel_id=1, source_target_pairs={{0,1},{1,0},{2,3},{3,2},{4,5},{5,4},{6,7},{7,6},{8,9},{9,8},{10,11... | collective-permute-start | bytes 1179656 | tf_op jit(solution)/shard_map/ppermute | solution.py:16
  59.7 8.7 %collective-permute-start.21 = (bf16[128,1024]{1,0:T(8,128)(2,1)S(1)}, bf16[128,1024]{1,0:T(8,128)(2,1)S(1)}, u32[]{:S(2)}, u32[]{:S(2)}) collective-permute-start(bf16[128,1024]{1,0:T(8,128)(2,1)S(1)} %get-tuple-element.201.refs_8_.refs_0_.refs_4_), channel_id=1, source_target_pairs={{0,4},{4,0},{8,12},{12,8},{16,20},{20,16},{24,28},{28,24},{1,5},{5... | collective-permute-start | bytes 786440 | tf_op jit(solution)/shard_map/ppermute | solution.py:16
  63.8 5.7 %collective-permute-start.20 = (bf16[32,1024]{1,0:T(8,128)(2,1)S(1)}, bf16[32,1024]{1,0:T(8,128)(2,1)S(1)}, u32[]{:S(2)}, u32[]{:S(2)}) collective-permute-start(bf16[32,1024]{1,0:T(8,128)(2,1)S(1)} %get-tuple-element.149), channel_id=1, source_target_pairs={{0,8},{4,12},{8,0},{12,4},{16,24},{20,28},{24,16},{28,20},{1,9},{5... | collective-permute-start | bytes 196616 | tf_op jit(solution)/shard_map/ppermute | solution.py:16
  75.8 6.3 %collective-permute-start.28 = (bf16[32,1024]{1,0:T(8,128)(2,1)S(1)}, bf16[32,1024]{1,0:T(8,128)(2,1)S(1)}, u32[]{:S(2)}, u32[]{:S(2)}) collective-permute-start(bf16[32,1024]{1,0:T(8,128)(2,1)S(1)} %get-tuple-element.159.refs_7_.refs_13_.refs_8_.refs_9_), channel_id=1, source_target_pairs={{0,16},{4,20},{8,24},{12,28},{16,0},{20,4},{24,8},{28,12},{1,17},{... | collective-permute-start | bytes 196616 | tf_op jit(solution)/shard_map/ppermute | solution.py:16
  79.6 8.4 %collective-permute-start.30 = (bf16[64,1024]{1,0:T(8,128)(2,1)S(1)}, bf16[64,1024]{1,0:T(8,128)(2,1)S(1)}, u32[]{:S(2)}, u32[]{:S(2)}) collective-permute-start(bf16[64,1024]{1,0:T(8,128)(2,1)S(1)} %get-tuple-element.163.refs_5_.refs_10_.refs_6_), channel_id=1, source_target_pairs={{0,8},{4,12},{8,0},{12,4},{16,24},{20,28},{24,16},{28,20},{1,9},{5... | collective-permute-start | bytes 393224 | tf_op jit(solution)/shard_map/ppermute | solution.py:16
  83.7 6.7 %collective-permute-start.31 = (bf16[64,1024]{1,0:T(8,128)(2,1)S(1)}, bf16[64,1024]{1,0:T(8,128)(2,1)S(1)}, u32[]{:S(2)}, u32[]{:S(2)}) collective-permute-start(bf16[64,1024]{1,0:T(8,128)(2,1)S(1)} %get-tuple-element.164), channel_id=1, source_target_pairs={{0,8},{4,12},{8,0},{12,4},{16,24},{20,28},{24,16},{28,20},{1,9},{5... | collective-permute-start | bytes 393224 | tf_op jit(solution)/shard_map/ppermute | solution.py:16
  84.5 5.9 %collective-permute-start.32 = (bf16[32,1024]{1,0:T(8,128)(2,1)S(1)}, bf16[32,1024]{1,0:T(8,128)(2,1)S(1)}, u32[]{:S(2)}, u32[]{:S(2)}) collective-permute-start(bf16[32,1024]{1,0:T(8,128)(2,1)S(1)} %get-tuple-element.165.refs_10_.refs_2_.refs_12_), channel_id=1, source_target_pairs={{0,16},{4,20},{8,24},{12,28},{16,0},{20,4},{24,8},{28,12},{1,17},{... | collective-permute-start | bytes 196616 | tf_op jit(solution)/shard_map/ppermute | solution.py:16
  91.2 17.4 %collective-permute-start.37 = (bf16[256,1024]{1,0:T(8,128)(2,1)S(1)}, bf16[256,1024]{1,0:T(8,128)(2,1)S(1)}, u32[]{:S(2)}, u32[]{:S(2)}) collective-permute-start(bf16[256,1024]{1,0:T(8,128)(2,1)S(1)} %get-tuple-element.177), channel_id=1, source_target_pairs={{0,4},{4,0},{8,12},{12,8},{16,20},{20,16},{24,28},{28,24},{1,5},{5... | collective-permute-start | bytes 1572872 | tf_op jit(solution)/shard_map/ppermute | solution.py:16
  92.7 5.6 %collective-permute-start.34 = (bf16[64,1024]{1,0:T(8,128)(2,1)S(1)}, bf16[64,1024]{1,0:T(8,128)(2,1)S(1)}, u32[]{:S(2)}, u32[]{:S(2)}) collective-permute-start(bf16[64,1024]{1,0:T(8,128)(2,1)S(1)} %get-tuple-element.170), channel_id=1, source_target_pairs={{0,8},{4,12},{8,0},{12,4},{16,24},{20,28},{24,16},{28,20},{1,9},{5... | collective-permute-start | bytes 393224 | tf_op jit(solution)/shard_map/ppermute | solution.py:16
  99.9 11.8 %collective-permute-start.38 = (bf16[384,512]{1,0:T(8,128)(2,1)S(1)}, bf16[384,512]{1,0:T(8,128)(2,1)S(1)}, u32[]{:S(2)}, u32[]{:S(2)}) collective-permute-start(bf16[384,512]{1,0:T(8,128)(2,1)S(1)} %get-tuple-element.179), channel_id=1, source_target_pairs={{0,2},{1,3},{2,0},{3,1},{4,6},{5,7},{6,4},{7,5},{8,10},{9,11},{10,... | collective-permute-start | bytes 1179656 | tf_op jit(solution)/shard_map/ppermute | solution.py:16
  102.6 6.0 %collective-permute-start.36 = (bf16[32,1024]{1,0:T(8,128)(2,1)S(1)}, bf16[32,1024]{1,0:T(8,128)(2,1)S(1)}, u32[]{:S(2)}, u32[]{:S(2)}) collective-permute-start(bf16[32,1024]{1,0:T(8,128)(2,1)S(1)} %get-tuple-element.174), channel_id=1, source_target_pairs={{0,16},{4,20},{8,24},{12,28},{16,0},{20,4},{24,8},{28,12},{1,17},{... | collective-permute-start | bytes 196616 | tf_op jit(solution)/shard_map/ppermute | solution.py:16
  111.1 16.5 %collective-permute-start.45 = (bf16[512,512]{1,0:T(8,128)(2,1)S(1)}, bf16[512,512]{1,0:T(8,128)(2,1)S(1)}, u32[]{:S(2)}, u32[]{:S(2)}) collective-permute-start(bf16[512,512]{1,0:T(8,128)(2,1)S(1)} %get-tuple-element.200), channel_id=1, source_target_pairs={{0,2},{1,3},{2,0},{3,1},{4,6},{5,7},{6,4},{7,5},{8,10},{9,11},{10,... | collective-permute-start | bytes 1572872 | tf_op jit(solution)/shard_map/ppermute | solution.py:16
  117.4 8.0 %collective-permute-start.43 = (bf16[128,896]{1,0:T(8,128)(2,1)S(1)}, bf16[128,896]{1,0:T(8,128)(2,1)S(1)}, u32[]{:S(2)}, u32[]{:S(2)}) collective-permute-start(bf16[128,896]{1,0:T(8,128)(2,1)S(1)} %get-tuple-element.190), channel_id=1, source_target_pairs={{0,4},{4,0},{8,12},{12,8},{16,20},{20,16},{24,28},{28,24},{1,5},{5... | collective-permute-start | bytes 688136 | tf_op jit(solution)/shard_map/ppermute | solution.py:16
  119.1 8.4 %collective-permute-start.42 = (bf16[128,1024]{1,0:T(8,128)(2,1)S(1)}, bf16[128,1024]{1,0:T(8,128)(2,1)S(1)}, u32[]{:S(2)}, u32[]{:S(2)}) collective-permute-start(bf16[128,1024]{1,0:T(8,128)(2,1)S(1)} %get-tuple-element.187), channel_id=1, source_target_pairs={{0,2},{1,3},{2,0},{3,1},{4,6},{5,7},{6,4},{7,5},{8,10},{9,11},{10,... | collective-permute-start | bytes 786440 | tf_op jit(solution)/shard_map/ppermute | solution.py:16
  125.5 13.6 %collective-permute-start.47 = (bf16[256,1024]{1,0:T(8,128)(2,1)S(1)}, bf16[256,1024]{1,0:T(8,128)(2,1)S(1)}, u32[]{:S(2)}, u32[]{:S(2)}) collective-permute-start(bf16[256,1024]{1,0:T(8,128)(2,1)S(1)} %side_by_side.1.refs_0_), channel_id=1, source_target_pairs={{0,2},{1,3},{2,0},{3,1},{4,6},{5,7},{6,4},{7,5},{8,10},{9,11},{10,... | collective-permute-start | bytes 1572872 | tf_op jit(solution)/shard_map/ppermute | solution.py:16
  128.3 10.8 %collective-permute-start.46 = (bf16[1792,256]{1,0:T(8,128)(2,1)S(1)}, bf16[1792,256]{1,0:T(8,128)(2,1)S(1)}, u32[]{:S(2)}, u32[]{:S(2)}) collective-permute-start(bf16[1792,256]{1,0:T(8,128)(2,1)S(1)} %near_inputs.1), channel_id=1, source_target_pairs={{0,1},{1,0},{2,3},{3,2},{4,5},{5,4},{6,7},{7,6},{8,9},{9,8},{10,11... | collective-permute-start | bytes 2752520 | tf_op jit(solution)/shard_map/ppermute | solution.py:16
  128.8 10.2 %collective-permute-start.48 = (bf16[256,1024]{1,0:T(8,128)(2,1)S(1)}, bf16[256,1024]{1,0:T(8,128)(2,1)S(1)}, u32[]{:S(2)}, u32[]{:S(2)}) collective-permute-start(bf16[256,1024]{1,0:T(8,128)(2,1)S(1)} %side_by_side.1.refs_0_), channel_id=1, source_target_pairs={{0,1},{1,0},{2,3},{3,2},{4,5},{5,4},{6,7},{7,6},{8,9},{9,8},{10,11... | collective-permute-start | bytes 1572872 | tf_op jit(solution)/shard_map/ppermute | solution.py:16
  (24 other events, 117.0 us)

commit v9 on v8

--- a/solution.py
+++ b/solution.py
@@ -807,18 +807,10 @@
     near2 = partner(term3, "rep", 1)
     gather.relay(1, 0, term3)
     near2 = after(near2, *[gather.relay(level, 0, term1) for level in range(2, depth)])
-    gather.exchange(0, near2)
-    gather.relay(depth, depth - 1, term1)
-    (pair,) = fused(pair_product, "pair_product", term2, near2)
-    far_pair = partner(pair, "rep", 2)
-    first_map = gather.weight(0)
-    packed = [gather.relay(depth, stage, first_map) for stage in reversed(range(1, depth - 1))]
-    far_pair = after(far_pair, gather.held[1][3][0], *packed)
-
     cotangents = {0: View(cotangent)}
     for stage in reversed(range(1, depth)):
         if stage == depth - 1:
-            value = after(cotangent_sent, first_map)
+            value = after(cotangent_sent, term1)
         else:
             half = next(iter(cotangents.values())).shape[0] // 2
             (value,) = step(
@@ -828,12 +820,21 @@
                 stacks=[[view.part(half, 2 * half) for view in cotangents.values()]],
                 ids=ids,
             )
-            far_pair = after(far_pair, value)
             cotangents = {key: view.part(0, half) for key, view in cotangents.items()}
         got = partner(value, "sub", 1 << stage)
         half = cotangents[0].shape[0]
         for place_at, key in enumerate(list(cotangents)):
             cotangents[key ^ (1 << stage)] = View(got, (place_at * half, (place_at + 1) * half))
+    near2 = after(near2, value)
+    gather.exchange(0, near2)
+    gather.relay(depth, depth - 1, term1)
+    (pair,) = fused(pair_product, "pair_product", term2, near2)
+    far_pair = partner(pair, "rep", 2)
+    first_map = gather.weight(0)
+    far_pair = after(far_pair, gather.held[1][3][0])
+
+    packed = [gather.relay(depth, stage, first_map) for stage in reversed(range(1, depth - 1))]
+    far_pair = after(far_pair, *packed)
 
     weights, messages, own_ups, other_ups = [], [], [], []
     for level in range(depth):

time: 144 us -> 142 us (0.986)
  waiting for transfers between devices: 60.9 us -> 57.9 us
    ppermute x50, waiting for transfers between devices: 60.9 us -> 57.9 us  [partner(): lax.ppermute(value, axis, [(i, i ^ offset) for i in range(lax.axis_size(a...]
  transfers between devices with their start and end apart: 50 -> 50, of which waited for: 21 -> 22; matrix products, arithmetic and copies ran while one was open for 0% -> 0% of each run, Pallas kernels for 18% -> 19%
where the time goes in v9:
time: 142 us
  waiting for transfers between devices  57.9 us (41%)
  starting transfers between devices  48 us (34%)
  Pallas kernels  32.6 us (23%)
  local copies, waits for them, and re-layouts  2.21 us (2%)
    ppermute x50, waiting for transfers between devices, partner(): lax.ppermute(value, axis, [(i, i ^ offset) for i in range(lax.axis_size(a...  57.9 us
    ppermute x50, starting transfers between devices, partner(): lax.ppermute(value, axis, [(i, i ^ offset) for i in range(lax.axis_size(a...  48 us
    pallas_call x16, Pallas kernels, fused(): pl.pallas_call(kernel, out_shape=shapes, in_specs=[smem_block()] * (len(a...  10 us
    pallas_call x1, Pallas kernels, leaf_backward(): pl.pallas_call(leaf_backward_kernel, out_shape=[jax.ShapeDtypeStruct(leaf...  5.81 us
    pallas_call x2, Pallas kernels, leaf_forward(): pl.pallas_call(functools.partial(leaf_forward_kernel, count), out_shape=[...  2.88 us
  transfers between devices with their start and end apart: 50, of which 22 were waited for; matrix products, arithmetic and copies ran while one was open for 0% of the time, Pallas kernels for 19%

profile of v9, /device:TPU:0, one launch (start us, length us, event | category | flops | bytes accessed | tf_op | source)
XLA Modules:
  0.0 141.7 jit_solution(14932709732318658891)
XLA Ops:
  0.7 2.2 %copy-done.2 = bf16[1,1024,2,1024]{3,2,1,0:T(2,128)(2,1)S(1)} copy-done((bf16[1,1024,2,1024]{3,2,1,0:T(2,128)(2,1)S(1)}, bf16[1,1024,2,1024]{3,2,1,0:T(2,128)(2,1)}, u32[]{:S(2)}) %copy-start.2) | copy-done | bytes 4194328
  2.9 2.7 %cut_maps.1 = (bf16[1024,512]{1,0:T(8,128)(2,1)S(1)}, bf16[512,512]{1,0:T(8,128)(2,1)}, bf16[512,512]{1,0:T(8,128)(2,1)S(1)}, bf16[1024,256]{1,0:T(8,128)(2,1)S(...) custom-call(s32[2]{0:T(128)S(1)} %pad_add_fusion.ids_ref.refs_0_, ...), custom_call_target="tpu_custom_call" | custom-call | tf_op jit(solution)/shard_map/cut_maps/pallas_call | solution.py:287
  5.7 3.0 %collective-permute-start.12 = (bf16[512,896]{1,0:T(8,128)(2,1)S(1)}, bf16[512,896]{1,0:T(8,128)(2,1)S(1)}, u32[]{:S(2)}, u32[]{:S(2)}) collective-permute-start(bf16[512,896]{1,0:T(8,128)(2,1)S(1)} %pack.6), channel_id=1, source_target_pairs={{0,4},{4,0},{8,12},{12,8},{16,20},{20,16},{24,28},{28,24},{1,5},{5... | collective-permute-start | bytes 2752520 | tf_op jit(solution)/shard_map/ppermute | solution.py:16
  8.7 2.1 %place.1 = (bf16[4,128,256]{2,1,0:T(8,128)(2,1)S(1)}, bf16[4,128,256]{2,1,0:T(8,128)(2,1)S(1)}, bf16[4,128,256]{2,1,0:T(8,128)(2,1)S(1)}, bf16[4,128,256]{2,1,0:...) custom-call(s32[2]{0:T(128)S(1)} %pad_add_fusion.ids_ref.refs_0_, s32[16]{0:T(128)S(1)} %copy-done.5, ...), custom_call_target="tpu_custom_call" | custom-call | tf_op jit(solution)/shard_map/place/pallas_call | solution.py:102
  14.9 2.6 %collective-permute-start.4 = (bf16[512,128]{1,0:T(8,128)(2,1)S(1)}, bf16[512,128]{1,0:T(8,128)(2,1)S(1)}, u32[]{:S(2)}, u32[]{:S(2)}) collective-permute-start(bf16[512,128]{1,0:T(8,128)(2,1)S(1)} %get-tuple-element.117), channel_id=1, source_target_pairs={{0,16},{4,20},{8,24},{12,28},{16,0},{20,4},{24,8},{28,12},{1,17},{... | collective-permute-start | bytes 393224 | tf_op jit(solution)/shard_map/ppermute | solution.py:16
  18.9 3.8 %collective-permute-done.4.refs_1_.refs_0_ = bf16[512,128]{1,0:T(8,128)(2,1)S(1)} collective-permute-done((bf16[512,128]{1,0:T(8,128)(2,1)S(1)}, bf16[512,128]{1,0:T(8,128)(2,1)S(1)}, u32[]{:S(2)}, u32[]{:S(2)}) %collective-permute-start.4) | collective-permute-done | bytes 131104 | tf_op jit(solution)/shard_map/ppermute | solution.py:16
  22.8 3.5 %collective-permute-start.7 = (bf16[512,256]{1,0:T(8,128)(2,1)S(1)}, bf16[512,256]{1,0:T(8,128)(2,1)S(1)}, u32[]{:S(2)}, u32[]{:S(2)}) collective-permute-start(bf16[512,256]{1,0:T(8,128)(2,1)S(1)} %pack.4), channel_id=1, source_target_pairs={{0,8},{4,12},{8,0},{12,4},{16,24},{20,28},{24,16},{28,20},{1,9},{5... | collective-permute-start | bytes 786440 | tf_op jit(solution)/shard_map/ppermute | solution.py:16
  27.8 1.6 %collective-permute-start.8 = (f32[64,128]{1,0:T(8,128)S(1)}, f32[64,128]{1,0:T(8,128)S(1)}, u32[]{:S(2)}, u32[]{:S(2)}) collective-permute-start(f32[64,128]{1,0:T(8,128)S(1)} %get-tuple-element.129), channel_id=1, source_target_pairs={{0,16},{4,20},{8,24},{12,28},{16,0},{20,4},{24,8},{28,12},{1,17},{... | collective-permute-start | bytes 98312 | tf_op jit(solution)/shard_map/ppermute | solution.py:16
  29.5 3.3 %collective-permute-done.8.refs_2_.refs_6_ = f32[64,128]{1,0:T(8,128)S(1)} collective-permute-done((f32[64,128]{1,0:T(8,128)S(1)}, f32[64,128]{1,0:T(8,128)S(1)}, u32[]{:S(2)}, u32[]{:S(2)}) %collective-permute-start.8) | collective-permute-done | bytes 32800 | tf_op jit(solution)/shard_map/ppermute | solution.py:16
  37.2 2.6 %collective-permute-start.11 = (bf16[512,256]{1,0:T(8,128)(2,1)S(1)}, bf16[512,256]{1,0:T(8,128)(2,1)S(1)}, u32[]{:S(2)}, u32[]{:S(2)}) collective-permute-start(bf16[512,256]{1,0:T(8,128)(2,1)S(1)} %get-tuple-element.134.refs_0_), channel_id=1, source_target_pairs={{0,16},{4,20},{8,24},{12,28},{16,0},{20,4},{24,8},{28,12},{1,17},{... | collective-permute-start | bytes 786440 | tf_op jit(solution)/shard_map/ppermute | solution.py:16
  39.8 2.9 %collective-permute-done.10.refs_2_ = bf16[512,256]{1,0:T(8,128)(2,1)S(1)} collective-permute-done((bf16[512,256]{1,0:T(8,128)(2,1)S(1)}, bf16[512,256]{1,0:T(8,128)(2,1)S(1)}, u32[]{:S(2)}, u32[]{:S(2)}) %collective-permute-start.10) | collective-permute-done | bytes 262176 | tf_op jit(solution)/shard_map/ppermute | solution.py:16
  44.6 6.9 %collective-permute-done.11.refs_1_.refs_0_ = bf16[512,256]{1,0:T(8,128)(2,1)S(1)} collective-permute-done((bf16[512,256]{1,0:T(8,128)(2,1)S(1)}, bf16[512,256]{1,0:T(8,128)(2,1)S(1)}, u32[]{:S(2)}, u32[]{:S(2)}) %collective-permute-start.11) | collective-permute-done | bytes 262176 | tf_op jit(solution)/shard_map/ppermute | solution.py:16
  53.4 4.7 %collective-permute-done.14.refs_1_.refs_2_ = bf16[64,1024]{1,0:T(8,128)(2,1)S(1)} collective-permute-done((bf16[64,1024]{1,0:T(8,128)(2,1)S(1)}, bf16[64,1024]{1,0:T(8,128)(2,1)S(1)}, u32[]{:S(2)}, u32[]{:S(2)}) %collective-permute-start.14) | collective-permute-done | bytes 131104 | tf_op jit(solution)/shard_map/ppermute | solution.py:16
  62.3 1.8 %collective-permute-start.20 = (bf16[32,1024]{1,0:T(8,128)(2,1)S(1)}, bf16[32,1024]{1,0:T(8,128)(2,1)S(1)}, u32[]{:S(2)}, u32[]{:S(2)}) collective-permute-start(bf16[32,1024]{1,0:T(8,128)(2,1)S(1)} %get-tuple-element.151), channel_id=1, source_target_pairs={{0,8},{4,12},{8,0},{12,4},{16,24},{20,28},{24,16},{28,20},{1,9},{5... | collective-permute-start | bytes 196616 | tf_op jit(solution)/shard_map/ppermute | solution.py:16
  64.1 2.8 %collective-permute-done.21.refs_9_.refs_1_.refs_5_ = bf16[128,1024]{1,0:T(8,128)(2,1)S(1)} collective-permute-done((bf16[128,1024]{1,0:T(8,128)(2,1)S(1)}, bf16[128,1024]{1,0:T(8,128)(2,1)S(1)}, u32[]{:S(2)}, u32[]{:S(2)}) %collective-permute-start.21) | collective-permute-done | bytes 262176 | tf_op jit(solution)/shard_map/ppermute | solution.py:16
  68.5 1.7 %collective-permute-start.22 = (bf16[16,1024]{1,0:T(8,128)(2,1)S(1)}, bf16[16,1024]{1,0:T(8,128)(2,1)S(1)}, u32[]{:S(2)}, u32[]{:S(2)}) collective-permute-start(bf16[16,1024]{1,0:T(8,128)(2,1)S(1)} %get-tuple-element.156), channel_id=1, source_target_pairs={{0,16},{4,20},{8,24},{12,28},{16,0},{20,4},{24,8},{28,12},{1,17},{... | collective-permute-start | bytes 98312 | tf_op jit(solution)/shard_map/ppermute | solution.py:16
  70.3 3.5 %collective-permute-done.22.refs_1_.refs_2_ = bf16[16,1024]{1,0:T(8,128)(2,1)S(1)} collective-permute-done((bf16[16,1024]{1,0:T(8,128)(2,1)S(1)}, bf16[16,1024]{1,0:T(8,128)(2,1)S(1)}, u32[]{:S(2)}, u32[]{:S(2)}) %collective-permute-start.22) | collective-permute-done | bytes 32800 | tf_op jit(solution)/shard_map/ppermute | solution.py:16
  81.4 1.7 %head.1 = (bf16[32,1024]{1,0:T(8,128)(2,1)S(1)}, bf16[32,512]{1,0:T(8,128)(2,1)S(1)}, bf16[32,512]{1,0:T(8,128)(2,1)S(1)}, f32[16,1024]{1,0:T(8,128)S(1)}, bf16[...) custom-call(s32[2]{0:T(128)S(1)} %pad_add_fusion.ids_ref.refs_0_, bf16[16,1024]{1,0:T(8,128)(2,1)S(1)} %top_forward.1.refs_1_, ...), custom_call_target="tpu_custom_call" | custom-call | tf_op jit(solution)/shard_map/head/pallas_call | solution.py:226
  83.5 1.7 %collective-permute-start.32 = (bf16[32,1024]{1,0:T(8,128)(2,1)S(1)}, bf16[32,1024]{1,0:T(8,128)(2,1)S(1)}, u32[]{:S(2)}, u32[]{:S(2)}) collective-permute-start(bf16[32,1024]{1,0:T(8,128)(2,1)S(1)} %get-tuple-element.167.refs_10_.refs_2_.refs_12_), channel_id=1, source_target_pairs={{0,16},{4,20},{8,24},{12,28},{16,0},{20,4},{24,8},{28,12},{1,17},{... | collective-permute-start | bytes 196616 | tf_op jit(solution)/shard_map/ppermute | solution.py:16
  85.7 3.4 %collective-permute-done.29.refs_4_ = bf16[16,1024]{1,0:T(8,128)(2,1)S(1)} collective-permute-done((bf16[16,1024]{1,0:T(8,128)(2,1)S(1)}, bf16[16,1024]{1,0:T(8,128)(2,1)S(1)}, u32[]{:S(2)}, u32[]{:S(2)}) %collective-permute-start.29) | collective-permute-done | bytes 32800 | tf_op jit(solution)/shard_map/ppermute | solution.py:16
  91.6 1.6 %collective-permute-start.33 = (bf16[16,1024]{1,0:T(8,128)(2,1)S(1)}, bf16[16,1024]{1,0:T(8,128)(2,1)S(1)}, u32[]{:S(2)}, u32[]{:S(2)}) collective-permute-start(bf16[16,1024]{1,0:T(8,128)(2,1)S(1)} %get-tuple-element.169), channel_id=1, source_target_pairs={{0,16},{4,20},{8,24},{12,28},{16,0},{20,4},{24,8},{28,12},{1,17},{... | collective-permute-start | bytes 98312 | tf_op jit(solution)/shard_map/ppermute | solution.py:16
  93.3 3.2 %collective-permute-done.33.refs_5_ = bf16[16,1024]{1,0:T(8,128)(2,1)S(1)} collective-permute-done((bf16[16,1024]{1,0:T(8,128)(2,1)S(1)}, bf16[16,1024]{1,0:T(8,128)(2,1)S(1)}, u32[]{:S(2)}, u32[]{:S(2)}) %collective-permute-start.33) | collective-permute-done | bytes 32800 | tf_op jit(solution)/shard_map/ppermute | solution.py:16
  103.0 2.8 %collective-permute-done.36.refs_7_ = bf16[32,1024]{1,0:T(8,128)(2,1)S(1)} collective-permute-done((bf16[32,1024]{1,0:T(8,128)(2,1)S(1)}, bf16[32,1024]{1,0:T(8,128)(2,1)S(1)}, u32[]{:S(2)}, u32[]{:S(2)}) %collective-permute-start.36) | collective-permute-done | bytes 65568 | tf_op jit(solution)/shard_map/ppermute | solution.py:16
  110.5 1.9 %collective-permute-done.39.refs_6_ = bf16[64,1024]{1,0:T(8,128)(2,1)S(1)} collective-permute-done((bf16[64,1024]{1,0:T(8,128)(2,1)S(1)}, bf16[64,1024]{1,0:T(8,128)(2,1)S(1)}, u32[]{:S(2)}, u32[]{:S(2)}) %collective-permute-start.39) | collective-permute-done | bytes 131104 | tf_op jit(solution)/shard_map/ppermute | solution.py:16
  113.8 1.7 %mid_back.1 = (bf16[128,1024]{1,0:T(8,128)(2,1)S(1)}, bf16[128,1024]{1,0:T(8,128)(2,1)S(1)}, bf16[128,1024]{1,0:T(8,128)(2,1)S(1)}, bf16[128,512]{1,0:T(8,128)(2...) custom-call(s32[2]{0:T(128)S(1)} %pad_add_fusion.ids_ref.refs_0_, ...), custom_call_target="tpu_custom_call" | custom-call | tf_op jit(solution)/shard_map/mid_back/pallas_call | solution.py:226
  117.7 2.1 %leaf_first.1.refs_14_ = bf16[4,256,1024]{2,1,0:T(8,128)(2,1)S(1)} custom-call(bf16[4,128,256]{2,1,0:T(8,128)(2,1)S(1)} %get-tuple-element.106.refs_0_, bf16[4,128,256]{2,1,0:T(8,128)(2,1)S(1)} %collective-permute-done.refs_1_, bf16[128,1024]{1,0:T(8,128)(2,1)S(1)} %get-tuple-element.187.refs_2_.refs_8_, ...), custom_call_target="tpu_custom_call" | custom-call | tf_op jit(solution)/shard_map/leaf_first/pallas_call | solution.py:172
  119.7 3.8 %collective-permute-done.43.refs_1_ = bf16[128,896]{1,0:T(8,128)(2,1)S(1)} collective-permute-done((bf16[128,896]{1,0:T(8,128)(2,1)S(1)}, bf16[128,896]{1,0:T(8,128)(2,1)S(1)}, u32[]{:S(2)}, u32[]{:S(2)}) %collective-permute-start.43) | collective-permute-done | bytes 229408 | tf_op jit(solution)/shard_map/ppermute | solution.py:16
  126.6 2.3 %collective-permute-done.44.refs_11_ = bf16[128,1024]{1,0:T(8,128)(2,1)S(1)} collective-permute-done((bf16[128,1024]{1,0:T(8,128)(2,1)S(1)}, bf16[128,1024]{1,0:T(8,128)(2,1)S(1)}, u32[]{:S(2)}, u32[]{:S(2)}) %collective-permute-start.44) | collective-permute-done | bytes 262176 | tf_op jit(solution)/shard_map/ppermute | solution.py:16
  128.8 5.8 %leaf_backward.1 = (bf16[4,256,1024]{2,1,0:T(8,128)(2,1)}, bf16[1024,1024]{1,0:T(8,128)(2,1)}) custom-call(bf16[4,128,256]{2,1,0:T(8,128)(2,1)S(1)} %get-tuple-element.106.refs_0_, bf16[4,128,256]{2,1,0:T(8,128)(2,1)S(1)} %collective-permute-done.refs_1_, bf16[4,128,256]{2,1,0:T(8,128)(2,1)S(1)} %collective-permute-done.1.refs_0_.refs_2_, ...), custom_call_target="tpu_custom_call" | custom-call | tf_op jit(solution)/shard_map/leaf_backward/pallas_call | solution.py:196
  134.6 2.6 %collective-permute-done.47.refs_1_ = bf16[256,1024]{1,0:T(8,128)(2,1)S(1)} collective-permute-done((bf16[256,1024]{1,0:T(8,128)(2,1)S(1)}, bf16[256,1024]{1,0:T(8,128)(2,1)S(1)}, u32[]{:S(2)}, u32[]{:S(2)}) %collective-permute-start.47) | collective-permute-done | bytes 524320 | tf_op jit(solution)/shard_map/ppermute | solution.py:16
  137.2 1.9 %collective-permute-done.49.refs_3_ = bf16[256,1024]{1,0:T(8,128)(2,1)S(1)} collective-permute-done((bf16[256,1024]{1,0:T(8,128)(2,1)S(1)}, bf16[256,1024]{1,0:T(8,128)(2,1)S(1)}, u32[]{:S(2)}, u32[]{:S(2)}) %collective-permute-start.49) | collective-permute-done | bytes 524320 | tf_op jit(solution)/shard_map/ppermute | solution.py:16
  139.1 2.6 %upper_grads.1 = bf16[256,2,1024]{2,1,0:T(2,128)(2,1)} custom-call(s32[2]{0:T(128)S(1)} %pad_add_fusion.ids_ref.refs_0_, bf16[384,512]{1,0:T(8,128)(2,1)S(1)} %collective-permute-done.38.first_ref, bf16[512,512]{1,0:T(8,128)(2,1)S(1)} %collective-permute-done.45.second_ref, bf16[1792,256]{1,0:T(8,128)(2,1)S(1)} %collective-permute-done.46.near_ref, ...), custom_call_target="tpu_custom_call" | custom-call | tf_op jit(solution)/shard_map/upper_grads/pallas_call | solution.py:677
  (110 shorter events, 50.0 us)
Async XLA Ops:
  5.7 27.8 %collective-permute-start.12 = (bf16[512,896]{1,0:T(8,128)(2,1)S(1)}, bf16[512,896]{1,0:T(8,128)(2,1)S(1)}, u32[]{:S(2)}, u32[]{:S(2)}) collective-permute-start(bf16[512,896]{1,0:T(8,128)(2,1)S(1)} %pack.6), channel_id=1, source_target_pairs={{0,4},{4,0},{8,12},{12,8},{16,20},{20,16},{24,28},{28,24},{1,5},{5... | collective-permute-start | bytes 2752520 | tf_op jit(solution)/shard_map/ppermute | solution.py:16
  10.8 15.4 %collective-permute-start.1 = (bf16[4,128,256]{2,1,0:T(8,128)(2,1)S(1)}, bf16[4,128,256]{2,1,0:T(8,128)(2,1)S(1)}, u32[]{:S(2)}, u32[]{:S(2)}) collective-permute-start(bf16[4,128,256]{2,1,0:T(8,128)(2,1)S(1)} %get-tuple-element.108), channel_id=1, source_target_pairs={{0,2},{1,3},{2,0},{3,1},{4,6},{5,7},{6,4},{7,5},{8,10},{9,11},{10,... | collective-permute-start | bytes 786440 | tf_op jit(solution)/shard_map/ppermute | solution.py:16
  12.4 13.9 %collective-permute-start.3 = (bf16[512,256]{1,0:T(8,128)(2,1)S(1)}, bf16[512,256]{1,0:T(8,128)(2,1)S(1)}, u32[]{:S(2)}, u32[]{:S(2)}) collective-permute-start(bf16[512,256]{1,0:T(8,128)(2,1)S(1)} %get-tuple-element.114), channel_id=1, source_target_pairs={{0,8},{4,12},{8,0},{12,4},{16,24},{20,28},{24,16},{28,20},{1,9},{5... | collective-permute-start | bytes 786440 | tf_op jit(solution)/shard_map/ppermute | solution.py:16
  14.0 12.3 %collective-permute-start.2 = (bf16[4,128,256]{2,1,0:T(8,128)(2,1)S(1)}, bf16[4,128,256]{2,1,0:T(8,128)(2,1)S(1)}, u32[]{:S(2)}, u32[]{:S(2)}) collective-permute-start(bf16[4,128,256]{2,1,0:T(8,128)(2,1)S(1)} %get-tuple-element.109), channel_id=1, source_target_pairs={{0,3},{1,2},{2,1},{3,0},{4,7},{5,6},{6,5},{7,4},{8,11},{9,10},{10,... | collective-permute-start | bytes 786440 | tf_op jit(solution)/shard_map/ppermute | solution.py:16
  14.9 7.8 %collective-permute-start.4 = (bf16[512,128]{1,0:T(8,128)(2,1)S(1)}, bf16[512,128]{1,0:T(8,128)(2,1)S(1)}, u32[]{:S(2)}, u32[]{:S(2)}) collective-permute-start(bf16[512,128]{1,0:T(8,128)(2,1)S(1)} %get-tuple-element.117), channel_id=1, source_target_pairs={{0,16},{4,20},{8,24},{12,28},{16,0},{20,4},{24,8},{28,12},{1,17},{... | collective-permute-start | bytes 393224 | tf_op jit(solution)/shard_map/ppermute | solution.py:16
  22.8 10.6 %collective-permute-start.7 = (bf16[512,256]{1,0:T(8,128)(2,1)S(1)}, bf16[512,256]{1,0:T(8,128)(2,1)S(1)}, u32[]{:S(2)}, u32[]{:S(2)}) collective-permute-start(bf16[512,256]{1,0:T(8,128)(2,1)S(1)} %pack.4), channel_id=1, source_target_pairs={{0,8},{4,12},{8,0},{12,4},{16,24},{20,28},{24,16},{28,20},{1,9},{5... | collective-permute-start | bytes 786440 | tf_op jit(solution)/shard_map/ppermute | solution.py:16
  33.4 10.4 %collective-permute-start.13 = (bf16[512,896]{1,0:T(8,128)(2,1)S(1)}, bf16[512,896]{1,0:T(8,128)(2,1)S(1)}, u32[]{:S(2)}, u32[]{:S(2)}) collective-permute-start(bf16[512,896]{1,0:T(8,128)(2,1)S(1)} %collective-permute-done.12.refs_0_), channel_id=1, source_target_pairs={{0,1},{1,0},{2,3},{3,2},{4,5},{5,4},{6,7},{7,6},{8,9},{9,8},{10,11... | collective-permute-start | bytes 2752520 | tf_op jit(solution)/shard_map/ppermute | solution.py:16
  33.5 9.2 %collective-permute-start.10 = (bf16[512,256]{1,0:T(8,128)(2,1)S(1)}, bf16[512,256]{1,0:T(8,128)(2,1)S(1)}, u32[]{:S(2)}, u32[]{:S(2)}) collective-permute-start(bf16[512,256]{1,0:T(8,128)(2,1)S(1)} %collective-permute-done.3.refs_1_), channel_id=1, source_target_pairs={{0,4},{4,0},{8,12},{12,8},{16,20},{20,16},{24,28},{28,24},{1,5},{5... | collective-permute-start | bytes 786440 | tf_op jit(solution)/shard_map/ppermute | solution.py:16
  34.1 18.9 %collective-permute-start.17 = (bf16[512,384]{1,0:T(8,128)(2,1)S(1)}, bf16[512,384]{1,0:T(8,128)(2,1)S(1)}, u32[]{:S(2)}, u32[]{:S(2)}) collective-permute-start(bf16[512,384]{1,0:T(8,128)(2,1)S(1)} %pack.5.refs_1_), channel_id=1, source_target_pairs={{0,4},{4,0},{8,12},{12,8},{16,20},{20,16},{24,28},{28,24},{1,5},{5... | collective-permute-start | bytes 1179656 | tf_op jit(solution)/shard_map/ppermute | solution.py:16
  35.7 8.2 %collective-permute-start.9 = (bf16[128,1024]{1,0:T(8,128)(2,1)S(1)}, bf16[128,1024]{1,0:T(8,128)(2,1)S(1)}, u32[]{:S(2)}, u32[]{:S(2)}) collective-permute-start(bf16[128,1024]{1,0:T(8,128)(2,1)S(1)} %pair_product.1), channel_id=1, source_target_pairs={{0,2},{1,3},{2,0},{3,1},{4,6},{5,7},{6,4},{7,5},{8,10},{9,11},{10,... | collective-permute-start | bytes 786440 | tf_op jit(solution)/shard_map/ppermute | solution.py:16
  37.2 14.3 %collective-permute-start.11 = (bf16[512,256]{1,0:T(8,128)(2,1)S(1)}, bf16[512,256]{1,0:T(8,128)(2,1)S(1)}, u32[]{:S(2)}, u32[]{:S(2)}) collective-permute-start(bf16[512,256]{1,0:T(8,128)(2,1)S(1)} %get-tuple-element.134.refs_0_), channel_id=1, source_target_pairs={{0,16},{4,20},{8,24},{12,28},{16,0},{20,4},{24,8},{28,12},{1,17},{... | collective-permute-start | bytes 786440 | tf_op jit(solution)/shard_map/ppermute | solution.py:16
  42.7 8.9 %collective-permute-start.5 = (bf16[128,1024]{1,0:T(8,128)(2,1)S(1)}, bf16[128,1024]{1,0:T(8,128)(2,1)S(1)}, u32[]{:S(2)}, u32[]{:S(2)}) collective-permute-start(bf16[128,1024]{1,0:T(8,128)(2,1)S(1)} %get-tuple-element.112), channel_id=1, source_target_pairs={{0,1},{1,0},{2,3},{3,2},{4,5},{5,4},{6,7},{7,6},{8,9},{9,8},{10,11... | collective-permute-start | bytes 786440 | tf_op jit(solution)/shard_map/ppermute | solution.py:16
  52.2 6.0 %collective-permute-start.15 = (bf16[512,256]{1,0:T(8,128)(2,1)S(1)}, bf16[512,256]{1,0:T(8,128)(2,1)S(1)}, u32[]{:S(2)}, u32[]{:S(2)}) collective-permute-start(bf16[512,256]{1,0:T(8,128)(2,1)S(1)} %collective-permute-done.3.refs_1_), channel_id=1, source_target_pairs={{0,1},{1,0},{2,3},{3,2},{4,5},{5,4},{6,7},{7,6},{8,9},{9,8},{10,11... | collective-permute-start | bytes 786440 | tf_op jit(solution)/shard_map/ppermute | solution.py:16
  52.3 21.4 %collective-permute-start.24 = (bf16[512,512]{1,0:T(8,128)(2,1)S(1)}, bf16[512,512]{1,0:T(8,128)(2,1)S(1)}, u32[]{:S(2)}, u32[]{:S(2)}) collective-permute-start(bf16[512,512]{1,0:T(8,128)(2,1)S(1)} %pack.7), channel_id=1, source_target_pairs={{0,8},{4,12},{8,0},{12,4},{16,24},{20,28},{24,16},{28,20},{1,9},{5... | collective-permute-start | bytes 1572872 | tf_op jit(solution)/shard_map/ppermute | solution.py:16
  52.4 5.8 %collective-permute-start.14 = (bf16[64,1024]{1,0:T(8,128)(2,1)S(1)}, bf16[64,1024]{1,0:T(8,128)(2,1)S(1)}, u32[]{:S(2)}, u32[]{:S(2)}) collective-permute-start(bf16[64,1024]{1,0:T(8,128)(2,1)S(1)} %get-tuple-element.142), channel_id=1, source_target_pairs={{0,4},{4,0},{8,12},{12,8},{16,20},{20,16},{24,28},{28,24},{1,5},{5... | collective-permute-start | bytes 393224 | tf_op jit(solution)/shard_map/ppermute | solution.py:16
  52.9 7.6 %collective-permute-start.18 = (bf16[512,384]{1,0:T(8,128)(2,1)S(1)}, bf16[512,384]{1,0:T(8,128)(2,1)S(1)}, u32[]{:S(2)}, u32[]{:S(2)}) collective-permute-start(bf16[512,384]{1,0:T(8,128)(2,1)S(1)} %pack.5.refs_1_), channel_id=1, source_target_pairs={{0,1},{1,0},{2,3},{3,2},{4,5},{5,4},{6,7},{7,6},{8,9},{9,8},{10,11... | collective-permute-start | bytes 1179656 | tf_op jit(solution)/shard_map/ppermute | solution.py:16
  53.0 7.6 %collective-permute-start.19 = (bf16[512,384]{1,0:T(8,128)(2,1)S(1)}, bf16[512,384]{1,0:T(8,128)(2,1)S(1)}, u32[]{:S(2)}, u32[]{:S(2)}) collective-permute-start(bf16[512,384]{1,0:T(8,128)(2,1)S(1)} %collective-permute-done.17.refs_2_), channel_id=1, source_target_pairs={{0,1},{1,0},{2,3},{3,2},{4,5},{5,4},{6,7},{7,6},{8,9},{9,8},{10,11... | collective-permute-start | bytes 1179656 | tf_op jit(solution)/shard_map/ppermute | solution.py:16
  58.2 8.7 %collective-permute-start.21 = (bf16[128,1024]{1,0:T(8,128)(2,1)S(1)}, bf16[128,1024]{1,0:T(8,128)(2,1)S(1)}, u32[]{:S(2)}, u32[]{:S(2)}) collective-permute-start(bf16[128,1024]{1,0:T(8,128)(2,1)S(1)} %get-tuple-element.203.refs_8_.refs_0_.refs_4_), channel_id=1, source_target_pairs={{0,4},{4,0},{8,12},{12,8},{16,20},{20,16},{24,28},{28,24},{1,5},{5... | collective-permute-start | bytes 786440 | tf_op jit(solution)/shard_map/ppermute | solution.py:16
  62.3 5.7 %collective-permute-start.20 = (bf16[32,1024]{1,0:T(8,128)(2,1)S(1)}, bf16[32,1024]{1,0:T(8,128)(2,1)S(1)}, u32[]{:S(2)}, u32[]{:S(2)}) collective-permute-start(bf16[32,1024]{1,0:T(8,128)(2,1)S(1)} %get-tuple-element.151), channel_id=1, source_target_pairs={{0,8},{4,12},{8,0},{12,4},{16,24},{20,28},{24,16},{28,20},{1,9},{5... | collective-permute-start | bytes 196616 | tf_op jit(solution)/shard_map/ppermute | solution.py:16
  74.2 7.2 %collective-permute-start.28 = (bf16[32,1024]{1,0:T(8,128)(2,1)S(1)}, bf16[32,1024]{1,0:T(8,128)(2,1)S(1)}, u32[]{:S(2)}, u32[]{:S(2)}) collective-permute-start(bf16[32,1024]{1,0:T(8,128)(2,1)S(1)} %get-tuple-element.161.refs_7_.refs_13_.refs_8_.refs_9_), channel_id=1, source_target_pairs={{0,16},{4,20},{8,24},{12,28},{16,0},{20,4},{24,8},{28,12},{1,17},{... | collective-permute-start | bytes 196616 | tf_op jit(solution)/shard_map/ppermute | solution.py:16
  78.0 7.7 %collective-permute-start.30 = (bf16[64,1024]{1,0:T(8,128)(2,1)S(1)}, bf16[64,1024]{1,0:T(8,128)(2,1)S(1)}, u32[]{:S(2)}, u32[]{:S(2)}) collective-permute-start(bf16[64,1024]{1,0:T(8,128)(2,1)S(1)} %get-tuple-element.165.refs_5_.refs_10_.refs_6_), channel_id=1, source_target_pairs={{0,8},{4,12},{8,0},{12,4},{16,24},{20,28},{24,16},{28,20},{1,9},{5... | collective-permute-start | bytes 393224 | tf_op jit(solution)/shard_map/ppermute | solution.py:16
  83.1 6.0 %collective-permute-start.31 = (bf16[64,1024]{1,0:T(8,128)(2,1)S(1)}, bf16[64,1024]{1,0:T(8,128)(2,1)S(1)}, u32[]{:S(2)}, u32[]{:S(2)}) collective-permute-start(bf16[64,1024]{1,0:T(8,128)(2,1)S(1)} %get-tuple-element.166), channel_id=1, source_target_pairs={{0,8},{4,12},{8,0},{12,4},{16,24},{20,28},{24,16},{28,20},{1,9},{5... | collective-permute-start | bytes 393224 | tf_op jit(solution)/shard_map/ppermute | solution.py:16
  89.9 15.9 %collective-permute-start.37 = (bf16[256,1024]{1,0:T(8,128)(2,1)S(1)}, bf16[256,1024]{1,0:T(8,128)(2,1)S(1)}, u32[]{:S(2)}, u32[]{:S(2)}) collective-permute-start(bf16[256,1024]{1,0:T(8,128)(2,1)S(1)} %get-tuple-element.179), channel_id=1, source_target_pairs={{0,4},{4,0},{8,12},{12,8},{16,20},{20,16},{24,28},{28,24},{1,5},{5... | collective-permute-start | bytes 1572872 | tf_op jit(solution)/shard_map/ppermute | solution.py:16
  90.4 6.0 %collective-permute-start.34 = (bf16[64,1024]{1,0:T(8,128)(2,1)S(1)}, bf16[64,1024]{1,0:T(8,128)(2,1)S(1)}, u32[]{:S(2)}, u32[]{:S(2)}) collective-permute-start(bf16[64,1024]{1,0:T(8,128)(2,1)S(1)} %get-tuple-element.172), channel_id=1, source_target_pairs={{0,8},{4,12},{8,0},{12,4},{16,24},{20,28},{24,16},{28,20},{1,9},{5... | collective-permute-start | bytes 393224 | tf_op jit(solution)/shard_map/ppermute | solution.py:16
  98.0 12.5 %collective-permute-start.38 = (bf16[384,512]{1,0:T(8,128)(2,1)S(1)}, bf16[384,512]{1,0:T(8,128)(2,1)S(1)}, u32[]{:S(2)}, u32[]{:S(2)}) collective-permute-start(bf16[384,512]{1,0:T(8,128)(2,1)S(1)} %get-tuple-element.181), channel_id=1, source_target_pairs={{0,2},{1,3},{2,0},{3,1},{4,6},{5,7},{6,4},{7,5},{8,10},{9,11},{10,... | collective-permute-start | bytes 1179656 | tf_op jit(solution)/shard_map/ppermute | solution.py:16
  99.9 5.9 %collective-permute-start.36 = (bf16[32,1024]{1,0:T(8,128)(2,1)S(1)}, bf16[32,1024]{1,0:T(8,128)(2,1)S(1)}, u32[]{:S(2)}, u32[]{:S(2)}) collective-permute-start(bf16[32,1024]{1,0:T(8,128)(2,1)S(1)} %get-tuple-element.176), channel_id=1, source_target_pairs={{0,16},{4,20},{8,24},{12,28},{16,0},{20,4},{24,8},{28,12},{1,17},{... | collective-permute-start | bytes 196616 | tf_op jit(solution)/shard_map/ppermute | solution.py:16
  109.2 16.1 %collective-permute-start.45 = (bf16[512,512]{1,0:T(8,128)(2,1)S(1)}, bf16[512,512]{1,0:T(8,128)(2,1)S(1)}, u32[]{:S(2)}, u32[]{:S(2)}) collective-permute-start(bf16[512,512]{1,0:T(8,128)(2,1)S(1)} %get-tuple-element.202), channel_id=1, source_target_pairs={{0,2},{1,3},{2,0},{3,1},{4,6},{5,7},{6,4},{7,5},{8,10},{9,11},{10,... | collective-permute-start | bytes 1572872 | tf_op jit(solution)/shard_map/ppermute | solution.py:16
  115.6 8.0 %collective-permute-start.43 = (bf16[128,896]{1,0:T(8,128)(2,1)S(1)}, bf16[128,896]{1,0:T(8,128)(2,1)S(1)}, u32[]{:S(2)}, u32[]{:S(2)}) collective-permute-start(bf16[128,896]{1,0:T(8,128)(2,1)S(1)} %get-tuple-element.192), channel_id=1, source_target_pairs={{0,4},{4,0},{8,12},{12,8},{16,20},{20,16},{24,28},{28,24},{1,5},{5... | collective-permute-start | bytes 688136 | tf_op jit(solution)/shard_map/ppermute | solution.py:16
  116.3 8.8 %collective-permute-start.42 = (bf16[128,1024]{1,0:T(8,128)(2,1)S(1)}, bf16[128,1024]{1,0:T(8,128)(2,1)S(1)}, u32[]{:S(2)}, u32[]{:S(2)}) collective-permute-start(bf16[128,1024]{1,0:T(8,128)(2,1)S(1)} %get-tuple-element.189), channel_id=1, source_target_pairs={{0,2},{1,3},{2,0},{3,1},{4,6},{5,7},{6,4},{7,5},{8,10},{9,11},{10,... | collective-permute-start | bytes 786440 | tf_op jit(solution)/shard_map/ppermute | solution.py:16
  123.7 13.6 %collective-permute-start.47 = (bf16[256,1024]{1,0:T(8,128)(2,1)S(1)}, bf16[256,1024]{1,0:T(8,128)(2,1)S(1)}, u32[]{:S(2)}, u32[]{:S(2)}) collective-permute-start(bf16[256,1024]{1,0:T(8,128)(2,1)S(1)} %side_by_side.1.refs_0_), channel_id=1, source_target_pairs={{0,2},{1,3},{2,0},{3,1},{4,6},{5,7},{6,4},{7,5},{8,10},{9,11},{10,... | collective-permute-start | bytes 1572872 | tf_op jit(solution)/shard_map/ppermute | solution.py:16
  125.9 11.3 %collective-permute-start.46 = (bf16[1792,256]{1,0:T(8,128)(2,1)S(1)}, bf16[1792,256]{1,0:T(8,128)(2,1)S(1)}, u32[]{:S(2)}, u32[]{:S(2)}) collective-permute-start(bf16[1792,256]{1,0:T(8,128)(2,1)S(1)} %near_inputs.1), channel_id=1, source_target_pairs={{0,1},{1,0},{2,3},{3,2},{4,5},{5,4},{6,7},{7,6},{8,9},{9,8},{10,11... | collective-permute-start | bytes 2752520 | tf_op jit(solution)/shard_map/ppermute | solution.py:16
  126.5 10.7 %collective-permute-start.48 = (bf16[256,1024]{1,0:T(8,128)(2,1)S(1)}, bf16[256,1024]{1,0:T(8,128)(2,1)S(1)}, u32[]{:S(2)}, u32[]{:S(2)}) collective-permute-start(bf16[256,1024]{1,0:T(8,128)(2,1)S(1)} %side_by_side.1.refs_0_), channel_id=1, source_target_pairs={{0,1},{1,0},{2,3},{3,2},{4,5},{5,4},{6,7},{7,6},{8,9},{9,8},{10,11... | collective-permute-start | bytes 1572872 | tf_op jit(solution)/shard_map/ppermute | solution.py:16
  (24 other events, 118.6 us)

commit v10 on v9

--- a/solution.py
+++ b/solution.py
@@ -833,16 +833,15 @@
     first_map = gather.weight(0)
     far_pair = after(far_pair, gather.held[1][3][0])
 
-    packed = [gather.relay(depth, stage, first_map) for stage in reversed(range(1, depth - 1))]
-    far_pair = after(far_pair, *packed)
-
     weights, messages, own_ups, other_ups = [], [], [], []
     for level in range(depth):
         if level == 1:
             for later in range(1, depth):
                 gather.exchange(later, own_ups[0])
             weights += [gather.weight(later) for later in range(1, depth)]
-            weights[1] = after(weights[1], weights[2])
+            last = reversed(range(1, depth - 1))
+            packed = [gather.relay(depth, stage, other_ups[0]) for stage in last]
+            weights[1] = after(weights[1], weights[2], *packed)
         if level == 0:
             weights.append(first_map)
             outs = fused(mid_forward, "mid_forward", term0, near0, far_pair, weights[0])

time: 142 us -> 144 us (1.014)
  waiting for transfers between devices: 57.9 us -> 60.9 us
    ppermute x50, waiting for transfers between devices: 57.9 us -> 60.9 us  [partner(): lax.ppermute(value, axis, [(i, i ^ offset) for i in range(lax.axis_size(a...]
  transfers between devices with their start and end apart: 50 -> 50, of which waited for: 22 -> 21; matrix products, arithmetic and copies ran while one was open for 0% -> 0% of each run, Pallas kernels for 19% -> 18%
where the time goes in v10:
time: 144 us
  waiting for transfers between devices  60.9 us (42%)
  starting transfers between devices  47.5 us (33%)
  Pallas kernels  32.6 us (23%)
  local copies, waits for them, and re-layouts  2.21 us (2%)
    ppermute x50, waiting for transfers between devices, partner(): lax.ppermute(value, axis, [(i, i ^ offset) for i in range(lax.axis_size(a...  60.9 us
    ppermute x50, starting transfers between devices, partner(): lax.ppermute(value, axis, [(i, i ^ offset) for i in range(lax.axis_size(a...  47.5 us
    pallas_call x16, Pallas kernels, fused(): pl.pallas_call(kernel, out_shape=shapes, in_specs=[smem_block()] * (len(a...  10 us
    pallas_call x1, Pallas kernels, leaf_backward(): pl.pallas_call(leaf_backward_kernel, out_shape=[jax.ShapeDtypeStruct(leaf...  5.8 us
  transfers between devices with their start and end apart: 50, of which 21 were waited for; matrix products, arithmetic and copies ran while one was open for 0% of the time, Pallas kernels for 18%

profile of v10, /device:TPU:0, one launch (start us, length us, event | category | flops | bytes accessed | tf_op | source)
XLA Modules:
  0.0 144.2 jit_solution(2356882404261456404)
XLA Ops:
  0.7 2.2 %copy-done.2 = bf16[1,1024,2,1024]{3,2,1,0:T(2,128)(2,1)S(1)} copy-done((bf16[1,1024,2,1024]{3,2,1,0:T(2,128)(2,1)S(1)}, bf16[1,1024,2,1024]{3,2,1,0:T(2,128)(2,1)}, u32[]{:S(2)}) %copy-start.2) | copy-done | bytes 4194328
  2.9 2.7 %cut_maps.1 = (bf16[1024,512]{1,0:T(8,128)(2,1)S(1)}, bf16[512,512]{1,0:T(8,128)(2,1)}, bf16[512,512]{1,0:T(8,128)(2,1)S(1)}, bf16[1024,256]{1,0:T(8,128)(2,1)S(...) custom-call(s32[2]{0:T(128)S(1)} %pad_add_fusion.ids_ref.refs_0_, ...), custom_call_target="tpu_custom_call" | custom-call | tf_op jit(solution)/shard_map/cut_maps/pallas_call | solution.py:287
  5.7 3.0 %collective-permute-start.11 = (bf16[512,896]{1,0:T(8,128)(2,1)S(1)}, bf16[512,896]{1,0:T(8,128)(2,1)S(1)}, u32[]{:S(2)}, u32[]{:S(2)}) collective-permute-start(bf16[512,896]{1,0:T(8,128)(2,1)S(1)} %pack.6), channel_id=1, source_target_pairs={{0,4},{4,0},{8,12},{12,8},{16,20},{20,16},{24,28},{28,24},{1,5},{5... | collective-permute-start | bytes 2752520 | tf_op jit(solution)/shard_map/ppermute | solution.py:16
  8.7 2.1 %place.1 = (bf16[4,128,256]{2,1,0:T(8,128)(2,1)S(1)}, bf16[4,128,256]{2,1,0:T(8,128)(2,1)S(1)}, bf16[4,128,256]{2,1,0:T(8,128)(2,1)S(1)}, bf16[4,128,256]{2,1,0:...) custom-call(s32[2]{0:T(128)S(1)} %pad_add_fusion.ids_ref.refs_0_, s32[16]{0:T(128)S(1)} %copy-done.5, ...), custom_call_target="tpu_custom_call" | custom-call | tf_op jit(solution)/shard_map/place/pallas_call | solution.py:102
  14.9 2.6 %collective-permute-start.4 = (bf16[512,128]{1,0:T(8,128)(2,1)S(1)}, bf16[512,128]{1,0:T(8,128)(2,1)S(1)}, u32[]{:S(2)}, u32[]{:S(2)}) collective-permute-start(bf16[512,128]{1,0:T(8,128)(2,1)S(1)} %get-tuple-element.116), channel_id=1, source_target_pairs={{0,16},{4,20},{8,24},{12,28},{16,0},{20,4},{24,8},{28,12},{1,17},{... | collective-permute-start | bytes 393224 | tf_op jit(solution)/shard_map/ppermute | solution.py:16
  18.9 3.8 %collective-permute-done.4.refs_1_.refs_0_ = bf16[512,128]{1,0:T(8,128)(2,1)S(1)} collective-permute-done((bf16[512,128]{1,0:T(8,128)(2,1)S(1)}, bf16[512,128]{1,0:T(8,128)(2,1)S(1)}, u32[]{:S(2)}, u32[]{:S(2)}) %collective-permute-start.4) | collective-permute-done | bytes 131104 | tf_op jit(solution)/shard_map/ppermute | solution.py:16
  22.8 3.5 %collective-permute-start.7 = (bf16[512,256]{1,0:T(8,128)(2,1)S(1)}, bf16[512,256]{1,0:T(8,128)(2,1)S(1)}, u32[]{:S(2)}, u32[]{:S(2)}) collective-permute-start(bf16[512,256]{1,0:T(8,128)(2,1)S(1)} %pack.4), channel_id=1, source_target_pairs={{0,8},{4,12},{8,0},{12,4},{16,24},{20,28},{24,16},{28,20},{1,9},{5... | collective-permute-start | bytes 786440 | tf_op jit(solution)/shard_map/ppermute | solution.py:16
  29.5 3.3 %collective-permute-done.8.refs_2_.refs_6_ = f32[64,128]{1,0:T(8,128)S(1)} collective-permute-done((f32[64,128]{1,0:T(8,128)S(1)}, f32[64,128]{1,0:T(8,128)S(1)}, u32[]{:S(2)}, u32[]{:S(2)}) %collective-permute-start.8) | collective-permute-done | bytes 32800 | tf_op jit(solution)/shard_map/ppermute | solution.py:16
  37.2 5.5 %collective-permute-done.10.refs_2_ = bf16[512,256]{1,0:T(8,128)(2,1)S(1)} collective-permute-done((bf16[512,256]{1,0:T(8,128)(2,1)S(1)}, bf16[512,256]{1,0:T(8,128)(2,1)S(1)}, u32[]{:S(2)}, u32[]{:S(2)}) %collective-permute-start.10) | collective-permute-done | bytes 262176 | tf_op jit(solution)/shard_map/ppermute | solution.py:16
  42.7 2.6 %collective-permute-start.19 = (bf16[512,256]{1,0:T(8,128)(2,1)S(1)}, bf16[512,256]{1,0:T(8,128)(2,1)S(1)}, u32[]{:S(2)}, u32[]{:S(2)}) collective-permute-start(bf16[512,256]{1,0:T(8,128)(2,1)S(1)} %get-tuple-element.145.refs_0_), channel_id=1, source_target_pairs={{0,16},{4,20},{8,24},{12,28},{16,0},{20,4},{24,8},{28,12},{1,17},{... | collective-permute-start | bytes 786440 | tf_op jit(solution)/shard_map/ppermute | solution.py:16
  47.3 9.3 %collective-permute-done.19.refs_1_.refs_0_ = bf16[512,256]{1,0:T(8,128)(2,1)S(1)} collective-permute-done((bf16[512,256]{1,0:T(8,128)(2,1)S(1)}, bf16[512,256]{1,0:T(8,128)(2,1)S(1)}, u32[]{:S(2)}, u32[]{:S(2)}) %collective-permute-start.19) | collective-permute-done | bytes 262176 | tf_op jit(solution)/shard_map/ppermute | solution.py:16
  62.0 2.0 %collective-permute-start.20 = (bf16[32,1024]{1,0:T(8,128)(2,1)S(1)}, bf16[32,1024]{1,0:T(8,128)(2,1)S(1)}, u32[]{:S(2)}, u32[]{:S(2)}) collective-permute-start(bf16[32,1024]{1,0:T(8,128)(2,1)S(1)} %get-tuple-element.149), channel_id=1, source_target_pairs={{0,8},{4,12},{8,0},{12,4},{16,24},{20,28},{24,16},{28,20},{1,9},{5... | collective-permute-start | bytes 196616 | tf_op jit(solution)/shard_map/ppermute | solution.py:16
  64.0 2.0 %collective-permute-done.21.refs_9_.refs_1_.refs_5_ = bf16[128,1024]{1,0:T(8,128)(2,1)S(1)} collective-permute-done((bf16[128,1024]{1,0:T(8,128)(2,1)S(1)}, bf16[128,1024]{1,0:T(8,128)(2,1)S(1)}, u32[]{:S(2)}, u32[]{:S(2)}) %collective-permute-start.21) | collective-permute-done | bytes 262176 | tf_op jit(solution)/shard_map/ppermute | solution.py:16
  66.1 4.7 %collective-permute-done.20.refs_1_.refs_2_ = bf16[32,1024]{1,0:T(8,128)(2,1)S(1)} collective-permute-done((bf16[32,1024]{1,0:T(8,128)(2,1)S(1)}, bf16[32,1024]{1,0:T(8,128)(2,1)S(1)}, u32[]{:S(2)}, u32[]{:S(2)}) %collective-permute-start.20) | collective-permute-done | bytes 65568 | tf_op jit(solution)/shard_map/ppermute | solution.py:16
  72.8 3.4 %collective-permute-done.22.refs_1_.refs_2_ = bf16[16,1024]{1,0:T(8,128)(2,1)S(1)} collective-permute-done((bf16[16,1024]{1,0:T(8,128)(2,1)S(1)}, bf16[16,1024]{1,0:T(8,128)(2,1)S(1)}, u32[]{:S(2)}, u32[]{:S(2)}) %collective-permute-start.22) | collective-permute-done | bytes 32800 | tf_op jit(solution)/shard_map/ppermute | solution.py:16
  78.1 1.8 %collective-permute-start.27 = (f32[64,128]{1,0:T(8,128)S(1)}, f32[64,128]{1,0:T(8,128)S(1)}, u32[]{:S(2)}, u32[]{:S(2)}) collective-permute-start(f32[64,128]{1,0:T(8,128)S(1)} %stack.13), channel_id=1, source_target_pairs={{0,8},{4,12},{8,0},{12,4},{16,24},{20,28},{24,16},{28,20},{1,9},{5... | collective-permute-start | bytes 98312 | tf_op jit(solution)/shard_map/ppermute | solution.py:16
  84.0 1.7 %head.1 = (bf16[32,1024]{1,0:T(8,128)(2,1)S(1)}, bf16[32,512]{1,0:T(8,128)(2,1)S(1)}, bf16[32,512]{1,0:T(8,128)(2,1)S(1)}, f32[16,1024]{1,0:T(8,128)S(1)}, bf16[...) custom-call(s32[2]{0:T(128)S(1)} %pad_add_fusion.ids_ref.refs_0_, bf16[16,1024]{1,0:T(8,128)(2,1)S(1)} %top_forward.1.refs_1_, ...), custom_call_target="tpu_custom_call" | custom-call | tf_op jit(solution)/shard_map/head/pallas_call | solution.py:226
  85.9 1.7 %collective-permute-start.32 = (bf16[32,1024]{1,0:T(8,128)(2,1)S(1)}, bf16[32,1024]{1,0:T(8,128)(2,1)S(1)}, u32[]{:S(2)}, u32[]{:S(2)}) collective-permute-start(bf16[32,1024]{1,0:T(8,128)(2,1)S(1)} %get-tuple-element.165.refs_10_.refs_2_.refs_12_), channel_id=1, source_target_pairs={{0,16},{4,20},{8,24},{12,28},{16,0},{20,4},{24,8},{28,12},{1,17},{... | collective-permute-start | bytes 196616 | tf_op jit(solution)/shard_map/ppermute | solution.py:16
  88.1 3.4 %collective-permute-done.29.refs_4_ = bf16[16,1024]{1,0:T(8,128)(2,1)S(1)} collective-permute-done((bf16[16,1024]{1,0:T(8,128)(2,1)S(1)}, bf16[16,1024]{1,0:T(8,128)(2,1)S(1)}, u32[]{:S(2)}, u32[]{:S(2)}) %collective-permute-start.29) | collective-permute-done | bytes 32800 | tf_op jit(solution)/shard_map/ppermute | solution.py:16
  95.9 3.2 %collective-permute-done.33.refs_5_ = bf16[16,1024]{1,0:T(8,128)(2,1)S(1)} collective-permute-done((bf16[16,1024]{1,0:T(8,128)(2,1)S(1)}, bf16[16,1024]{1,0:T(8,128)(2,1)S(1)}, u32[]{:S(2)}, u32[]{:S(2)}) %collective-permute-start.33) | collective-permute-done | bytes 32800 | tf_op jit(solution)/shard_map/ppermute | solution.py:16
  104.6 1.7 %collective-permute-done.35.refs_5_ = bf16[32,1024]{1,0:T(8,128)(2,1)S(1)} collective-permute-done((bf16[32,1024]{1,0:T(8,128)(2,1)S(1)}, bf16[32,1024]{1,0:T(8,128)(2,1)S(1)}, u32[]{:S(2)}, u32[]{:S(2)}) %collective-permute-start.35) | collective-permute-done | bytes 65568 | tf_op jit(solution)/shard_map/ppermute | solution.py:16
  106.4 2.6 %collective-permute-done.36.refs_7_ = bf16[32,1024]{1,0:T(8,128)(2,1)S(1)} collective-permute-done((bf16[32,1024]{1,0:T(8,128)(2,1)S(1)}, bf16[32,1024]{1,0:T(8,128)(2,1)S(1)}, u32[]{:S(2)}, u32[]{:S(2)}) %collective-permute-start.36) | collective-permute-done | bytes 65568 | tf_op jit(solution)/shard_map/ppermute | solution.py:16
  111.3 1.9 %collective-permute-start.40 = (bf16[64,1024]{1,0:T(8,128)(2,1)S(1)}, bf16[64,1024]{1,0:T(8,128)(2,1)S(1)}, u32[]{:S(2)}, u32[]{:S(2)}) collective-permute-start(bf16[64,1024]{1,0:T(8,128)(2,1)S(1)} %get-tuple-element.183), channel_id=1, source_target_pairs={{0,8},{4,12},{8,0},{12,4},{16,24},{20,28},{24,16},{28,20},{1,9},{5... | collective-permute-start | bytes 393224 | tf_op jit(solution)/shard_map/ppermute | solution.py:16
  113.6 2.0 %collective-permute-done.39.refs_6_ = bf16[64,1024]{1,0:T(8,128)(2,1)S(1)} collective-permute-done((bf16[64,1024]{1,0:T(8,128)(2,1)S(1)}, bf16[64,1024]{1,0:T(8,128)(2,1)S(1)}, u32[]{:S(2)}, u32[]{:S(2)}) %collective-permute-start.39) | collective-permute-done | bytes 131104 | tf_op jit(solution)/shard_map/ppermute | solution.py:16
  116.3 1.7 %mid_back.1 = (bf16[128,1024]{1,0:T(8,128)(2,1)S(1)}, bf16[128,1024]{1,0:T(8,128)(2,1)S(1)}, bf16[128,1024]{1,0:T(8,128)(2,1)S(1)}, bf16[128,512]{1,0:T(8,128)(2...) custom-call(s32[2]{0:T(128)S(1)} %pad_add_fusion.ids_ref.refs_0_, ...), custom_call_target="tpu_custom_call" | custom-call | tf_op jit(solution)/shard_map/mid_back/pallas_call | solution.py:226
  120.1 2.1 %leaf_first.1.refs_14_ = bf16[4,256,1024]{2,1,0:T(8,128)(2,1)S(1)} custom-call(bf16[4,128,256]{2,1,0:T(8,128)(2,1)S(1)} %get-tuple-element.105.refs_0_, bf16[4,128,256]{2,1,0:T(8,128)(2,1)S(1)} %collective-permute-done.refs_1_, bf16[128,1024]{1,0:T(8,128)(2,1)S(1)} %get-tuple-element.185.refs_2_.refs_8_, ...), custom_call_target="tpu_custom_call" | custom-call | tf_op jit(solution)/shard_map/leaf_first/pallas_call | solution.py:172
  122.2 3.9 %collective-permute-done.43.refs_1_ = bf16[128,896]{1,0:T(8,128)(2,1)S(1)} collective-permute-done((bf16[128,896]{1,0:T(8,128)(2,1)S(1)}, bf16[128,896]{1,0:T(8,128)(2,1)S(1)}, u32[]{:S(2)}, u32[]{:S(2)}) %collective-permute-start.43) | collective-permute-done | bytes 229408 | tf_op jit(solution)/shard_map/ppermute | solution.py:16
  129.4 2.3 %collective-permute-done.44.refs_11_ = bf16[128,1024]{1,0:T(8,128)(2,1)S(1)} collective-permute-done((bf16[128,1024]{1,0:T(8,128)(2,1)S(1)}, bf16[128,1024]{1,0:T(8,128)(2,1)S(1)}, u32[]{:S(2)}, u32[]{:S(2)}) %collective-permute-start.44) | collective-permute-done | bytes 262176 | tf_op jit(solution)/shard_map/ppermute | solution.py:16
  131.7 5.8 %leaf_backward.1 = (bf16[4,256,1024]{2,1,0:T(8,128)(2,1)}, bf16[1024,1024]{1,0:T(8,128)(2,1)}) custom-call(bf16[4,128,256]{2,1,0:T(8,128)(2,1)S(1)} %get-tuple-element.105.refs_0_, bf16[4,128,256]{2,1,0:T(8,128)(2,1)S(1)} %collective-permute-done.refs_1_, bf16[4,128,256]{2,1,0:T(8,128)(2,1)S(1)} %collective-permute-done.1.refs_0_.refs_2_, ...), custom_call_target="tpu_custom_call" | custom-call | tf_op jit(solution)/shard_map/leaf_backward/pallas_call | solution.py:196
  137.5 2.2 %collective-permute-done.47.refs_1_ = bf16[256,1024]{1,0:T(8,128)(2,1)S(1)} collective-permute-done((bf16[256,1024]{1,0:T(8,128)(2,1)S(1)}, bf16[256,1024]{1,0:T(8,128)(2,1)S(1)}, u32[]{:S(2)}, u32[]{:S(2)}) %collective-permute-start.47) | collective-permute-done | bytes 524320 | tf_op jit(solution)/shard_map/ppermute | solution.py:16
  139.7 1.9 %collective-permute-done.49.refs_3_ = bf16[256,1024]{1,0:T(8,128)(2,1)S(1)} collective-permute-done((bf16[256,1024]{1,0:T(8,128)(2,1)S(1)}, bf16[256,1024]{1,0:T(8,128)(2,1)S(1)}, u32[]{:S(2)}, u32[]{:S(2)}) %collective-permute-start.49) | collective-permute-done | bytes 524320 | tf_op jit(solution)/shard_map/ppermute | solution.py:16
  141.6 2.6 %upper_grads.1 = bf16[256,2,1024]{2,1,0:T(2,128)(2,1)} custom-call(s32[2]{0:T(128)S(1)} %pad_add_fusion.ids_ref.refs_0_, bf16[384,512]{1,0:T(8,128)(2,1)S(1)} %collective-permute-done.38.first_ref, bf16[512,512]{1,0:T(8,128)(2,1)S(1)} %collective-permute-done.45.second_ref, bf16[1792,256]{1,0:T(8,128)(2,1)S(1)} %collective-permute-done.46.near_ref, ...), custom_call_target="tpu_custom_call" | custom-call | tf_op jit(solution)/shard_map/upper_grads/pallas_call | solution.py:677
  (110 shorter events, 48.0 us)
Async XLA Ops:
  5.7 27.8 %collective-permute-start.11 = (bf16[512,896]{1,0:T(8,128)(2,1)S(1)}, bf16[512,896]{1,0:T(8,128)(2,1)S(1)}, u32[]{:S(2)}, u32[]{:S(2)}) collective-permute-start(bf16[512,896]{1,0:T(8,128)(2,1)S(1)} %pack.6), channel_id=1, source_target_pairs={{0,4},{4,0},{8,12},{12,8},{16,20},{20,16},{24,28},{28,24},{1,5},{5... | collective-permute-start | bytes 2752520 | tf_op jit(solution)/shard_map/ppermute | solution.py:16
  10.8 15.4 %collective-permute-start.1 = (bf16[4,128,256]{2,1,0:T(8,128)(2,1)S(1)}, bf16[4,128,256]{2,1,0:T(8,128)(2,1)S(1)}, u32[]{:S(2)}, u32[]{:S(2)}) collective-permute-start(bf16[4,128,256]{2,1,0:T(8,128)(2,1)S(1)} %get-tuple-element.107), channel_id=1, source_target_pairs={{0,2},{1,3},{2,0},{3,1},{4,6},{5,7},{6,4},{7,5},{8,10},{9,11},{10,... | collective-permute-start | bytes 786440 | tf_op jit(solution)/shard_map/ppermute | solution.py:16
  12.4 13.9 %collective-permute-start.3 = (bf16[512,256]{1,0:T(8,128)(2,1)S(1)}, bf16[512,256]{1,0:T(8,128)(2,1)S(1)}, u32[]{:S(2)}, u32[]{:S(2)}) collective-permute-start(bf16[512,256]{1,0:T(8,128)(2,1)S(1)} %get-tuple-element.113), channel_id=1, source_target_pairs={{0,8},{4,12},{8,0},{12,4},{16,24},{20,28},{24,16},{28,20},{1,9},{5... | collective-permute-start | bytes 786440 | tf_op jit(solution)/shard_map/ppermute | solution.py:16
  14.0 12.3 %collective-permute-start.2 = (bf16[4,128,256]{2,1,0:T(8,128)(2,1)S(1)}, bf16[4,128,256]{2,1,0:T(8,128)(2,1)S(1)}, u32[]{:S(2)}, u32[]{:S(2)}) collective-permute-start(bf16[4,128,256]{2,1,0:T(8,128)(2,1)S(1)} %get-tuple-element.108), channel_id=1, source_target_pairs={{0,3},{1,2},{2,1},{3,0},{4,7},{5,6},{6,5},{7,4},{8,11},{9,10},{10,... | collective-permute-start | bytes 786440 | tf_op jit(solution)/shard_map/ppermute | solution.py:16
  14.9 7.8 %collective-permute-start.4 = (bf16[512,128]{1,0:T(8,128)(2,1)S(1)}, bf16[512,128]{1,0:T(8,128)(2,1)S(1)}, u32[]{:S(2)}, u32[]{:S(2)}) collective-permute-start(bf16[512,128]{1,0:T(8,128)(2,1)S(1)} %get-tuple-element.116), channel_id=1, source_target_pairs={{0,16},{4,20},{8,24},{12,28},{16,0},{20,4},{24,8},{28,12},{1,17},{... | collective-permute-start | bytes 393224 | tf_op jit(solution)/shard_map/ppermute | solution.py:16
  22.8 10.6 %collective-permute-start.7 = (bf16[512,256]{1,0:T(8,128)(2,1)S(1)}, bf16[512,256]{1,0:T(8,128)(2,1)S(1)}, u32[]{:S(2)}, u32[]{:S(2)}) collective-permute-start(bf16[512,256]{1,0:T(8,128)(2,1)S(1)} %pack.4), channel_id=1, source_target_pairs={{0,8},{4,12},{8,0},{12,4},{16,24},{20,28},{24,16},{28,20},{1,9},{5... | collective-permute-start | bytes 786440 | tf_op jit(solution)/shard_map/ppermute | solution.py:16
  27.7 5.7 %collective-permute-start.6 = (bf16[128,1024]{1,0:T(8,128)(2,1)S(1)}, bf16[128,1024]{1,0:T(8,128)(2,1)S(1)}, u32[]{:S(2)}, u32[]{:S(2)}) collective-permute-start(bf16[128,1024]{1,0:T(8,128)(2,1)S(1)} %get-tuple-element.123), channel_id=1, source_target_pairs={{0,1},{1,0},{2,3},{3,2},{4,5},{5,4},{6,7},{7,6},{8,9},{9,8},{10,11... | collective-permute-start | bytes 786440 | tf_op jit(solution)/shard_map/ppermute | solution.py:16
  33.4 11.9 %collective-permute-start.12 = (bf16[512,896]{1,0:T(8,128)(2,1)S(1)}, bf16[512,896]{1,0:T(8,128)(2,1)S(1)}, u32[]{:S(2)}, u32[]{:S(2)}) collective-permute-start(bf16[512,896]{1,0:T(8,128)(2,1)S(1)} %collective-permute-done.11.refs_0_), channel_id=1, source_target_pairs={{0,1},{1,0},{2,3},{3,2},{4,5},{5,4},{6,7},{7,6},{8,9},{9,8},{10,11... | collective-permute-start | bytes 2752520 | tf_op jit(solution)/shard_map/ppermute | solution.py:16
  33.5 9.2 %collective-permute-start.10 = (bf16[512,256]{1,0:T(8,128)(2,1)S(1)}, bf16[512,256]{1,0:T(8,128)(2,1)S(1)}, u32[]{:S(2)}, u32[]{:S(2)}) collective-permute-start(bf16[512,256]{1,0:T(8,128)(2,1)S(1)} %collective-permute-done.3.refs_1_), channel_id=1, source_target_pairs={{0,4},{4,0},{8,12},{12,8},{16,20},{20,16},{24,28},{28,24},{1,5},{5... | collective-permute-start | bytes 786440 | tf_op jit(solution)/shard_map/ppermute | solution.py:16
  34.2 11.1 %collective-permute-start.9 = (bf16[128,1024]{1,0:T(8,128)(2,1)S(1)}, bf16[128,1024]{1,0:T(8,128)(2,1)S(1)}, u32[]{:S(2)}, u32[]{:S(2)}) collective-permute-start(bf16[128,1024]{1,0:T(8,128)(2,1)S(1)} %pair_product.1), channel_id=1, source_target_pairs={{0,2},{1,3},{2,0},{3,1},{4,6},{5,7},{6,4},{7,5},{8,10},{9,11},{10,... | collective-permute-start | bytes 786440 | tf_op jit(solution)/shard_map/ppermute | solution.py:16
  35.6 10.4 %collective-permute-start.5 = (bf16[128,1024]{1,0:T(8,128)(2,1)S(1)}, bf16[128,1024]{1,0:T(8,128)(2,1)S(1)}, u32[]{:S(2)}, u32[]{:S(2)}) collective-permute-start(bf16[128,1024]{1,0:T(8,128)(2,1)S(1)} %get-tuple-element.111), channel_id=1, source_target_pairs={{0,1},{1,0},{2,3},{3,2},{4,5},{5,4},{6,7},{7,6},{8,9},{9,8},{10,11... | collective-permute-start | bytes 786440 | tf_op jit(solution)/shard_map/ppermute | solution.py:16
  35.6 21.2 %collective-permute-start.16 = (bf16[512,384]{1,0:T(8,128)(2,1)S(1)}, bf16[512,384]{1,0:T(8,128)(2,1)S(1)}, u32[]{:S(2)}, u32[]{:S(2)}) collective-permute-start(bf16[512,384]{1,0:T(8,128)(2,1)S(1)} %pack.5.refs_1_), channel_id=1, source_target_pairs={{0,4},{4,0},{8,12},{12,8},{16,20},{20,16},{24,28},{28,24},{1,5},{5... | collective-permute-start | bytes 1179656 | tf_op jit(solution)/shard_map/ppermute | solution.py:16
  42.7 13.9 %collective-permute-start.19 = (bf16[512,256]{1,0:T(8,128)(2,1)S(1)}, bf16[512,256]{1,0:T(8,128)(2,1)S(1)}, u32[]{:S(2)}, u32[]{:S(2)}) collective-permute-start(bf16[512,256]{1,0:T(8,128)(2,1)S(1)} %get-tuple-element.145.refs_0_), channel_id=1, source_target_pairs={{0,16},{4,20},{8,24},{12,28},{16,0},{20,4},{24,8},{28,12},{1,17},{... | collective-permute-start | bytes 786440 | tf_op jit(solution)/shard_map/ppermute | solution.py:16
  46.7 9.9 %collective-permute-start.13 = (bf16[64,1024]{1,0:T(8,128)(2,1)S(1)}, bf16[64,1024]{1,0:T(8,128)(2,1)S(1)}, u32[]{:S(2)}, u32[]{:S(2)}) collective-permute-start(bf16[64,1024]{1,0:T(8,128)(2,1)S(1)} %get-tuple-element.137), channel_id=1, source_target_pairs={{0,4},{4,0},{8,12},{12,8},{16,20},{20,16},{24,28},{28,24},{1,5},{5... | collective-permute-start | bytes 393224 | tf_op jit(solution)/shard_map/ppermute | solution.py:16
  47.3 10.1 %collective-permute-start.14 = (bf16[512,256]{1,0:T(8,128)(2,1)S(1)}, bf16[512,256]{1,0:T(8,128)(2,1)S(1)}, u32[]{:S(2)}, u32[]{:S(2)}) collective-permute-start(bf16[512,256]{1,0:T(8,128)(2,1)S(1)} %collective-permute-done.3.refs_1_), channel_id=1, source_target_pairs={{0,1},{1,0},{2,3},{3,2},{4,5},{5,4},{6,7},{7,6},{8,9},{9,8},{10,11... | collective-permute-start | bytes 786440 | tf_op jit(solution)/shard_map/ppermute | solution.py:16
  56.7 19.6 %collective-permute-start.24 = (bf16[512,512]{1,0:T(8,128)(2,1)S(1)}, bf16[512,512]{1,0:T(8,128)(2,1)S(1)}, u32[]{:S(2)}, u32[]{:S(2)}) collective-permute-start(bf16[512,512]{1,0:T(8,128)(2,1)S(1)} %pack.7), channel_id=1, source_target_pairs={{0,8},{4,12},{8,0},{12,4},{16,24},{20,28},{24,16},{28,20},{1,9},{5... | collective-permute-start | bytes 1572872 | tf_op jit(solution)/shard_map/ppermute | solution.py:16
  57.4 8.7 %collective-permute-start.21 = (bf16[128,1024]{1,0:T(8,128)(2,1)S(1)}, bf16[128,1024]{1,0:T(8,128)(2,1)S(1)}, u32[]{:S(2)}, u32[]{:S(2)}) collective-permute-start(bf16[128,1024]{1,0:T(8,128)(2,1)S(1)} %get-tuple-element.201.refs_8_.refs_0_.refs_4_), channel_id=1, source_target_pairs={{0,4},{4,0},{8,12},{12,8},{16,20},{20,16},{24,28},{28,24},{1,5},{5... | collective-permute-start | bytes 786440 | tf_op jit(solution)/shard_map/ppermute | solution.py:16
  62.0 8.8 %collective-permute-start.20 = (bf16[32,1024]{1,0:T(8,128)(2,1)S(1)}, bf16[32,1024]{1,0:T(8,128)(2,1)S(1)}, u32[]{:S(2)}, u32[]{:S(2)}) collective-permute-start(bf16[32,1024]{1,0:T(8,128)(2,1)S(1)} %get-tuple-element.149), channel_id=1, source_target_pairs={{0,8},{4,12},{8,0},{12,4},{16,24},{20,28},{24,16},{28,20},{1,9},{5... | collective-permute-start | bytes 196616 | tf_op jit(solution)/shard_map/ppermute | solution.py:16
  76.7 7.3 %collective-permute-start.28 = (bf16[32,1024]{1,0:T(8,128)(2,1)S(1)}, bf16[32,1024]{1,0:T(8,128)(2,1)S(1)}, u32[]{:S(2)}, u32[]{:S(2)}) collective-permute-start(bf16[32,1024]{1,0:T(8,128)(2,1)S(1)} %get-tuple-element.159.refs_7_.refs_13_.refs_8_.refs_9_), channel_id=1, source_target_pairs={{0,16},{4,20},{8,24},{12,28},{16,0},{20,4},{24,8},{28,12},{1,17},{... | collective-permute-start | bytes 196616 | tf_op jit(solution)/shard_map/ppermute | solution.py:16
  80.6 7.5 %collective-permute-start.30 = (bf16[64,1024]{1,0:T(8,128)(2,1)S(1)}, bf16[64,1024]{1,0:T(8,128)(2,1)S(1)}, u32[]{:S(2)}, u32[]{:S(2)}) collective-permute-start(bf16[64,1024]{1,0:T(8,128)(2,1)S(1)} %get-tuple-element.163.refs_5_.refs_10_.refs_6_), channel_id=1, source_target_pairs={{0,8},{4,12},{8,0},{12,4},{16,24},{20,28},{24,16},{28,20},{1,9},{5... | collective-permute-start | bytes 393224 | tf_op jit(solution)/shard_map/ppermute | solution.py:16
  85.7 5.9 %collective-permute-start.31 = (bf16[64,1024]{1,0:T(8,128)(2,1)S(1)}, bf16[64,1024]{1,0:T(8,128)(2,1)S(1)}, u32[]{:S(2)}, u32[]{:S(2)}) collective-permute-start(bf16[64,1024]{1,0:T(8,128)(2,1)S(1)} %get-tuple-element.164), channel_id=1, source_target_pairs={{0,8},{4,12},{8,0},{12,4},{16,24},{20,28},{24,16},{28,20},{1,9},{5... | collective-permute-start | bytes 393224 | tf_op jit(solution)/shard_map/ppermute | solution.py:16
  85.9 5.6 %collective-permute-start.32 = (bf16[32,1024]{1,0:T(8,128)(2,1)S(1)}, bf16[32,1024]{1,0:T(8,128)(2,1)S(1)}, u32[]{:S(2)}, u32[]{:S(2)}) collective-permute-start(bf16[32,1024]{1,0:T(8,128)(2,1)S(1)} %get-tuple-element.165.refs_10_.refs_2_.refs_12_), channel_id=1, source_target_pairs={{0,16},{4,20},{8,24},{12,28},{16,0},{20,4},{24,8},{28,12},{1,17},{... | collective-permute-start | bytes 196616 | tf_op jit(solution)/shard_map/ppermute | solution.py:16
  92.3 16.7 %collective-permute-start.37 = (bf16[256,1024]{1,0:T(8,128)(2,1)S(1)}, bf16[256,1024]{1,0:T(8,128)(2,1)S(1)}, u32[]{:S(2)}, u32[]{:S(2)}) collective-permute-start(bf16[256,1024]{1,0:T(8,128)(2,1)S(1)} %get-tuple-element.177), channel_id=1, source_target_pairs={{0,4},{4,0},{8,12},{12,8},{16,20},{20,16},{24,28},{28,24},{1,5},{5... | collective-permute-start | bytes 1572872 | tf_op jit(solution)/shard_map/ppermute | solution.py:16
  93.0 6.1 %collective-permute-start.34 = (bf16[64,1024]{1,0:T(8,128)(2,1)S(1)}, bf16[64,1024]{1,0:T(8,128)(2,1)S(1)}, u32[]{:S(2)}, u32[]{:S(2)}) collective-permute-start(bf16[64,1024]{1,0:T(8,128)(2,1)S(1)} %get-tuple-element.170), channel_id=1, source_target_pairs={{0,8},{4,12},{8,0},{12,4},{16,24},{20,28},{24,16},{28,20},{1,9},{5... | collective-permute-start | bytes 393224 | tf_op jit(solution)/shard_map/ppermute | solution.py:16
  100.6 13.0 %collective-permute-start.38 = (bf16[384,512]{1,0:T(8,128)(2,1)S(1)}, bf16[384,512]{1,0:T(8,128)(2,1)S(1)}, u32[]{:S(2)}, u32[]{:S(2)}) collective-permute-start(bf16[384,512]{1,0:T(8,128)(2,1)S(1)} %get-tuple-element.179), channel_id=1, source_target_pairs={{0,2},{1,3},{2,0},{3,1},{4,6},{5,7},{6,4},{7,5},{8,10},{9,11},{10,... | collective-permute-start | bytes 1179656 | tf_op jit(solution)/shard_map/ppermute | solution.py:16
  103.1 5.9 %collective-permute-start.36 = (bf16[32,1024]{1,0:T(8,128)(2,1)S(1)}, bf16[32,1024]{1,0:T(8,128)(2,1)S(1)}, u32[]{:S(2)}, u32[]{:S(2)}) collective-permute-start(bf16[32,1024]{1,0:T(8,128)(2,1)S(1)} %get-tuple-element.174), channel_id=1, source_target_pairs={{0,16},{4,20},{8,24},{12,28},{16,0},{20,4},{24,8},{28,12},{1,17},{... | collective-permute-start | bytes 196616 | tf_op jit(solution)/shard_map/ppermute | solution.py:16
  113.2 15.0 %collective-permute-start.45 = (bf16[512,512]{1,0:T(8,128)(2,1)S(1)}, bf16[512,512]{1,0:T(8,128)(2,1)S(1)}, u32[]{:S(2)}, u32[]{:S(2)}) collective-permute-start(bf16[512,512]{1,0:T(8,128)(2,1)S(1)} %get-tuple-element.200), channel_id=1, source_target_pairs={{0,2},{1,3},{2,0},{3,1},{4,6},{5,7},{6,4},{7,5},{8,10},{9,11},{10,... | collective-permute-start | bytes 1572872 | tf_op jit(solution)/shard_map/ppermute | solution.py:16
  118.0 8.0 %collective-permute-start.43 = (bf16[128,896]{1,0:T(8,128)(2,1)S(1)}, bf16[128,896]{1,0:T(8,128)(2,1)S(1)}, u32[]{:S(2)}, u32[]{:S(2)}) collective-permute-start(bf16[128,896]{1,0:T(8,128)(2,1)S(1)} %get-tuple-element.190), channel_id=1, source_target_pairs={{0,4},{4,0},{8,12},{12,8},{16,20},{20,16},{24,28},{28,24},{1,5},{5... | collective-permute-start | bytes 688136 | tf_op jit(solution)/shard_map/ppermute | solution.py:16
  119.5 8.5 %collective-permute-start.42 = (bf16[128,1024]{1,0:T(8,128)(2,1)S(1)}, bf16[128,1024]{1,0:T(8,128)(2,1)S(1)}, u32[]{:S(2)}, u32[]{:S(2)}) collective-permute-start(bf16[128,1024]{1,0:T(8,128)(2,1)S(1)} %get-tuple-element.187), channel_id=1, source_target_pairs={{0,2},{1,3},{2,0},{3,1},{4,6},{5,7},{6,4},{7,5},{8,10},{9,11},{10,... | collective-permute-start | bytes 786440 | tf_op jit(solution)/shard_map/ppermute | solution.py:16
  126.1 13.6 %collective-permute-start.47 = (bf16[256,1024]{1,0:T(8,128)(2,1)S(1)}, bf16[256,1024]{1,0:T(8,128)(2,1)S(1)}, u32[]{:S(2)}, u32[]{:S(2)}) collective-permute-start(bf16[256,1024]{1,0:T(8,128)(2,1)S(1)} %side_by_side.1.refs_0_), channel_id=1, source_target_pairs={{0,2},{1,3},{2,0},{3,1},{4,6},{5,7},{6,4},{7,5},{8,10},{9,11},{10,... | collective-permute-start | bytes 1572872 | tf_op jit(solution)/shard_map/ppermute | solution.py:16
  128.8 10.9 %collective-permute-start.46 = (bf16[1792,256]{1,0:T(8,128)(2,1)S(1)}, bf16[1792,256]{1,0:T(8,128)(2,1)S(1)}, u32[]{:S(2)}, u32[]{:S(2)}) collective-permute-start(bf16[1792,256]{1,0:T(8,128)(2,1)S(1)} %near_inputs.1), channel_id=1, source_target_pairs={{0,1},{1,0},{2,3},{3,2},{4,5},{5,4},{6,7},{7,6},{8,9},{9,8},{10,11... | collective-permute-start | bytes 2752520 | tf_op jit(solution)/shard_map/ppermute | solution.py:16
  129.4 10.3 %collective-permute-start.48 = (bf16[256,1024]{1,0:T(8,128)(2,1)S(1)}, bf16[256,1024]{1,0:T(8,128)(2,1)S(1)}, u32[]{:S(2)}, u32[]{:S(2)}) collective-permute-start(bf16[256,1024]{1,0:T(8,128)(2,1)S(1)} %side_by_side.1.refs_0_), channel_id=1, source_target_pairs={{0,1},{1,0},{2,3},{3,2},{4,5},{5,4},{6,7},{7,6},{8,9},{9,8},{10,11... | collective-permute-start | bytes 1572872 | tf_op jit(solution)/shard_map/ppermute | solution.py:16
  (24 other events, 114.8 us)
